TPU v7x, 32 devices: a whole 2x2x4 slice. The times are simulated.
32 devices in a mesh: seq: 8 (over y, x, core), fsdp: 4 (over z).
Axes of the slice: x: 2, y: 2, z: 4, core: 2. Of those that a mesh axis runs over, the one named last changes fastest.
Arguments:
- tokens: bfloat16 [4, 2048, 1024], P('fsdp', 'seq'), may hold values from -6 to 6
- norm1_gain: bfloat16 [1024], P(('seq', 'fsdp')), may hold values from 0.5 to 1.5
- qkv_weight: bfloat16 [1024, 3072], P(('seq', 'fsdp')), may hold values from -0.1875 to 0.1875
- gate_weight: bfloat16 [1024, 48], P(('seq', 'fsdp')), may hold values from -0.1875 to 0.1875
- conv_weight: bfloat16 [4, 3072], P(None, ('seq', 'fsdp')), may hold values from -2.5 to 2.5
- memory_w1: bfloat16 [16, 64, 256], P(None, None, ('seq', 'fsdp')), may hold values from -0.75 to 0.75
- memory_w2: bfloat16 [16, 256, 64], P(None, ('seq', 'fsdp')), may hold values from -0.375 to 0.375
- persistent_keys: bfloat16 [16, 1024], P(None, ('seq', 'fsdp')), may hold values from -9 to 9
- persistent_values: bfloat16 [16, 1024], P(None, ('seq', 'fsdp')), may hold values from -6 to 6
- out_weight: bfloat16 [1024, 1024], P(('seq', 'fsdp')), may hold values from -0.5 to 0.5
- norm2_gain: bfloat16 [1024], P(('seq', 'fsdp')), may hold values from 0.5 to 1.5
- ffn_gate: bfloat16 [1024, 4096], P('seq', 'fsdp'), may hold values from -0.1875 to 0.1875
- ffn_up: bfloat16 [1024, 4096], P('seq', 'fsdp'), may hold values from -0.1875 to 0.1875
- ffn_down: bfloat16 [4096, 1024], P('fsdp', 'seq'), may hold values from -0.09375 to 0.09375
- gate_bias: float32 [3, 16], replicated, may hold values from -1.5 to 1.5
- doc_lengths: int32 [4, 4], P('fsdp'), may hold values from 1 to 2045, as said below
- live_mask: int32 [4, 2048], P('fsdp', 'seq'), may hold values 0 or 1
- cotangent: bfloat16 [4, 2048, 1024], P('fsdp', 'seq'), may hold values from -6 to 6
Outputs:
- output: bfloat16 [4, 2048, 1024], P('fsdp', 'seq')
- input_grad: float32 [4, 2048, 1024], P('fsdp', 'seq')
- grad_norm1_gain: float32 [1024], P(('seq', 'fsdp'))
- grad_qkv_weight: float32 [1024, 3072], P(('seq', 'fsdp'))
- grad_gate_weight: float32 [1024, 48], P(('seq', 'fsdp'))
- grad_conv_weight: float32 [4, 3072], P(None, ('seq', 'fsdp'))
- grad_memory_w1: float32 [16, 64, 256], P(None, None, ('seq', 'fsdp'))
- grad_memory_w2: float32 [16, 256, 64], P(None, ('seq', 'fsdp'))
- grad_persistent_keys: float32 [16, 1024], P(None, ('seq', 'fsdp'))
- grad_persistent_values: float32 [16, 1024], P(None, ('seq', 'fsdp'))
- grad_out_weight: float32 [1024, 1024], P(('seq', 'fsdp'))
- grad_norm2_gain: float32 [1024], P(('seq', 'fsdp'))
- grad_ffn_gate: float32 [1024, 4096], P('seq', 'fsdp')
- grad_ffn_up: float32 [1024, 4096], P('seq', 'fsdp')
- grad_ffn_down: float32 [4096, 1024], P('fsdp', 'seq')
- grad_gate_bias: float32 [3, 16], replicated
Inputs may be any that keep to these rules, and one draw needn't show every extreme that they name: `doc_lengths`: each row's 4 lengths sum to 2048; one document of each row, at a place drawn from the seed, spans all but fewer than 256 of its positions, and every other holds at most 64; in every row the document after the long one (cyclically) holds 1, and in one row all others hold 1.
All inputs are finite; a program needn't handle non-finite values. No bound on the sum of `live_mask` on one device may be relied on, other than what follows from the above.
Results may differ from a plain program's by a relative error of at most 0.023.
Values may be sent and summed in bfloat16 or wider, within the bound.
A program may use at most 512 MiB of HBM per device.

v0:
```python
from functools import partial

import jax
import jax.numpy as jnp
from jax import lax
from jax.sharding import PartitionSpec as P

HEAD_COUNT = 16
HEAD_SIZE = 64
MH = 256
P_SIZE = 16
SEG = 256


EXACT_PRECISION = lax.Precision.HIGHEST
NORM_EPS = 1e-05
UNIT_EPS = 1e-06
SCORE_SCALE = 8.0
MEMORY_SCALE = 8.0
THETA_SCALE = 0.0005
MASKED = -1000000000.0
HEAD_GROUPS = 4


def shifted(value, axis, steps):
    count = lax.axis_size(axis)
    first, last = (max(0, -steps), min(count, count - steps))
    return lax.ppermute(value, axis, [(source, source + steps) for source in range(first, last)])


def prefix_2(array, axis, combine, identity, reverse):
    count, mine = (lax.axis_size(axis), lax.axis_index(axis))
    everything = jax.tree.map(
        lambda part, kind: lax.all_gather(part.astype(kind), axis),
        array,
        jax.tree.map(lambda a: jnp.bfloat16 if a.dtype == jnp.float32 else a.dtype, array),
    )
    start = jax.tree.map(
        lambda part, zero: jnp.broadcast_to(jnp.asarray(zero, part.dtype), part.shape),
        array,
        identity,
    )

    def step(k, before):
        at = count - 1 - k if reverse else k
        reached = at > mine if reverse else at < mine
        new = combine(
            before, jax.tree.map(lambda part, own: part[at].astype(own.dtype), everything, array)
        )
        return jax.tree.map(lambda a, b: jnp.where(reached, a, b), new, before)

    return lax.fori_loop(0, count, step, start)


def rms_scale(values, gain_row):
    return (
        values * lax.rsqrt(jnp.mean(values * values, axis=-1, keepdims=True) + NORM_EPS) * gain_row
    )


def unit_heads(values):
    shaped = values.reshape(values.shape[0], HEAD_COUNT, HEAD_SIZE)
    shaped = shaped * lax.rsqrt(jnp.sum(shaped * shaped, axis=-1, keepdims=True) + UNIT_EPS)
    return shaped.reshape(values.shape[0], HEAD_COUNT * HEAD_SIZE)


def swish_derivative(values):
    sigmoid_rows = jax.nn.sigmoid(values)
    return sigmoid_rows * (1.0 + values * (1.0 - sigmoid_rows))


def doc_table(lengths, positions):
    starts = jnp.cumsum(lengths) - lengths
    inside = starts[None, :] <= positions[:, None]
    doc_number = jnp.sum(inside.astype(jnp.int32), axis=1) - 1
    doc_begin = jnp.max(jnp.where(inside, starts[None, :], -1), axis=1)
    return (doc_number, doc_begin)


def same_table(ext_number, doc_number):
    length = doc_number.shape[0]
    return jnp.stack(
        [
            (ext_number[3 - offset : 3 - offset + length] == doc_number).astype(jnp.float32)
            for offset in range(4)
        ]
    )


def gate_values(gate_input, gate_shift):
    forget_rate = jax.nn.sigmoid(gate_input[:, :HEAD_COUNT] + 3.0 * gate_shift[0] - 7.5)
    momentum_rate = jax.nn.sigmoid(gate_input[:, HEAD_COUNT : 2 * HEAD_COUNT] + gate_shift[1] + 1.5)
    step_size = THETA_SCALE * jax.nn.sigmoid(gate_input[:, 2 * HEAD_COUNT :] + gate_shift[2])
    return (forget_rate, momentum_rate, step_size)


def compose_pairs(later_pair, earlier_pair):
    return (
        later_pair[0] * earlier_pair[0],
        later_pair[1] * earlier_pair[0] + later_pair[2] * earlier_pair[1],
        later_pair[2] * earlier_pair[2],
    )


def transition(
    key_rows,
    value_rows,
    gate_input,
    gate_shift,
    first_layer,
    layer_second_output,
    live_rows,
    fresh_rows,
):
    forget_rate, momentum_rate, step_size = gate_values(gate_input, gate_shift)
    element_count = key_rows.shape[0]
    key_heads = key_rows.reshape(element_count, HEAD_COUNT, HEAD_SIZE)
    value_head_split = value_rows.reshape(element_count, HEAD_COUNT, HEAD_SIZE)
    inner_hidden_rows = jnp.einsum(
        "thd,hdm->thm", key_heads, first_layer, precision=EXACT_PRECISION
    )
    hidden_activation = jax.nn.silu(inner_hidden_rows)
    residual_error_rows = (
        jnp.einsum(
            "fwq,wqz->fwz", hidden_activation, layer_second_output, precision=EXACT_PRECISION
        )
        - value_head_split
    )
    derivative_rows = jnp.einsum(
        "zkx,ksx->zks", residual_error_rows, layer_second_output, precision=EXACT_PRECISION
    ) * swish_derivative(inner_hidden_rows)
    keeping = 1.0 - fresh_rows[:, None]
    carry_gate = keeping * momentum_rate
    fade_gate = keeping * (1.0 - forget_rate)
    flipped = (jnp.flip(carry_gate, 0), jnp.flip(carry_gate, 0), jnp.flip(fade_gate, 0))
    inclusive = lax.associative_scan(compose_pairs, flipped)
    inclusive = tuple((jnp.flip(member, 0) for member in inclusive))
    ones_row = jnp.ones((1, HEAD_COUNT), jnp.float32)
    zeros_row = jnp.zeros((1, HEAD_COUNT), jnp.float32)
    after_keep = jnp.concatenate([inclusive[0][1:], ones_row], axis=0)
    after_mix = jnp.concatenate([inclusive[1][1:], zeros_row], axis=0)
    after_fade = jnp.concatenate([inclusive[2][1:], ones_row], axis=0)
    written = -step_size * live_rows[:, None]
    state_weight_matrix = written * after_keep
    memory_weight_matrix = written * (after_mix + after_fade)
    add_s1 = jnp.einsum(
        "thd,thm->hdm",
        state_weight_matrix[:, :, None] * key_heads,
        derivative_rows,
        precision=EXACT_PRECISION,
    )
    increment_second_state = jnp.einsum(
        "aig,ais->igs",
        state_weight_matrix[:, :, None] * hidden_activation,
        residual_error_rows,
        precision=EXACT_PRECISION,
    )
    add_w1 = jnp.einsum(
        "thd,thm->hdm",
        memory_weight_matrix[:, :, None] * key_heads,
        derivative_rows,
        precision=EXACT_PRECISION,
    )
    increment_second_weight = jnp.einsum(
        "aig,ais->igs",
        memory_weight_matrix[:, :, None] * hidden_activation,
        residual_error_rows,
        precision=EXACT_PRECISION,
    )
    return (
        inclusive[0][0],
        inclusive[2][0],
        inclusive[1][0],
        add_s1,
        increment_second_state,
        add_w1,
        increment_second_weight,
    )


def recall(queries, first_layer, layer_second_output):
    element_count = queries.shape[0]
    query_heads = queries.reshape(element_count, HEAD_COUNT, HEAD_SIZE)
    hidden_activation = jax.nn.silu(
        jnp.einsum("thd,hdm->thm", query_heads, first_layer, precision=EXACT_PRECISION)
    )
    return jnp.einsum(
        "fwq,wqz->fwz", hidden_activation, layer_second_output, precision=EXACT_PRECISION
    ).reshape(element_count, HEAD_COUNT * HEAD_SIZE)


def memory_read(queries, first_layer, layer_second_output, state_first, state_second, older):
    carried = recall(queries, first_layer + state_first, layer_second_output + state_second)
    initial = recall(queries, first_layer, layer_second_output)
    return older[:, None] * carried + (1.0 - older[:, None]) * initial


def conv_mix(extended, conv_taps, same_doc):
    length = extended.shape[0] - 3
    summed = jnp.zeros((length, extended.shape[1]), jnp.float32)
    for offset in range(4):
        summed = (
            summed
            + conv_taps[offset]
            * extended[3 - offset : 3 - offset + length]
            * same_doc[offset][:, None]
        )
    return summed


def head_view(scalars):
    return scalars[:, None, None]


def chain_forward(earlier, later):
    result = [
        later[0] * earlier[0],
        later[1] * earlier[1],
        later[2] * earlier[0] + later[1] * earlier[2],
    ]
    for member in range(2):
        result.append(head_view(later[0]) * earlier[3 + member] + later[3 + member])
    for member in range(2):
        result.append(
            head_view(later[2]) * earlier[3 + member]
            + head_view(later[1]) * earlier[5 + member]
            + later[5 + member]
        )
    return tuple(result)


def chain_backward(earlier, later):
    result = [
        later[0] * earlier[0],
        later[1] * earlier[1],
        later[0] * earlier[2] + later[2] * earlier[1],
    ]
    for member in range(2):
        result.append(
            head_view(later[0]) * earlier[3 + member]
            + head_view(later[2]) * earlier[5 + member]
            + later[3 + member]
        )
    for member in range(2):
        result.append(head_view(later[1]) * earlier[5 + member] + later[5 + member])
    return tuple(result)


def split_heads(rows, element_count):
    return rows.reshape(element_count, HEAD_GROUPS, HEAD_COUNT // HEAD_GROUPS, HEAD_SIZE).transpose(
        1, 2, 0, 3
    )


def join_heads(grouped):
    element_count = grouped.shape[2]
    return grouped.transpose(2, 0, 1, 3).reshape(element_count, HEAD_COUNT * HEAD_SIZE)


def group_scores(query_part, key_part, pkey_part, visible):
    fixed = jnp.einsum("hqd,hpd->hqp", query_part, pkey_part, preferred_element_type=jnp.float32)
    window = SCORE_SCALE * jnp.einsum(
        "hqd,hkd->hqk", query_part, key_part, preferred_element_type=jnp.float32
    )
    window = jnp.where(visible[None], window, MASKED)
    return jnp.concatenate([fixed, window], axis=-1)


def attend_forward(queries, key_rows, value_rows, persist_keys, persist_values, visible):

    def one_group(pieces):
        query_part, key_part, value_part, pkey_part, pvalue_part = pieces
        scores = group_scores(query_part, key_part, pkey_part, visible)
        highest = jnp.max(scores, axis=-1, keepdims=True)
        weights = jnp.exp(scores - highest)
        summed = jnp.sum(weights, axis=-1, keepdims=True)
        probs_low = (weights / summed).astype(jnp.bfloat16)
        merged = jnp.einsum(
            "hqp,hpd->hqd", probs_low[..., :P_SIZE], pvalue_part, preferred_element_type=jnp.float32
        )
        merged = merged + jnp.einsum(
            "hqk,hkd->hqd", probs_low[..., P_SIZE:], value_part, preferred_element_type=jnp.float32
        )
        return (merged, (highest + jnp.log(summed))[..., 0])

    seg_rows = queries.shape[0]
    merged, log_totals = lax.map(
        one_group,
        (
            split_heads(queries, seg_rows),
            split_heads(key_rows, 2 * seg_rows),
            split_heads(value_rows, 2 * seg_rows),
            split_heads(persist_keys, P_SIZE),
            split_heads(persist_values, P_SIZE),
        ),
    )
    return (join_heads(merged), log_totals)


def attend_backward(
    queries, key_rows, value_rows, persist_keys, persist_values, visible, log_totals, grad_rows
):

    def one_group(pieces):
        query_part, key_part, value_part, pkey_part, pvalue_part, total_part, grad_part = pieces
        scores = group_scores(query_part, key_part, pkey_part, visible)
        probs = jnp.exp(scores - total_part[..., None])
        probs_low = probs.astype(jnp.bfloat16)
        grad_probs = jnp.concatenate(
            [
                jnp.einsum(
                    "hqd,hpd->hqp", grad_part, pvalue_part, preferred_element_type=jnp.float32
                ),
                jnp.einsum(
                    "hqd,hkd->hqk", grad_part, value_part, preferred_element_type=jnp.float32
                ),
            ],
            axis=-1,
        )
        spread = jnp.sum(probs * grad_probs, axis=-1, keepdims=True)
        grad_scores = (probs * (grad_probs - spread)).astype(jnp.bfloat16)
        grad_query = jnp.einsum(
            "hqp,hpd->hqd", grad_scores[..., :P_SIZE], pkey_part, preferred_element_type=jnp.float32
        )
        grad_query = grad_query + SCORE_SCALE * jnp.einsum(
            "hqk,hkd->hqd", grad_scores[..., P_SIZE:], key_part, preferred_element_type=jnp.float32
        )
        grad_key = SCORE_SCALE * jnp.einsum(
            "hqk,hqd->hkd",
            grad_scores[..., P_SIZE:],
            query_part,
            preferred_element_type=jnp.float32,
        )
        grad_pkey = jnp.einsum(
            "hqp,hqd->hpd",
            grad_scores[..., :P_SIZE],
            query_part,
            preferred_element_type=jnp.float32,
        )
        grad_value = jnp.einsum(
            "hqk,hqd->hkd", probs_low[..., P_SIZE:], grad_part, preferred_element_type=jnp.float32
        )
        grad_pvalue = jnp.einsum(
            "hqp,hqd->hpd", probs_low[..., :P_SIZE], grad_part, preferred_element_type=jnp.float32
        )
        return (grad_query, grad_key, grad_value, grad_pkey, grad_pvalue)

    seg_rows = queries.shape[0]
    grouped = lax.map(
        one_group,
        (
            split_heads(queries, seg_rows),
            split_heads(key_rows, 2 * seg_rows),
            split_heads(value_rows, 2 * seg_rows),
            split_heads(persist_keys, P_SIZE),
            split_heads(persist_values, P_SIZE),
            log_totals,
            split_heads(grad_rows, seg_rows),
        ),
    )
    return tuple((join_heads(member) for member in grouped))


def on_device(
    tokens,
    norm1_gain,
    qkv_weight,
    gate_weight,
    conv_weight,
    memory_w1,
    memory_w2,
    persistent_keys,
    persistent_values,
    out_weight,
    norm2_gain,
    ffn_gate,
    ffn_up,
    ffn_down,
    gate_bias,
    doc_lengths,
    live_mask,
    cotangent,
):
    shards = (
        norm1_gain,
        qkv_weight,
        gate_weight,
        conv_weight,
        memory_w1,
        memory_w2,
        persistent_keys,
        persistent_values,
        out_weight,
        norm2_gain,
    )
    gathered = (
        lax.all_gather(shards[0], ("seq", "fsdp"), axis=0, tiled=True),
        lax.all_gather(shards[1], ("seq", "fsdp"), axis=0, tiled=True),
        lax.all_gather(shards[2], ("seq", "fsdp"), axis=0, tiled=True),
        lax.all_gather(shards[3], ("seq", "fsdp"), axis=1, tiled=True),
        lax.all_gather(shards[4], ("seq", "fsdp"), axis=2, tiled=True),
        lax.all_gather(shards[5], ("seq", "fsdp"), axis=1, tiled=True),
        lax.all_gather(shards[6], ("seq", "fsdp"), axis=1, tiled=True),
        lax.all_gather(shards[7], ("seq", "fsdp"), axis=1, tiled=True),
        lax.all_gather(shards[8], ("seq", "fsdp"), axis=0, tiled=True),
        lax.all_gather(shards[9], ("seq", "fsdp"), axis=0, tiled=True),
    )
    (
        gain_one,
        qkv_matrix,
        gate_matrix,
        conv_taps,
        memory_first,
        memory_second,
        persist_keys,
        persist_values,
        out_matrix,
        gain_two,
    ) = gathered
    ffn_parts = (
        lax.all_gather(ffn_gate, "seq", axis=0, tiled=True),
        lax.all_gather(ffn_up, "seq", axis=0, tiled=True),
        lax.all_gather(ffn_down, "seq", axis=1, tiled=True),
    )
    width = HEAD_COUNT * HEAD_SIZE
    inputs = tokens[0].astype(jnp.float32)
    lengths = doc_lengths[0]
    live_rows = live_mask[0].astype(jnp.float32)
    block_start = lax.axis_index("seq") * SEG
    positions = block_start + jnp.arange(SEG, dtype=jnp.int32)
    doc_number, doc_begin = doc_table(lengths, positions)
    prev_number = doc_table(lengths, positions - SEG)[0]
    normed_full, norm_one_pull = jax.vjp(rms_scale, inputs, gain_one.astype(jnp.float32))
    normed = normed_full.astype(jnp.bfloat16)
    raw_rows = jnp.dot(normed, qkv_matrix, preferred_element_type=jnp.float32).astype(jnp.bfloat16)
    gate_input = jnp.dot(normed, gate_matrix, preferred_element_type=jnp.float32)
    prev_rows = shifted(raw_rows[SEG - 3 :], "seq", 1)
    extended = jnp.concatenate([prev_rows, raw_rows], axis=0).astype(jnp.float32)
    same_doc = same_table(jnp.concatenate([prev_number[SEG - 3 :], doc_number]), doc_number)
    mixed_rows, conv_pull = jax.vjp(
        partial(conv_mix, same_doc=same_doc), extended, conv_taps.astype(jnp.float32)
    )
    query_unit, query_pull = jax.vjp(unit_heads, mixed_rows[:, :width])
    key_unit, key_pull = jax.vjp(unit_heads, mixed_rows[:, width : 2 * width])
    value_rows = mixed_rows[:, 2 * width :]
    query_att = query_unit.astype(jnp.bfloat16)
    key_att = key_unit.astype(jnp.bfloat16)
    value_att = value_rows.astype(jnp.bfloat16)
    prev_keys, prev_values, prev_live = shifted(
        (key_att, value_att, live_rows.astype(jnp.bfloat16)), "seq", 1
    )
    fresh_rows = (doc_begin == positions).astype(jnp.float32)
    older = (doc_begin < block_start).astype(jnp.float32)
    first_layer = memory_first.astype(jnp.float32)
    layer_second_output = memory_second.astype(jnp.float32)

    def local_change(key_part, value_part, input_part, shift_part, first_part, second_part):
        return transition(
            MEMORY_SCALE * key_part,
            value_part,
            input_part,
            shift_part,
            first_part,
            second_part,
            live_rows,
            fresh_rows,
        )

    change, change_pull = jax.vjp(
        local_change, key_unit, value_rows, gate_input, gate_bias, first_layer, layer_second_output
    )
    identity = (
        jnp.ones((HEAD_COUNT,), jnp.float32),
        jnp.ones((HEAD_COUNT,), jnp.float32),
        jnp.zeros((HEAD_COUNT,), jnp.float32),
        jnp.zeros((HEAD_COUNT, HEAD_SIZE, MH), jnp.float32),
        jnp.zeros((HEAD_COUNT, MH, HEAD_SIZE), jnp.float32),
        jnp.zeros((HEAD_COUNT, HEAD_SIZE, MH), jnp.float32),
        jnp.zeros((HEAD_COUNT, MH, HEAD_SIZE), jnp.float32),
    )
    prefix = prefix_2(change, "seq", chain_forward, identity, False)
    start_s1, start_s2, start_w1, start_w2 = (prefix[3], prefix[4], prefix[5], prefix[6])

    def local_recall(query_part, first_part, second_part, state_first, state_second):
        return memory_read(
            MEMORY_SCALE * query_part, first_part, second_part, state_first, state_second, older
        )

    recalled, recall_pull = jax.vjp(
        local_recall, query_unit, first_layer, layer_second_output, start_w1, start_w2
    )
    key_positions = jnp.concatenate([positions - SEG, positions])
    key_number = jnp.concatenate([prev_number, doc_number])
    key_live = jnp.concatenate([prev_live.astype(jnp.float32), live_rows])
    distance = positions[:, None] - key_positions[None, :]
    visible = (
        (key_number[None, :] == doc_number[:, None])
        & (key_live[None, :] > 0.5)
        & (distance >= 0)
        & (distance < SEG)
    )
    keys_all = jnp.concatenate([prev_keys, key_att], axis=0)
    values_all = jnp.concatenate([prev_values, value_att], axis=0)
    attended, log_totals = attend_forward(
        query_att, keys_all, values_all, persist_keys, persist_values, visible
    )
    combined = (attended + recalled).astype(jnp.bfloat16)
    middle = inputs + jnp.dot(combined, out_matrix, preferred_element_type=jnp.float32)
    normed_two_full, norm_two_pull = jax.vjp(rms_scale, middle, gain_two.astype(jnp.float32))
    normed_two = normed_two_full.astype(jnp.bfloat16)
    up_gate, up_matrix, down_matrix = (
        lax.all_gather(ffn_parts[0], "fsdp", axis=1, tiled=True),
        lax.all_gather(ffn_parts[1], "fsdp", axis=1, tiled=True),
        lax.all_gather(ffn_parts[2], "fsdp", axis=0, tiled=True),
    )
    ffn_cot = cotangent[0]
    gate_rows = jnp.dot(normed_two, up_gate, preferred_element_type=jnp.float32)
    up_rows = jnp.dot(normed_two, up_matrix, preferred_element_type=jnp.float32)
    gate_act = jax.nn.silu(gate_rows)
    hidden = (gate_act * up_rows).astype(jnp.bfloat16)
    down_part = jnp.dot(hidden, down_matrix, preferred_element_type=jnp.float32)
    output = (middle + down_part).astype(jnp.bfloat16)
    grad_out = cotangent[0]
    grad_down = jnp.dot(hidden.T, ffn_cot, preferred_element_type=jnp.float32)
    grad_hidden = jnp.dot(ffn_cot, down_matrix.T, preferred_element_type=jnp.float32)
    grad_gate = (grad_hidden * up_rows * swish_derivative(gate_rows)).astype(jnp.bfloat16)
    grad_up = (grad_hidden * gate_act).astype(jnp.bfloat16)
    grad_up_gate = jnp.dot(normed_two.T, grad_gate, preferred_element_type=jnp.float32)
    grad_up_matrix = jnp.dot(normed_two.T, grad_up, preferred_element_type=jnp.float32)
    normed_part = jnp.dot(grad_gate, up_gate.T, preferred_element_type=jnp.float32)
    normed_part = normed_part + jnp.dot(grad_up, up_matrix.T, preferred_element_type=jnp.float32)
    ffn_local = (
        lax.psum_scatter(
            grad_up_gate.astype(jnp.bfloat16), "fsdp", scatter_dimension=1, tiled=True
        ).astype(jnp.float32),
        lax.psum_scatter(
            grad_up_matrix.astype(jnp.bfloat16), "fsdp", scatter_dimension=1, tiled=True
        ).astype(jnp.float32),
        lax.psum_scatter(
            grad_down.astype(jnp.bfloat16), "fsdp", scatter_dimension=0, tiled=True
        ).astype(jnp.float32),
    )
    grad_middle_norm, grad_gain_two = norm_two_pull(normed_part)
    grad_middle = grad_out.astype(jnp.float32) + grad_middle_norm
    grad_branch = grad_middle.astype(jnp.bfloat16)
    grad_out_matrix = jnp.dot(combined.T, grad_branch, preferred_element_type=jnp.float32)
    grad_combined = jnp.dot(grad_branch, out_matrix.T, preferred_element_type=jnp.float32).astype(
        jnp.bfloat16
    )
    grad_query_att, grad_keys_all, grad_values_all, grad_pkeys, grad_pvalues = attend_backward(
        query_att,
        keys_all,
        values_all,
        persist_keys,
        persist_values,
        visible,
        log_totals,
        grad_combined,
    )
    grad_query_mem, grad_first_recall, grad_second_recall, grad_start_w1, grad_start_w2 = (
        recall_pull(grad_combined.astype(jnp.float32))
    )
    suffix = prefix_2(
        (
            change[0],
            change[1],
            change[2],
            jnp.zeros_like(start_s1),
            jnp.zeros_like(start_s2),
            grad_start_w1,
            grad_start_w2,
        ),
        "seq",
        chain_backward,
        identity,
        True,
    )
    late_s1, late_s2, late_w1, late_w2 = (suffix[3], suffix[4], suffix[5], suffix[6])
    grad_keep = jnp.sum(late_s1 * start_s1, axis=(1, 2)) + jnp.sum(late_s2 * start_s2, axis=(1, 2))
    grad_mix = jnp.sum(late_w1 * start_s1, axis=(1, 2)) + jnp.sum(late_w2 * start_s2, axis=(1, 2))
    grad_fade = jnp.sum(late_w1 * start_w1, axis=(1, 2)) + jnp.sum(late_w2 * start_w2, axis=(1, 2))
    (
        grad_key_mem,
        grad_value_mem,
        grad_gate_input,
        grad_shift,
        grad_first_change,
        grad_second_change,
    ) = change_pull((grad_keep, grad_fade, grad_mix, late_s1, late_s2, late_w1, late_w2))
    back_keys, back_values = (
        shifted(grad_keys_all[:SEG].astype(jnp.bfloat16), "seq", -1).astype(jnp.float32),
        shifted(grad_values_all[:SEG].astype(jnp.bfloat16), "seq", -1).astype(jnp.float32),
    )
    grad_key_unit = grad_keys_all[SEG:] + back_keys + grad_key_mem
    grad_value = grad_values_all[SEG:] + back_values + grad_value_mem
    grad_query_unit = grad_query_att + grad_query_mem
    grad_mixed = jnp.concatenate(
        [query_pull(grad_query_unit)[0], key_pull(grad_key_unit)[0], grad_value], axis=1
    )
    grad_extended, grad_taps = conv_pull(grad_mixed)
    back_rows = shifted(grad_extended[:3].astype(jnp.bfloat16), "seq", -1).astype(jnp.float32)
    grad_raw = grad_extended[3:] + jnp.concatenate(
        [jnp.zeros((SEG - 3, 3 * width), jnp.float32), back_rows], axis=0
    )
    grad_raw_low = grad_raw.astype(jnp.bfloat16)
    grad_qkv = jnp.dot(normed.T, grad_raw_low, preferred_element_type=jnp.float32)
    grad_gate_matrix = jnp.dot(
        normed.astype(jnp.float32).T, grad_gate_input, precision=EXACT_PRECISION
    )
    grad_normed = jnp.dot(grad_raw_low, qkv_matrix.T, preferred_element_type=jnp.float32)
    grad_normed = grad_normed + jnp.dot(
        grad_gate_input, gate_matrix.astype(jnp.float32).T, precision=EXACT_PRECISION
    )
    grad_inputs_norm, grad_gain_one = norm_one_pull(grad_normed)
    grad_inputs = grad_middle + grad_inputs_norm
    reduced = (
        lax.psum_scatter(grad_gain_one, ("seq", "fsdp"), scatter_dimension=0, tiled=True),
        lax.psum_scatter(grad_qkv, ("seq", "fsdp"), scatter_dimension=0, tiled=True),
        lax.psum_scatter(grad_gate_matrix, ("seq", "fsdp"), scatter_dimension=0, tiled=True),
        lax.psum_scatter(grad_taps, ("seq", "fsdp"), scatter_dimension=1, tiled=True),
        lax.psum_scatter(
            grad_first_recall + grad_first_change, ("seq", "fsdp"), scatter_dimension=2, tiled=True
        ),
        lax.psum_scatter(
            grad_second_recall + grad_second_change,
            ("seq", "fsdp"),
            scatter_dimension=1,
            tiled=True,
        ),
        lax.psum_scatter(grad_pkeys, ("seq", "fsdp"), scatter_dimension=1, tiled=True),
        lax.psum_scatter(grad_pvalues, ("seq", "fsdp"), scatter_dimension=1, tiled=True),
        lax.psum_scatter(grad_out_matrix, ("seq", "fsdp"), scatter_dimension=0, tiled=True),
        lax.psum_scatter(grad_gain_two, ("seq", "fsdp"), scatter_dimension=0, tiled=True),
    )
    ffn_reduced = (
        lax.psum_scatter(
            ffn_local[0].astype(jnp.bfloat16), "seq", scatter_dimension=0, tiled=True
        ).astype(jnp.float32),
        lax.psum_scatter(
            ffn_local[1].astype(jnp.bfloat16), "seq", scatter_dimension=0, tiled=True
        ).astype(jnp.float32),
        lax.psum_scatter(
            ffn_local[2].astype(jnp.bfloat16), "seq", scatter_dimension=1, tiled=True
        ).astype(jnp.float32),
    )
    grad_bias = lax.psum(grad_shift, ("seq", "fsdp"))
    return (output[None], grad_inputs[None]) + tuple(reduced) + tuple(ffn_reduced) + (grad_bias,)


def solution(mesh):
    return jax.shard_map(
        on_device,
        mesh=mesh,
        in_specs=(
            P("fsdp", "seq", None),
            P(("seq", "fsdp")),
            P(("seq", "fsdp"), None),
            P(("seq", "fsdp"), None),
            P(None, ("seq", "fsdp")),
            P(None, None, ("seq", "fsdp")),
            P(None, ("seq", "fsdp"), None),
            P(None, ("seq", "fsdp")),
            P(None, ("seq", "fsdp")),
            P(("seq", "fsdp"), None),
            P(("seq", "fsdp")),
            P("seq", "fsdp"),
            P("seq", "fsdp"),
            P("fsdp", "seq"),
            P(),
            P("fsdp", None),
            P("fsdp", "seq"),
            P("fsdp", "seq", None),
        ),
        out_specs=(
            P("fsdp", "seq", None),
            P("fsdp", "seq", None),
            P(("seq", "fsdp")),
            P(("seq", "fsdp"), None),
            P(("seq", "fsdp"), None),
            P(None, ("seq", "fsdp")),
            P(None, None, ("seq", "fsdp")),
            P(None, ("seq", "fsdp"), None),
            P(None, ("seq", "fsdp")),
            P(None, ("seq", "fsdp")),
            P(("seq", "fsdp"), None),
            P(("seq", "fsdp")),
            P("seq", "fsdp"),
            P("seq", "fsdp"),
            P("fsdp", "seq"),
            P(),
        ),
        check_vma=False,
    )
```

profile of v0, /device:TPU:0, one launch (start us, length us, event | category | flops | bytes accessed | tf_op | source)
XLA Modules:
  0.0 2883.6 jit_solution(10594986320753994637)
XLA Ops:
  13.4 42.1 %all-reduce.187 = (bf16[1024]{0:T(1024)(128)(2,1)S(1)}, bf16[1024]{0:T(1024)(128)(2,1)S(1)}) all-reduce(bf16[1024]{0:T(1024)(128)(2,1)S(1)} %dynamic-update-slice, bf16[1024]{0:T(1024)(128)(2,1)S(1)} %dynamic-update-slice.1), channel_id=1, replica_groups=mesh['seq'=8,'fsdp'=4] {'seq','fsdp'}, use_global_device_ids=true, to_apply=%add.182 | all-reduce | flops 2048 | bytes 8192
  57.3 70.0 %all_gather.112 = bf16[1024,48]{1,0:T(8,128)(2,1)S(1)} all-gather(bf16[32,48]{1,0:T(8,128)(2,1)} %param.29), channel_id=1, replica_groups=mesh['seq'=8,'fsdp'=4] {'seq','fsdp'}, dimensions={0}, use_global_device_ids=true | all-gather | bytes 101376 | tf_op jit(solution)/shard_map/all_gather | solution.py:399
  173.4 63.5 %all-gather.6 = bf16[32,96,4]{1,2,0:T(4,128)(2,1)S(1)} all-gather(bf16[1,96,4]{1,2,0:T(4,128)(2,1)S(1)} %bitcast.753), channel_id=1, replica_groups=mesh['seq'=8,'fsdp'=4] {'seq','fsdp'}, dimensions={0}, use_global_device_ids=true | all-gather | bytes 25344 | tf_op jit(solution)/shard_map/all_gather | solution.py:400
  237.2 74.6 %all_gather.114 = bf16[16,64,256]{1,0,2:T(8,128)(2,1)S(1)} all-gather(bf16[16,64,8]{1,0,2:T(8,128)(2,1)S(1)} %copy.489), channel_id=1, replica_groups=mesh['seq'=8,'fsdp'=4] {'seq','fsdp'}, dimensions={2}, use_global_device_ids=true | all-gather | bytes 540672 | tf_op jit(solution)/shard_map/all_gather | solution.py:401
  311.8 78.7 %all_gather.111 = bf16[16,256,64]{2,1,0:T(8,128)(2,1)} all-gather(bf16[16,8,64]{2,1,0:T(8,128)(2,1)S(1)} %copy-done.255), channel_id=1, replica_groups=mesh['seq'=8,'fsdp'=4] {'seq','fsdp'}, dimensions={1}, use_global_device_ids=true | all-gather | bytes 540672 | tf_op jit(solution)/shard_map/all_gather | solution.py:402
  503.1 65.2 %all-gather.7 = bf16[32,32,16]{1,2,0:T(8,128)(2,1)S(1)} all-gather(bf16[1,32,16]{1,2,0:T(8,128)(2,1)S(1)} %bitcast.745), channel_id=1, replica_groups=mesh['seq'=8,'fsdp'=4] {'seq','fsdp'}, dimensions={0}, use_global_device_ids=true | all-gather | bytes 33792 | tf_op jit(solution)/shard_map/all_gather | solution.py:403
  568.7 66.6 %all-gather.8 = bf16[32,32,16]{1,2,0:T(8,128)(2,1)S(1)} all-gather(bf16[1,32,16]{1,2,0:T(8,128)(2,1)S(1)} %bitcast.746), channel_id=1, replica_groups=mesh['seq'=8,'fsdp'=4] {'seq','fsdp'}, dimensions={0}, use_global_device_ids=true | all-gather | bytes 33792 | tf_op jit(solution)/shard_map/all_gather | solution.py:404
  690.6 90.1 %while.76 = (s32[]{:T(128)}, f32[16,64,256]{2,1,0:T(8,128)}, f32[16,256,64]{2,1,0:T(8,128)}, f32[16,64,256]{2,1,0:T(8,128)}, f32[16,256,64]{2,1,0:T(8,128)}, /*i...) while((s32[]{:T(128)}, f32[16,64,256]{2,1,0:T(8,128)}, ...), condition=%wide.region_13.14_spmd.clone, body=%wide.region_12.13_spmd.clone.sunk | while | flops 6291508 | bytes 31458244 | solution.py:52
  808.6 141.7 %all-gather.37.cloned.1.call-done = bf16[1024,4096]{1,0:T(8,128)(2,1)} async-done(((bf16[1024,1024]{1,0:T(8,128)(2,1)}), bf16[1024,4096]{1,0:T(8,128)(2,1)}) %all-gather.37.cloned.1.call-update) | async-done | bytes 8388624 | tf_op jit(solution)/shard_map/all_gather | solution.py:513
  958.3 141.2 %all-gather.41.cloned.1.call-done = bf16[4096,1024]{1,0:T(8,128)(2,1)} async-done(((bf16[1024,1024]{1,0:T(8,128)(2,1)}), bf16[4096,1024]{1,0:T(8,128)(2,1)}) %all-gather.41.cloned.1.call-update) | async-done | bytes 8388624 | tf_op jit(solution)/shard_map/all_gather | solution.py:514
  1176.4 89.0 %while.75 = (s32[]{:T(128)}, f32[4,4,256,64]{2,3,1,0:T(8,128)}, f32[4,4,512,64]{2,3,1,0:T(8,128)}, f32[4,4,512,64]{2,3,1,0:T(8,128)}, f32[4,4,16,64]{3,2,1,0:T(8...) while((s32[]{:T(128)}, f32[4,4,256,64]{2,3,1,0:T(8,128)}, ...), condition=%wide.region_18.19_spmd.clone, body=%wide.region_16.18_spmd.clone.sunk | while | flops 355288576 | bytes 20988080 | solution.py:349
  1313.6 90.8 %while.77 = (s32[]{:T(128)}, f32[16,64,256]{2,1,0:T(8,128)}, f32[16,256,64]{2,1,0:T(8,128)}, f32[16,64,256]{2,1,0:T(8,128)}, f32[16,256,64]{2,1,0:T(8,128)S(1)},...) while((s32[]{:T(128)}, f32[16,64,256]{2,1,0:T(8,128)}, ...), condition=%wide.region_21.22_spmd.clone, body=%wide.region_20.21_spmd.clone.sunk | while | flops 5242936 | bytes 11535233 | solution.py:52
  1597.5 54.6 %reduce-scatter.37.cloned.1.call-done = bf16[1024,1024]{1,0:T(8,128)(2,1)} async-done(((bf16[1024,4096]{1,0:T(8,128)(2,1)}), bf16[1024,1024]{1,0:T(8,128)(2,1)}) %reduce-scatter.37.cloned.1.call-update) | async-done | bytes 2097168 | tf_op jit(solution)/shard_map/reduce_scatter | solution.py:536
  1692.7 96.4 %reduce-scatter.45.cloned.1.call-done = f32[32,16]{1,0:T(8,128)} async-done(((f32[1024,16]{1,0:T(8,128)}), f32[32,16]{1,0:T(8,128)}) %reduce-scatter.45.cloned.1.call-update) | async-done | bytes 2064
  1790.4 132.3 %reduce-scatter.47.cloned.1.call-done = f32[32,16]{1,0:T(8,128)} async-done(((f32[1024,16]{1,0:T(8,128)}), f32[32,16]{1,0:T(8,128)}) %reduce-scatter.47.cloned.1.call-update) | async-done | bytes 2064
  1970.9 50.7 %reduce-scatter.43.cloned.1.call-done = f32[96,4]{1,0:T(8,128)} async-done(((f32[3072,4]{1,0:T(8,128)}), f32[96,4]{1,0:T(8,128)}) %reduce-scatter.43.cloned.1.call-update) | async-done | bytes 1552
  2023.0 138.0 %reduce-scatter.29.cloned.1.call-done = f32[16,8,64]{2,0,1:T(8,128)} async-done(((f32[16,256,64]{2,0,1:T(8,128)}), f32[16,8,64]{2,0,1:T(8,128)}) %reduce-scatter.29.cloned.1.call-update) | async-done | bytes 32784 | tf_op jit(solution)/shard_map/reduce_scatter | solution.py:624
  2162.5 137.3 %reduce-scatter.27.cloned.1.call-done = f32[16,64,8]{1,0,2:T(8,128)} async-done(((f32[16,64,256]{1,0,2:T(8,128)}), f32[16,64,8]{1,0,2:T(8,128)}) %reduce-scatter.27.cloned.1.call-update) | async-done | bytes 32784 | tf_op jit(solution)/shard_map/reduce_scatter | solution.py:621
  2301.4 41.0 %reduce-scatter.49.cloned.1.call-done = bf16[128,1024]{1,0:T(8,128)(2,1)} async-done(((bf16[1024,1024]{1,0:T(8,128)(2,1)}), bf16[128,1024]{1,0:T(8,128)(2,1)}) %reduce-scatter.49.cloned.1.call-update) | async-done | bytes 262160
  2344.3 42.8 %reduce-scatter.35.cloned.1.call-done = bf16[128,1024]{1,0:T(8,128)(2,1)} async-done(((bf16[1024,1024]{1,0:T(8,128)(2,1)}), bf16[128,1024]{1,0:T(8,128)(2,1)}) %reduce-scatter.35.cloned.1.call-update) | async-done | bytes 262160 | tf_op jit(solution)/shard_map/reduce_scatter | solution.py:636
  2388.9 42.7 %reduce-scatter.39.cloned.1.call-done = bf16[128,1024]{1,0:T(8,128)(2,1)} async-done(((bf16[1024,1024]{1,0:T(8,128)(2,1)}), bf16[128,1024]{1,0:T(8,128)(2,1)}) %reduce-scatter.39.cloned.1.call-update) | async-done | bytes 262160 | tf_op jit(solution)/shard_map/reduce_scatter | solution.py:639
  2433.4 135.5 %reduce-scatter.25.cloned.1.call-done = f32[32,48]{1,0:T(8,128)} async-done(((f32[1024,48]{1,0:T(8,128)}), f32[32,48]{1,0:T(8,128)}) %reduce-scatter.25.cloned.1.call-update) | async-done | bytes 6160 | tf_op jit(solution)/shard_map/reduce_scatter | solution.py:619
  2568.9 146.8 %reduce-scatter.31.cloned.1.call-done = f32[32,1024]{1,0:T(8,128)} async-done(((f32[1024,1024]{1,0:T(8,128)}), f32[32,1024]{1,0:T(8,128)}) %reduce-scatter.31.cloned.1.call-update) | async-done | bytes 131088 | tf_op jit(solution)/shard_map/reduce_scatter | solution.py:632
  2715.7 160.8 %reduce-scatter.23.cloned.1.call-done = f32[32,3072]{1,0:T(8,128)} async-done(((f32[1024,3072]{1,0:T(8,128)}), f32[32,3072]{1,0:T(8,128)}) %reduce-scatter.23.cloned.1.call-update) | async-done | bytes 393232 | tf_op jit(solution)/shard_map/reduce_scatter | solution.py:618
  (1475 shorter events, 968.7 us)
Async XLA Ops:
  7.2 384.2 %all-gather.27.cloned.1.call-start = ((), (), s32[]{:S(2)}) async-start(), calls=%async_computation.14 | async-start | bytes 6488064 | tf_op jit(solution)/shard_map/all_gather | solution.py:398
  7.9 462.3 %all-gather.31.cloned.1.call-start = ((), (), s32[]{:S(2)}) async-start(), calls=%async_computation.16 | async-start | bytes 2359296 | tf_op jit(solution)/shard_map/all_gather | solution.py:421
  8.7 462.1 %all-gather.35.cloned.1.call-start = ((), (), s32[]{:S(2)}) async-start(), calls=%async_computation.18 | async-start | bytes 2359296 | tf_op jit(solution)/shard_map/all_gather | solution.py:422
  9.4 627.0 %all-gather.39.cloned.1.call-start = ((), (), s32[]{:S(2)}) async-start(), calls=%async_computation.20 | async-start | bytes 2359296 | tf_op jit(solution)/shard_map/all_gather | solution.py:423
  10.0 680.6 %all-gather.49.cloned.1.call-start = ((), (), s32[]{:S(2)}) async-start(), calls=%async_computation.35 | async-start | bytes 4718592 | tf_op jit(solution)/shard_map/all_gather | solution.py:34
  469.4 326.7 %all-gather.29.cloned.1.call-start = ((), (), s32[]{:S(2)}) async-start(), calls=%async_computation.15 | async-start | bytes 2162688 | tf_op jit(solution)/shard_map/all_gather | solution.py:405
  470.1 330.8 %all-gather.33.cloned.1.call-start = ((), (), s32[]{:S(2)}) async-start(), calls=%async_computation.17 | async-start | bytes 10485760 | tf_op jit(solution)/shard_map/all_gather | solution.py:512
  470.7 479.6 %all-gather.37.cloned.1.call-start = ((), (), s32[]{:S(2)}) async-start(), calls=%async_computation.19 | async-start | bytes 10485760 | tf_op jit(solution)/shard_map/all_gather | solution.py:513
  471.4 628.2 %all-gather.41.cloned.1.call-start = ((), (), s32[]{:S(2)}) async-start(), calls=%async_computation.21 | async-start | bytes 10485760 | tf_op jit(solution)/shard_map/all_gather | solution.py:514
  636.5 677.1 %all-gather.53.cloned.1.call-start = ((), (), s32[]{:S(2)}) async-start(), calls=%async_computation.37 | async-start | bytes 4718592 | tf_op jit(solution)/shard_map/all_gather | solution.py:34
  1149.7 395.8 %reduce-scatter.41.cloned.1.call-start = ((), (), s32[]{:S(2)}) async-start(), calls=%async_computation.31 | async-start | bytes 10485760 | tf_op jit(solution)/shard_map/reduce_scatter | solution.py:539
  1156.5 395.8 %reduce-scatter.33.cloned.1.call-start = ((), (), s32[]{:S(2)}) async-start(), calls=%async_computation.27 | async-start | bytes 10485760 | tf_op jit(solution)/shard_map/reduce_scatter | solution.py:533
  1164.1 488.1 %reduce-scatter.37.cloned.1.call-start = ((), (), s32[]{:S(2)}) async-start(), calls=%async_computation.29 | async-start | bytes 10485760 | tf_op jit(solution)/shard_map/reduce_scatter | solution.py:536
  1171.4 617.6 %reduce-scatter.45.cloned.1.call-start = ((), (), s32[]{:S(2)}) async-start(), calls=%async_computation.39 | async-start | bytes 540672
  1290.4 632.3 %reduce-scatter.47.cloned.1.call-start = ((), (), s32[]{:S(2)}) async-start(), calls=%async_computation.40 | async-start | bytes 540672
  1313.5 708.1 %reduce-scatter.43.cloned.1.call-start = ((), (), s32[]{:S(2)}) async-start(), calls=%async_computation.38 | async-start | bytes 1622016
  1528.0 633.1 %reduce-scatter.29.cloned.1.call-start = ((), (), s32[]{:S(2)}) async-start(), calls=%async_computation.25 | async-start | bytes 2162688 | tf_op jit(solution)/shard_map/reduce_scatter | solution.py:624
  1531.5 768.4 %reduce-scatter.27.cloned.1.call-start = ((), (), s32[]{:S(2)}) async-start(), calls=%async_computation.24 | async-start | bytes 2162688 | tf_op jit(solution)/shard_map/reduce_scatter | solution.py:621
  1539.1 803.3 %reduce-scatter.49.cloned.1.call-start = ((), (), s32[]{:S(2)}) async-start(), calls=%async_computation.41 | async-start | bytes 2359296
  1549.7 837.5 %reduce-scatter.35.cloned.1.call-start = ((), (), s32[]{:S(2)}) async-start(), calls=%async_computation.28 | async-start | bytes 2359296 | tf_op jit(solution)/shard_map/reduce_scatter | solution.py:636
  1552.5 879.2 %reduce-scatter.39.cloned.1.call-start = ((), (), s32[]{:S(2)}) async-start(), calls=%async_computation.30 | async-start | bytes 2359296 | tf_op jit(solution)/shard_map/reduce_scatter | solution.py:639
  1652.2 916.7 %reduce-scatter.25.cloned.1.call-start = ((), (), s32[]{:S(2)}) async-start(), calls=%async_computation.23 | async-start | bytes 540672 | tf_op jit(solution)/shard_map/reduce_scatter | solution.py:619
  1665.1 1050.6 %reduce-scatter.31.cloned.1.call-start = ((), (), s32[]{:S(2)}) async-start(), calls=%async_computation.26 | async-start | bytes 4325376 | tf_op jit(solution)/shard_map/reduce_scatter | solution.py:632
  1668.1 1208.5 %reduce-scatter.23.cloned.1.call-start = ((), (), s32[]{:S(2)}) async-start(), calls=%async_computation.22 | async-start | bytes 12976128 | tf_op jit(solution)/shard_map/reduce_scatter | solution.py:618
  (317 other events, 12870.0 us)
Sparse Core Ops, SparseCore 0:
  10.9 72.3 all-gather.26
  437.9 36.1 all-gather.48
  475.8 36.7 all-gather.46
  514.5 36.8 all-gather.44
  553.3 36.8 all-gather.42
  593.1 56.4 all-gather.28
  651.1 149.7 all-gather.32
  802.4 147.8 all-gather.36
  951.7 147.8 all-gather.40
  1173.7 36.7 all-gather.50
  1212.7 144.4 reduce-scatter.40
  1359.5 145.1 reduce-scatter.32
  1506.9 145.2 reduce-scatter.36
  1654.2 134.7 reduce-scatter.44
  1791.9 130.7 reduce-scatter.46
  1927.8 93.6 reduce-scatter.42
  2023.8 137.1 reduce-scatter.28
  2163.4 136.4 reduce-scatter.26
  2303.2 39.1 reduce-scatter.48
  2345.8 41.2 reduce-scatter.34
  2390.4 41.1 reduce-scatter.38
  2434.4 134.4 reduce-scatter.24
  2571.6 144.0 reduce-scatter.30
  2722.3 154.1 reduce-scatter.22
  (4 shorter events, 118.5 us)
where the time goes:
time: 2900 us; the launch traced here: 2880 us
  waiting for transfers between devices  1470 us (51%)
  blocking collectives  526 us (18%)
  matrix products  330 us (11%)
  other arithmetic  269 us (9%)
  local copies, waits for them, and re-layouts  254 us (9%)
    unnamed x32, waiting for transfers between devices  325 us
    reduce_scatter x1, waiting for transfers between devices, on_device(): lax.psum_scatter(grad_qkv, ('seq', 'fsdp'), scatter_dimension=0, tiled=True)  161 us
    reduce_scatter x1, waiting for transfers between devices, on_device(): lax.psum_scatter(grad_out_matrix, ('seq', 'fsdp'), scatter_dimension=0, t...  147 us
    all_gather x1, waiting for transfers between devices, on_device(): lax.all_gather(ffn_parts[1], 'fsdp', axis=1, tiled=True)  142 us
    all_gather x1, waiting for transfers between devices, on_device(): lax.all_gather(ffn_parts[2], 'fsdp', axis=0, tiled=True)  141 us
    reduce_scatter x1, waiting for transfers between devices, on_device(): lax.psum_scatter(grad_second_recall + grad_second_change, ('seq', 'fsdp')...  138 us
    reduce_scatter x1, waiting for transfers between devices, on_device(): lax.psum_scatter(grad_first_recall + grad_first_change, ('seq', 'fsdp'),...  137 us
    reduce_scatter x1, waiting for transfers between devices, on_device(): lax.psum_scatter(grad_gate_matrix, ('seq', 'fsdp'), scatter_dimension=0,...  135 us
  transfers between devices with their start and end apart: 35, of which 16 were waited for; matrix products, arithmetic and copies ran while one was open for 27% of the time, Pallas kernels for 0%

commit v1 on v0

v1 whole, which is shorter than its diff:
```python
from functools import partial

import jax
import jax.numpy as jnp
from jax import lax
from jax.experimental import pallas as pl
from jax.experimental.pallas import tpu as pltpu
from jax.sharding import PartitionSpec as P

HEAD_COUNT = 16
HEAD_SIZE = 64
D = 1024
MH = 256
P_SIZE = 16
SEG = 256
LANES = 128

NORM_EPS = 1e-05
UNIT_EPS = 1e-06
SCORE_SCALE = 8.0
MEMORY_SCALE = 8.0
THETA_SCALE = 0.0005
MASKED = -1000000000.0
VMEM_GRANT = 56 * 1024 * 1024
MESH = pl.DeviceIdType.MESH

f32 = jnp.float32
bf16 = jnp.bfloat16


def dot_nt(left, right):
    return lax.dot_general(left, right, (((1,), (1,)), ((), ())), preferred_element_type=f32)


def dot_nn(left, right):
    return lax.dot_general(left, right, (((1,), (0,)), ((), ())), preferred_element_type=f32)


def dot_tn(left, right):
    return lax.dot_general(left, right, (((0,), (0,)), ((), ())), preferred_element_type=f32)


def lane_index(shape):
    return lax.broadcasted_iota(jnp.int32, shape, 1)


def to_low(rows, head):
    return rows if head == 0 else pltpu.roll(rows, HEAD_SIZE, 1)


def swap_halves(rows):
    return pltpu.roll(rows, HEAD_SIZE, 1)


def lane_sum(rows):
    return jnp.sum(rows, axis=1, keepdims=True)


def unit_pair(rows, low):
    squares = rows * rows
    first = lane_sum(jnp.where(low, squares, 0.0))
    second = lane_sum(jnp.where(low, 0.0, squares))
    inverse = jnp.where(low, lax.rsqrt(first + UNIT_EPS), lax.rsqrt(second + UNIT_EPS))
    return rows * inverse, inverse


def unit_pair_pull(unit, inverse, grad, low):
    along = unit * grad
    first = lane_sum(jnp.where(low, along, 0.0))
    second = lane_sum(jnp.where(low, 0.0, along))
    return inverse * (grad - unit * jnp.where(low, first, second))


def mix_taps(ext_ref, conv_ref, place):
    mixed = conv_ref[0:1, :] * ext_ref[8 : 8 + SEG, :]
    for offset in range(1, 4):
        kept = jnp.where(place >= offset, ext_ref[8 - offset : 8 - offset + SEG, :], 0.0)
        mixed = mixed + conv_ref[offset : offset + 1, :] * kept
    return mixed


def gate_scan(gate_rows):
    lane = lane_index((8, SEG))
    keep = jnp.where(gate_rows[24:25] < 0.5, 0.0, 1.0)
    live = gate_rows[25:26]
    forget = jax.nn.sigmoid(gate_rows[0:8])
    momentum = jax.nn.sigmoid(gate_rows[8:16])
    step = jax.nn.sigmoid(gate_rows[16:24])
    carry = keep * momentum
    fade = keep * (1.0 - forget)
    keep_all, mix_all, fade_all = carry, carry, fade
    distance = 1
    while distance < SEG:
        inside = lane < SEG - distance
        turn = SEG - distance
        keep_next = jnp.where(inside, pltpu.roll(keep_all, turn, 1), 1.0)
        mix_next = jnp.where(inside, pltpu.roll(mix_all, turn, 1), 0.0)
        fade_next = jnp.where(inside, pltpu.roll(fade_all, turn, 1), 1.0)
        mix_all = mix_next * keep_all + fade_next * mix_all
        keep_all = keep_next * keep_all
        fade_all = fade_next * fade_all
        distance *= 2
    inside = lane < SEG - 1
    keep_after = jnp.where(inside, pltpu.roll(keep_all, SEG - 1, 1), 1.0)
    mix_after = jnp.where(inside, pltpu.roll(mix_all, SEG - 1, 1), 0.0)
    fade_after = jnp.where(inside, pltpu.roll(fade_all, SEG - 1, 1), 1.0)
    written = -THETA_SCALE * step * live
    return dict(
        keep=keep,
        live=live,
        forget=forget,
        momentum=momentum,
        step=step,
        carry=carry,
        fade=fade,
        keep_after=keep_after,
        reach=mix_after + fade_after,
        fade_after=fade_after,
        written=written,
        totals=(keep_all, mix_all, fade_all),
    )


def write_columns(scan):
    rows = jnp.concatenate(
        [scan["written"] * scan["keep_after"], scan["written"] * scan["reach"]], axis=0
    )
    return jnp.transpose(rows)


def state_factors(totals, head, low):
    keep_all, mix_all, fade_all = (member[head : head + 1, 0:1] for member in totals)
    return jnp.where(low, keep_all, fade_all), mix_all


def visible_masks(place, live_prev, live_now):
    row = lax.broadcasted_iota(jnp.int32, (SEG, SEG), 0)
    gap = row - lane_index((SEG, SEG))
    now = (gap >= 0) & (gap <= place) & (live_now > 0.5)
    prev = (gap < 0) & (gap + SEG <= place) & (live_prev > 0.5)
    return prev, now


def layer_scores(query, key_prev, key_now, pkeys, masks):
    fixed = dot_nt(query, pkeys)
    prev = jnp.where(masks[0], SCORE_SCALE * dot_nt(query, key_prev), MASKED)
    now = jnp.where(masks[1], SCORE_SCALE * dot_nt(query, key_now), MASKED)
    return fixed, prev, now


def forward_kernel(
    heads,
    raw_ref,
    gate_ref,
    place_ref,
    conv_ref,
    mem_ref,
    swap_ref,
    pkey_ref,
    pvalue_ref,
    comb_ref,
    key_out,
    value_out,
    total_out,
    state_out,
    ext,
    key_prev,
    value_prev,
    live_prev,
    state,
):
    at = pl.program_id(0)

    @pl.when(at == 0)
    def _():
        ext[0:8, :] = jnp.zeros((8, 3 * LANES), f32)
        key_prev[...] = jnp.zeros_like(key_prev)
        value_prev[...] = jnp.zeros_like(value_prev)
        live_prev[...] = jnp.zeros_like(live_prev)
        state[...] = jnp.zeros_like(state)

    low = lane_index((SEG, LANES)) < HEAD_SIZE
    ext[8 : 8 + SEG, :] = raw_ref[...].astype(f32)
    place = place_ref[...]
    mixed = mix_taps(ext, conv_ref, place)
    ext[0:8, :] = ext[SEG : SEG + 8, :]
    query_unit, _ = unit_pair(mixed[:, :LANES], low)
    key_unit, _ = unit_pair(mixed[:, LANES : 2 * LANES], low)
    value = mixed[:, 2 * LANES :]
    key_now = key_unit.astype(bf16)
    value_now = value.astype(bf16)
    key_out[...] = key_now
    value_out[...] = value_now
    scan = gate_scan(gate_ref[0])
    columns = write_columns(scan)
    masks = visible_masks(place, live_prev[0:1, :], scan["live"])
    older = jnp.where(place > lax.broadcasted_iota(jnp.int32, (SEG, 1), 0), 1.0, 0.0)
    kept_prev, kept_value = key_prev[...], value_prev[...]
    combined = jnp.zeros((SEG, LANES), f32)
    log_totals = jnp.zeros((SEG, 8), f32)
    for head in range(heads):
        own = low if head == 0 else jnp.logical_not(low)
        query = jnp.where(own, query_unit, 0.0).astype(bf16)
        fixed, prev, now = layer_scores(query, kept_prev, key_now, pkey_ref[...], masks)
        highest = jnp.maximum(
            jnp.max(fixed, axis=1, keepdims=True),
            jnp.maximum(
                jnp.max(prev, axis=1, keepdims=True), jnp.max(now, axis=1, keepdims=True)
            ),
        )
        fixed, prev, now = (jnp.exp(member - highest) for member in (fixed, prev, now))
        summed = lane_sum(fixed) + lane_sum(prev + now)
        inverse = 1.0 / summed
        attended = dot_nn((prev * inverse).astype(bf16), kept_value)
        attended = attended + dot_nn((now * inverse).astype(bf16), value_now)
        attended = attended + dot_nn((fixed * inverse).astype(bf16), pvalue_ref[...])
        log_totals = jnp.where(lane_index((SEG, 8)) == head, highest + jnp.log(summed), log_totals)

        key_low = to_low(key_unit, head) * MEMORY_SCALE
        value_low = to_low(value, head)
        query_low = to_low(query_unit, head) * MEMORY_SCALE
        mem, swap = mem_ref[head], swap_ref[head]
        state_one, state_two = state[head, 0], state[head, 1]
        state_out[0, head, 0] = state_one.astype(bf16)
        state_out[0, head, 1] = state_two.astype(bf16)

        first = jnp.where(low, mem.astype(f32), state_one).astype(bf16)
        second = jnp.where(low, swap.astype(f32), state_two).astype(bf16)
        asked = jnp.where(low, query_low, older * swap_halves(query_low)).astype(bf16)
        inner = dot_nt(asked, first)
        answer = dot_nn((inner * jax.nn.sigmoid(inner)).astype(bf16), second)
        recalled = jnp.where(low, answer, 0.0) + jnp.where(low, older * swap_halves(answer), 0.0)
        if head:
            recalled = swap_halves(recalled)
        combined = combined + jnp.where(own, attended, 0.0) + recalled

        key_cut = jnp.where(low, key_low, 0.0)
        inner = dot_nt(key_cut.astype(bf16), mem)
        sigmoid = jax.nn.sigmoid(inner)
        active = inner * sigmoid
        slope = sigmoid * (1.0 + inner - active)
        active = active.astype(bf16)
        error = jnp.where(low, dot_nn(active, swap) - value_low, 0.0)
        descent = (dot_nt(error.astype(bf16), swap) * slope).astype(bf16)
        scale = jnp.where(low, columns[:, head : head + 1], columns[:, 8 + head : 9 + head])
        key_scaled = ((key_cut + swap_halves(key_cut)) * scale).astype(bf16)
        error_scaled = ((error + swap_halves(error)) * scale).astype(bf16)
        factor, blend = state_factors(scan["totals"], head, low)
        for member, old, added in (
            (0, state_one, dot_tn(descent, key_scaled)),
            (1, state_two, dot_tn(active, error_scaled)),
        ):
            turned = jnp.where(low, 0.0, blend * swap_halves(old))
            state[head, member] = factor * old + turned + added
    comb_ref[...] = combined.astype(bf16)
    total_out[...] = log_totals
    key_prev[...] = key_now
    value_prev[...] = value_now
    live_prev[...] = jnp.broadcast_to(scan["live"], (8, SEG))


def chain_rows(factor, term, start, lane):
    distance = 1
    while distance < SEG:
        inside = lane >= distance
        factor_before = jnp.where(inside, pltpu.roll(factor, distance, 1), 1.0)
        term_before = jnp.where(inside, pltpu.roll(term, distance, 1), 0.0)
        term = term + factor * term_before
        factor = factor * factor_before
        distance *= 2
    after = factor * start + term
    return jnp.where(lane == 0, start, pltpu.roll(after, 1, 1))


def backward_kernel(
    heads,
    raw_ref,
    tail_ref,
    gate_ref,
    gate_prev_ref,
    place_ref,
    key_ref,
    key_prev_ref,
    value_ref,
    value_prev_ref,
    total_ref,
    state_ref,
    grad_ref,
    conv_ref,
    mem_ref,
    swap_ref,
    pkey_ref,
    pvalue_ref,
    draw_ref,
    dgate_ref,
    dmem_ref,
    dconv_ref,
    dpkey_ref,
    dpvalue_ref,
    ext,
    shifted_rows,
    key_carry,
    value_carry,
    late,
):
    at = pl.program_id(0)

    @pl.when(at == 0)
    def _():
        dmem_ref[...] = jnp.zeros_like(dmem_ref)
        dconv_ref[...] = jnp.zeros_like(dconv_ref)
        dpkey_ref[...] = jnp.zeros_like(dpkey_ref)
        dpvalue_ref[...] = jnp.zeros_like(dpvalue_ref)
        shifted_rows[:, 0:8, :] = jnp.zeros((3, 8, 3 * LANES), f32)
        key_carry[...] = jnp.zeros_like(key_carry)
        value_carry[...] = jnp.zeros_like(value_carry)
        late[...] = jnp.zeros_like(late)

    low = lane_index((SEG, LANES)) < HEAD_SIZE
    ext[0:8, :] = tail_ref[8:16, :].astype(f32)
    ext[8 : 8 + SEG, :] = raw_ref[...].astype(f32)
    place = place_ref[...]
    mixed = mix_taps(ext, conv_ref, place)
    query_unit, query_inverse = unit_pair(mixed[:, :LANES], low)
    key_unit, key_inverse = unit_pair(mixed[:, LANES : 2 * LANES], low)
    value = mixed[:, 2 * LANES :]
    key_now, key_prev = key_ref[...], key_prev_ref[...]
    value_now, value_prev = value_ref[...], value_prev_ref[...]
    gate_rows = gate_ref[0]
    scan = gate_scan(gate_rows)
    columns = write_columns(scan)
    masks = visible_masks(place, gate_prev_ref[0, 25:26, :], scan["live"])
    older = jnp.where(place > lax.broadcasted_iota(jnp.int32, (SEG, 1), 0), 1.0, 0.0)
    grad = grad_ref[...].astype(f32)
    grad_query = jnp.zeros((SEG, LANES), f32)
    grad_key = key_carry[...]
    grad_value = value_carry[...]
    carry_key = jnp.zeros((SEG, LANES), f32)
    carry_value = jnp.zeros((SEG, LANES), f32)
    wide = lane_index((SEG, LANES))
    write_grads = jnp.zeros((SEG, LANES), f32)
    sublane = lax.broadcasted_iota(jnp.int32, (8, 1), 0)
    keep_start = jnp.zeros((8, 1), f32)
    mix_start = jnp.zeros((8, 1), f32)
    fade_start = jnp.zeros((8, 1), f32)
    for head in range(heads):
        own = low if head == 0 else jnp.logical_not(low)
        query = jnp.where(own, query_unit, 0.0).astype(bf16)
        grad_own = jnp.where(own, grad, 0.0).astype(bf16)
        total = total_ref[:, head : head + 1]
        scores = layer_scores(query, key_prev, key_now, pkey_ref[...], masks)
        probs = [jnp.exp(member - total) for member in scores]
        grads = [
            dot_nt(grad_own, pvalue_ref[...]),
            dot_nt(grad_own, value_prev),
            dot_nt(grad_own, value_now),
        ]
        spread = lane_sum(probs[0] * grads[0]) + lane_sum(probs[1] * grads[1] + probs[2] * grads[2])
        score_grads = [(one * (other - spread)).astype(bf16) for one, other in zip(probs, grads)]
        probs = [member.astype(bf16) for member in probs]
        back = dot_nn(score_grads[1], key_prev) + dot_nn(score_grads[2], key_now)
        back = SCORE_SCALE * back + dot_nn(score_grads[0], pkey_ref[...])
        grad_query = grad_query + jnp.where(own, back, 0.0)
        carry_key = carry_key + SCORE_SCALE * dot_tn(score_grads[1], query)
        grad_key = grad_key + SCORE_SCALE * dot_tn(score_grads[2], query)
        carry_value = carry_value + dot_tn(probs[1], grad_own)
        grad_value = grad_value + dot_tn(probs[2], grad_own)
        dpkey_ref[...] += dot_tn(score_grads[0], query)
        dpvalue_ref[...] += dot_tn(probs[0], grad_own)

        mem, swap = mem_ref[head], swap_ref[head]
        state_one, state_two = (state_ref[0, head, member].astype(f32) for member in range(2))
        late_one, late_two = late[head, 0], late[head, 1]

        query_low = to_low(query_unit, head) * MEMORY_SCALE
        grad_low = to_low(grad, head)
        first = jnp.where(low, mem.astype(f32), state_one).astype(bf16)
        second = jnp.where(low, swap.astype(f32), state_two).astype(bf16)
        asked = jnp.where(low, query_low, older * swap_halves(query_low)).astype(bf16)
        told = jnp.where(low, grad_low, older * swap_halves(grad_low)).astype(bf16)
        inner = dot_nt(asked, first)
        sigmoid = jax.nn.sigmoid(inner)
        active = inner * sigmoid
        slope = sigmoid * (1.0 + inner - active)
        grad_inner = (dot_nt(told, second) * slope).astype(bf16)
        back = dot_nn(grad_inner, first)
        back = jnp.where(low, MEMORY_SCALE * (back + older * swap_halves(back)), 0.0)
        grad_query = grad_query + (back if head == 0 else swap_halves(back))
        read_one = dot_tn(grad_inner, asked)
        read_two = dot_tn(active.astype(bf16), told)

        key_low = to_low(key_unit, head) * MEMORY_SCALE
        key_cut = jnp.where(low, key_low, 0.0)
        key_bf = key_cut.astype(bf16)
        inner = dot_nt(key_bf, mem)
        sigmoid = jax.nn.sigmoid(inner)
        active = inner * sigmoid
        slope = sigmoid * (1.0 + inner - active)
        curve = sigmoid * (1.0 - sigmoid) * (2.0 + inner - 2.0 * active)
        active = active.astype(bf16)
        error = jnp.where(low, dot_nn(active, swap) - to_low(value, head), 0.0)
        error_bf = error.astype(bf16)
        pulled = dot_nt(error_bf, swap)
        descent = (pulled * slope).astype(bf16)
        scale = jnp.where(low, columns[:, head : head + 1], columns[:, 8 + head : 9 + head])
        key_twice = key_cut + swap_halves(key_cut)
        error_twice = error + swap_halves(error)
        key_scaled = (key_twice * scale).astype(bf16)
        error_scaled = (error_twice * scale).astype(bf16)
        late_one_bf, late_two_bf = late_one.astype(bf16), late_two.astype(bf16)
        grad_descent = dot_nt(key_scaled, late_one_bf)
        back_key = dot_nn(descent, late_one_bf)
        back_error = dot_nn(active, late_two_bf)
        weight_grad = key_twice * back_key + error_twice * back_error
        grad_state_weight = lane_sum(jnp.where(low, weight_grad, 0.0))
        grad_write_weight = lane_sum(jnp.where(low, 0.0, weight_grad))
        write_grads = jnp.where(wide == head, grad_state_weight, write_grads)
        write_grads = jnp.where(wide == 8 + head, grad_write_weight, write_grads)
        grad_pulled = (grad_descent * slope).astype(bf16)
        back_error = back_error * scale
        back_error = back_error + swap_halves(back_error) + dot_nn(grad_pulled, swap)
        back_error = jnp.where(low, back_error, 0.0)
        back_error_bf = back_error.astype(bf16)
        grad_active = dot_nt(error_scaled, late_two_bf) + dot_nt(back_error_bf, swap)
        grad_inner = (grad_descent * pulled * curve + grad_active * slope).astype(bf16)
        back_key = back_key * scale
        back_key = back_key + swap_halves(back_key) + dot_nn(grad_inner, mem)
        back_key = jnp.where(low, MEMORY_SCALE * back_key, 0.0)
        grad_key = grad_key + (back_key if head == 0 else swap_halves(back_key))
        grad_value = grad_value - (back_error if head == 0 else swap_halves(back_error))
        write_one = dot_tn(grad_inner, key_bf)
        write_two = dot_tn(grad_pulled, error_bf) + dot_tn(active, back_error_bf)
        dmem_ref[head] += jnp.where(low, read_one + write_one, swap_halves(read_two + write_two))

        factor, blend = state_factors(scan["totals"], head, low)
        same = late_one * state_one + late_two * state_two
        cross = late_one * swap_halves(state_one) + late_two * swap_halves(state_two)
        same_low = jnp.sum(lane_sum(jnp.where(low, same, 0.0)), axis=0, keepdims=True)
        same_high = jnp.sum(lane_sum(jnp.where(low, 0.0, same)), axis=0, keepdims=True)
        cross_high = jnp.sum(lane_sum(jnp.where(low, 0.0, cross)), axis=0, keepdims=True)
        keep_start = jnp.where(sublane == head, same_low, keep_start)
        fade_start = jnp.where(sublane == head, same_high, fade_start)
        mix_start = jnp.where(sublane == head, cross_high, mix_start)
        for member, old, read in ((0, late_one, read_one), (1, late_two, read_two)):
            turned = jnp.where(low, blend * swap_halves(old), read)
            late[head, member] = factor * old + turned

    lane = lane_index((8, SEG))
    write_rows = jnp.transpose(write_grads)
    grad_state_rows, grad_write_rows = write_rows[0:8], write_rows[8:16]
    written = scan["written"]
    keep_grads = chain_rows(scan["carry"], grad_state_rows * written, keep_start, lane)
    mix_grads = chain_rows(scan["carry"], grad_write_rows * written, mix_start, lane)
    mix_next = scan["carry"] * mix_grads + grad_write_rows * written
    fade_grads = chain_rows(scan["fade"], mix_next, fade_start, lane)
    grad_written = grad_state_rows * scan["keep_after"] + grad_write_rows * scan["reach"]
    grad_carry = keep_grads * scan["keep_after"] + mix_grads * scan["reach"]
    grad_fade = fade_grads * scan["fade_after"]
    used = sublane < heads
    forget, momentum, step = scan["forget"], scan["momentum"], scan["step"]
    forget_back = -grad_fade * scan["keep"] * forget * (1.0 - forget)
    momentum_back = grad_carry * scan["keep"] * momentum * (1.0 - momentum)
    step_back = -THETA_SCALE * grad_written * scan["live"] * step * (1.0 - step)
    dgate_ref[0, 0:8] = jnp.where(used, forget_back, 0.0)
    dgate_ref[0, 8:16] = jnp.where(used, momentum_back, 0.0)
    dgate_ref[0, 16:24] = jnp.where(used, step_back, 0.0)

    key_carry[...] = carry_key
    value_carry[...] = carry_value
    grad_mixed = jnp.concatenate(
        [
            unit_pair_pull(query_unit, query_inverse, grad_query, low),
            unit_pair_pull(key_unit, key_inverse, grad_key, low),
            grad_value,
        ],
        axis=1,
    )
    back = conv_ref[0:1, :] * grad_mixed
    dconv_ref[0:1, :] += jnp.sum(grad_mixed * ext[8 : 8 + SEG, :], axis=0, keepdims=True)
    for offset in range(1, 4):
        kept = jnp.where(place >= offset, grad_mixed, 0.0)
        member = offset - 1
        shifted_rows[member, SEG : SEG + 8, :] = shifted_rows[member, 0:8, :]
        shifted_rows[member, 0:SEG, :] = kept
        back = back + conv_ref[offset : offset + 1, :] * shifted_rows[
            member, offset : offset + SEG, :
        ]
        dconv_ref[offset : offset + 1, :] += jnp.sum(
            kept * ext[8 - offset : 8 - offset + SEG, :], axis=0, keepdims=True
        )
    draw_ref[...] = back.astype(bf16)


def block_of(shape, index):
    return pl.BlockSpec(shape, index)


def whole_of(array):
    zeros = (0,) * array.ndim
    return pl.BlockSpec(array.shape, lambda n: zeros)


def mix_forward(heads, raw, gates, place, conv, mem, swap, pkeys, pvalues):
    length = raw.shape[0]
    count = length // SEG
    row_block = pl.BlockSpec((SEG, LANES), lambda n: (n, 0))
    return pl.pallas_call(
        partial(forward_kernel, heads),
        grid=(count,),
        in_specs=[
            pl.BlockSpec((SEG, 3 * LANES), lambda n: (n, 0)),
            pl.BlockSpec((1, 32, SEG), lambda n: (n, 0, 0)),
            pl.BlockSpec((SEG, 1), lambda n: (n, 0)),
        ]
        + [whole_of(member) for member in (conv, mem, swap, pkeys, pvalues)],
        out_specs=[
            row_block,
            row_block,
            row_block,
            pl.BlockSpec((SEG, 8), lambda n: (n, 0)),
            pl.BlockSpec((1, heads, 2, MH, LANES), lambda n: (n, 0, 0, 0, 0)),
        ],
        out_shape=[
            jax.ShapeDtypeStruct((length, LANES), bf16),
            jax.ShapeDtypeStruct((length, LANES), bf16),
            jax.ShapeDtypeStruct((length, LANES), bf16),
            jax.ShapeDtypeStruct((length, 8), f32),
            jax.ShapeDtypeStruct((count, heads, 2, MH, LANES), bf16),
        ],
        scratch_shapes=[
            pltpu.VMEM((SEG + 8, 3 * LANES), f32),
            pltpu.VMEM((SEG, LANES), bf16),
            pltpu.VMEM((SEG, LANES), bf16),
            pltpu.VMEM((8, SEG), f32),
            pltpu.VMEM((heads, 2, MH, LANES), f32),
        ],
        compiler_params=pltpu.CompilerParams(
            dimension_semantics=("arbitrary",), vmem_limit_bytes=VMEM_GRANT
        ),
        name="mix_forward",
    )(raw, gates, place, conv, mem, swap, pkeys, pvalues)


def mix_backward(
    heads, raw, gates, place, keys, values, totals, states, grad, conv, mem, swap, pkeys, pvalues
):
    length = raw.shape[0]
    count = length // SEG

    def here(n):
        return count - 1 - n

    def before(n):
        return jnp.maximum(count - 2 - n, 0)

    row_block = pl.BlockSpec((SEG, LANES), lambda n: (here(n), 0))
    prev_block = pl.BlockSpec((SEG, LANES), lambda n: (before(n), 0))
    tail_rows = SEG // 16
    return pl.pallas_call(
        partial(backward_kernel, heads),
        grid=(count,),
        in_specs=[
            pl.BlockSpec((SEG, 3 * LANES), lambda n: (here(n), 0)),
            pl.BlockSpec((16, 3 * LANES), lambda n: (jnp.maximum(here(n) * tail_rows - 1, 0), 0)),
            pl.BlockSpec((1, 32, SEG), lambda n: (here(n), 0, 0)),
            pl.BlockSpec((1, 32, SEG), lambda n: (before(n), 0, 0)),
            pl.BlockSpec((SEG, 1), lambda n: (here(n), 0)),
            row_block,
            prev_block,
            row_block,
            prev_block,
            pl.BlockSpec((SEG, 8), lambda n: (here(n), 0)),
            pl.BlockSpec((1, heads, 2, MH, LANES), lambda n: (here(n), 0, 0, 0, 0)),
            row_block,
        ]
        + [whole_of(member) for member in (conv, mem, swap, pkeys, pvalues)],
        out_specs=[
            pl.BlockSpec((SEG, 3 * LANES), lambda n: (here(n), 0)),
            pl.BlockSpec((1, 24, SEG), lambda n: (here(n), 0, 0)),
            pl.BlockSpec((heads, MH, LANES), lambda n: (0, 0, 0)),
            pl.BlockSpec((8, 3 * LANES), lambda n: (0, 0)),
            pl.BlockSpec((P_SIZE, LANES), lambda n: (0, 0)),
            pl.BlockSpec((P_SIZE, LANES), lambda n: (0, 0)),
        ],
        out_shape=[
            jax.ShapeDtypeStruct((length, 3 * LANES), bf16),
            jax.ShapeDtypeStruct((count, 24, SEG), f32),
            jax.ShapeDtypeStruct((heads, MH, LANES), f32),
            jax.ShapeDtypeStruct((8, 3 * LANES), f32),
            jax.ShapeDtypeStruct((P_SIZE, LANES), f32),
            jax.ShapeDtypeStruct((P_SIZE, LANES), f32),
        ],
        scratch_shapes=[
            pltpu.VMEM((SEG + 8, 3 * LANES), f32),
            pltpu.VMEM((3, SEG + 8, 3 * LANES), f32),
            pltpu.VMEM((SEG, LANES), f32),
            pltpu.VMEM((SEG, LANES), f32),
            pltpu.VMEM((heads, 2, MH, LANES), f32),
        ],
        compiler_params=pltpu.CompilerParams(
            dimension_semantics=("arbitrary",), vmem_limit_bytes=VMEM_GRANT
        ),
        name="mix_backward",
    )(
        raw,
        raw,
        gates,
        gates,
        place,
        keys,
        keys,
        values,
        values,
        totals,
        states,
        grad,
        conv,
        mem,
        swap,
        pkeys,
        pvalues,
    )


def exchange_kernel(name, axes, counts, *refs):
    seqs, lines = axes
    chips = seqs // 2
    devices = seqs * lines
    gathers, planes, rows_to, everys, alls, scatters = counts
    total_in = sum(counts)
    inputs, outputs, scratch = refs[:total_in], refs[total_in : 2 * total_in], refs[2 * total_in :]
    seq, line = lax.axis_index("seq"), lax.axis_index("fsdp")
    me = seq * lines + line
    chip, core = seq // 2, lax.rem(seq, 2)
    sibling = (2 * chip + 1 - core, line)

    def twin(q):
        return (2 * q + core, line)

    def point(i):
        return (i // lines, lax.rem(i, lines))

    def loop(first, last, body):
        def step(k, carry):
            body(k)
            return carry

        lax.fori_loop(first, last, step, 0)

    barrier = pltpu.get_barrier_semaphore()
    if everys or alls or rows_to:

        def greet(k):
            pl.semaphore_signal(
                barrier, inc=1, device_id=point(lax.rem(me + k, devices)), device_id_type=MESH
            )

        loop(1, devices, greet)
        pl.semaphore_wait(barrier, devices - 1)
    else:

        def greet(k):
            pl.semaphore_signal(
                barrier, inc=1, device_id=(lax.rem(seq + k, seqs), line), device_id_type=MESH
            )

        loop(1, seqs, greet)
        pl.semaphore_wait(barrier, seqs - 1)

    position = 0
    groups = []
    for count in counts:
        groups.append((inputs[position : position + count], outputs[position : position + count]))
        position += count
    scratch = list(scratch)

    def take(number):
        taken = scratch[:number]
        del scratch[:number]
        return taken

    sums = []
    for source, target in zip(*groups[5]):
        pair, landed, pair_send, pair_recv, far_send, far_recv = take(6)

        def pair_copy(q, source=source, pair=pair, send=pair_send, recv=pair_recv):
            return pltpu.make_async_remote_copy(
                src_ref=source.at[2 * q + 1 - core],
                dst_ref=pair.at[q],
                send_sem=send.at[q],
                recv_sem=recv.at[q],
                device_id=sibling,
                device_id_type=MESH,
            )

        def far_copy(q, slot, pair=pair, landed=landed, send=far_send, recv=far_recv):
            return pltpu.make_async_remote_copy(
                src_ref=pair.at[q],
                dst_ref=landed.at[slot],
                send_sem=send.at[q],
                recv_sem=recv.at[slot],
                device_id=twin(q),
                device_id_type=MESH,
            )

        loop(1, chips + 1, lambda k, f=pair_copy: f(lax.rem(chip + k, chips)).start())
        sums.append((source, target, pair, landed, pair_copy, far_copy))

    spread = []
    for source, target in zip(*groups[0]):
        local, far_send, far_recv, near_send, near_recv = take(5)

        def own(target=target, source=source, local=local):
            return pltpu.make_async_copy(source, target.at[seq], local.at[0])

        def far(q, slot, source=source, target=target, send=far_send, recv=far_recv):
            return pltpu.make_async_remote_copy(
                src_ref=source,
                dst_ref=target.at[2 * slot + core],
                send_sem=send.at[q],
                recv_sem=recv.at[slot],
                device_id=twin(q),
                device_id_type=MESH,
            )

        def near_own(source=source, target=target, send=near_send, recv=near_recv):
            return pltpu.make_async_remote_copy(
                src_ref=source,
                dst_ref=target.at[seq],
                send_sem=send.at[chip],
                recv_sem=recv.at[chip],
                device_id=sibling,
                device_id_type=MESH,
            )

        def near(q, target=target, send=near_send, recv=near_recv):
            return pltpu.make_async_remote_copy(
                src_ref=target.at[2 * q + core],
                dst_ref=target.at[2 * q + core],
                send_sem=send.at[q],
                recv_sem=recv.at[q],
                device_id=sibling,
                device_id_type=MESH,
            )

        def near_arrival(q, target=target, send=near_send, recv=near_recv):
            return pltpu.make_async_remote_copy(
                src_ref=target.at[2 * q + 1 - core],
                dst_ref=target.at[2 * q + 1 - core],
                send_sem=send.at[q],
                recv_sem=recv.at[q],
                device_id=sibling,
                device_id_type=MESH,
            )

        loop(1, chips, lambda k, f=far: f(lax.rem(chip + k, chips), chip).start())
        near_own().start()
        own().start()
        spread.append((own, far, near_own, near, near_arrival))

    direct = []
    for kind, (sources, targets) in (
        ("plane", groups[1]),
        ("line", groups[2]),
        ("every", groups[3]),
        ("all", groups[4]),
    ):
        for source, target in zip(sources, targets):
            local, send, recv = take(3)
            if kind == "plane":
                number, mine = seqs, seq
            elif kind == "line":
                number, mine = lines, line
            else:
                number, mine = devices, me

            def piece(i, source=source, kind=kind, number=number):
                if kind in ("line", "all"):
                    return source
                if kind == "every" and source.shape[0] != number:
                    return source.at[i // lines]
                return source.at[i]

            def place(i, kind=kind):
                if kind == "plane":
                    return (i, line)
                if kind == "line":
                    return (seq, i)
                return point(i)

            def copy(i, slot, target=target, send=send, recv=recv, piece=piece, place=place):
                return pltpu.make_async_remote_copy(
                    src_ref=piece(i),
                    dst_ref=target.at[slot],
                    send_sem=send.at[i],
                    recv_sem=recv.at[slot],
                    device_id=place(i),
                    device_id_type=MESH,
                )

            def own(target=target, local=local, piece=piece, mine=mine):
                return pltpu.make_async_copy(piece(mine), target.at[mine], local.at[0])

            loop(
                1,
                number,
                lambda k, f=copy, m=mine, c=number: f(lax.rem(m + k, c), m).start(),
            )
            own().start()
            direct.append((own, copy, mine, number))

    rows = 32
    for source, target, pair, landed, pair_copy, far_copy in sums:

        def combine(k, source=source, pair=pair, pair_copy=pair_copy, far_copy=far_copy):
            q = lax.rem(chip + k, chips)
            pair_copy(q).wait_recv()

            def add(r):
                part = pl.ds(pl.multiple_of(r * rows, rows), rows)
                both = source[2 * q + core, part, :].astype(f32) + pair[q, part, :].astype(f32)
                pair[q, part, :] = both.astype(bf16)

            loop(0, source.shape[1] // rows, add)

            @pl.when(k < chips)
            def _():
                far_copy(q, chip).start()

        loop(1, chips + 1, combine)
    for own, far, near_own, near, near_arrival in spread:

        def forward(k, far=far, near=near):
            q = lax.rem(chip + k, chips)
            far(q, q).wait_recv()
            near(q).start()

        loop(1, chips, forward)

    for own, copy, mine, number in direct:

        def end(k, copy=copy, mine=mine, number=number):
            i = lax.rem(mine + k, number)
            copy(i, i).wait_recv()
            copy(i, i).wait_send()

        loop(1, number, end)
        own().wait()
    for own, far, near_own, near, near_arrival in spread:
        own().wait()
        near_own().wait_send()

        def end_far(k, far=far, near=near):
            q = lax.rem(chip + k, chips)
            far(q, q).wait_send()
            near(q).wait_send()

        loop(1, chips, end_far)
        loop(0, chips, lambda q, f=near_arrival: f(q).wait_recv())
    for source, target, pair, landed, pair_copy, far_copy in sums:

        def end_sum(k, far_copy=far_copy, pair_copy=pair_copy):
            q = lax.rem(chip + k, chips)
            far_copy(q, q).wait_recv()

        loop(1, chips, end_sum)

        def add_all(r, target=target, pair=pair, landed=landed):
            part = pl.ds(pl.multiple_of(r * rows, rows), rows)
            whole = pair[chip, part, :].astype(f32)
            for k in range(1, chips):
                whole = whole + landed[lax.rem(chip + k, chips), part, :].astype(f32)
            target[part, :] = whole

        loop(0, target.shape[0] // rows, add_all)
        loop(1, chips, lambda k, f=far_copy: f(lax.rem(chip + k, chips), chip).wait_send())
        loop(0, chips, lambda q, f=pair_copy: f(q).wait_send())


def exchange(
    name, collective, gathers=(), planes=(), to_line=(), everys=(), alls=(), scatters=()
):
    seqs, lines = lax.axis_size("seq"), lax.axis_size("fsdp")
    chips, devices = seqs // 2, seqs * lines
    arrays = [*gathers, *planes, *to_line, *everys, *alls, *scatters]
    counts = tuple(len(kind) for kind in (gathers, planes, to_line, everys, alls, scatters))
    dma = pltpu.SemaphoreType.DMA
    scratch = []
    for array in scatters:
        half = (chips,) + array.shape[1:]
        scratch += [pltpu.VMEM(half, bf16), pltpu.VMEM(half, bf16)] + [dma((chips,))] * 4
    for array in gathers:
        scratch += [dma((1,))] + [dma((chips,))] * 4
    shapes = [jax.ShapeDtypeStruct((seqs,) + array.shape, array.dtype) for array in gathers]
    for array in planes:
        scratch += [dma((1,)), dma((seqs,)), dma((seqs,))]
        shapes.append(jax.ShapeDtypeStruct(array.shape, array.dtype))
    for array in to_line:
        scratch += [dma((1,)), dma((lines,)), dma((lines,))]
        shapes.append(jax.ShapeDtypeStruct((lines,) + array.shape, array.dtype))
    for array in everys:
        scratch += [dma((1,)), dma((devices,)), dma((devices,))]
        shapes.append(jax.ShapeDtypeStruct((devices,) + array.shape[1:], array.dtype))
    for array in alls:
        scratch += [dma((1,)), dma((devices,)), dma((devices,))]
        shapes.append(jax.ShapeDtypeStruct((devices,) + array.shape, array.dtype))
    for array in scatters:
        shapes.append(jax.ShapeDtypeStruct(array.shape[1:], f32))
    plain = len(arrays) - len(scatters)
    any_spec, vmem_spec = pl.BlockSpec(memory_space=pl.ANY), pl.BlockSpec(memory_space=pltpu.VMEM)
    specs = [any_spec] * plain + [vmem_spec] * len(scatters)
    return pl.pallas_call(
        partial(exchange_kernel, name, (seqs, lines), counts),
        out_shape=shapes,
        in_specs=specs,
        out_specs=specs,
        scratch_shapes=scratch,
        compiler_params=pltpu.CompilerParams(
            collective_id=collective, has_side_effects=True, vmem_limit_bytes=VMEM_GRANT
        ),
        name=name,
    )(*arrays)


def norm_scale(values):
    return lax.rsqrt(jnp.mean(values * values, axis=-1, keepdims=True) + NORM_EPS)


def norm_pull(values, scale, gain, grad):
    inner = jnp.mean(grad * gain * values, axis=-1, keepdims=True)
    return scale * (grad * gain - values * (scale * scale) * inner)


def swish_slope(values, sigmoid):
    return sigmoid * (1.0 + values * (1.0 - sigmoid))


def widen(rows, width):
    return jnp.pad(rows, [(0, 0)] * (rows.ndim - 1) + [(0, width - rows.shape[-1])])


def on_device(
    tokens,
    norm1_gain,
    qkv_weight,
    gate_weight,
    conv_weight,
    memory_w1,
    memory_w2,
    persistent_keys,
    persistent_values,
    out_weight,
    norm2_gain,
    ffn_gate,
    ffn_up,
    ffn_down,
    gate_bias,
    doc_lengths,
    live_mask,
    cotangent,
):
    seqs, lines = lax.axis_size("seq"), lax.axis_size("fsdp")
    devices = seqs * lines
    seq, line = lax.axis_index("seq"), lax.axis_index("fsdp")
    me = seq * lines + line
    groups = min(HEAD_COUNT, seqs)
    copies = seqs // groups
    heads = HEAD_COUNT // groups
    width = heads * HEAD_SIZE
    group = seq // copies
    first_copy = (seq % copies == 0).astype(f32)
    share = D // devices
    hidden_share = MH // devices
    length = seqs * SEG
    piece = D // seqs
    slab = ffn_gate.shape[1] // seqs

    def for_copies(array):
        return jnp.repeat(array, copies, axis=0) if copies > 1 else array

    def head_columns(array):
        rows = array.shape[0]
        split = array.reshape(rows, 3, groups, width).transpose(2, 0, 1, 3)
        return for_copies(widen(split, LANES).reshape(groups, rows, 3 * LANES))

    qkv_blocks = head_columns(qkv_weight)
    memory_pack = jnp.concatenate([memory_w1.transpose(0, 2, 1), memory_w2], axis=2)
    memory_blocks = for_copies(memory_pack.reshape(groups, heads * hidden_share, LANES))
    live_rows = live_mask[0].astype(bf16).reshape(SEG // LANES, LANES)
    small = [
        gate_weight,
        conv_weight,
        persistent_keys,
        persistent_values,
        norm1_gain[None],
        norm2_gain[None],
        live_rows,
    ]
    small_at = [0]
    for member in small:
        small_at.append(small_at[-1] + member.shape[0])
    small_pack = jnp.concatenate([widen(member, LANES) for member in small], axis=0)
    small_pack = jnp.pad(small_pack, ((0, -small_pack.shape[0] % 16), (0, 0)))
    ffn_local = jnp.stack([ffn_gate, ffn_up, ffn_down.T])
    ffn_blocks = ffn_local.reshape(3, piece, seqs, slab).transpose(2, 0, 1, 3)
    ffn_blocks = ffn_blocks.reshape(seqs, 3 * piece, slab)
    token_rows, ffn_got, qkv_got, memory_got, small_got = exchange(
        "first_exchange",
        0,
        gathers=[tokens[0]],
        planes=[ffn_blocks],
        everys=[qkv_blocks, memory_blocks],
        alls=[small_pack],
    )
    out_matrix = lax.all_gather(out_weight, ("seq", "fsdp"), axis=0, tiled=True)
    ffn_part = ffn_got.reshape(seqs, 3, piece, slab).transpose(1, 0, 2, 3).reshape(3 * D, slab)
    ffn_full = lax.all_gather(ffn_part, "fsdp", axis=1, tiled=True).reshape(3, D, lines * slab)
    cot_rows = lax.all_gather(cotangent[0], "seq", axis=0, tiled=True)

    token_rows = token_rows.reshape(length, D)
    qkv_matrix = qkv_got.reshape(D, 3 * LANES)
    memory_both = memory_got.reshape(devices, heads, hidden_share, LANES)
    memory_both = memory_both.transpose(1, 0, 2, 3).reshape(heads, MH, LANES)
    memory_turned = jnp.concatenate(
        [memory_both[..., HEAD_SIZE:], memory_both[..., :HEAD_SIZE]], axis=-1
    )

    def small_part(number, columns):
        return small_got[:, small_at[number] : small_at[number + 1], :columns]

    gate_matrix = small_part(0, 3 * HEAD_COUNT).reshape(D, 3, HEAD_COUNT).transpose(1, 2, 0)
    gate_rows = lax.dynamic_slice_in_dim(gate_matrix, group * heads, heads, 1)
    gate_rows = jnp.pad(gate_rows, ((0, 0), (0, 8 - heads), (0, 0))).reshape(24, D)
    taps = small_part(1, 3 * share).transpose(1, 0, 2).reshape(4, 3, groups, width)
    taps = lax.dynamic_slice_in_dim(taps, group, 1, 2)[:, :, 0]
    taps = jnp.pad(widen(taps, LANES).reshape(4, 3 * LANES), ((0, 4), (0, 0))).astype(f32)

    def own_columns(number):
        whole = small_part(number, share).transpose(1, 0, 2).reshape(P_SIZE, D)
        return widen(lax.dynamic_slice_in_dim(whole, group * width, width, 1), LANES)

    pkeys, pvalues = own_columns(2), own_columns(3)
    gain_one = small_part(4, share).reshape(1, D).astype(f32)
    gain_two = small_part(5, share).reshape(1, D).astype(f32)
    live_all = small_part(6, LANES).reshape(seqs, lines, SEG)
    live_all = lax.dynamic_index_in_dim(live_all, line, 1, False).astype(f32)

    lengths = doc_lengths[0]
    starts = jnp.cumsum(lengths) - lengths

    def place_of(positions):
        inside = starts <= positions[..., None]
        return positions - jnp.max(jnp.where(inside, starts, -1), axis=-1)

    place_rows = place_of(jnp.arange(length, dtype=jnp.int32).reshape(seqs, SEG))
    place_column = place_of(jnp.arange(length, dtype=jnp.int32).reshape(length, 1))

    wide_tokens = token_rows.astype(f32)
    normed = (wide_tokens * norm_scale(wide_tokens) * gain_one).astype(bf16)
    raw = jnp.dot(normed, qkv_matrix, preferred_element_type=f32).astype(bf16)
    gate_input = dot_nt(gate_rows, normed)
    shift = lax.dynamic_slice_in_dim(gate_bias, group * heads, heads, 1)
    shift = shift * jnp.array([[3.0], [1.0], [1.0]], f32) + jnp.array([[-7.5], [1.5], [0.0]], f32)
    shift = jnp.pad(shift, ((0, 0), (0, 8 - heads))).reshape(24, 1)
    gate_input = (gate_input + shift).reshape(24, seqs, SEG).transpose(1, 0, 2)
    extra = jnp.stack([place_rows.astype(f32), live_all], axis=1)
    gates = jnp.concatenate([gate_input, jnp.pad(extra, ((0, 0), (0, 6), (0, 0)))], axis=1)
    constants = (taps, memory_both, memory_turned, pkeys, pvalues)
    mixed, keys, values, totals, states = mix_forward(heads, raw, gates, place_column, *constants)

    (mixed_got,) = exchange("to_segments", 1, planes=[mixed.reshape(seqs, SEG, LANES)])
    combined = mixed_got[::copies, :, :width].transpose(1, 0, 2).reshape(SEG, D)
    inputs = tokens[0].astype(f32)
    middle = inputs + jnp.dot(combined, out_matrix, preferred_element_type=f32)
    scale_two = norm_scale(middle)
    normed_two_own = (middle * scale_two * gain_two).astype(bf16)
    (normed_two,) = exchange("second_rows", 2, gathers=[normed_two_own])
    normed_two = normed_two.reshape(length, D)

    up_gate, up_matrix, down_matrix = ffn_full[0], ffn_full[1], ffn_full[2]
    gate_act = jnp.dot(normed_two, up_gate, preferred_element_type=f32)
    up_act = jnp.dot(normed_two, up_matrix, preferred_element_type=f32)
    sigmoid = jax.nn.sigmoid(gate_act)
    swish = gate_act * sigmoid
    hidden = (swish * up_act).astype(bf16)
    grad_hidden = jnp.dot(cot_rows, down_matrix, preferred_element_type=f32)
    grad_gate = (grad_hidden * up_act * swish_slope(gate_act, sigmoid)).astype(bf16)
    grad_up = (grad_hidden * swish).astype(bf16)
    normed_part = dot_nt(grad_gate, up_gate) + dot_nt(grad_up, up_matrix)
    (grad_normed_two,) = exchange(
        "second_sums", 3, scatters=[normed_part.astype(bf16).reshape(seqs, SEG, D)]
    )
    down_part = dot_nt(hidden, down_matrix).astype(bf16)
    down_sum = lax.psum_scatter(down_part, "seq", scatter_dimension=0, tiled=True)
    output = (middle + down_sum.astype(f32)).astype(bf16)
    ffn_grads = jnp.concatenate(
        [dot_tn(normed_two, grad_gate), dot_tn(normed_two, grad_up), dot_tn(cot_rows, hidden)],
        axis=0,
    ).astype(bf16)
    ffn_grads = lax.psum_scatter(ffn_grads, "fsdp", scatter_dimension=1, tiled=True)

    grad_middle = cotangent[0].astype(f32) + norm_pull(middle, scale_two, gain_two, grad_normed_two)
    grad_gain_two = jnp.sum(grad_normed_two * middle * scale_two, axis=0, keepdims=True)
    grad_branch = grad_middle.astype(bf16)
    grad_combined = dot_nt(grad_branch, out_matrix).astype(bf16)
    grad_out = dot_tn(combined, grad_branch).astype(bf16)
    grad_out = lax.psum_scatter(grad_out, ("seq", "fsdp"), scatter_dimension=0, tiled=True)
    blocks = widen(grad_combined.reshape(SEG, groups, width).transpose(1, 0, 2), LANES)
    (grad_mixed,) = exchange("to_heads", 4, planes=[for_copies(blocks)])

    grad_raw, grad_gates, grad_memory, grad_taps, grad_pkeys, grad_pvalues = mix_backward(
        heads,
        raw,
        gates,
        place_column,
        keys,
        values,
        totals,
        states,
        grad_mixed.reshape(length, LANES),
        *constants,
    )
    grad_gates = grad_gates.transpose(1, 0, 2).reshape(24, length)
    grad_gates_low = grad_gates.astype(bf16)
    grad_qkv = dot_tn(normed, grad_raw)
    grad_gate_rows = dot_nn(grad_gates_low, normed)
    grad_normed = dot_nt(grad_raw, qkv_matrix) + dot_tn(grad_gates_low, gate_rows)
    grad_normed = (grad_normed * first_copy).astype(bf16).reshape(seqs, SEG, D)

    def to_owners(rows):
        return rows.reshape(rows.shape[0], devices, share).transpose(1, 0, 2)

    memory_part = grad_memory.reshape(heads, devices, hidden_share, LANES).transpose(1, 0, 2, 3)
    memory_part = memory_part.reshape(devices, heads * hidden_share, LANES)
    owner_rows = widen(to_owners(jnp.concatenate([grad_gate_rows, grad_gain_two], axis=0)), LANES)
    owner_pack = jnp.concatenate([memory_part, owner_rows], axis=1).astype(bf16)
    owner_pack = jnp.pad(owner_pack, ((0, 0), (0, -owner_pack.shape[1] % 16), (0, 0)))
    bias_sums = widen(jnp.sum(grad_gates, axis=1)[None], LANES)
    shared_pack = jnp.concatenate(
        [grad_taps[:4].reshape(12, LANES), bias_sums, jnp.zeros((3, LANES), f32)], axis=0
    )
    line_pack = jnp.concatenate([grad_pkeys, grad_pvalues], axis=0)
    ffn_out = ffn_grads.reshape(3, seqs, piece, slab).transpose(1, 0, 2, 3)
    ffn_got, line_got, qkv_got, owner_got, shared_got, grad_normed = exchange(
        "last_exchange",
        5,
        planes=[ffn_out.reshape(seqs, 3 * piece, slab)],
        to_line=[line_pack],
        everys=[grad_qkv.astype(bf16).reshape(devices, share, 3 * LANES), owner_pack],
        alls=[shared_pack],
        scatters=[grad_normed],
    )

    scale_one = norm_scale(inputs)
    input_grad = grad_middle + norm_pull(inputs, scale_one, gain_one, grad_normed)

    def over_rows(got):
        summed = jnp.sum(got.astype(f32).reshape((seqs, lines) + got.shape[1:]), axis=1)
        return summed[::copies]

    grad_qkv = over_rows(qkv_got).reshape(groups, share, 3, LANES)[..., :width]
    grad_qkv = grad_qkv.transpose(1, 2, 0, 3).reshape(share, 3 * D)
    owner_sums = over_rows(owner_got)
    memory_rows = heads * hidden_share
    grad_memory = owner_sums[:, :memory_rows].reshape(HEAD_COUNT, hidden_share, LANES)
    grad_memory_w1 = grad_memory[..., :HEAD_SIZE].transpose(0, 2, 1)
    grad_memory_w2 = grad_memory[..., HEAD_SIZE:]
    grad_gate = owner_sums[:, memory_rows : memory_rows + 24, :share]
    grad_gate = grad_gate.reshape(groups, 3, 8, share)[:, :, :heads].transpose(3, 1, 0, 2)
    grad_gate = grad_gate.reshape(share, 3 * HEAD_COUNT)
    grad_gain_two = jnp.sum(owner_got[:, memory_rows + 24, :share].astype(f32), axis=0)
    own_gain = norm1_gain.astype(f32)
    along = jnp.sum(grad_qkv * qkv_weight.astype(f32), axis=1)
    along = along + jnp.sum(grad_gate * gate_weight.astype(f32), axis=1)
    grad_gain_one = along / own_gain
    shared_sums = over_rows(shared_got)
    grad_conv = shared_sums[:, :12].reshape(groups, 4, 3, LANES)[..., :width]
    grad_conv = grad_conv.transpose(1, 2, 0, 3).reshape(4, 3 * D)
    grad_conv = lax.dynamic_slice_in_dim(grad_conv, me * 3 * share, 3 * share, 1)
    grad_bias = shared_sums[:, 12, :24].reshape(groups, 3, 8)[:, :, :heads]
    grad_bias = grad_bias.transpose(1, 0, 2).reshape(3, HEAD_COUNT)
    grad_bias = grad_bias * jnp.array([[3.0], [1.0], [1.0]], f32)
    line_sums = jnp.sum(line_got, axis=0)
    line_sums = lax.dynamic_slice_in_dim(line_sums, me * share - group * width, share, 1)
    ffn_sums = ffn_got.astype(f32).reshape(seqs, 3, piece, slab).transpose(1, 2, 0, 3)
    ffn_sums = ffn_sums.reshape(3, piece, seqs * slab)
    return (
        output[None],
        input_grad[None],
        grad_gain_one,
        grad_qkv,
        grad_gate,
        grad_conv,
        grad_memory_w1,
        grad_memory_w2,
        line_sums[:P_SIZE],
        line_sums[P_SIZE:],
        grad_out.astype(f32),
        grad_gain_two,
        ffn_sums[0],
        ffn_sums[1],
        ffn_sums[2].T,
        grad_bias,
    )


def solution(mesh):
    return jax.shard_map(
        on_device,
        mesh=mesh,
        in_specs=(
            P("fsdp", "seq", None),
            P(("seq", "fsdp")),
            P(("seq", "fsdp"), None),
            P(("seq", "fsdp"), None),
            P(None, ("seq", "fsdp")),
            P(None, None, ("seq", "fsdp")),
            P(None, ("seq", "fsdp"), None),
            P(None, ("seq", "fsdp")),
            P(None, ("seq", "fsdp")),
            P(("seq", "fsdp"), None),
            P(("seq", "fsdp")),
            P("seq", "fsdp"),
            P("seq", "fsdp"),
            P("fsdp", "seq"),
            P(),
            P("fsdp", None),
            P("fsdp", "seq"),
            P("fsdp", "seq", None),
        ),
        out_specs=(
            P("fsdp", "seq", None),
            P("fsdp", "seq", None),
            P(("seq", "fsdp")),
            P(("seq", "fsdp"), None),
            P(("seq", "fsdp"), None),
            P(None, ("seq", "fsdp")),
            P(None, None, ("seq", "fsdp")),
            P(None, ("seq", "fsdp"), None),
            P(None, ("seq", "fsdp")),
            P(None, ("seq", "fsdp")),
            P(("seq", "fsdp"), None),
            P(("seq", "fsdp")),
            P("seq", "fsdp"),
            P("seq", "fsdp"),
            P("fsdp", "seq"),
            P(),
        ),
        check_vma=False,
    )
```

time: 2900 us -> 556 us (0.19)
  waiting for transfers between devices: 1470 us -> 50.5 us
  blocking collectives: 526 us -> 0 us
  Pallas kernels: 0 us -> 315 us
  matrix products: 330 us -> 79.8 us
  other arithmetic: 269 us -> 38.3 us
  local copies, waits for them, and re-layouts: 254 us -> 45.6 us
    reduce_scatter x10 -> x2, waiting for transfers between devices: 859 us -> 49 us  [the longest x1 49 us: on_device(): lax.psum_scatter(grad_out, ('seq', 'fsdp'), scatter_dimension=0, tiled=True)]
    all_gather x9 -> x0, blocking collectives: 447 us -> none  [the longest x1 78.7 us: on_device(): lax.all_gather(shards[5], ('seq', 'fsdp'), axis=1, tiled=True)]
    unnamed x32 -> x7, waiting for transfers between devices: 325 us -> 1.45 us
    pallas_call x0 -> x8, Pallas kernels: none -> 315 us  [the longest x6 221 us: exchange(): pl.pallas_call(partial(exchange_kernel, name, (seqs, lines), counts), out...]
    all_gather x14 -> x3, waiting for transfers between devices: 284 us -> 0.04 us  [the longest x1 0.02 us: on_device(): out_matrix = lax.all_gather(out_weight, ('seq', 'fsdp'), axis=0, tiled=True)]
    dot_general x107 -> x18, matrix products: 330 us -> 79.8 us  [the longest x6 23.1 us: dot_nt(): lax.dot_general(left, right, (((1,), (1,)), ((), ())), preferred_element_...]
    select_n x32 -> x0, other arithmetic: 119 us -> none  [step(): return jax.tree.map(lambda a, b: jnp.where(reached, a, b), new, before)]
    unnamed x2 -> x0, blocking collectives: 79.2 us -> none
  transfers between devices with their start and end apart: 35 -> 6, of which waited for: 16 -> 1; matrix products, arithmetic and copies ran while one was open for 27% -> 23% of each run, Pallas kernels for 0% -> 58%
where the time goes in v1:
time: 556 us; the launch traced here: 545 us
  Pallas kernels  315 us (57%)
  matrix products  79.8 us (14%)
  waiting for transfers between devices  50.5 us (9%)
  local copies, waits for them, and re-layouts  45.6 us (8%)
  other arithmetic  38.3 us (7%)
  between operations  15.4 us (3%)
    pallas_call x6, Pallas kernels, exchange(): pl.pallas_call(partial(exchange_kernel, name, (seqs, lines), counts), out...  221 us
    pallas_call x1, Pallas kernels, mix_backward(): pl.pallas_call(partial(backward_kernel, heads), grid=(count,), in_specs=[...  64.7 us
    reduce_scatter x1, waiting for transfers between devices, on_device(): lax.psum_scatter(grad_out, ('seq', 'fsdp'), scatter_dimension=0, tiled=True)  49 us
    pallas_call x1, Pallas kernels, mix_forward(): pl.pallas_call(partial(forward_kernel, heads), grid=(count,), in_specs=[p...  29.5 us
    dot_general x6, matrix products, dot_nt(): lax.dot_general(left, right, (((1,), (1,)), ((), ())), preferred_element_...  23.1 us
    dot_general x6, matrix products, dot_tn(): lax.dot_general(left, right, (((0,), (0,)), ((), ())), preferred_element_...  22 us
    unnamed x86, local copies, waits for them, and re-layouts  17.8 us
  transfers between devices with their start and end apart: 6, of which 1 were waited for; matrix products, arithmetic and copies ran while one was open for 23% of the time, Pallas kernels for 58%

profile of v1, /device:TPU:0, one launch (start us, length us, event | category | flops | bytes accessed | tf_op | source)
XLA Modules:
  0.0 545.3 jit_solution(1859963846429390822)
XLA Ops:
  21.3 65.3 %first_exchange.1 = (bf16[8,256,1024]{2,1,0:T(8,128)(2,1)}, bf16[8,384,128]{2,1,0:T(8,128)(2,1)}, bf16[32,32,384]{2,1,0:T(8,128)(2,1)}, bf16[32,16,128]{2,1,0:T(8,128)(2,1)}, bf16[32,80,128]{2,1,0:T(8,128)(2,1)}) custom-call(bf16[256,1024]{1,0:T(8,128)(2,1)} %bitcast.224, bf16[8,384,128]{2,1,0:T(8,128)(2,1)} %bitcast.234, ...), custom_call_target="tpu_custom_call" | custom-call | tf_op jit(solution)/shard_map/first_exchange/pallas_call | solution.py:912
  94.4 3.4 multiply_reduce_fusion
  106.5 5.7 %convolution_convert_fusion.1.raw_ref.tail_ref = bf16[2048,384]{1,0:T(8,128)(2,1)} fusion(bf16[2048,1024]{1,0:T(8,128)(2,1)} %bitcast.221, bf16[1024,384]{1,0:T(8,128)(2,1)S(1)} %bitcast.247), kind=kOutput, calls=%fused_computation.21 | convolution fusion | flops 1611399168 | bytes 6553600 | tf_op jit(solution)/shard_map/dot_general | solution.py:1060
  112.3 29.5 %mix_forward.1 = (bf16[2048,128]{1,0:T(8,128)(2,1)}, bf16[2048,128]{1,0:T(8,128)(2,1)}, bf16[2048,128]{1,0:T(8,128)(2,1)}, f32[2048,8]{1,0:T(8,128)}, bf16[8,2,2,256,128]{4,3,2,1,0:T(8,128)(2,1)}) custom-call(bf16[2048,384]{1,0:T(8,128)(2,1)} %convolution_convert_fusion.1.raw_ref.tail_ref, f32[8,32,256]{2,1,0:T(8,128)} %pad_maximum_fusion.2.gate_ref.gate_prev_ref, ...), custom_call_target="tpu_custom_call" | custom-call | tf_op jit(solution)/shard_map/mix_forward/pallas_call | solution.py:507
  141.8 8.8 %to_segments.1 = bf16[8,256,128]{2,1,0:T(8,128)(2,1)} custom-call(bf16[8,256,128]{2,1,0:T(8,128)(2,1)} %bitcast.261), custom_call_target="tpu_custom_call" | custom-call | tf_op jit(solution)/shard_map/to_segments/pallas_call | solution.py:912
  155.3 36.3 %second_rows.1 = bf16[8,256,1024]{2,1,0:T(8,128)(2,1)} custom-call(bf16[256,1024]{1,0:T(8,128)(2,1)} %multiply_convert_fusion.2.refs_0_), custom_call_target="tpu_custom_call" | custom-call | tf_op jit(solution)/shard_map/second_rows/pallas_call | solution.py:912
  191.7 7.0 %fusion.27 = f32[2048,512]{1,0:T(8,128)} fusion(bf16[2048,1024]{1,0:T(8,128)(2,1)} %bitcast.228, bf16[3072,512]{1,0:T(8,128)(2,1)} %all-gather.7.cloned.1.call-done), kind=kOutput, calls=%fused_computation.55 | convolution fusion | flops 2147483648 | bytes 9437184 | tf_op jit(solution)/shard_map/dot_general | solution.py:1082
  198.6 5.5 %fusion.31 = f32[2048,512]{1,0:T(8,128)} fusion(bf16[2048,1024]{1,0:T(8,128)(2,1)S(1)} %bitcast.230, bf16[3072,512]{1,0:T(8,128)(2,1)} %all-gather.7.cloned.1.call-done), kind=kOutput, calls=%fused_computation.59 | convolution fusion | flops 2147483648 | bytes 9437184 | tf_op jit(solution)/shard_map/dot_general | solution.py:1081
  204.2 11.1 %fusion.4 = (bf16[2048,512]{1,0:T(8,128)(2,1)}, bf16[2048,512]{1,0:T(8,128)(2,1)}, bf16[2048,512]{1,0:T(8,128)(2,1)S(1)}) fusion(f32[2048,512]{1,0:T(8,128)} %fusion.31, f32[2048,512]{1,0:T(8,128)} %fusion.27, bf16[3072,512]{1,0:T(8,128)(2,1)} %all-gather.7.cloned.1.call-done, bf16[1,2048,1024]{2,1,0:T(8,128)(2,1)} %all-gather.9.cloned.1.call-done), kind=kOutput, calls=%fused_computation.11 | convolution fusion | flops 2163212288 | bytes 19922944 | tf_op jit(solution)/shard_map/dot_general | solution.py:1086
  216.5 5.6 %convolution_convert_fusion = bf16[2048,1024]{1,0:T(8,128)(2,1)} fusion(bf16[2048,512]{1,0:T(8,128)(2,1)S(1)} %get-tuple-element.150, bf16[3072,512]{1,0:T(8,128)(2,1)} %all-gather.7.cloned.1.call-done), kind=kOutput, calls=%fused_computation.19 | convolution fusion | flops 2149580800 | bytes 7340032 | tf_op jit(solution)/shard_map/dot_general | solution.py:32
  222.6 5.4 convolution_convert_fusion.3
  235.6 4.7 copy.205
  240.8 4.4 fusion.1
  248.4 4.5 add_convert_fusion.1
  252.9 39.4 %second_sums.1 = f32[256,1024]{1,0:T(8,128)} custom-call(bf16[8,256,1024]{2,1,0:T(8,128)(2,1)} %bitcast.227), custom_call_target="tpu_custom_call" | custom-call | tf_op jit(solution)/shard_map/second_sums/pallas_call | solution.py:912
  294.0 2.6 convert_add_fusion.1
  300.2 9.2 %to_heads.1 = bf16[8,256,128]{2,1,0:T(8,128)(2,1)} custom-call(bf16[8,256,128]{2,1,0:T(8,128)(2,1)} %bitcast.240), custom_call_target="tpu_custom_call" | custom-call | tf_op jit(solution)/shard_map/to_heads/pallas_call | solution.py:912
  309.4 64.7 %mix_backward.1 = (bf16[2048,384]{1,0:T(8,128)(2,1)}, f32[8,24,256]{2,1,0:T(8,128)}, f32[2,256,128]{2,1,0:T(8,128)}, f32[8,384]{1,0:T(8,128)}, f32[16,128]{1,0:T(8,128)}, /*index=5*/f32[16,128]{1,0:T(8,128)}) custom-call(bf16[2048,384]{1,0:T(8,128)(2,1)} %convolution_convert_fusion.1.raw_ref.tail_ref, ...), custom_call_target="tpu_custom_call" | custom-call | tf_op jit(solution)/shard_map/mix_backward/pallas_call | solution.py:559
  377.3 3.0 fusion.16
  382.8 7.2 %fusion.55 = f32[2048,1024]{1,0:T(8,128)} fusion(bf16[2048,384]{1,0:T(8,128)(2,1)} %get-tuple-element.50, bf16[1024,384]{1,0:T(8,128)(2,1)S(1)} %bitcast.248), kind=kOutput, calls=%fused_computation.144 | convolution fusion | flops 1610612736 | bytes 10747904 | tf_op jit(solution)/shard_map/dot_general | solution.py:32
  390.0 3.2 convolution_convert_fusion.5
  394.5 6.6 %add_convert_fusion = bf16[2048,1024]{1,0:T(8,128)(2,1)} fusion(f32[2048,1024]{1,0:T(8,128)} %fusion.55, bf16[24,2048]{1,0:T(8,128)(2,1)S(1)} %bitcast.262, bf16[3,2,1024]{2,1,0:T(2,128)(2,1)S(1)} %dynamic-slice_bitcast_fusion), kind=kOutput, calls=%fused_computation.3 | convolution fusion | flops 104857600 | bytes 12693504 | tf_op jit(solution)/shard_map/dot_general | solution.py:40
  402.4 61.7 %last_exchange.1 = (bf16[8,384,128]{2,1,0:T(8,128)(2,1)}, f32[4,32,128]{2,1,0:T(8,128)}, bf16[32,32,384]{2,1,0:T(8,128)(2,1)}, bf16[32,48,128]{2,1,0:T(8,128)(2,...) custom-call(bf16[8,384,128]{2,1,0:T(8,128)(2,1)} %bitcast.232, f32[32,128]{1,0:T(8,128)} %pad_maximum_fusion.5.refs_1_, ...), custom_call_target="tpu_custom_call" | custom-call | tf_op jit(solution)/shard_map/last_exchange/pallas_call | solution.py:912
  487.5 49.0 %reduce-scatter.8.cloned.1.call-done = bf16[32,1024]{1,0:T(8,128)(2,1)} async-done(((bf16[1024,1024]{1,0:T(8,128)(2,1)}), bf16[32,1024]{1,0:T(8,128)(2,1)}) %reduce-scatter.8.cloned.1.call-update) | async-done | bytes 65552 | tf_op jit(solution)/shard_map/reduce_scatter | solution.py:1107
  (225 shorter events, 86.1 us)
Async XLA Ops:
  7.2 144.7 %all-gather.5.cloned.1.call-start = ((), (), s32[]{:S(2)}) async-start(), calls=%async_computation.3 | async-start | bytes 2162688 | tf_op jit(solution)/shard_map/all_gather | solution.py:1015
  7.9 183.7 %all-gather.7.cloned.1.call-start = ((), (), s32[]{:S(2)}) async-start(), calls=%async_computation.4 | async-start | bytes 3932160 | tf_op jit(solution)/shard_map/all_gather | solution.py:1017
  16.6 74.9 %copy-start.31 = (s32[1,4]{1,0:T(1,128)S(1)}, s32[1,4]{1,0:T(1,128)}, u32[]{:S(2)}) copy-start(s32[1,4]{1,0:T(1,128)} %param.36) | copy-start | bytes 52
  16.6 75.1 %copy-start.24 = (f32[3,16]{1,0:T(4,128)S(1)}, f32[3,16]{1,0:T(4,128)}, u32[]{:S(2)}) copy-start(f32[3,16]{1,0:T(4,128)} %param.35) | copy-start | bytes 580
  16.6 75.1 %copy-start.25 = (f32[3]{0:T(128)S(1)}, f32[3]{0:T(128)}, u32[]{:S(2)}) copy-start(f32[3]{0:T(128)} %constant.126) | copy-start | bytes 40
  16.7 75.1 %copy-start.28 = (f32[3]{0:T(128)S(1)}, f32[3]{0:T(128)}, u32[]{:S(2)}) copy-start(f32[3]{0:T(128)} %constant.127) | copy-start | bytes 40
  86.6 5.8 %copy-start.13 = (bf16[32,80,128]{2,1,0:T(8,128)(2,1)S(1)}, bf16[32,80,128]{2,1,0:T(8,128)(2,1)}, u32[]{:S(2)}) copy-start(bf16[32,80,128]{2,1,0:T(8,128)(2,1)} %get-tuple-element.39) | copy-start | bytes 1966084
  88.9 115.3 %all-gather.9.cloned.1.call-start = ((), (), s32[]{:S(2)}) async-start(), calls=%async_computation.7 | async-start | bytes 4718592 | tf_op jit(solution)/shard_map/all_gather | solution.py:1018
  89.6 204.4 %reduce-scatter.6.cloned.1.call-start = ((), (), s32[]{:S(2)}) async-start(), calls=%async_computation.5 | async-start | bytes 4718592 | tf_op jit(solution)/shard_map/reduce_scatter | solution.py:1094
  103.9 8.4 %copy-start.7 = (bf16[2,256,128]{2,1,0:T(8,128)(2,1)}, bf16[2,256,128]{2,1,0:T(8,128)(2,1)S(1)}, u32[]{:S(2)}) copy-start(bf16[2,256,128]{2,1,0:T(8,128)(2,1)S(1)} %copy_bitcast_fusion.5.mem_ref) | copy-start | bytes 393220
  112.3 39.6 %copy-start.2 = (bf16[1,256,1024]{2,1,0:T(8,128)(2,1)S(1)}, bf16[1,256,1024]{2,1,0:T(8,128)(2,1)}, u32[]{:S(2)}) copy-start(bf16[1,256,1024]{2,1,0:T(8,128)(2,1)} %param.21) | copy-start | bytes 1572868
  191.7 7.0 %copy-start.4 = (bf16[8,256,1024]{2,1,0:T(8,128)(2,1)S(1)}, bf16[8,256,1024]{2,1,0:T(8,128)(2,1)}, u32[]{:S(2)}) copy-start(bf16[8,256,1024]{2,1,0:T(8,128)(2,1)} %second_rows.1) | copy-start | bytes 12582916
  222.1 158.2 %reduce-scatter.10.cloned.1.call-start = ((), (), s32[]{:S(2)}) async-start(), calls=%async_computation.8 | async-start | bytes 3932160
  240.4 296.1 %reduce-scatter.8.cloned.1.call-start = ((), (), s32[]{:S(2)}) async-start(), calls=%async_computation.6 | async-start | bytes 2162688 | tf_op jit(solution)/shard_map/reduce_scatter | solution.py:1107
  382.8 7.2 %copy-start.6 = (bf16[2048,1024]{1,0:T(8,128)(2,1)S(1)}, bf16[2048,1024]{1,0:T(8,128)(2,1)}, u32[]{:S(2)}) copy-start(bf16[2048,1024]{1,0:T(8,128)(2,1)} %fusion.1) | copy-start | bytes 12582916
  382.8 7.2 %copy-start.8 = (bf16[2048,384]{1,0:T(8,128)(2,1)S(1)}, bf16[2048,384]{1,0:T(8,128)(2,1)}, u32[]{:S(2)}) copy-start(bf16[2048,384]{1,0:T(8,128)(2,1)} %get-tuple-element.50) | copy-start | bytes 4718596
  394.5 7.3 %copy-start.21 = (f32[16,128]{1,0:T(8,128)S(1)}, f32[16,128]{1,0:T(8,128)}, u32[]{:S(2)}) copy-start(f32[16,128]{1,0:T(8,128)} %get-tuple-element.48) | copy-start | bytes 24580
  394.5 7.3 %copy-start.22 = (f32[16,128]{1,0:T(8,128)S(1)}, f32[16,128]{1,0:T(8,128)}, u32[]{:S(2)}) copy-start(f32[16,128]{1,0:T(8,128)} %get-tuple-element.49) | copy-start | bytes 24580
  472.8 10.2 %copy-start.3 = (f32[256,1024]{1,0:T(8,128)S(1)}, f32[256,1024]{1,0:T(8,128)}, u32[]{:S(2)}) copy-start(f32[256,1024]{1,0:T(8,128)} %get-tuple-element.54) | copy-start | bytes 3145732
  476.0 7.4 %copy-start.11 = (bf16[32,3072]{1,0:T(8,128)(2,1)S(1)}, bf16[32,3072]{1,0:T(8,128)(2,1)}, u32[]{:S(2)}) copy-start(bf16[32,3072]{1,0:T(8,128)(2,1)} %param.23) | copy-start | bytes 589828
  476.0 8.3 %copy-start.27 = (bf16[32]{0:T(256)(128)(2,1)S(1)}, bf16[32]{0:T(256)(128)(2,1)}, u32[]{:S(2)}) copy-start(bf16[32]{0:T(256)(128)(2,1)} %param.22) | copy-start | bytes 196
  476.0 8.8 %copy-start.20 = (f32[3,16]{1,0:T(4,128)S(1)}, f32[3,16]{1,0:T(4,128)}, u32[]{:S(2)}) copy-start(f32[3,16]{1,0:T(4,128)} %reshape.486) | copy-start | bytes 580
  476.0 8.8 %copy-start.26 = (f32[3]{0:T(128)S(1)}, f32[3]{0:T(128)}, u32[]{:S(2)}) copy-start(f32[3]{0:T(128)} %constant.126) | copy-start | bytes 40
  476.0 9.5 %slice-start = ((f32[8,48,128]{2,1,0:T(8,128)}), f32[8,16,128]{2,1,0:T(8,128)S(1)}, s32[]{:S(2)}) async-start(f32[8,48,128]{2,1,0:T(8,128)} %copy-done.12), calls=%async_computation.9 | async-start | bytes 131072 | tf_op jit(solution)/shard_map/slice | solution.py:1165
  (20 other events, 74.7 us)
Sparse Core Ops, SparseCore 0:
  10.9 74.2 all-gather.4
  89.0 61.9 all-gather.6
  152.8 48.1 all-gather.8
  222.2 63.8 reduce-scatter.5
  288.4 58.2 reduce-scatter.9
  394.6 141.8 reduce-scatter.7

commit v2 on v1

--- a/solution.py
+++ b/solution.py
@@ -1,3 +1,4 @@
+import math
 from functools import partial
 
 import jax
@@ -148,7 +149,29 @@
     return fixed, prev, now
 
 
-def forward_kernel(
+def forward_kernel(heads, plan, *refs):
+    carried = len(plan.arrays)
+    own, refs = refs[:8], refs[8:]
+    sent, refs = refs[:carried], refs[carried:]
+    made, refs = refs[:5], refs[5:]
+    got, refs = refs[:carried], refs[carried:]
+    begin, middle, finish = plan.phases(sent, got, refs[5:])
+    at, last = pl.program_id(0), pl.num_programs(0) - 1
+
+    @pl.when(at == 0)
+    def _():
+        greet_all(plan.axes, plan.kinds)
+        begin()
+
+    forward_step(heads, *own, *made, *refs[:5])
+
+    @pl.when(at == last)
+    def _():
+        middle()
+        finish()
+
+
+def forward_step(
     heads,
     raw_ref,
     gate_ref,
@@ -272,7 +295,32 @@
     return jnp.where(lane == 0, start, pltpu.roll(after, 1, 1))
 
 
-def backward_kernel(
+def backward_kernel(heads, plan, *refs):
+    carried = len(plan.arrays)
+    own, refs = refs[:17], refs[17:]
+    sent, refs = refs[:carried], refs[carried:]
+    made, refs = refs[:6], refs[6:]
+    got, refs = refs[:carried], refs[carried:]
+    begin, middle, finish = plan.phases(sent, got, refs[5:])
+    at, last = pl.program_id(0), pl.num_programs(0) - 1
+
+    @pl.when(at == 0)
+    def _():
+        greet_all(plan.axes, plan.kinds)
+        begin()
+
+    backward_step(heads, *own, *made, *refs[:5])
+
+    @pl.when(at == 1)
+    def _():
+        middle()
+
+    @pl.when(at == last)
+    def _():
+        finish()
+
+
+def backward_step(
     heads,
     raw_ref,
     tail_ref,
@@ -500,49 +548,71 @@
     return pl.BlockSpec(array.shape, lambda n: zeros)
 
 
-def mix_forward(heads, raw, gates, place, conv, mem, swap, pkeys, pvalues):
+def mix_forward(collective, plan, heads, raw, gates, place, conv, mem, swap, pkeys, pvalues):
     length = raw.shape[0]
     count = length // SEG
     row_block = pl.BlockSpec((SEG, LANES), lambda n: (n, 0))
     return pl.pallas_call(
-        partial(forward_kernel, heads),
+        partial(forward_kernel, heads, plan),
         grid=(count,),
         in_specs=[
             pl.BlockSpec((SEG, 3 * LANES), lambda n: (n, 0)),
             pl.BlockSpec((1, 32, SEG), lambda n: (n, 0, 0)),
             pl.BlockSpec((SEG, 1), lambda n: (n, 0)),
         ]
-        + [whole_of(member) for member in (conv, mem, swap, pkeys, pvalues)],
+        + [whole_of(member) for member in (conv, mem, swap, pkeys, pvalues)]
+        + plan.specs(True)[0],
         out_specs=[
             row_block,
             row_block,
             row_block,
             pl.BlockSpec((SEG, 8), lambda n: (n, 0)),
             pl.BlockSpec((1, heads, 2, MH, LANES), lambda n: (n, 0, 0, 0, 0)),
-        ],
+        ]
+        + plan.specs(True)[1],
         out_shape=[
             jax.ShapeDtypeStruct((length, LANES), bf16),
             jax.ShapeDtypeStruct((length, LANES), bf16),
             jax.ShapeDtypeStruct((length, LANES), bf16),
             jax.ShapeDtypeStruct((length, 8), f32),
             jax.ShapeDtypeStruct((count, heads, 2, MH, LANES), bf16),
-        ],
+        ]
+        + plan.shapes,
         scratch_shapes=[
             pltpu.VMEM((SEG + 8, 3 * LANES), f32),
             pltpu.VMEM((SEG, LANES), bf16),
             pltpu.VMEM((SEG, LANES), bf16),
             pltpu.VMEM((8, SEG), f32),
             pltpu.VMEM((heads, 2, MH, LANES), f32),
-        ],
+        ]
+        + plan.scratch,
         compiler_params=pltpu.CompilerParams(
-            dimension_semantics=("arbitrary",), vmem_limit_bytes=VMEM_GRANT
+            dimension_semantics=("arbitrary",),
+            collective_id=collective,
+            has_side_effects=True,
+            vmem_limit_bytes=VMEM_GRANT,
         ),
         name="mix_forward",
-    )(raw, gates, place, conv, mem, swap, pkeys, pvalues)
+    )(raw, gates, place, conv, mem, swap, pkeys, pvalues, *plan.arrays)
 
 
 def mix_backward(
-    heads, raw, gates, place, keys, values, totals, states, grad, conv, mem, swap, pkeys, pvalues
+    collective,
+    plan,
+    heads,
+    raw,
+    gates,
+    place,
+    keys,
+    values,
+    totals,
+    states,
+    grad,
+    conv,
+    mem,
+    swap,
+    pkeys,
+    pvalues,
 ):
     length = raw.shape[0]
     count = length // SEG
@@ -557,7 +627,7 @@
     prev_block = pl.BlockSpec((SEG, LANES), lambda n: (before(n), 0))
     tail_rows = SEG // 16
     return pl.pallas_call(
-        partial(backward_kernel, heads),
+        partial(backward_kernel, heads, plan),
         grid=(count,),
         in_specs=[
             pl.BlockSpec((SEG, 3 * LANES), lambda n: (here(n), 0)),
@@ -573,7 +643,8 @@
             pl.BlockSpec((1, heads, 2, MH, LANES), lambda n: (here(n), 0, 0, 0, 0)),
             row_block,
         ]
-        + [whole_of(member) for member in (conv, mem, swap, pkeys, pvalues)],
+        + [whole_of(member) for member in (conv, mem, swap, pkeys, pvalues)]
+        + plan.specs(True)[0],
         out_specs=[
             pl.BlockSpec((SEG, 3 * LANES), lambda n: (here(n), 0)),
             pl.BlockSpec((1, 24, SEG), lambda n: (here(n), 0, 0)),
@@ -581,7 +652,8 @@
             pl.BlockSpec((8, 3 * LANES), lambda n: (0, 0)),
             pl.BlockSpec((P_SIZE, LANES), lambda n: (0, 0)),
             pl.BlockSpec((P_SIZE, LANES), lambda n: (0, 0)),
-        ],
+        ]
+        + plan.specs(True)[1],
         out_shape=[
             jax.ShapeDtypeStruct((length, 3 * LANES), bf16),
             jax.ShapeDtypeStruct((count, 24, SEG), f32),
@@ -589,16 +661,21 @@
             jax.ShapeDtypeStruct((8, 3 * LANES), f32),
             jax.ShapeDtypeStruct((P_SIZE, LANES), f32),
             jax.ShapeDtypeStruct((P_SIZE, LANES), f32),
-        ],
+        ]
+        + plan.shapes,
         scratch_shapes=[
             pltpu.VMEM((SEG + 8, 3 * LANES), f32),
             pltpu.VMEM((3, SEG + 8, 3 * LANES), f32),
             pltpu.VMEM((SEG, LANES), f32),
             pltpu.VMEM((SEG, LANES), f32),
             pltpu.VMEM((heads, 2, MH, LANES), f32),
-        ],
+        ]
+        + plan.scratch,
         compiler_params=pltpu.CompilerParams(
-            dimension_semantics=("arbitrary",), vmem_limit_bytes=VMEM_GRANT
+            dimension_semantics=("arbitrary",),
+            collective_id=collective,
+            has_side_effects=True,
+            vmem_limit_bytes=VMEM_GRANT,
         ),
         name="mix_backward",
     )(
@@ -619,16 +696,14 @@
         swap,
         pkeys,
         pvalues,
+        *plan.arrays,
     )
 
 
-def exchange_kernel(name, axes, counts, *refs):
+def exchange_phases(axes, counts, inputs, outputs, scratch):
     seqs, lines = axes
     chips = seqs // 2
     devices = seqs * lines
-    gathers, planes, rows_to, everys, alls, scatters = counts
-    total_in = sum(counts)
-    inputs, outputs, scratch = refs[:total_in], refs[total_in : 2 * total_in], refs[2 * total_in :]
     seq, line = lax.axis_index("seq"), lax.axis_index("fsdp")
     me = seq * lines + line
     chip, core = seq // 2, lax.rem(seq, 2)
@@ -646,26 +721,6 @@
             return carry
 
         lax.fori_loop(first, last, step, 0)
-
-    barrier = pltpu.get_barrier_semaphore()
-    if everys or alls or rows_to:
-
-        def greet(k):
-            pl.semaphore_signal(
-                barrier, inc=1, device_id=point(lax.rem(me + k, devices)), device_id_type=MESH
-            )
-
-        loop(1, devices, greet)
-        pl.semaphore_wait(barrier, devices - 1)
-    else:
-
-        def greet(k):
-            pl.semaphore_signal(
-                barrier, inc=1, device_id=(lax.rem(seq + k, seqs), line), device_id_type=MESH
-            )
-
-        loop(1, seqs, greet)
-        pl.semaphore_wait(barrier, seqs - 1)
 
     position = 0
     groups = []
@@ -678,6 +733,8 @@
         taken = scratch[:number]
         del scratch[:number]
         return taken
+
+    starts = []
 
     sums = []
     for source, target in zip(*groups[5]):
@@ -703,7 +760,9 @@
                 device_id_type=MESH,
             )
 
-        loop(1, chips + 1, lambda k, f=pair_copy: f(lax.rem(chip + k, chips)).start())
+        starts.append(
+            lambda f=pair_copy: loop(1, chips + 1, lambda k: f(lax.rem(chip + k, chips)).start())
+        )
         sums.append((source, target, pair, landed, pair_copy, far_copy))
 
     spread = []
@@ -753,9 +812,12 @@
                 device_id_type=MESH,
             )
 
-        loop(1, chips, lambda k, f=far: f(lax.rem(chip + k, chips), chip).start())
-        near_own().start()
-        own().start()
+        def start(far=far, near_own=near_own, own=own):
+            loop(1, chips, lambda k: far(lax.rem(chip + k, chips), chip).start())
+            near_own().start()
+            own().start()
+
+        starts.append(start)
         spread.append((own, far, near_own, near, near_arrival))
 
     direct = []
@@ -775,7 +837,7 @@
                 number, mine = devices, me
 
             def piece(i, source=source, kind=kind, number=number):
-                if kind in ("line", "all"):
+                if kind == "all" or (kind == "line" and source.ndim == 2):
                     return source
                 if kind == "every" and source.shape[0] != number:
                     return source.at[i // lines]
@@ -801,125 +863,576 @@
             def own(target=target, local=local, piece=piece, mine=mine):
                 return pltpu.make_async_copy(piece(mine), target.at[mine], local.at[0])
 
-            loop(
-                1,
-                number,
-                lambda k, f=copy, m=mine, c=number: f(lax.rem(m + k, c), m).start(),
+            def start(copy=copy, own=own, mine=mine, number=number):
+                loop(1, number, lambda k: copy(lax.rem(mine + k, number), mine).start())
+                own().start()
+
+            starts.append(start)
+            direct.append((own, copy, mine, number))
+
+    relays = []
+    for source, target in zip(*groups[6]):
+        local, plane_send, plane_recv, line_send, line_recv = take(5)
+
+        def copy(i, slot, source=source, target=target, send=plane_send, recv=plane_recv):
+            return pltpu.make_async_remote_copy(
+                src_ref=source.at[i],
+                dst_ref=target.at[line, slot],
+                send_sem=send.at[i],
+                recv_sem=recv.at[slot],
+                device_id=(i, line),
+                device_id_type=MESH,
             )
+
+        def own(source=source, target=target, local=local):
+            return pltpu.make_async_copy(source.at[seq], target.at[line, seq], local.at[0])
+
+        def onward(i, slot, target=target, send=line_send, recv=line_recv):
+            return pltpu.make_async_remote_copy(
+                src_ref=target.at[slot],
+                dst_ref=target.at[slot],
+                send_sem=send.at[i],
+                recv_sem=recv.at[slot],
+                device_id=(seq, i),
+                device_id_type=MESH,
+            )
+
+        def start(copy=copy, own=own):
+            loop(1, seqs, lambda k: copy(lax.rem(seq + k, seqs), seq).start())
             own().start()
-            direct.append((own, copy, mine, number))
-
+
+        starts.insert(0, start)
+        relays.append((own, copy, onward))
+
+    merges = []
     rows = 32
-    for source, target, pair, landed, pair_copy, far_copy in sums:
-
-        def combine(k, source=source, pair=pair, pair_copy=pair_copy, far_copy=far_copy):
-            q = lax.rem(chip + k, chips)
-            pair_copy(q).wait_recv()
-
-            def add(r):
+    for source, target in zip(*groups[7]):
+        landed, summed, local, line_send, line_recv, plane_send, plane_recv = take(7)
+
+        def copy(i, slot, source=source, landed=landed, send=line_send, recv=line_recv):
+            return pltpu.make_async_remote_copy(
+                src_ref=source.at[i],
+                dst_ref=landed.at[slot],
+                send_sem=send.at[i],
+                recv_sem=recv.at[slot],
+                device_id=(seq, i),
+                device_id_type=MESH,
+            )
+
+        def own(source=source, landed=landed, local=local):
+            return pltpu.make_async_copy(source.at[line], landed.at[line], local.at[0])
+
+        def onward(i, slot, summed=summed, target=target, send=plane_send, recv=plane_recv):
+            return pltpu.make_async_remote_copy(
+                src_ref=summed.at[i],
+                dst_ref=target.at[slot],
+                send_sem=send.at[i],
+                recv_sem=recv.at[slot],
+                device_id=(i, line),
+                device_id_type=MESH,
+            )
+
+        def keep(summed=summed, target=target, local=local):
+            return pltpu.make_async_copy(summed.at[seq], target.at[seq], local.at[0])
+
+        def start(copy=copy, own=own):
+            loop(1, lines, lambda k: copy(lax.rem(line + k, lines), line).start())
+            own().start()
+
+        starts.insert(0, start)
+        merges.append((landed, summed, own, copy, onward, keep))
+
+    def begin():
+        for start in starts:
+            start()
+
+    def middle():
+        for source, target, pair, landed, pair_copy, far_copy in sums:
+
+            def combine(k, source=source, pair=pair, pair_copy=pair_copy, far_copy=far_copy):
+                q = lax.rem(chip + k, chips)
+                pair_copy(q).wait_recv()
+
+                def add(r):
+                    part = pl.ds(pl.multiple_of(r * rows, rows), rows)
+                    both = source[2 * q + core, part, :].astype(f32) + pair[q, part, :].astype(f32)
+                    pair[q, part, :] = both.astype(bf16)
+
+                loop(0, source.shape[1] // rows, add)
+
+                @pl.when(k < chips)
+                def _():
+                    far_copy(q, chip).start()
+
+            loop(1, chips + 1, combine)
+        for own, copy, onward in relays:
+            loop(1, seqs, lambda k, f=copy: f(lax.rem(seq + k, seqs), lax.rem(seq + k, seqs)).wait_recv())
+            own().wait()
+            loop(1, lines, lambda k, f=onward: f(lax.rem(line + k, lines), line).start())
+        for own, far, near_own, near, near_arrival in spread:
+
+            def forward(k, far=far, near=near):
+                q = lax.rem(chip + k, chips)
+                far(q, q).wait_recv()
+                near(q).start()
+
+            loop(1, chips, forward)
+        for landed, summed, own, copy, onward, keep in merges:
+            loop(1, lines, lambda k, f=copy: f(lax.rem(line + k, lines), lax.rem(line + k, lines)).wait_recv())
+            own().wait()
+
+            def add_up(k, landed=landed, summed=summed, onward=onward):
+                i = lax.rem(seq + k, seqs)
+                whole = landed[0, i].astype(f32)
+                for member in range(1, lines):
+                    whole = whole + landed[member, i].astype(f32)
+                summed[i] = whole.astype(bf16)
+
+                @pl.when(k < seqs)
+                def _():
+                    onward(i, seq).start()
+
+            loop(1, seqs + 1, add_up)
+            keep().start()
+
+    def finish():
+        for own, copy, mine, number in direct:
+
+            def end(k, copy=copy, mine=mine, number=number):
+                i = lax.rem(mine + k, number)
+                copy(i, i).wait_recv()
+                copy(i, i).wait_send()
+
+            loop(1, number, end)
+            own().wait()
+        for own, copy, onward in relays:
+            loop(1, seqs, lambda k, f=copy: f(lax.rem(seq + k, seqs), seq).wait_send())
+
+            def end_relay(k, onward=onward):
+                i = lax.rem(line + k, lines)
+                onward(i, i).wait_recv()
+                onward(i, line).wait_send()
+
+            loop(1, lines, end_relay)
+        for own, far, near_own, near, near_arrival in spread:
+            own().wait()
+            near_own().wait_send()
+
+            def end_far(k, far=far, near=near):
+                q = lax.rem(chip + k, chips)
+                far(q, q).wait_send()
+                near(q).wait_send()
+
+            loop(1, chips, end_far)
+            loop(0, chips, lambda q, f=near_arrival: f(q).wait_recv())
+        for source, target, pair, landed, pair_copy, far_copy in sums:
+
+            def end_sum(k, far_copy=far_copy):
+                q = lax.rem(chip + k, chips)
+                far_copy(q, q).wait_recv()
+
+            loop(1, chips, end_sum)
+
+            def add_all(r, target=target, pair=pair, landed=landed):
                 part = pl.ds(pl.multiple_of(r * rows, rows), rows)
-                both = source[2 * q + core, part, :].astype(f32) + pair[q, part, :].astype(f32)
-                pair[q, part, :] = both.astype(bf16)
-
-            loop(0, source.shape[1] // rows, add)
-
-            @pl.when(k < chips)
-            def _():
-                far_copy(q, chip).start()
-
-        loop(1, chips + 1, combine)
-    for own, far, near_own, near, near_arrival in spread:
-
-        def forward(k, far=far, near=near):
-            q = lax.rem(chip + k, chips)
-            far(q, q).wait_recv()
-            near(q).start()
-
-        loop(1, chips, forward)
-
-    for own, copy, mine, number in direct:
-
-        def end(k, copy=copy, mine=mine, number=number):
-            i = lax.rem(mine + k, number)
-            copy(i, i).wait_recv()
-            copy(i, i).wait_send()
-
-        loop(1, number, end)
-        own().wait()
-    for own, far, near_own, near, near_arrival in spread:
-        own().wait()
-        near_own().wait_send()
-
-        def end_far(k, far=far, near=near):
-            q = lax.rem(chip + k, chips)
-            far(q, q).wait_send()
-            near(q).wait_send()
-
-        loop(1, chips, end_far)
-        loop(0, chips, lambda q, f=near_arrival: f(q).wait_recv())
-    for source, target, pair, landed, pair_copy, far_copy in sums:
-
-        def end_sum(k, far_copy=far_copy, pair_copy=pair_copy):
-            q = lax.rem(chip + k, chips)
-            far_copy(q, q).wait_recv()
-
-        loop(1, chips, end_sum)
-
-        def add_all(r, target=target, pair=pair, landed=landed):
-            part = pl.ds(pl.multiple_of(r * rows, rows), rows)
-            whole = pair[chip, part, :].astype(f32)
-            for k in range(1, chips):
-                whole = whole + landed[lax.rem(chip + k, chips), part, :].astype(f32)
-            target[part, :] = whole
-
-        loop(0, target.shape[0] // rows, add_all)
-        loop(1, chips, lambda k, f=far_copy: f(lax.rem(chip + k, chips), chip).wait_send())
-        loop(0, chips, lambda q, f=pair_copy: f(q).wait_send())
-
-
-def exchange(
-    name, collective, gathers=(), planes=(), to_line=(), everys=(), alls=(), scatters=()
-):
-    seqs, lines = lax.axis_size("seq"), lax.axis_size("fsdp")
-    chips, devices = seqs // 2, seqs * lines
-    arrays = [*gathers, *planes, *to_line, *everys, *alls, *scatters]
-    counts = tuple(len(kind) for kind in (gathers, planes, to_line, everys, alls, scatters))
-    dma = pltpu.SemaphoreType.DMA
-    scratch = []
-    for array in scatters:
-        half = (chips,) + array.shape[1:]
-        scratch += [pltpu.VMEM(half, bf16), pltpu.VMEM(half, bf16)] + [dma((chips,))] * 4
-    for array in gathers:
-        scratch += [dma((1,))] + [dma((chips,))] * 4
-    shapes = [jax.ShapeDtypeStruct((seqs,) + array.shape, array.dtype) for array in gathers]
-    for array in planes:
-        scratch += [dma((1,)), dma((seqs,)), dma((seqs,))]
-        shapes.append(jax.ShapeDtypeStruct(array.shape, array.dtype))
-    for array in to_line:
-        scratch += [dma((1,)), dma((lines,)), dma((lines,))]
-        shapes.append(jax.ShapeDtypeStruct((lines,) + array.shape, array.dtype))
-    for array in everys:
-        scratch += [dma((1,)), dma((devices,)), dma((devices,))]
-        shapes.append(jax.ShapeDtypeStruct((devices,) + array.shape[1:], array.dtype))
-    for array in alls:
-        scratch += [dma((1,)), dma((devices,)), dma((devices,))]
-        shapes.append(jax.ShapeDtypeStruct((devices,) + array.shape, array.dtype))
-    for array in scatters:
-        shapes.append(jax.ShapeDtypeStruct(array.shape[1:], f32))
-    plain = len(arrays) - len(scatters)
-    any_spec, vmem_spec = pl.BlockSpec(memory_space=pl.ANY), pl.BlockSpec(memory_space=pltpu.VMEM)
-    specs = [any_spec] * plain + [vmem_spec] * len(scatters)
+                whole = pair[chip, part, :].astype(f32)
+                for k in range(1, chips):
+                    whole = whole + landed[lax.rem(chip + k, chips), part, :].astype(f32)
+                target[part, :] = whole
+
+            loop(0, target.shape[0] // rows, add_all)
+            loop(1, chips, lambda k, f=far_copy: f(lax.rem(chip + k, chips), chip).wait_send())
+            loop(0, chips, lambda q, f=pair_copy: f(q).wait_send())
+        for landed, summed, own, copy, onward, keep in merges:
+            loop(1, lines, lambda k, f=copy: f(lax.rem(line + k, lines), line).wait_send())
+
+            def end_merge(k, onward=onward):
+                i = lax.rem(seq + k, seqs)
+                onward(i, i).wait_recv()
+                onward(i, seq).wait_send()
+
+            loop(1, seqs, end_merge)
+            keep().wait()
+
+    return begin, middle, finish
+
+
+def greet_all(axes, kinds):
+    seqs, lines = axes
+    seq, line = lax.axis_index("seq"), lax.axis_index("fsdp")
+    barrier = pltpu.get_barrier_semaphore()
+
+    def signal(place):
+        pl.semaphore_signal(barrier, inc=1, device_id=place, device_id_type=MESH)
+
+    def loop(last, body):
+        def step(k, carry):
+            body(k)
+            return carry
+
+        lax.fori_loop(1, last, step, 0)
+
+    if "all" in kinds:
+        devices = seqs * lines
+        me = seq * lines + line
+
+        def greet(k):
+            i = lax.rem(me + k, devices)
+            signal((i // lines, lax.rem(i, lines)))
+
+        loop(devices, greet)
+        pl.semaphore_wait(barrier, devices - 1)
+        return
+    met = 0
+    if "plane" in kinds:
+        loop(seqs, lambda k: signal((lax.rem(seq + k, seqs), line)))
+        met += seqs - 1
+    if "line" in kinds:
+        loop(lines, lambda k: signal((seq, lax.rem(line + k, lines))))
+        met += lines - 1
+    pl.semaphore_wait(barrier, met)
+
+
+KINDS = ("gathers", "planes", "to_line", "everys", "alls", "scatters", "relays", "merges")
+
+
+class Exchange:
+    def __init__(self, **arrays):
+        self.axes = seqs, lines = lax.axis_size("seq"), lax.axis_size("fsdp")
+        chips, devices = seqs // 2, seqs * lines
+        dma = pltpu.SemaphoreType.DMA
+        groups = [tuple(arrays.get(kind, ())) for kind in KINDS]
+        self.counts = tuple(len(group) for group in groups)
+        self.arrays = [array for group in groups for array in group]
+        scratch = {kind: [] for kind in KINDS}
+        shapes, self.in_vmem = [], []
+        kinds = set()
+        for kind, group in zip(KINDS, groups):
+            for array in group:
+                shape, dtype = array.shape, array.dtype
+                if kind == "gathers":
+                    scratch[kind] += [dma((1,))] + [dma((chips,))] * 4
+                    shape = (seqs,) + shape
+                elif kind == "planes":
+                    scratch[kind] += [dma((1,)), dma((seqs,)), dma((seqs,))]
+                elif kind == "to_line":
+                    scratch[kind] += [dma((1,)), dma((lines,)), dma((lines,))]
+                    shape = (lines,) + shape[-2:]
+                elif kind == "everys":
+                    scratch[kind] += [dma((1,)), dma((devices,)), dma((devices,))]
+                    shape = (devices,) + shape[1:]
+                elif kind == "alls":
+                    scratch[kind] += [dma((1,)), dma((devices,)), dma((devices,))]
+                    shape = (devices,) + shape
+                elif kind == "scatters":
+                    half = pltpu.VMEM((chips,) + shape[1:], bf16)
+                    scratch[kind] += [half, half] + [dma((chips,))] * 4
+                    shape, dtype = shape[1:], f32
+                elif kind == "relays":
+                    scratch[kind] += [dma((1,))] + [dma((seqs,))] * 2 + [dma((lines,))] * 2
+                    shape = (lines,) + shape
+                else:
+                    scratch[kind] += [pltpu.VMEM(shape, bf16), pltpu.VMEM(shape[1:], bf16), dma((1,))]
+                    scratch[kind] += [dma((lines,))] * 2 + [dma((seqs,))] * 2
+                    shape = shape[1:]
+                shapes.append(jax.ShapeDtypeStruct(shape, dtype))
+                self.in_vmem.append(kind == "scatters")
+                if kind in ("everys", "alls"):
+                    kinds.add("all")
+                if kind not in ("to_line",):
+                    kinds.add("plane")
+                if kind in ("to_line", "relays", "merges"):
+                    kinds.add("line")
+        self.kinds = kinds
+        self.shapes = shapes
+        order = ("scatters", "gathers", "planes", "to_line", "everys", "alls", "relays", "merges")
+        self.scratch = [member for kind in order for member in scratch[kind]]
+
+    def specs(self, gridded):
+        if gridded:
+            vmem = [
+                pl.BlockSpec(
+                    array.shape, lambda n, z=(0,) * array.ndim: z, pipeline_mode=pl.Buffered(1)
+                )
+                for array in self.arrays
+            ]
+            out = [
+                pl.BlockSpec(array.shape, lambda n, z=(0,) * len(array.shape): z)
+                for array in self.shapes
+            ]
+        else:
+            vmem = out = [pl.BlockSpec(memory_space=pltpu.VMEM)] * len(self.arrays)
+        plain = pl.BlockSpec(memory_space=pl.ANY)
+        first = [one if inside else plain for one, inside in zip(vmem, self.in_vmem)]
+        second = [one if inside else plain for one, inside in zip(out, self.in_vmem)]
+        return first, second
+
+    def phases(self, inputs, outputs, scratch):
+        return exchange_phases(self.axes, self.counts, inputs, outputs, scratch)
+
+
+def exchange_kernel(plan, *refs):
+    number = len(plan.arrays)
+    greet_all(plan.axes, plan.kinds)
+    for phase in plan.phases(refs[:number], refs[number : 2 * number], refs[2 * number :]):
+        phase()
+
+
+def exchange(name, collective, **arrays):
+    plan = Exchange(**arrays)
+    in_specs, out_specs = plan.specs(False)
     return pl.pallas_call(
-        partial(exchange_kernel, name, (seqs, lines), counts),
-        out_shape=shapes,
-        in_specs=specs,
-        out_specs=specs,
-        scratch_shapes=scratch,
+        partial(exchange_kernel, plan),
+        out_shape=plan.shapes,
+        in_specs=in_specs,
+        out_specs=out_specs,
+        scratch_shapes=plan.scratch,
         compiler_params=pltpu.CompilerParams(
             collective_id=collective, has_side_effects=True, vmem_limit_bytes=VMEM_GRANT
         ),
         name=name,
-    )(*arrays)
+    )(*plan.arrays)
+
+
+def ffn_kernel(
+    axes,
+    rows_ref,
+    cot_ref,
+    weight_ref,
+    sum_ref,
+    down_ref,
+    grad_ref,
+    rows_all,
+    other,
+    pair,
+    landed,
+    cot_slot,
+    down_slot,
+    grad_sum,
+    far_send,
+    far_recv,
+    near_send,
+    near_recv,
+    pair_send,
+    pair_recv,
+    back_send,
+    back_recv,
+    cot_sem,
+    down_sem,
+    grad_sem,
+):
+    seqs, lines = axes
+    chips = seqs // 2
+    side = math.isqrt(chips)
+    seq, line = lax.axis_index("seq"), lax.axis_index("fsdp")
+    chip, core = seq // 2, lax.rem(seq, 2)
+    sibling = (2 * chip + 1 - core, line)
+
+    def at_step(k):
+        across = lax.rem(lax.rem(chip, side) + lax.rem(k, side), side)
+        along = lax.rem(chip // side + k // side, side)
+        return along * side + across
+
+    def loop(first, last, body):
+        def step(k, carry):
+            body(k)
+            return carry
+
+        lax.fori_loop(first, last, step, 0)
+
+    barrier = pltpu.get_barrier_semaphore()
+
+    def greet(k):
+        pl.semaphore_signal(
+            barrier, inc=1, device_id=(lax.rem(seq + k, seqs), line), device_id_type=MESH
+        )
+
+    loop(1, seqs, greet)
+    pl.semaphore_wait(barrier, seqs - 1)
+
+    def remote(source, target, send, recv, place):
+        return pltpu.make_async_remote_copy(
+            src_ref=source,
+            dst_ref=target,
+            send_sem=send,
+            recv_sem=recv,
+            device_id=place,
+            device_id_type=MESH,
+        )
+
+    def far(q, slot):
+        return remote(
+            rows_ref,
+            rows_all.at[2 * slot + core],
+            far_send.at[q],
+            far_recv.at[slot],
+            (2 * q + core, line),
+        )
+
+    def near(q):
+        block = rows_all.at[2 * q + core]
+        return remote(block, block, near_send.at[q], near_recv.at[q], sibling)
+
+    def near_own():
+        return remote(
+            rows_ref, rows_all.at[seq], near_send.at[chip], near_recv.at[chip], sibling
+        )
+
+    def near_arrival(q):
+        block = rows_all.at[2 * q + 1 - core]
+        return remote(block, block, near_send.at[q], near_recv.at[q], sibling)
+
+    def to_pair(q):
+        return remote(other.at[q], pair.at[q], pair_send.at[q], pair_recv.at[q], sibling)
+
+    def back(q, slot):
+        return remote(
+            pair.at[q],
+            landed.at[slot],
+            back_send.at[q],
+            back_recv.at[slot],
+            (2 * q + core, line),
+        )
+
+    def block_at(step):
+        q = at_step(step // 2)
+        return 2 * q + jnp.where(lax.rem(step, 2) == 0, 1 - core, core)
+
+    def cot_copy(step):
+        slot = lax.rem(step, 2)
+        return pltpu.make_async_copy(
+            cot_ref.at[block_at(step)], cot_slot.at[slot], cot_sem.at[slot]
+        )
+
+    def down_copy(step):
+        slot = lax.rem(step, 2)
+        return pltpu.make_async_copy(
+            down_slot.at[slot], down_ref.at[block_at(step)], down_sem.at[slot]
+        )
+
+    near_own().start()
+    loop(1, chips, lambda k: far(at_step(k), chip).start())
+    cot_copy(0).start()
+    rows_all[seq] = rows_ref[...]
+    grad_sum[...] = jnp.zeros_like(grad_sum)
+
+    def work(step):
+        k = step // 2
+        q = at_step(k)
+        mine = lax.rem(step, 2)
+        block = block_at(step)
+        slot = lax.rem(step, 2)
+
+        @pl.when(step + 1 < seqs)
+        def _():
+            cot_copy(step + 1).start()
+
+        @pl.when(jnp.logical_and(mine == 0, k > 0))
+        def _():
+            far(q, q).wait_recv()
+            near(q).start()
+
+        @pl.when(mine == 0)
+        def _():
+            near_arrival(q).wait_recv()
+
+        cot_copy(step).wait()
+
+        @pl.when(step >= 2)
+        def _():
+            down_copy(step - 2).wait()
+
+        rows = rows_all[block]
+        cot = cot_slot[slot]
+        up_gate, up_matrix, down_matrix = weight_ref[0], weight_ref[1], weight_ref[2]
+        gate_act = dot_nn(rows, up_gate)
+        up_act = dot_nn(rows, up_matrix)
+        grad_hidden = dot_nn(cot, down_matrix)
+        sigmoid = jax.nn.sigmoid(gate_act)
+        swish = gate_act * sigmoid
+        hidden = (swish * up_act).astype(bf16)
+        slope = sigmoid * (1.0 + gate_act - swish)
+        grad_gate = (grad_hidden * up_act * slope).astype(bf16)
+        grad_up = (grad_hidden * swish).astype(bf16)
+        part = dot_nt(grad_gate, up_gate) + dot_nt(grad_up, up_matrix)
+
+        @pl.when(mine == 0)
+        def _():
+            other[q] = part.astype(bf16)
+            to_pair(q).start()
+
+        @pl.when(mine == 1)
+        def _():
+            to_pair(q).wait_recv()
+            both = part + pair[q].astype(f32)
+
+            @pl.when(k == 0)
+            def _():
+                sum_ref[...] = both
+
+            @pl.when(k > 0)
+            def _():
+                pair[q] = both.astype(bf16)
+                back(q, chip).start()
+
+        down_slot[slot] = dot_nt(hidden, down_matrix).astype(bf16)
+        down_copy(step).start()
+        grad_sum[0] += dot_tn(rows, grad_gate)
+        grad_sum[1] += dot_tn(rows, grad_up)
+        grad_sum[2] += dot_tn(cot, hidden)
+
+    loop(0, seqs, work)
+    for member in range(3):
+        other_grad = grad_sum[member].astype(bf16)
+        grad_ref[member] = other_grad
+    down_copy(seqs - 2).wait()
+    down_copy(seqs - 1).wait()
+    near_own().wait_send()
+    loop(0, chips, lambda q: to_pair(q).wait_send())
+
+    def end(k):
+        q = at_step(k)
+        far(q, q).wait_send()
+        near(q).wait_send()
+        back(q, chip).wait_send()
+        back(q, q).wait_recv()
+        sum_ref[...] += landed[q].astype(f32)
+
+    loop(1, chips, end)
+
+
+def feed_forward(collective, rows, cot, weights):
+    seqs, lines = lax.axis_size("seq"), lax.axis_size("fsdp")
+    chips = seqs // 2
+    hidden = weights.shape[2]
+    dma = pltpu.SemaphoreType.DMA
+    any_spec, vmem_spec = pl.BlockSpec(memory_space=pl.ANY), pl.BlockSpec(memory_space=pltpu.VMEM)
+    half = pltpu.VMEM((chips, SEG, D), bf16)
+    return pl.pallas_call(
+        partial(ffn_kernel, (seqs, lines)),
+        out_shape=[
+            jax.ShapeDtypeStruct((SEG, D), f32),
+            jax.ShapeDtypeStruct((seqs, SEG, D), bf16),
+            jax.ShapeDtypeStruct((3, D, hidden), bf16),
+        ],
+        in_specs=[vmem_spec, any_spec, vmem_spec],
+        out_specs=[vmem_spec, any_spec, vmem_spec],
+        scratch_shapes=[
+            pltpu.VMEM((seqs, SEG, D), bf16),
+            half,
+            half,
+            half,
+            pltpu.VMEM((2, SEG, D), bf16),
+            pltpu.VMEM((2, SEG, D), bf16),
+            pltpu.VMEM((3, D, hidden), f32),
+        ]
+        + [dma((chips,))] * 8
+        + [dma((2,)), dma((2,)), dma((1,))],
+        compiler_params=pltpu.CompilerParams(
+            collective_id=collective, has_side_effects=True, vmem_limit_bytes=VMEM_GRANT
+        ),
+        name="feed_forward",
+    )(rows, cot, weights)
 
 
 def norm_scale(values):
@@ -978,71 +1491,68 @@
     def for_copies(array):
         return jnp.repeat(array, copies, axis=0) if copies > 1 else array
 
-    def head_columns(array):
-        rows = array.shape[0]
-        split = array.reshape(rows, 3, groups, width).transpose(2, 0, 1, 3)
-        return for_copies(widen(split, LANES).reshape(groups, rows, 3 * LANES))
-
-    qkv_blocks = head_columns(qkv_weight)
+    qkv_blocks = qkv_weight.reshape(share, 3, groups, width).transpose(2, 1, 0, 3)
+    qkv_blocks = widen(qkv_blocks, LANES).reshape(groups, 3 * share, LANES)
     memory_pack = jnp.concatenate([memory_w1.transpose(0, 2, 1), memory_w2], axis=2)
-    memory_blocks = for_copies(memory_pack.reshape(groups, heads * hidden_share, LANES))
-    live_rows = live_mask[0].astype(bf16).reshape(SEG // LANES, LANES)
-    small = [
-        gate_weight,
-        conv_weight,
-        persistent_keys,
-        persistent_values,
-        norm1_gain[None],
-        norm2_gain[None],
-        live_rows,
-    ]
-    small_at = [0]
-    for member in small:
-        small_at.append(small_at[-1] + member.shape[0])
-    small_pack = jnp.concatenate([widen(member, LANES) for member in small], axis=0)
-    small_pack = jnp.pad(small_pack, ((0, -small_pack.shape[0] % 16), (0, 0)))
+    memory_blocks = memory_pack.reshape(groups, heads * hidden_share, LANES)
+    persistent = jnp.concatenate([persistent_keys, persistent_values], axis=0)
+    gate_part = jnp.pad(gate_weight, ((0, 2 * P_SIZE - share), (0, HEAD_SIZE - 3 * HEAD_COUNT)))
+    small_pack = jnp.concatenate(
+        [
+            jnp.concatenate([gate_part, widen(persistent, HEAD_SIZE)], axis=1),
+            widen(conv_weight, LANES),
+            widen(norm1_gain[None], LANES),
+            widen(norm2_gain[None], LANES),
+            live_mask[0].astype(bf16).reshape(SEG // LANES, LANES),
+        ],
+        axis=0,
+    )
+    small_pack = jnp.broadcast_to(small_pack, (groups,) + small_pack.shape)
+    weight_pack = jnp.concatenate([qkv_blocks, memory_blocks, small_pack], axis=1)
+    weight_pack = jnp.pad(weight_pack, ((0, 0), (0, -weight_pack.shape[1] % 16), (0, 0)))
     ffn_local = jnp.stack([ffn_gate, ffn_up, ffn_down.T])
     ffn_blocks = ffn_local.reshape(3, piece, seqs, slab).transpose(2, 0, 1, 3)
     ffn_blocks = ffn_blocks.reshape(seqs, 3 * piece, slab)
-    token_rows, ffn_got, qkv_got, memory_got, small_got = exchange(
+    token_rows, ffn_got, out_rows, weights_got = exchange(
         "first_exchange",
         0,
         gathers=[tokens[0]],
         planes=[ffn_blocks],
-        everys=[qkv_blocks, memory_blocks],
-        alls=[small_pack],
+        to_line=[out_weight],
+        relays=[for_copies(weight_pack)],
     )
-    out_matrix = lax.all_gather(out_weight, ("seq", "fsdp"), axis=0, tiled=True)
     ffn_part = ffn_got.reshape(seqs, 3, piece, slab).transpose(1, 0, 2, 3).reshape(3 * D, slab)
     ffn_full = lax.all_gather(ffn_part, "fsdp", axis=1, tiled=True).reshape(3, D, lines * slab)
-    cot_rows = lax.all_gather(cotangent[0], "seq", axis=0, tiled=True)
 
     token_rows = token_rows.reshape(length, D)
-    qkv_matrix = qkv_got.reshape(D, 3 * LANES)
-    memory_both = memory_got.reshape(devices, heads, hidden_share, LANES)
-    memory_both = memory_both.transpose(1, 0, 2, 3).reshape(heads, MH, LANES)
+    memory_at = 3 * share
+    small_at = memory_at + heads * hidden_share
+    qkv_matrix = weights_got[:, :, :memory_at].reshape(lines, seqs, 3, share, LANES)
+    qkv_matrix = qkv_matrix.transpose(1, 0, 3, 2, 4).reshape(D, 3 * LANES)
+    memory_both = weights_got[:, :, memory_at:small_at]
+    memory_both = memory_both.reshape(lines, seqs, heads, hidden_share, LANES)
+    memory_both = memory_both.transpose(2, 1, 0, 3, 4).reshape(heads, MH, LANES)
     memory_turned = jnp.concatenate(
         [memory_both[..., HEAD_SIZE:], memory_both[..., :HEAD_SIZE]], axis=-1
     )
-
-    def small_part(number, columns):
-        return small_got[:, small_at[number] : small_at[number + 1], :columns]
-
-    gate_matrix = small_part(0, 3 * HEAD_COUNT).reshape(D, 3, HEAD_COUNT).transpose(1, 2, 0)
-    gate_rows = lax.dynamic_slice_in_dim(gate_matrix, group * heads, heads, 1)
+    small_got = weights_got[:, :, small_at:].transpose(1, 0, 2, 3)
+    small_all = small_got.reshape((devices,) + small_got.shape[2:])
+    gate_matrix = small_all[:, :share, : 3 * HEAD_COUNT].reshape(D, 3, HEAD_COUNT)
+    gate_rows = gate_matrix.transpose(1, 2, 0)
+    gate_rows = lax.dynamic_slice_in_dim(gate_rows, group * heads, heads, 1)
     gate_rows = jnp.pad(gate_rows, ((0, 0), (0, 8 - heads), (0, 0))).reshape(24, D)
-    taps = small_part(1, 3 * share).transpose(1, 0, 2).reshape(4, 3, groups, width)
+    after = 2 * P_SIZE
+    taps = small_all[:, after : after + 4, : 3 * share].transpose(1, 0, 2)
+    taps = taps.reshape(4, 3, groups, width)
     taps = lax.dynamic_slice_in_dim(taps, group, 1, 2)[:, :, 0]
     taps = jnp.pad(widen(taps, LANES).reshape(4, 3 * LANES), ((0, 4), (0, 0))).astype(f32)
-
-    def own_columns(number):
-        whole = small_part(number, share).transpose(1, 0, 2).reshape(P_SIZE, D)
-        return widen(lax.dynamic_slice_in_dim(whole, group * width, width, 1), LANES)
-
-    pkeys, pvalues = own_columns(2), own_columns(3)
-    gain_one = small_part(4, share).reshape(1, D).astype(f32)
-    gain_two = small_part(5, share).reshape(1, D).astype(f32)
-    live_all = small_part(6, LANES).reshape(seqs, lines, SEG)
+    persistent = small_all[:, :after, HEAD_SIZE : HEAD_SIZE + share].transpose(1, 0, 2)
+    persistent = persistent.reshape(after, D)
+    persistent = widen(lax.dynamic_slice_in_dim(persistent, group * width, width, 1), LANES)
+    pkeys, pvalues = persistent[:P_SIZE], persistent[P_SIZE:]
+    gain_one = small_all[:, after + 4, :share].reshape(1, D).astype(f32)
+    gain_two = small_all[:, after + 5, :share].reshape(1, D).astype(f32)
+    live_all = small_got[:, :, after + 6 : after + 6 + SEG // LANES].reshape(seqs, lines, SEG)
     live_all = lax.dynamic_index_in_dim(live_all, line, 1, False).astype(f32)
 
     lengths = doc_lengths[0]
@@ -1066,7 +1576,11 @@
     extra = jnp.stack([place_rows.astype(f32), live_all], axis=1)
     gates = jnp.concatenate([gate_input, jnp.pad(extra, ((0, 0), (0, 6), (0, 0)))], axis=1)
     constants = (taps, memory_both, memory_turned, pkeys, pvalues)
-    mixed, keys, values, totals, states = mix_forward(heads, raw, gates, place_column, *constants)
+    plan = Exchange(gathers=[out_rows.reshape(lines * share, D), cotangent[0]])
+    mixed, keys, values, totals, states, out_matrix, cot_rows = mix_forward(
+        6, plan, heads, raw, gates, place_column, *constants
+    )
+    out_matrix = out_matrix.reshape(D, D)
 
     (mixed_got,) = exchange("to_segments", 1, planes=[mixed.reshape(seqs, SEG, LANES)])
     combined = mixed_got[::copies, :, :width].transpose(1, 0, 2).reshape(SEG, D)
@@ -1074,29 +1588,10 @@
     middle = inputs + jnp.dot(combined, out_matrix, preferred_element_type=f32)
     scale_two = norm_scale(middle)
     normed_two_own = (middle * scale_two * gain_two).astype(bf16)
-    (normed_two,) = exchange("second_rows", 2, gathers=[normed_two_own])
-    normed_two = normed_two.reshape(length, D)
-
-    up_gate, up_matrix, down_matrix = ffn_full[0], ffn_full[1], ffn_full[2]
-    gate_act = jnp.dot(normed_two, up_gate, preferred_element_type=f32)
-    up_act = jnp.dot(normed_two, up_matrix, preferred_element_type=f32)
-    sigmoid = jax.nn.sigmoid(gate_act)
-    swish = gate_act * sigmoid
-    hidden = (swish * up_act).astype(bf16)
-    grad_hidden = jnp.dot(cot_rows, down_matrix, preferred_element_type=f32)
-    grad_gate = (grad_hidden * up_act * swish_slope(gate_act, sigmoid)).astype(bf16)
-    grad_up = (grad_hidden * swish).astype(bf16)
-    normed_part = dot_nt(grad_gate, up_gate) + dot_nt(grad_up, up_matrix)
-    (grad_normed_two,) = exchange(
-        "second_sums", 3, scatters=[normed_part.astype(bf16).reshape(seqs, SEG, D)]
+    grad_normed_two, down_part, ffn_grads = feed_forward(
+        2, normed_two_own, cot_rows, ffn_full
     )
-    down_part = dot_nt(hidden, down_matrix).astype(bf16)
-    down_sum = lax.psum_scatter(down_part, "seq", scatter_dimension=0, tiled=True)
-    output = (middle + down_sum.astype(f32)).astype(bf16)
-    ffn_grads = jnp.concatenate(
-        [dot_tn(normed_two, grad_gate), dot_tn(normed_two, grad_up), dot_tn(cot_rows, hidden)],
-        axis=0,
-    ).astype(bf16)
+    ffn_grads = ffn_grads.reshape(3 * D, lines * slab)
     ffn_grads = lax.psum_scatter(ffn_grads, "fsdp", scatter_dimension=1, tiled=True)
 
     grad_middle = cotangent[0].astype(f32) + norm_pull(middle, scale_two, gain_two, grad_normed_two)
@@ -1104,11 +1599,13 @@
     grad_branch = grad_middle.astype(bf16)
     grad_combined = dot_nt(grad_branch, out_matrix).astype(bf16)
     grad_out = dot_tn(combined, grad_branch).astype(bf16)
-    grad_out = lax.psum_scatter(grad_out, ("seq", "fsdp"), scatter_dimension=0, tiled=True)
+    plan = Exchange(scatters=[down_part, grad_out.reshape(seqs, piece, D)])
     blocks = widen(grad_combined.reshape(SEG, groups, width).transpose(1, 0, 2), LANES)
     (grad_mixed,) = exchange("to_heads", 4, planes=[for_copies(blocks)])
 
-    grad_raw, grad_gates, grad_memory, grad_taps, grad_pkeys, grad_pvalues = mix_backward(
+    grad_raw, grad_gates, grad_memory, grad_taps, grad_pkeys, grad_pvalues, down_sum, grad_out = mix_backward(
+        7,
+        plan,
         heads,
         raw,
         gates,
@@ -1120,64 +1617,62 @@
         grad_mixed.reshape(length, LANES),
         *constants,
     )
+    output = (middle + down_sum).astype(bf16)
     grad_gates = grad_gates.transpose(1, 0, 2).reshape(24, length)
     grad_gates_low = grad_gates.astype(bf16)
-    grad_qkv = dot_tn(normed, grad_raw)
     grad_gate_rows = dot_nn(grad_gates_low, normed)
     grad_normed = dot_nt(grad_raw, qkv_matrix) + dot_tn(grad_gates_low, gate_rows)
     grad_normed = (grad_normed * first_copy).astype(bf16).reshape(seqs, SEG, D)
 
-    def to_owners(rows):
-        return rows.reshape(rows.shape[0], devices, share).transpose(1, 0, 2)
-
-    memory_part = grad_memory.reshape(heads, devices, hidden_share, LANES).transpose(1, 0, 2, 3)
-    memory_part = memory_part.reshape(devices, heads * hidden_share, LANES)
-    owner_rows = widen(to_owners(jnp.concatenate([grad_gate_rows, grad_gain_two], axis=0)), LANES)
-    owner_pack = jnp.concatenate([memory_part, owner_rows], axis=1).astype(bf16)
-    owner_pack = jnp.pad(owner_pack, ((0, 0), (0, -owner_pack.shape[1] % 16), (0, 0)))
+    qkv_part = dot_tn(normed, grad_raw).astype(bf16).reshape(seqs, lines, share, 3, LANES)
+    qkv_part = qkv_part.transpose(1, 0, 3, 2, 4).reshape(lines, seqs, 3 * share, LANES)
+    memory_part = grad_memory.astype(bf16).reshape(heads, seqs, lines, hidden_share, LANES)
+    memory_part = memory_part.transpose(2, 1, 0, 3, 4)
+    memory_part = memory_part.reshape(lines, seqs, heads * hidden_share, LANES)
+    owner_rows = jnp.concatenate([grad_gate_rows, grad_gain_two], axis=0).astype(bf16)
+    owner_rows = owner_rows.reshape(25, seqs, lines, share).transpose(2, 1, 0, 3)
     bias_sums = widen(jnp.sum(grad_gates, axis=1)[None], LANES)
-    shared_pack = jnp.concatenate(
-        [grad_taps[:4].reshape(12, LANES), bias_sums, jnp.zeros((3, LANES), f32)], axis=0
+    shared_rows = jnp.concatenate([grad_taps[:4].reshape(12, LANES), bias_sums], axis=0)
+    shared_rows = jnp.broadcast_to(shared_rows.astype(bf16), (lines, seqs, 13, LANES))
+    grad_pack = jnp.concatenate(
+        [qkv_part, memory_part, widen(owner_rows, LANES), shared_rows], axis=2
     )
+    grad_pack = jnp.pad(grad_pack, ((0, 0), (0, 0), (0, -grad_pack.shape[2] % 16), (0, 0)))
     line_pack = jnp.concatenate([grad_pkeys, grad_pvalues], axis=0)
+    out_part = grad_out.astype(bf16).reshape(lines, share, D)
     ffn_out = ffn_grads.reshape(3, seqs, piece, slab).transpose(1, 0, 2, 3)
-    ffn_got, line_got, qkv_got, owner_got, shared_got, grad_normed = exchange(
+    ffn_got, out_got, line_got, grad_normed, grads_got = exchange(
         "last_exchange",
         5,
         planes=[ffn_out.reshape(seqs, 3 * piece, slab)],
-        to_line=[line_pack],
-        everys=[grad_qkv.astype(bf16).reshape(devices, share, 3 * LANES), owner_pack],
-        alls=[shared_pack],
+        to_line=[out_part, line_pack],
         scatters=[grad_normed],
+        merges=[grad_pack],
     )
 
     scale_one = norm_scale(inputs)
     input_grad = grad_middle + norm_pull(inputs, scale_one, gain_one, grad_normed)
 
-    def over_rows(got):
-        summed = jnp.sum(got.astype(f32).reshape((seqs, lines) + got.shape[1:]), axis=1)
-        return summed[::copies]
-
-    grad_qkv = over_rows(qkv_got).reshape(groups, share, 3, LANES)[..., :width]
-    grad_qkv = grad_qkv.transpose(1, 2, 0, 3).reshape(share, 3 * D)
-    owner_sums = over_rows(owner_got)
-    memory_rows = heads * hidden_share
-    grad_memory = owner_sums[:, :memory_rows].reshape(HEAD_COUNT, hidden_share, LANES)
+    grad_sums = grads_got[::copies].astype(f32)
+    grad_qkv = grad_sums[:, : 3 * share].reshape(groups, 3, share, LANES)[..., :width]
+    grad_qkv = grad_qkv.transpose(2, 1, 0, 3).reshape(share, 3 * D)
+    owner_at = small_at
+    grad_memory = grad_sums[:, memory_at:owner_at].reshape(HEAD_COUNT, hidden_share, LANES)
     grad_memory_w1 = grad_memory[..., :HEAD_SIZE].transpose(0, 2, 1)
     grad_memory_w2 = grad_memory[..., HEAD_SIZE:]
-    grad_gate = owner_sums[:, memory_rows : memory_rows + 24, :share]
+    grad_gate = grad_sums[:, owner_at : owner_at + 24, :share]
     grad_gate = grad_gate.reshape(groups, 3, 8, share)[:, :, :heads].transpose(3, 1, 0, 2)
     grad_gate = grad_gate.reshape(share, 3 * HEAD_COUNT)
-    grad_gain_two = jnp.sum(owner_got[:, memory_rows + 24, :share].astype(f32), axis=0)
+    grad_gain_two = jnp.sum(grads_got[:, owner_at + 24, :share].astype(f32), axis=0)
     own_gain = norm1_gain.astype(f32)
     along = jnp.sum(grad_qkv * qkv_weight.astype(f32), axis=1)
     along = along + jnp.sum(grad_gate * gate_weight.astype(f32), axis=1)
     grad_gain_one = along / own_gain
-    shared_sums = over_rows(shared_got)
-    grad_conv = shared_sums[:, :12].reshape(groups, 4, 3, LANES)[..., :width]
+    shared_at = owner_at + 25
+    grad_conv = grad_sums[:, shared_at : shared_at + 12].reshape(groups, 4, 3, LANES)[..., :width]
     grad_conv = grad_conv.transpose(1, 2, 0, 3).reshape(4, 3 * D)
     grad_conv = lax.dynamic_slice_in_dim(grad_conv, me * 3 * share, 3 * share, 1)
-    grad_bias = shared_sums[:, 12, :24].reshape(groups, 3, 8)[:, :, :heads]
+    grad_bias = grad_sums[:, shared_at + 12, :24].reshape(groups, 3, 8)[:, :, :heads]
     grad_bias = grad_bias.transpose(1, 0, 2).reshape(3, HEAD_COUNT)
     grad_bias = grad_bias * jnp.array([[3.0], [1.0], [1.0]], f32)
     line_sums = jnp.sum(line_got, axis=0)
@@ -1195,7 +1690,7 @@
         grad_memory_w2,
         line_sums[:P_SIZE],
         line_sums[P_SIZE:],
-        grad_out.astype(f32),
+        jnp.sum(out_got.astype(f32), axis=0),
         grad_gain_two,
         ffn_sums[0],
         ffn_sums[1],

time: 556 us -> 411 us (0.74); the launches traced: 545 us -> 406 us
  matrix products: 79.8 us -> 29.1 us
  waiting for transfers between devices: 50.5 us -> 0.04 us
  Pallas kernels: 315 us -> 278 us
    reduce_scatter x2 -> x0, waiting for transfers between devices: 49 us -> none  [the longest x1 49 us: on_device(): lax.psum_scatter(grad_out, ('seq', 'fsdp'), scatter_dimension=0, tiled=True)]
    pallas_call x8 -> x7, Pallas kernels: 315 us -> 278 us  [the longest x4 102 us: exchange(): pl.pallas_call(partial(exchange_kernel, plan), out_shape=plan.shapes, in_...]
    dot_general x3 -> x0, matrix products: 23.5 us -> none  [the longest x1 11.1 us: on_device(): grad_hidden = jnp.dot(cot_rows, down_matrix, preferred_element_type=f32)]
    dot_general x6 -> x3, matrix products: 23.1 us -> 7.45 us  [dot_nt(): lax.dot_general(left, right, (((1,), (1,)), ((), ())), preferred_element_...]
    dot_general x6 -> x3, matrix products: 22 us -> 10.3 us  [dot_tn(): lax.dot_general(left, right, (((0,), (0,)), ((), ())), preferred_element_...]
    unnamed x86 -> x73, local copies, waits for them, and re-layouts: 17.8 us -> 12.1 us
  transfers between devices with their start and end apart: 6 -> 2, of which waited for: 1 -> 0; matrix products, arithmetic and copies ran while one was open for 23% -> 18% of each run, Pallas kernels for 58% -> 33%
where the time goes in v2:
time: 411 us; the launch traced here: 406 us
  Pallas kernels  278 us (68%)
  local copies, waits for them, and re-layouts  48.8 us (12%)
  other arithmetic  35.4 us (9%)
  matrix products  29.1 us (7%)
  between operations  15.1 us (4%)
    pallas_call x4, Pallas kernels, exchange(): pl.pallas_call(partial(exchange_kernel, plan), out_shape=plan.shapes, in_...  102 us
    pallas_call x1, Pallas kernels, mix_backward(): pl.pallas_call(partial(backward_kernel, heads, plan), grid=(count,), in_s...  72.6 us
    pallas_call x1, Pallas kernels, feed_forward(): pl.pallas_call(partial(ffn_kernel, (seqs, lines)), out_shape=[jax.ShapeDt...  58.3 us
    pallas_call x1, Pallas kernels, mix_forward(): pl.pallas_call(partial(forward_kernel, heads, plan), grid=(count,), in_sp...  44.4 us
    unnamed x73, local copies, waits for them, and re-layouts  12.1 us
    dot_general x3, matrix products, dot_tn(): lax.dot_general(left, right, (((0,), (0,)), ((), ())), preferred_element_...  10.3 us
    convert_element_type x2, other arithmetic, on_device(): normed = (wide_tokens * norm_scale(wide_tokens) * gain_one).astype(bf16)  9.24 us
  transfers between devices with their start and end apart: 2, of which 0 were waited for; matrix products, arithmetic and copies ran while one was open for 18% of the time, Pallas kernels for 33%

profile of v2, /device:TPU:0, one launch (start us, length us, event | category | flops | bytes accessed | tf_op | source)
XLA Modules:
  0.0 406.4 jit_solution(14274574105284314258)
XLA Ops:
  16.2 41.5 %first_exchange.1 = (bf16[8,256,1024]{2,1,0:T(8,128)(2,1)}, bf16[8,384,128]{2,1,0:T(8,128)(2,1)}, bf16[4,32,1024]{2,1,0:T(8,128)(2,1)}, bf16[4,8,160,128]{3,2,1,0:T(8,128)(2,1)}) custom-call(bf16[256,1024]{1,0:T(8,128)(2,1)} %bitcast.203, bf16[8,384,128]{2,1,0:T(8,128)(2,1)} %bitcast.218, bf16[32,1024]{1,0:T(8,128)(2,1)} %refs_2_.1, ...), custom_call_target="tpu_custom_call" | custom-call | tf_op jit(solution)/shard_map/first_exchange/pallas_call | solution.py:1184
  57.7 2.1 copy.162
  61.1 3.1 multiply_reduce_fusion
  65.3 5.0 %multiply_convert_fusion = bf16[8,256,1024]{2,1,0:T(8,128)(2,1)} fusion(f32[1024]{0:T(1024)S(1)} %reshape.481, f32[8,256]{1,0:T(8,128)S(1)} %get-tuple-element.156, bf16[8,256,1024]{2,1,0:T(8,128)(2,1)} %get-tuple-element.43), kind=kLoop, calls=%fused_computation.4 | loop fusion | flops 8388608 | bytes 8400896 | tf_op jit(solution)/shard_map/convert_element_type | solution.py:1569
  72.5 3.5 convolution_add_fusion
  82.2 5.7 %convolution_convert_fusion.refs_0_.refs_1_ = bf16[2048,384]{1,0:T(8,128)(2,1)} fusion(bf16[2048,1024]{1,0:T(8,128)(2,1)} %bitcast.199, bf16[128,8,3,128]{3,2,1,0:T(4,128)(2,1)S(1)} %bitcast.210), kind=kOutput, calls=%fused_computation.8 | convolution fusion | flops 1611399168 | bytes 6553600 | tf_op jit(solution)/shard_map/dot_general | solution.py:1570
  87.9 44.4 %mix_forward.1 = (bf16[2048,128]{1,0:T(8,128)(2,1)}, bf16[2048,128]{1,0:T(8,128)(2,1)}, bf16[2048,128]{1,0:T(8,128)(2,1)}, f32[2048,8]{1,0:T(8,128)}, bf16[8,2,2...) custom-call(bf16[2048,384]{1,0:T(8,128)(2,1)} %convolution_convert_fusion.refs_0_.refs_1_, ...), custom_call_target="tpu_custom_call" | custom-call | tf_op jit(solution)/shard_map/mix_forward/pallas_call | solution.py:555
  132.3 8.8 %to_segments.1 = bf16[8,256,128]{2,1,0:T(8,128)(2,1)} custom-call(bf16[8,256,128]{2,1,0:T(8,128)(2,1)} %bitcast.248), custom_call_target="tpu_custom_call" | custom-call | tf_op jit(solution)/shard_map/to_segments/pallas_call | solution.py:1184
  141.2 2.6 multiply_reduce_fusion.3
  144.8 58.3 %feed_forward.1 = (f32[256,1024]{1,0:T(8,128)}, bf16[8,256,1024]{2,1,0:T(8,128)(2,1)}, bf16[3,1024,512]{2,1,0:T(8,128)(2,1)}) custom-call(bf16[256,1024]{1,0:T(8,128)(2,1)} %multiply_convert_fusion.1.rows_ref, bf16[8,256,1024]{2,1,0:T(8,128)(2,1)} %get-tuple-element.52.cot_ref, bf16[3,1024,512]{2,1,0:T(8,128)(2,1)} %bitcast.219), custom_call_target="tpu_custom_call" | custom-call | tf_op jit(solution)/shard_map/feed_forward/pallas_call | solution.py:1411
  203.1 4.7 %copy.182 = bf16[3072,512]{0,1:T(8,128)(2,1)} copy(bf16[3072,512]{1,0:T(8,128)(2,1)} %bitcast.214) | data formatting | bytes 6291456
  209.1 4.2 %fusion.1 = bf16[2048,1024]{1,0:T(8,128)(2,1)} fusion(f32[1024]{0:T(1024)S(1)} %reshape.481, f32[2048]{0:T(1024)S(1)} %bitcast.259, bf16[8,256,1024]{2,1,0:T(8,128)(2,1)} %get-tuple-element.43), kind=kLoop, calls=%fused_computation.2 | loop fusion | flops 8388608 | bytes 8400896 | tf_op jit(solution)/shard_map/convert_element_type | solution.py:1569
  216.7 2.0 copy.163
  218.7 2.0 copy.164
  220.7 8.8 %to_heads.1 = bf16[8,256,128]{2,1,0:T(8,128)(2,1)} custom-call(bf16[8,256,128]{2,1,0:T(8,128)(2,1)} %bitcast.228), custom_call_target="tpu_custom_call" | custom-call | tf_op jit(solution)/shard_map/to_heads/pallas_call | solution.py:1184
  229.6 2.1 convolution_convert_fusion.1
  231.7 72.6 %mix_backward.1 = (bf16[2048,384]{1,0:T(8,128)(2,1)}, f32[8,24,256]{2,1,0:T(8,128)}, f32[2,256,128]{2,1,0:T(8,128)}, f32[8,384]{1,0:T(8,128)}, f32[16,128]{1,0:T...) custom-call(bf16[2048,384]{1,0:T(8,128)(2,1)} %convolution_convert_fusion.refs_0_.refs_1_, ...), custom_call_target="tpu_custom_call" | custom-call | tf_op jit(solution)/shard_map/mix_backward/pallas_call | solution.py:629
  309.2 3.0 fusion.6
  314.5 5.0 %convolution_convert_fusion.2 = bf16[1024,384]{1,0:T(8,128)(2,1)S(1)} fusion(bf16[2048,1024]{1,0:T(8,128)(2,1)} %fusion.1, bf16[2048,384]{1,0:T(8,128)(2,1)} %get-tuple-element.61), kind=kOutput, calls=%fused_computation.18 | convolution fusion | flops 1611005952 | bytes 6553600 | tf_op jit(solution)/shard_map/dot_general | solution.py:41
  327.1 2.4 fusion.14
  329.5 3.2 add_convert_fusion
  335.2 43.4 %last_exchange.1 = (bf16[8,384,128]{2,1,0:T(8,128)(2,1)}, bf16[4,32,1024]{2,1,0:T(8,128)(2,1)}, f32[4,32,128]{2,1,0:T(8,128)}, f32[256,1024]{1,0:T(8,128)}, bf16[8,160,128]{2,1,0:T(8,128)(2,1)}) custom-call(bf16[8,384,128]{2,1,0:T(8,128)(2,1)} %bitcast.212, bf16[4,32,1024]{2,1,0:T(8,128)(2,1)} %bitcast.233, f32[32,128]{1,0:T(8,128)} %pad_maximum_fusion.4.refs_2_, ...), custom_call_target="tpu_custom_call" | custom-call | tf_op jit(solution)/shard_map/last_exchange/pallas_call | solution.py:1184
  391.1 2.0 copy.178
  395.8 2.2 copy_bitcast_fusion
  (194 shorter events, 58.6 us)
Async XLA Ops:
  7.2 7.0 %copy-start.23 = (bf16[16,32]{1,0:T(8,128)(2,1)S(1)}, bf16[16,32]{1,0:T(8,128)(2,1)}, u32[]{:S(2)}) copy-start(bf16[16,32]{1,0:T(8,128)(2,1)} %param.29) | copy-start | bytes 3076
  7.2 7.0 %copy-start.24 = (bf16[16,32]{1,0:T(8,128)(2,1)S(1)}, bf16[16,32]{1,0:T(8,128)(2,1)}, u32[]{:S(2)}) copy-start(bf16[16,32]{1,0:T(8,128)(2,1)} %param.28) | copy-start | bytes 3076
  7.2 7.0 %copy-start.20 = (bf16[32,48]{1,0:T(8,128)(2,1)S(1)}, bf16[32,48]{1,0:T(8,128)(2,1)}, u32[]{:S(2)}) copy-start(bf16[32,48]{1,0:T(8,128)(2,1)} %param.24) | copy-start | bytes 9220
  7.2 7.1 %copy-start.18 = (bf16[16,8,64]{2,1,0:T(8,128)(2,1)S(1)}, bf16[16,8,64]{2,1,0:T(8,128)(2,1)}, u32[]{:S(2)}) copy-start(bf16[16,8,64]{2,1,0:T(8,128)(2,1)} %param.27) | copy-start | bytes 49156
  7.2 7.1 %copy-start.19 = (bf16[16,64,8]{1,2,0:T(8,128)(2,1)S(1)}, bf16[16,64,8]{1,2,0:T(8,128)(2,1)}, u32[]{:S(2)}) copy-start(bf16[16,64,8]{1,2,0:T(8,128)(2,1)} %param.26) | copy-start | bytes 49156
  7.2 137.5 %all-gather.2.cloned.1.call-start = ((), (), s32[]{:S(2)}) async-start(), calls=%async_computation.1 | async-start | bytes 3932160 | tf_op jit(solution)/shard_map/all_gather | solution.py:1525
  59.8 272.9 %reduce-scatter.4.cloned.1.call-start = ((), (), s32[]{:S(2)}) async-start(), calls=%async_computation.2 | async-start | bytes 3932160
  65.2 5.0 %copy-start.25 = (f32[3,16]{1,0:T(4,128)S(1)}, f32[3,16]{1,0:T(4,128)}, u32[]{:S(2)}) copy-start(f32[3,16]{1,0:T(4,128)} %param.35) | copy-start | bytes 580
  65.3 5.0 %copy-start.26 = (f32[3]{0:T(128)S(1)}, f32[3]{0:T(128)}, u32[]{:S(2)}) copy-start(f32[3]{0:T(128)} %constant.121) | copy-start | bytes 40
  65.3 5.0 %copy-start.29 = (f32[3]{0:T(128)S(1)}, f32[3]{0:T(128)}, u32[]{:S(2)}) copy-start(f32[3]{0:T(128)} %constant.122) | copy-start | bytes 40
  72.2 10.0 %copy-start.6 = (bf16[4,8,3,32,128]{4,2,3,0,1:T(4,128)(2,1)}, bf16[4,8,3,32,128]{4,2,3,0,1:T(4,128)(2,1)S(1)}, u32[]{:S(2)}) copy-start(bf16[4,8,3,32,128]{4,2,3,0,1:T(4,128)(2,1)S(1)} %copy.154) | copy-start | bytes 2359300
  77.6 10.3 %copy-start.5 = (bf16[4,8,2,8,128]{4,3,0,1,2:T(8,128)(2,1)}, bf16[4,8,2,8,128]{4,3,0,1,2:T(8,128)(2,1)S(1)}, u32[]{:S(2)}) copy-start(bf16[4,8,2,8,128]{4,3,0,1,2:T(8,128)(2,1)S(1)} %copy.160) | copy-start | bytes 393220
  87.9 53.3 %copy-start.1 = (bf16[1,256,1024]{2,1,0:T(8,128)(2,1)S(1)}, bf16[1,256,1024]{2,1,0:T(8,128)(2,1)}, u32[]{:S(2)}) copy-start(bf16[1,256,1024]{2,1,0:T(8,128)(2,1)} %param.21) | copy-start | bytes 1572868
  209.0 4.3 %copy-start.4 = (f32[256,1024]{1,0:T(8,128)S(1)}, f32[256,1024]{1,0:T(8,128)}, u32[]{:S(2)}) copy-start(f32[256,1024]{1,0:T(8,128)} %get-tuple-element.54) | copy-start | bytes 3145732
  209.1 4.6 %copy-start.9 = (bf16[1,256,1024]{2,1,0:T(8,128)(2,1)S(1)}, bf16[1,256,1024]{2,1,0:T(8,128)(2,1)}, u32[]{:S(2)}) copy-start(bf16[1,256,1024]{2,1,0:T(8,128)(2,1)} %param.38) | copy-start | bytes 1572868
  304.3 10.1 %copy-start.15 = (f32[2,256,128]{2,1,0:T(8,128)S(1)}, f32[2,256,128]{2,1,0:T(8,128)}, u32[]{:S(2)}) copy-start(f32[2,256,128]{2,1,0:T(8,128)} %get-tuple-element.63) | copy-start | bytes 786436
  378.6 6.8 %copy-start.11 = (bf16[32,3072]{1,0:T(8,128)(2,1)S(1)}, bf16[32,3072]{1,0:T(8,128)(2,1)}, u32[]{:S(2)}) copy-start(bf16[32,3072]{1,0:T(8,128)(2,1)} %param.23) | copy-start | bytes 589828
  378.6 8.5 %copy-start.17 = (bf16[32,48]{0,1:T(8,128)(2,1)S(1)}, bf16[32,48]{0,1:T(8,128)(2,1)}, u32[]{:S(2)}) copy-start(bf16[32,48]{0,1:T(8,128)(2,1)} %copy.174) | copy-start | bytes 9220
  378.6 9.2 %copy-start.16 = (f32[4,32,128]{2,1,0:T(8,128)S(1)}, f32[4,32,128]{2,1,0:T(8,128)}, u32[]{:S(2)}) copy-start(f32[4,32,128]{2,1,0:T(8,128)} %get-tuple-element.67) | copy-start | bytes 196612
  378.6 9.2 %copy-start.14 = (bf16[4,32,1024]{2,1,0:T(8,128)(2,1)S(1)}, bf16[4,32,1024]{2,1,0:T(8,128)(2,1)}, u32[]{:S(2)}) copy-start(bf16[4,32,1024]{2,1,0:T(8,128)(2,1)} %get-tuple-element.68) | copy-start | bytes 786436
  379.6 8.9 %copy-start.12 = (bf16[8,384,128]{2,1,0:T(8,128)(2,1)S(1)}, bf16[8,384,128]{2,1,0:T(8,128)(2,1)}, u32[]{:S(2)}) copy-start(bf16[8,384,128]{2,1,0:T(8,128)(2,1)} %get-tuple-element.69) | copy-start | bytes 2359300
  388.7 4.6 %copy-start.27 = (f32[3]{0:T(128)S(1)}, f32[3]{0:T(128)}, u32[]{:S(2)}) copy-start(f32[3]{0:T(128)} %constant.121) | copy-start | bytes 40
  388.7 5.2 %copy-start.28 = (bf16[32]{0:T(256)(128)(2,1)S(1)}, bf16[32]{0:T(256)(128)(2,1)}, u32[]{:S(2)}) copy-start(bf16[32]{0:T(256)(128)(2,1)} %param.22) | copy-start | bytes 196
  389.7 8.3 %copy-start.3 = (f32[256,1024]{1,0:T(8,128)S(1)}, f32[256,1024]{1,0:T(8,128)}, u32[]{:S(2)}) copy-start(f32[256,1024]{1,0:T(8,128)} %get-tuple-element.65) | copy-start | bytes 3145732
  (9 other events, 23.1 us)
Sparse Core Ops, SparseCore 0:
  59.9 63.6 all-gather.1
  207.9 59.7 reduce-scatter.3

commit v3 on v2

--- a/solution.py
+++ b/solution.py
@@ -11,6 +11,7 @@
 HEAD_COUNT = 16
 HEAD_SIZE = 64
 D = 1024
+FF = 4096
 MH = 256
 P_SIZE = 16
 SEG = 256
@@ -80,13 +81,30 @@
     return mixed
 
 
-def gate_scan(gate_rows):
+def places(length_ref, positions):
+    start = jnp.int32(0)
+    begin = jnp.zeros_like(positions)
+    for document in range(1, length_ref.shape[1]):
+        start = start + length_ref[0, document - 1]
+        begin = jnp.where(positions >= start, start, begin)
+    return positions - begin
+
+
+def gate_scan(heads, first_head, gate_columns, bias_ref, place_row, live):
     lane = lane_index((8, SEG))
-    keep = jnp.where(gate_rows[24:25] < 0.5, 0.0, 1.0)
-    live = gate_rows[25:26]
-    forget = jax.nn.sigmoid(gate_rows[0:8])
-    momentum = jax.nn.sigmoid(gate_rows[8:16])
-    step = jax.nn.sigmoid(gate_rows[16:24])
+    sublane = lax.broadcasted_iota(jnp.int32, (8, SEG), 0)
+    gate_rows = jnp.transpose(gate_columns)
+    shifts = []
+    for kind, (scale, shift) in enumerate(((3.0, -7.5), (1.0, 1.5), (1.0, 0.0))):
+        bias = jnp.zeros((8, SEG), f32)
+        for head in range(heads):
+            own = scale * bias_ref[kind, first_head + head] + shift
+            bias = jnp.where(sublane == head, own, bias)
+        shifts.append(bias)
+    keep = jnp.where(place_row < 1, 0.0, 1.0)
+    forget = jax.nn.sigmoid(gate_rows[0:8] + shifts[0])
+    momentum = jax.nn.sigmoid(gate_rows[8:16] + shifts[1])
+    step = jax.nn.sigmoid(gate_rows[16:24] + shifts[2])
     carry = keep * momentum
     fade = keep * (1.0 - forget)
     keep_all, mix_all, fade_all = carry, carry, fade
@@ -151,7 +169,7 @@
 
 def forward_kernel(heads, plan, *refs):
     carried = len(plan.arrays)
-    own, refs = refs[:8], refs[8:]
+    own, refs = refs[:9], refs[9:]
     sent, refs = refs[:carried], refs[carried:]
     made, refs = refs[:5], refs[5:]
     got, refs = refs[:carried], refs[carried:]
@@ -165,9 +183,12 @@
 
     forward_step(heads, *own, *made, *refs[:5])
 
+    @pl.when(at == (5 * last) // 8)
+    def _():
+        middle()
+
     @pl.when(at == last)
     def _():
-        middle()
         finish()
 
 
@@ -175,12 +196,13 @@
     heads,
     raw_ref,
     gate_ref,
-    place_ref,
+    live_ref,
     conv_ref,
     mem_ref,
     swap_ref,
-    pkey_ref,
-    pvalue_ref,
+    persist_ref,
+    length_ref,
+    bias_ref,
     comb_ref,
     key_out,
     value_out,
@@ -204,7 +226,10 @@
 
     low = lane_index((SEG, LANES)) < HEAD_SIZE
     ext[8 : 8 + SEG, :] = raw_ref[...].astype(f32)
-    place = place_ref[...]
+    place = places(length_ref, at * SEG + lax.broadcasted_iota(jnp.int32, (SEG, 1), 0))
+    place_row = places(length_ref, at * SEG + lane_index((1, SEG)))
+    pkeys, pvalues = persist_ref[0:P_SIZE, :], persist_ref[P_SIZE:, :]
+    first_head = (lax.axis_index("seq") * HEAD_COUNT) // lax.axis_size("seq")
     mixed = mix_taps(ext, conv_ref, place)
     ext[0:8, :] = ext[SEG : SEG + 8, :]
     query_unit, _ = unit_pair(mixed[:, :LANES], low)
@@ -214,7 +239,7 @@
     value_now = value.astype(bf16)
     key_out[...] = key_now
     value_out[...] = value_now
-    scan = gate_scan(gate_ref[0])
+    scan = gate_scan(heads, first_head, gate_ref[...], bias_ref, place_row, live_ref[0, 0:1, :])
     columns = write_columns(scan)
     masks = visible_masks(place, live_prev[0:1, :], scan["live"])
     older = jnp.where(place > lax.broadcasted_iota(jnp.int32, (SEG, 1), 0), 1.0, 0.0)
@@ -224,7 +249,7 @@
     for head in range(heads):
         own = low if head == 0 else jnp.logical_not(low)
         query = jnp.where(own, query_unit, 0.0).astype(bf16)
-        fixed, prev, now = layer_scores(query, kept_prev, key_now, pkey_ref[...], masks)
+        fixed, prev, now = layer_scores(query, kept_prev, key_now, pkeys, masks)
         highest = jnp.maximum(
             jnp.max(fixed, axis=1, keepdims=True),
             jnp.maximum(
@@ -236,7 +261,7 @@
         inverse = 1.0 / summed
         attended = dot_nn((prev * inverse).astype(bf16), kept_value)
         attended = attended + dot_nn((now * inverse).astype(bf16), value_now)
-        attended = attended + dot_nn((fixed * inverse).astype(bf16), pvalue_ref[...])
+        attended = attended + dot_nn((fixed * inverse).astype(bf16), pvalues)
         log_totals = jnp.where(lane_index((SEG, 8)) == head, highest + jnp.log(summed), log_totals)
 
         key_low = to_low(key_unit, head) * MEMORY_SCALE
@@ -297,9 +322,9 @@
 
 def backward_kernel(heads, plan, *refs):
     carried = len(plan.arrays)
-    own, refs = refs[:17], refs[17:]
+    own, refs = refs[:18], refs[18:]
     sent, refs = refs[:carried], refs[carried:]
-    made, refs = refs[:6], refs[6:]
+    made, refs = refs[:5], refs[5:]
     got, refs = refs[:carried], refs[carried:]
     begin, middle, finish = plan.phases(sent, got, refs[5:])
     at, last = pl.program_id(0), pl.num_programs(0) - 1
@@ -325,8 +350,8 @@
     raw_ref,
     tail_ref,
     gate_ref,
-    gate_prev_ref,
-    place_ref,
+    live_ref,
+    live_prev_ref,
     key_ref,
     key_prev_ref,
     value_ref,
@@ -337,14 +362,14 @@
     conv_ref,
     mem_ref,
     swap_ref,
-    pkey_ref,
-    pvalue_ref,
+    persist_ref,
+    length_ref,
+    bias_ref,
     draw_ref,
-    dgate_ref,
     dmem_ref,
     dconv_ref,
-    dpkey_ref,
-    dpvalue_ref,
+    dpersist_ref,
+    dbias_ref,
     ext,
     shifted_rows,
     key_carry,
@@ -357,8 +382,8 @@
     def _():
         dmem_ref[...] = jnp.zeros_like(dmem_ref)
         dconv_ref[...] = jnp.zeros_like(dconv_ref)
-        dpkey_ref[...] = jnp.zeros_like(dpkey_ref)
-        dpvalue_ref[...] = jnp.zeros_like(dpvalue_ref)
+        dpersist_ref[...] = jnp.zeros_like(dpersist_ref)
+        dbias_ref[...] = jnp.zeros_like(dbias_ref)
         shifted_rows[:, 0:8, :] = jnp.zeros((3, 8, 3 * LANES), f32)
         key_carry[...] = jnp.zeros_like(key_carry)
         value_carry[...] = jnp.zeros_like(value_carry)
@@ -367,17 +392,20 @@
     low = lane_index((SEG, LANES)) < HEAD_SIZE
     ext[0:8, :] = tail_ref[8:16, :].astype(f32)
     ext[8 : 8 + SEG, :] = raw_ref[...].astype(f32)
-    place = place_ref[...]
+    here = (pl.num_programs(0) - 1 - at) * SEG
+    place = places(length_ref, here + lax.broadcasted_iota(jnp.int32, (SEG, 1), 0))
+    place_row = places(length_ref, here + lane_index((1, SEG)))
+    pkeys, pvalues = persist_ref[0:P_SIZE, :], persist_ref[P_SIZE:, :]
+    first_head = (lax.axis_index("seq") * HEAD_COUNT) // lax.axis_size("seq")
     mixed = mix_taps(ext, conv_ref, place)
     query_unit, query_inverse = unit_pair(mixed[:, :LANES], low)
     key_unit, key_inverse = unit_pair(mixed[:, LANES : 2 * LANES], low)
     value = mixed[:, 2 * LANES :]
     key_now, key_prev = key_ref[...], key_prev_ref[...]
     value_now, value_prev = value_ref[...], value_prev_ref[...]
-    gate_rows = gate_ref[0]
-    scan = gate_scan(gate_rows)
+    scan = gate_scan(heads, first_head, gate_ref[...], bias_ref, place_row, live_ref[0, 0:1, :])
     columns = write_columns(scan)
-    masks = visible_masks(place, gate_prev_ref[0, 25:26, :], scan["live"])
+    masks = visible_masks(place, live_prev_ref[0, 0:1, :], scan["live"])
     older = jnp.where(place > lax.broadcasted_iota(jnp.int32, (SEG, 1), 0), 1.0, 0.0)
     grad = grad_ref[...].astype(f32)
     grad_query = jnp.zeros((SEG, LANES), f32)
@@ -396,10 +424,10 @@
         query = jnp.where(own, query_unit, 0.0).astype(bf16)
         grad_own = jnp.where(own, grad, 0.0).astype(bf16)
         total = total_ref[:, head : head + 1]
-        scores = layer_scores(query, key_prev, key_now, pkey_ref[...], masks)
+        scores = layer_scores(query, key_prev, key_now, pkeys, masks)
         probs = [jnp.exp(member - total) for member in scores]
         grads = [
-            dot_nt(grad_own, pvalue_ref[...]),
+            dot_nt(grad_own, pvalues),
             dot_nt(grad_own, value_prev),
             dot_nt(grad_own, value_now),
         ]
@@ -407,14 +435,14 @@
         score_grads = [(one * (other - spread)).astype(bf16) for one, other in zip(probs, grads)]
         probs = [member.astype(bf16) for member in probs]
         back = dot_nn(score_grads[1], key_prev) + dot_nn(score_grads[2], key_now)
-        back = SCORE_SCALE * back + dot_nn(score_grads[0], pkey_ref[...])
+        back = SCORE_SCALE * back + dot_nn(score_grads[0], pkeys)
         grad_query = grad_query + jnp.where(own, back, 0.0)
         carry_key = carry_key + SCORE_SCALE * dot_tn(score_grads[1], query)
         grad_key = grad_key + SCORE_SCALE * dot_tn(score_grads[2], query)
         carry_value = carry_value + dot_tn(probs[1], grad_own)
         grad_value = grad_value + dot_tn(probs[2], grad_own)
-        dpkey_ref[...] += dot_tn(score_grads[0], query)
-        dpvalue_ref[...] += dot_tn(probs[0], grad_own)
+        dpersist_ref[0:P_SIZE, :] += dot_tn(score_grads[0], query)
+        dpersist_ref[P_SIZE:, :] += dot_tn(probs[0], grad_own)
 
         mem, swap = mem_ref[head], swap_ref[head]
         state_one, state_two = (state_ref[0, head, member].astype(f32) for member in range(2))
@@ -509,9 +537,18 @@
     forget_back = -grad_fade * scan["keep"] * forget * (1.0 - forget)
     momentum_back = grad_carry * scan["keep"] * momentum * (1.0 - momentum)
     step_back = -THETA_SCALE * grad_written * scan["live"] * step * (1.0 - step)
-    dgate_ref[0, 0:8] = jnp.where(used, forget_back, 0.0)
-    dgate_ref[0, 8:16] = jnp.where(used, momentum_back, 0.0)
-    dgate_ref[0, 16:24] = jnp.where(used, step_back, 0.0)
+    gate_back = jnp.concatenate(
+        [
+            jnp.where(used, forget_back, 0.0),
+            jnp.where(used, momentum_back, 0.0),
+            jnp.where(used, step_back, 0.0),
+            jnp.zeros((LANES - 24, SEG), f32),
+        ],
+        axis=0,
+    )
+    gate_back = jnp.transpose(gate_back)
+    dbias_ref[0:1, :] += jnp.sum(gate_back, axis=0, keepdims=True)
+    draw_ref[:, 3 * LANES :] = gate_back.astype(bf16)
 
     key_carry[...] = carry_key
     value_carry[...] = carry_value
@@ -536,7 +573,7 @@
         dconv_ref[offset : offset + 1, :] += jnp.sum(
             kept * ext[8 - offset : 8 - offset + SEG, :], axis=0, keepdims=True
         )
-    draw_ref[...] = back.astype(bf16)
+    draw_ref[:, : 3 * LANES] = back.astype(bf16)
 
 
 def block_of(shape, index):
@@ -548,20 +585,23 @@
     return pl.BlockSpec(array.shape, lambda n: zeros)
 
 
-def mix_forward(collective, plan, heads, raw, gates, place, conv, mem, swap, pkeys, pvalues):
+def mix_forward(collective, plan, heads, raw, gates, live, *constants):
     length = raw.shape[0]
     count = length // SEG
     row_block = pl.BlockSpec((SEG, LANES), lambda n: (n, 0))
+    smem = pl.BlockSpec(memory_space=pltpu.SMEM)
+    carried_in, carried_out = plan.specs(True)
     return pl.pallas_call(
         partial(forward_kernel, heads, plan),
         grid=(count,),
         in_specs=[
             pl.BlockSpec((SEG, 3 * LANES), lambda n: (n, 0)),
-            pl.BlockSpec((1, 32, SEG), lambda n: (n, 0, 0)),
-            pl.BlockSpec((SEG, 1), lambda n: (n, 0)),
+            row_block,
+            pl.BlockSpec((1, 8, SEG), lambda n: (n, 0, 0)),
         ]
-        + [whole_of(member) for member in (conv, mem, swap, pkeys, pvalues)]
-        + plan.specs(True)[0],
+        + [whole_of(member) for member in constants[:4]]
+        + [smem, smem]
+        + carried_in,
         out_specs=[
             row_block,
             row_block,
@@ -569,7 +609,7 @@
             pl.BlockSpec((SEG, 8), lambda n: (n, 0)),
             pl.BlockSpec((1, heads, 2, MH, LANES), lambda n: (n, 0, 0, 0, 0)),
         ]
-        + plan.specs(True)[1],
+        + carried_out,
         out_shape=[
             jax.ShapeDtypeStruct((length, LANES), bf16),
             jax.ShapeDtypeStruct((length, LANES), bf16),
@@ -593,26 +633,11 @@
             vmem_limit_bytes=VMEM_GRANT,
         ),
         name="mix_forward",
-    )(raw, gates, place, conv, mem, swap, pkeys, pvalues, *plan.arrays)
+    )(raw, gates, live, *constants, *plan.arrays)
 
 
 def mix_backward(
-    collective,
-    plan,
-    heads,
-    raw,
-    gates,
-    place,
-    keys,
-    values,
-    totals,
-    states,
-    grad,
-    conv,
-    mem,
-    swap,
-    pkeys,
-    pvalues,
+    collective, plan, heads, raw, gates, live, keys, values, totals, states, grad, *constants
 ):
     length = raw.shape[0]
     count = length // SEG
@@ -626,15 +651,17 @@
     row_block = pl.BlockSpec((SEG, LANES), lambda n: (here(n), 0))
     prev_block = pl.BlockSpec((SEG, LANES), lambda n: (before(n), 0))
     tail_rows = SEG // 16
+    smem = pl.BlockSpec(memory_space=pltpu.SMEM)
+    carried_in, carried_out = plan.specs(True)
     return pl.pallas_call(
         partial(backward_kernel, heads, plan),
         grid=(count,),
         in_specs=[
             pl.BlockSpec((SEG, 3 * LANES), lambda n: (here(n), 0)),
             pl.BlockSpec((16, 3 * LANES), lambda n: (jnp.maximum(here(n) * tail_rows - 1, 0), 0)),
-            pl.BlockSpec((1, 32, SEG), lambda n: (here(n), 0, 0)),
-            pl.BlockSpec((1, 32, SEG), lambda n: (before(n), 0, 0)),
-            pl.BlockSpec((SEG, 1), lambda n: (here(n), 0)),
+            row_block,
+            pl.BlockSpec((1, 8, SEG), lambda n: (here(n), 0, 0)),
+            pl.BlockSpec((1, 8, SEG), lambda n: (before(n), 0, 0)),
             row_block,
             prev_block,
             row_block,
@@ -643,24 +670,23 @@
             pl.BlockSpec((1, heads, 2, MH, LANES), lambda n: (here(n), 0, 0, 0, 0)),
             row_block,
         ]
-        + [whole_of(member) for member in (conv, mem, swap, pkeys, pvalues)]
-        + plan.specs(True)[0],
+        + [whole_of(member) for member in constants[:4]]
+        + [smem, smem]
+        + carried_in,
         out_specs=[
-            pl.BlockSpec((SEG, 3 * LANES), lambda n: (here(n), 0)),
-            pl.BlockSpec((1, 24, SEG), lambda n: (here(n), 0, 0)),
+            pl.BlockSpec((SEG, 4 * LANES), lambda n: (here(n), 0)),
             pl.BlockSpec((heads, MH, LANES), lambda n: (0, 0, 0)),
             pl.BlockSpec((8, 3 * LANES), lambda n: (0, 0)),
-            pl.BlockSpec((P_SIZE, LANES), lambda n: (0, 0)),
-            pl.BlockSpec((P_SIZE, LANES), lambda n: (0, 0)),
+            pl.BlockSpec((2 * P_SIZE, LANES), lambda n: (0, 0)),
+            pl.BlockSpec((8, LANES), lambda n: (0, 0)),
         ]
-        + plan.specs(True)[1],
+        + carried_out,
         out_shape=[
-            jax.ShapeDtypeStruct((length, 3 * LANES), bf16),
-            jax.ShapeDtypeStruct((count, 24, SEG), f32),
+            jax.ShapeDtypeStruct((length, 4 * LANES), bf16),
             jax.ShapeDtypeStruct((heads, MH, LANES), f32),
             jax.ShapeDtypeStruct((8, 3 * LANES), f32),
-            jax.ShapeDtypeStruct((P_SIZE, LANES), f32),
-            jax.ShapeDtypeStruct((P_SIZE, LANES), f32),
+            jax.ShapeDtypeStruct((2 * P_SIZE, LANES), f32),
+            jax.ShapeDtypeStruct((8, LANES), f32),
         ]
         + plan.shapes,
         scratch_shapes=[
@@ -682,8 +708,8 @@
         raw,
         raw,
         gates,
-        gates,
-        place,
+        live,
+        live,
         keys,
         keys,
         values,
@@ -691,13 +717,129 @@
         totals,
         states,
         grad,
-        conv,
-        mem,
-        swap,
-        pkeys,
-        pvalues,
+        *constants,
         *plan.arrays,
     )
+
+
+class PlaneGather:
+    def __init__(self, seqs, source, target, sems):
+        self.source, self.target = source, target
+        self.local, self.far_send, self.far_recv = sems[:3]
+        self.near_send, self.near_recv, self.relay_send, self.relay_recv = sems[3:]
+        self.chips = seqs // 2
+        self.relayed = self.chips == 4
+        self.seq, self.line = lax.axis_index("seq"), lax.axis_index("fsdp")
+        self.chip, self.core = self.seq // 2, lax.rem(self.seq, 2)
+        self.half = source.shape[0] // 2
+
+    @staticmethod
+    def sems(seqs):
+        dma = pltpu.SemaphoreType.DMA
+        return [dma((1,))] + [dma((seqs // 2,))] * 4 + [dma((2,))] * 2
+
+    def chip_at(self, k):
+        side = math.isqrt(self.chips)
+        across = lax.rem(lax.rem(self.chip, side) + lax.rem(k, side), side)
+        along = lax.rem(self.chip // side + k // side, side)
+        return along * side + across
+
+    def copy(self, source, target, send, recv, place):
+        return pltpu.make_async_remote_copy(
+            src_ref=source,
+            dst_ref=target,
+            send_sem=send,
+            recv_sem=recv,
+            device_id=(place, self.line),
+            device_id_type=MESH,
+        )
+
+    def own(self):
+        return pltpu.make_async_copy(self.source, self.target.at[self.seq], self.local.at[0])
+
+    def far(self, q, slot):
+        place = 2 * q + self.core
+        block = self.target.at[2 * slot + self.core]
+        return self.copy(self.source, block, self.far_send.at[q], self.far_recv.at[slot], place)
+
+    def near(self, q, side):
+        block = self.target.at[2 * q + (self.core if side == 0 else 1 - self.core)]
+        place = 2 * self.chip + 1 - self.core
+        return self.copy(block, block, self.near_send.at[q], self.near_recv.at[q], place)
+
+    def near_own(self):
+        block = self.target.at[self.seq]
+        place = 2 * self.chip + 1 - self.core
+        send, recv = self.near_send.at[self.chip], self.near_recv.at[self.chip]
+        return self.copy(self.source, block, send, recv, place)
+
+    def relay(self, part, q, to):
+        rows = pl.ds(part * self.half, self.half)
+        block = self.target.at[2 * q + self.core, rows]
+        send, recv = self.relay_send.at[part], self.relay_recv.at[part]
+        return self.copy(block, block, send, recv, 2 * to + self.core)
+
+    def loop(self, first, body):
+        def step(k, carry):
+            body(k)
+            return carry
+
+        lax.fori_loop(first, self.chips, step, 0)
+
+    def start(self):
+        self.near_own().start()
+        if self.relayed:
+            for k in (1, 2):
+                self.far(self.chip_at(k), self.chip).start()
+        else:
+            self.loop(1, lambda k: self.far(self.chip_at(k), self.chip).start())
+        self.own().start()
+
+    def step(self, k):
+        q = self.chip_at(k)
+
+        @pl.when(k == 0)
+        def _():
+            self.own().wait()
+
+        if self.relayed:
+            across, along, diagonal = (self.chip_at(i) for i in (1, 2, 3))
+
+            @pl.when(k == 1)
+            def _():
+                self.far(across, across).wait_recv()
+                self.relay(0, across, along).start()
+                self.near(across, 0).start()
+                self.far(along, along).wait_recv()
+                self.relay(1, along, across).start()
+                self.near(along, 0).start()
+
+            @pl.when(k == 3)
+            def _():
+                self.relay(0, diagonal, along).wait_recv()
+                self.relay(1, diagonal, across).wait_recv()
+                self.near(diagonal, 0).start()
+
+        else:
+
+            @pl.when(k > 0)
+            def _():
+                self.far(q, q).wait_recv()
+                self.near(q, 0).start()
+
+        self.near(q, 1).wait_recv()
+
+    def finish(self):
+        self.near_own().wait_send()
+        self.loop(1, lambda k: self.near(self.chip_at(k), 0).wait_send())
+        if self.relayed:
+            across, along = self.chip_at(1), self.chip_at(2)
+            self.far(across, across).wait_send()
+            self.far(along, along).wait_send()
+            self.relay(0, across, along).wait_send()
+            self.relay(1, along, across).wait_send()
+        else:
+            self.loop(1, lambda k: self.far(self.chip_at(k), self.chip_at(k)).wait_send())
 
 
 def exchange_phases(axes, counts, inputs, outputs, scratch):
@@ -767,58 +909,9 @@
 
     spread = []
     for source, target in zip(*groups[0]):
-        local, far_send, far_recv, near_send, near_recv = take(5)
-
-        def own(target=target, source=source, local=local):
-            return pltpu.make_async_copy(source, target.at[seq], local.at[0])
-
-        def far(q, slot, source=source, target=target, send=far_send, recv=far_recv):
-            return pltpu.make_async_remote_copy(
-                src_ref=source,
-                dst_ref=target.at[2 * slot + core],
-                send_sem=send.at[q],
-                recv_sem=recv.at[slot],
-                device_id=twin(q),
-                device_id_type=MESH,
-            )
-
-        def near_own(source=source, target=target, send=near_send, recv=near_recv):
-            return pltpu.make_async_remote_copy(
-                src_ref=source,
-                dst_ref=target.at[seq],
-                send_sem=send.at[chip],
-                recv_sem=recv.at[chip],
-                device_id=sibling,
-                device_id_type=MESH,
-            )
-
-        def near(q, target=target, send=near_send, recv=near_recv):
-            return pltpu.make_async_remote_copy(
-                src_ref=target.at[2 * q + core],
-                dst_ref=target.at[2 * q + core],
-                send_sem=send.at[q],
-                recv_sem=recv.at[q],
-                device_id=sibling,
-                device_id_type=MESH,
-            )
-
-        def near_arrival(q, target=target, send=near_send, recv=near_recv):
-            return pltpu.make_async_remote_copy(
-                src_ref=target.at[2 * q + 1 - core],
-                dst_ref=target.at[2 * q + 1 - core],
-                send_sem=send.at[q],
-                recv_sem=recv.at[q],
-                device_id=sibling,
-                device_id_type=MESH,
-            )
-
-        def start(far=far, near_own=near_own, own=own):
-            loop(1, chips, lambda k: far(lax.rem(chip + k, chips), chip).start())
-            near_own().start()
-            own().start()
-
-        starts.append(start)
-        spread.append((own, far, near_own, near, near_arrival))
+        gather = PlaneGather(seqs, source, target, take(7))
+        starts.append(gather.start)
+        spread.append(gather)
 
     direct = []
     for kind, (sources, targets) in (
@@ -969,14 +1062,9 @@
             loop(1, seqs, lambda k, f=copy: f(lax.rem(seq + k, seqs), lax.rem(seq + k, seqs)).wait_recv())
             own().wait()
             loop(1, lines, lambda k, f=onward: f(lax.rem(line + k, lines), line).start())
-        for own, far, near_own, near, near_arrival in spread:
-
-            def forward(k, far=far, near=near):
-                q = lax.rem(chip + k, chips)
-                far(q, q).wait_recv()
-                near(q).start()
-
-            loop(1, chips, forward)
+        for gather in spread:
+            gather.step(0)
+            gather.step(1)
         for landed, summed, own, copy, onward, keep in merges:
             loop(1, lines, lambda k, f=copy: f(lax.rem(line + k, lines), lax.rem(line + k, lines)).wait_recv())
             own().wait()
@@ -1014,17 +1102,9 @@
                 onward(i, line).wait_send()
 
             loop(1, lines, end_relay)
-        for own, far, near_own, near, near_arrival in spread:
-            own().wait()
-            near_own().wait_send()
-
-            def end_far(k, far=far, near=near):
-                q = lax.rem(chip + k, chips)
-                far(q, q).wait_send()
-                near(q).wait_send()
-
-            loop(1, chips, end_far)
-            loop(0, chips, lambda q, f=near_arrival: f(q).wait_recv())
+        for gather in spread:
+            gather.loop(2, gather.step)
+            gather.finish()
         for source, target, pair, landed, pair_copy, far_copy in sums:
 
             def end_sum(k, far_copy=far_copy):
@@ -1111,7 +1191,7 @@
             for array in group:
                 shape, dtype = array.shape, array.dtype
                 if kind == "gathers":
-                    scratch[kind] += [dma((1,))] + [dma((chips,))] * 4
+                    scratch[kind] += PlaneGather.sems(seqs)
                     shape = (seqs,) + shape
                 elif kind == "planes":
                     scratch[kind] += [dma((1,)), dma((seqs,)), dma((seqs,))]
@@ -1194,8 +1274,249 @@
     )(*plan.arrays)
 
 
+def round_up(number, step):
+    return -(-number // step) * step
+
+
+class Sizes:
+    def __init__(self, seqs, lines):
+        self.seqs, self.lines = seqs, lines
+        self.chips, self.devices = seqs // 2, seqs * lines
+        self.groups = min(HEAD_COUNT, seqs)
+        self.copies = seqs // self.groups
+        self.heads = HEAD_COUNT // self.groups
+        self.width = self.heads * HEAD_SIZE
+        self.share = D // self.devices
+        self.memory = MH // self.devices
+        self.piece = D // seqs
+        self.hidden = FF // lines
+        self.slab = self.hidden // seqs
+        self.gate_at = round_up(3 * self.share, 8)
+        self.mem_at = self.gate_at + round_up(max(self.share, 2 * P_SIZE), 8)
+        self.rest_at = self.mem_at + round_up(self.heads * self.memory, 8)
+        self.weight_rows = round_up(self.rest_at + 8, 16)
+        self.grad_mem_at = round_up(4 * self.share, 8)
+        self.grad_rest_at = self.grad_mem_at + round_up(self.heads * self.memory, 8)
+        self.grad_rows = round_up(self.grad_rest_at + 16, 16)
+
+
+def gate_choice(sizes, group, turned):
+    shape = (LANES, 3 * HEAD_COUNT) if turned else (3 * HEAD_COUNT, LANES)
+    lane = lax.broadcasted_iota(jnp.int32, shape, 0 if turned else 1)
+    column = lax.broadcasted_iota(jnp.int32, shape, 1 if turned else 0)
+    head = lane % 8
+    chosen = (lane // 8 == column // HEAD_COUNT) & (head < sizes.heads)
+    chosen = chosen & (column % HEAD_COUNT == group * sizes.heads + head)
+    return jnp.where(chosen, 1.0, 0.0).astype(bf16)
+
+
+def first_kernel(
+    sizes,
+    token_ref,
+    qkv_ref,
+    gate_ref,
+    conv_ref,
+    pkey_ref,
+    pvalue_ref,
+    gain_one_ref,
+    gain_two_ref,
+    live_ref,
+    mem_ref,
+    ffn_gate_ref,
+    ffn_up_ref,
+    ffn_down_ref,
+    out_ref,
+    normed_out,
+    raw_out,
+    gate_out,
+    matrix_out,
+    mem_out,
+    swap_out,
+    gain_out,
+    taps_out,
+    persist_out,
+    live_out,
+    ffn_out,
+    out_rows,
+    rows_all,
+    pack,
+    pack_rows,
+    ffn_pack,
+    got,
+    conv_full,
+    persist_full,
+    mem_full,
+    matrix_full,
+    *sems,
+):
+    seqs, lines, share, width = sizes.seqs, sizes.lines, sizes.share, sizes.width
+    seq, line = lax.axis_index("seq"), lax.axis_index("fsdp")
+    group = seq // sizes.copies
+    axes = (seqs, lines)
+    greet_all(axes, ("plane", "line"))
+    gather = PlaneGather(seqs, token_ref, rows_all, sems[:7])
+    gather.start()
+    weights = exchange_phases(axes, (0, 0, 0, 0, 0, 0, 1, 0), [pack], [got], sems[7:12])
+    ffn = exchange_phases(axes, (0, 1, 0, 0, 0, 0, 0, 0), [ffn_pack], [ffn_out], sems[12:15])
+    outs = exchange_phases(axes, (0, 0, 1, 0, 0, 0, 0, 0), [out_ref], [out_rows], sems[15:18])
+
+    gate_at, mem_at, rest_at = sizes.gate_at, sizes.mem_at, sizes.rest_at
+    pack_rows[...] = jnp.zeros_like(pack_rows)
+    pack_rows[gate_at : gate_at + P_SIZE, HEAD_SIZE : HEAD_SIZE + share] = pkey_ref[...].astype(f32)
+    pack_rows[gate_at + P_SIZE : gate_at + 2 * P_SIZE, HEAD_SIZE : HEAD_SIZE + share] = pvalue_ref[
+        ...
+    ].astype(f32)
+    pack_rows[rest_at : rest_at + 4, : 3 * share] = conv_ref[...].astype(f32)
+    pack_rows[rest_at + 4 : rest_at + 5, :share] = gain_one_ref[...].astype(f32)
+    pack_rows[rest_at + 5 : rest_at + 6, :share] = gain_two_ref[...].astype(f32)
+    live = live_ref[...].astype(f32)
+    pack_rows[rest_at + 6 : rest_at + 7, :] = live[:, :LANES]
+    pack_rows[rest_at + 7 : rest_at + 8, :] = live[:, LANES:]
+    qkv = qkv_ref[...].astype(f32)
+    gate = gate_ref[...]
+    for to in range(seqs):
+        other = to // sizes.copies
+        for part in range(3):
+            first = part * D + other * width
+            pack_rows[part * share : (part + 1) * share, :width] = qkv[:, first : first + width]
+        chosen = dot_nn(gate, gate_choice(sizes, other, False))
+        pack_rows[gate_at : gate_at + share, :HEAD_SIZE] = chosen[:, :HEAD_SIZE]
+        for head in range(sizes.heads):
+            first = mem_at + head * sizes.memory
+            pack_rows[first : first + sizes.memory, :] = mem_ref[other * sizes.heads + head].astype(
+                f32
+            )
+        pack[to] = pack_rows[...].astype(bf16)
+    weights[0]()
+    for to in range(seqs):
+        columns = slice(to * sizes.slab, (to + 1) * sizes.slab)
+        piece = sizes.piece
+        ffn_pack[to, :piece, :] = ffn_gate_ref[:, columns]
+        ffn_pack[to, piece : 2 * piece, :] = ffn_up_ref[:, columns]
+        turned = jnp.transpose(ffn_down_ref[columns, :].astype(f32))
+        ffn_pack[to, 2 * piece :, :] = turned.astype(bf16)
+    ffn[0]()
+    outs[0]()
+    weights[1]()
+    gather.step(0)
+    gather.step(1)
+    weights[2]()
+
+    aligned = share % 16 == 0
+    matrix = matrix_out if aligned else matrix_full
+    lane = lane_index((share, LANES))
+    for i in range(sizes.devices):
+        block = got[i % lines, i // lines].astype(f32)
+        rows = slice(i * share, (i + 1) * share)
+        for part in range(3):
+            columns = slice(part * LANES, (part + 1) * LANES)
+            matrix[rows, columns] = block[part * share : (part + 1) * share].astype(matrix.dtype)
+        chosen = jnp.where(lane < 24, block[gate_at : gate_at + share], 0.0)
+        matrix[rows, 3 * LANES :] = chosen.astype(matrix.dtype)
+        for head in range(sizes.heads):
+            first = mem_at + head * sizes.memory
+            mem_full[head, i * sizes.memory : (i + 1) * sizes.memory, :] = block[
+                first : first + sizes.memory
+            ]
+        rest = block[rest_at : rest_at + 8]
+        conv_full[0:4, i * 3 * share : (i + 1) * 3 * share] = rest[0:4, : 3 * share]
+        gain_out[4:6, i * share : (i + 1) * share] = rest[4:6, :share]
+    if not aligned:
+        matrix_out[...] = matrix_full[...].astype(bf16)
+    for head in range(sizes.heads):
+        mem_out[head] = mem_full[head].astype(bf16)
+        swap_out[head] = swap_halves(mem_full[head]).astype(bf16)
+    taps_out[...] = jnp.zeros_like(taps_out)
+    for part in range(3):
+        whole = conv_full[:, part * D : (part + 1) * D]
+        turned = pltpu.roll(whole, lax.rem(D - group * width, D), 1)
+        taps_out[0:4, part * LANES : part * LANES + width] = turned[0:4, :width]
+    persist_full[...] = jnp.zeros_like(persist_full)
+    for part in range(width // share):
+        i = group * (width // share) + part
+        block = got[lax.rem(i, lines), i // lines].astype(f32)
+        persist_full[:, part * share : (part + 1) * share] = block[
+            gate_at : gate_at + 2 * P_SIZE, HEAD_SIZE : HEAD_SIZE + share
+        ]
+    persist_out[...] = persist_full[...].astype(bf16)
+    for s in range(seqs):
+        block = got[line, s].astype(f32)
+        live_out[s] = jnp.zeros((8, SEG), f32)
+        live_out[s, 0:1, :LANES] = block[rest_at + 6 : rest_at + 7]
+        live_out[s, 0:1, LANES:] = block[rest_at + 7 : rest_at + 8]
+
+    gain = gain_out[4:5, :]
+
+    def work(k, carry):
+        q = gather.chip_at(k)
+
+        @pl.when(k > 1)
+        def _():
+            gather.step(k)
+
+        both = pl.ds(2 * q, 2)
+        rows = rows_all[both].reshape(2 * SEG, D).astype(f32)
+        normed = (rows * norm_scale(rows) * gain).astype(bf16)
+        projected = dot_nn(normed, matrix_out[...])
+        normed_out[both] = normed.reshape(2, SEG, D)
+        raw_out[both] = projected[:, : 3 * LANES].astype(bf16).reshape(2, SEG, 3 * LANES)
+        gate_out[both] = projected[:, 3 * LANES :].reshape(2, SEG, LANES)
+        return carry
+
+    lax.fori_loop(0, sizes.chips, work, 0)
+    gather.finish()
+    ffn[2]()
+    outs[2]()
+
+
+def first_call(sizes, tokens, *operands):
+    seqs, lines = sizes.seqs, sizes.lines
+    dma = pltpu.SemaphoreType.DMA
+    any_spec, vmem_spec = pl.BlockSpec(memory_space=pl.ANY), pl.BlockSpec(memory_space=pltpu.VMEM)
+    shape = jax.ShapeDtypeStruct
+    matrix_shape = (D, 4 * LANES)
+    return pl.pallas_call(
+        partial(first_kernel, sizes),
+        out_shape=[
+            shape((seqs, SEG, D), bf16),
+            shape((seqs, SEG, 3 * LANES), bf16),
+            shape((seqs, SEG, LANES), f32),
+            shape(matrix_shape, bf16),
+            shape((sizes.heads, MH, LANES), bf16),
+            shape((sizes.heads, MH, LANES), bf16),
+            shape((8, D), f32),
+            shape((8, 3 * LANES), f32),
+            shape((2 * P_SIZE, LANES), bf16),
+            shape((seqs, 8, SEG), f32),
+            shape((seqs, 3 * sizes.piece, sizes.slab), bf16),
+            shape((lines, sizes.share, D), bf16),
+        ],
+        in_specs=[any_spec] + [vmem_spec] * 12 + [any_spec],
+        out_specs=[vmem_spec] * 10 + [any_spec] * 2,
+        scratch_shapes=[
+            pltpu.VMEM((seqs, SEG, D), bf16),
+            pltpu.VMEM((seqs, sizes.weight_rows, LANES), bf16),
+            pltpu.VMEM((sizes.weight_rows, LANES), f32),
+            pltpu.VMEM((seqs, 3 * sizes.piece, sizes.slab), bf16),
+            pltpu.VMEM((lines, seqs, sizes.weight_rows, LANES), bf16),
+            pltpu.VMEM((8, 3 * D), f32),
+            pltpu.VMEM((2 * P_SIZE, LANES), f32),
+            pltpu.VMEM((sizes.heads, MH, LANES), f32),
+            pltpu.VMEM((8, LANES) if sizes.share % 16 == 0 else matrix_shape, f32),
+        ]
+        + PlaneGather.sems(seqs)
+        + [dma((1,)), dma((seqs,)), dma((seqs,)), dma((lines,)), dma((lines,))]
+        + [dma((1,)), dma((seqs,)), dma((seqs,))]
+        + [dma((1,)), dma((lines,)), dma((lines,))],
+        compiler_params=pltpu.CompilerParams(
+            collective_id=0, has_side_effects=True, vmem_limit_bytes=VMEM_GRANT
+        ),
+        name="first",
+    )(tokens, *operands)
+
+
 def ffn_kernel(
-    axes,
+    sizes,
     rows_ref,
     cot_ref,
     weight_ref,
@@ -1208,30 +1529,27 @@
     landed,
     cot_slot,
     down_slot,
-    grad_sum,
-    far_send,
-    far_recv,
-    near_send,
-    near_recv,
+    both_matrix,
+    down_matrix,
+    both_grad,
+    down_grad,
+    acts,
+    part,
+    blocks,
+    block_sem,
     pair_send,
     pair_recv,
     back_send,
     back_recv,
     cot_sem,
     down_sem,
-    grad_sem,
+    *gather_sems,
 ):
-    seqs, lines = axes
-    chips = seqs // 2
-    side = math.isqrt(chips)
+    seqs, lines, chips = sizes.seqs, sizes.lines, sizes.chips
+    hidden_size, slab, piece = sizes.slab * sizes.lines, sizes.slab, sizes.piece
     seq, line = lax.axis_index("seq"), lax.axis_index("fsdp")
     chip, core = seq // 2, lax.rem(seq, 2)
     sibling = (2 * chip + 1 - core, line)
-
-    def at_step(k):
-        across = lax.rem(lax.rem(chip, side) + lax.rem(k, side), side)
-        along = lax.rem(chip // side + k // side, side)
-        return along * side + across
 
     def loop(first, last, body):
         def step(k, carry):
@@ -1239,16 +1557,6 @@
             return carry
 
         lax.fori_loop(first, last, step, 0)
-
-    barrier = pltpu.get_barrier_semaphore()
-
-    def greet(k):
-        pl.semaphore_signal(
-            barrier, inc=1, device_id=(lax.rem(seq + k, seqs), line), device_id_type=MESH
-        )
-
-    loop(1, seqs, greet)
-    pl.semaphore_wait(barrier, seqs - 1)
 
     def remote(source, target, send, recv, place):
         return pltpu.make_async_remote_copy(
@@ -1260,140 +1568,158 @@
             device_id_type=MESH,
         )
 
-    def far(q, slot):
-        return remote(
-            rows_ref,
-            rows_all.at[2 * slot + core],
-            far_send.at[q],
-            far_recv.at[slot],
-            (2 * q + core, line),
+    gather = PlaneGather(seqs, rows_ref, rows_all, gather_sems)
+
+    def order(j):
+        return jnp.where(j >= 2, 5 - j, j) if chips == 4 else j
+
+    def chip_at(j):
+        return gather.chip_at(order(j))
+
+    def to_pair(j):
+        q, slot = chip_at(j), lax.rem(j, 2)
+        return remote(other.at[slot], pair.at[q], pair_send.at[slot], pair_recv.at[q], sibling)
+
+    def back(q, slot):
+        place = (2 * q + core, line)
+        return remote(pair.at[q], landed.at[slot], back_send.at[q], back_recv.at[slot], place)
+
+    def cot_copy(j, slot):
+        return pltpu.make_async_copy(
+            cot_ref.at[pl.ds(2 * chip_at(j), 2)], cot_slot.at[slot], cot_sem.at[slot]
         )
 
-    def near(q):
-        block = rows_all.at[2 * q + core]
-        return remote(block, block, near_send.at[q], near_recv.at[q], sibling)
-
-    def near_own():
-        return remote(
-            rows_ref, rows_all.at[seq], near_send.at[chip], near_recv.at[chip], sibling
+    def down_copy(j):
+        slot = lax.rem(j, 2)
+        return pltpu.make_async_copy(
+            down_slot.at[slot], down_ref.at[pl.ds(2 * chip_at(j), 2)], down_sem.at[slot]
         )
 
-    def near_arrival(q):
-        block = rows_all.at[2 * q + 1 - core]
-        return remote(block, block, near_send.at[q], near_recv.at[q], sibling)
-
-    def to_pair(q):
-        return remote(other.at[q], pair.at[q], pair_send.at[q], pair_recv.at[q], sibling)
-
-    def back(q, slot):
-        return remote(
-            pair.at[q],
-            landed.at[slot],
-            back_send.at[q],
-            back_recv.at[slot],
-            (2 * q + core, line),
-        )
-
-    def block_at(step):
-        q = at_step(step // 2)
-        return 2 * q + jnp.where(lax.rem(step, 2) == 0, 1 - core, core)
-
-    def cot_copy(step):
-        slot = lax.rem(step, 2)
-        return pltpu.make_async_copy(
-            cot_ref.at[block_at(step)], cot_slot.at[slot], cot_sem.at[slot]
-        )
-
-    def down_copy(step):
-        slot = lax.rem(step, 2)
-        return pltpu.make_async_copy(
-            down_slot.at[slot], down_ref.at[block_at(step)], down_sem.at[slot]
-        )
-
-    near_own().start()
-    loop(1, chips, lambda k: far(at_step(k), chip).start())
-    cot_copy(0).start()
-    rows_all[seq] = rows_ref[...]
-    grad_sum[...] = jnp.zeros_like(grad_sum)
-
-    def work(step):
-        k = step // 2
-        q = at_step(k)
-        mine = lax.rem(step, 2)
-        block = block_at(step)
-        slot = lax.rem(step, 2)
-
-        @pl.when(step + 1 < seqs)
+    greet_all((seqs, lines), ("plane",))
+    gather.start()
+    cot_copy(0, 0).start()
+    slots = blocks.shape[0]
+
+    def weight_copy(f):
+        return pltpu.make_async_copy(weight_ref.at[f], blocks.at[f % slots], block_sem.at[f % slots])
+
+    def grad_copy(f):
+        return pltpu.make_async_copy(blocks.at[f % slots], grad_ref.at[f], block_sem.at[f % slots])
+
+    for f in range(slots):
+        weight_copy(f).start()
+    for f in range(lines):
+        weight_copy(f).wait()
+        columns = slice(f * slab, (f + 1) * slab)
+        up_columns = slice(hidden_size + f * slab, hidden_size + (f + 1) * slab)
+        for s in range(seqs):
+            rows = slice(s * piece, (s + 1) * piece)
+            both_matrix[rows, columns] = blocks[f % slots, s, :piece, :]
+            both_matrix[rows, up_columns] = blocks[f % slots, s, piece : 2 * piece, :]
+            down_matrix[rows, columns] = blocks[f % slots, s, 2 * piece :, :]
+        if f + slots < lines:
+            weight_copy(f + slots).start()
+
+    def forth(j):
+        k, q = order(j), chip_at(j)
+        gather.step(k)
+        cot_copy(j, lax.rem(j, 2)).wait()
+
+        @pl.when(jnp.logical_and(j > 0, j + 1 < chips))
         def _():
-            cot_copy(step + 1).start()
-
-        @pl.when(jnp.logical_and(mine == 0, k > 0))
-        def _():
-            far(q, q).wait_recv()
-            near(q).start()
-
-        @pl.when(mine == 0)
-        def _():
-            near_arrival(q).wait_recv()
-
-        cot_copy(step).wait()
-
-        @pl.when(step >= 2)
-        def _():
-            down_copy(step - 2).wait()
-
-        rows = rows_all[block]
-        cot = cot_slot[slot]
-        up_gate, up_matrix, down_matrix = weight_ref[0], weight_ref[1], weight_ref[2]
-        gate_act = dot_nn(rows, up_gate)
-        up_act = dot_nn(rows, up_matrix)
-        grad_hidden = dot_nn(cot, down_matrix)
+            cot_copy(j + 1, lax.rem(j + 1, 2)).start()
+
+        rows = rows_all[pl.ds(2 * q, 2)].reshape(2 * SEG, D)
+        cot = cot_slot[lax.rem(j, 2)].reshape(2 * SEG, D)
+        grad_hidden = dot_nn(cot, down_matrix[...])
+        ups = dot_nn(rows, both_matrix[...])
+        gate_act, up_act = ups[:, :hidden_size], ups[:, hidden_size:]
         sigmoid = jax.nn.sigmoid(gate_act)
         swish = gate_act * sigmoid
-        hidden = (swish * up_act).astype(bf16)
         slope = sigmoid * (1.0 + gate_act - swish)
-        grad_gate = (grad_hidden * up_act * slope).astype(bf16)
-        grad_up = (grad_hidden * swish).astype(bf16)
-        part = dot_nt(grad_gate, up_gate) + dot_nt(grad_up, up_matrix)
-
-        @pl.when(mine == 0)
+        acts[j, :, :hidden_size] = (grad_hidden * up_act * slope).astype(bf16)
+        acts[j, :, hidden_size : 2 * hidden_size] = (grad_hidden * swish).astype(bf16)
+        acts[j, :, 2 * hidden_size :] = (swish * up_act).astype(bf16)
+        part[...] = dot_nt(acts[j, :, : 2 * hidden_size], both_matrix[...])
+
+        @pl.when(j >= 2)
         def _():
-            other[q] = part.astype(bf16)
-            to_pair(q).start()
-
-        @pl.when(mine == 1)
+            to_pair(j - 2).wait_send()
+
+        theirs = part[pl.ds(pl.multiple_of((1 - core) * SEG, SEG), SEG), :].astype(bf16)
+        other[lax.rem(j, 2)] = theirs
+        to_pair(j).start()
+        to_pair(j).wait_recv()
+        own = part[pl.ds(pl.multiple_of(core * SEG, SEG), SEG), :] + pair[q].astype(f32)
+
+        @pl.when(j == 0)
         def _():
-            to_pair(q).wait_recv()
-            both = part + pair[q].astype(f32)
-
-            @pl.when(k == 0)
+            sum_ref[...] = own
+
+        @pl.when(j > 0)
+        def _():
+            pair[q] = own.astype(bf16)
+            back(q, chip).start()
+
+    def weigh(j):
+        q = chip_at(j)
+        slot = lax.rem(j, 2)
+
+        @pl.when(j > 0)
+        def _():
+            cot_copy(j, slot).wait()
+
+            @pl.when(j + 1 < chips)
             def _():
-                sum_ref[...] = both
-
-            @pl.when(k > 0)
-            def _():
-                pair[q] = both.astype(bf16)
-                back(q, chip).start()
-
-        down_slot[slot] = dot_nt(hidden, down_matrix).astype(bf16)
-        down_copy(step).start()
-        grad_sum[0] += dot_tn(rows, grad_gate)
-        grad_sum[1] += dot_tn(rows, grad_up)
-        grad_sum[2] += dot_tn(cot, hidden)
-
-    loop(0, seqs, work)
-    for member in range(3):
-        other_grad = grad_sum[member].astype(bf16)
-        grad_ref[member] = other_grad
-    down_copy(seqs - 2).wait()
-    down_copy(seqs - 1).wait()
-    near_own().wait_send()
-    loop(0, chips, lambda q: to_pair(q).wait_send())
-
-    def end(k):
-        q = at_step(k)
-        far(q, q).wait_send()
-        near(q).wait_send()
+                cot_copy(j + 1, lax.rem(j + 1, 2)).start()
+
+        @pl.when(j >= 2)
+        def _():
+            down_copy(j - 2).wait()
+
+        hidden = acts[j, :, 2 * hidden_size :]
+        down_slot[slot] = dot_nt(hidden, down_matrix[...]).astype(bf16).reshape(2, SEG, D)
+        down_copy(j).start()
+        rows = rows_all[pl.ds(2 * q, 2)].reshape(2 * SEG, D)
+        cot = cot_slot[slot].reshape(2 * SEG, D)
+        both_new = dot_tn(rows, acts[j, :, : 2 * hidden_size])
+        down_new = dot_tn(cot, hidden)
+
+        @pl.when(j == 0)
+        def _():
+            both_grad[...] = both_new
+            down_grad[...] = down_new
+
+        @pl.when(j > 0)
+        def _():
+            both_grad[...] += both_new
+            down_grad[...] += down_new
+
+    forth(jnp.int32(0))
+    weigh(jnp.int32(0))
+    cot_copy(1, 1).start()
+    loop(1, chips, forth)
+    cot_copy(1, 1).start()
+    loop(1, chips, weigh)
+    for f in range(lines):
+        if f >= slots:
+            grad_copy(f - slots).wait()
+        columns = slice(f * slab, (f + 1) * slab)
+        up_columns = slice(hidden_size + f * slab, hidden_size + (f + 1) * slab)
+        for s in range(seqs):
+            rows = slice(s * piece, (s + 1) * piece)
+            blocks[f % slots, s, :piece, :] = both_grad[rows, columns].astype(bf16)
+            blocks[f % slots, s, piece : 2 * piece, :] = both_grad[rows, up_columns].astype(bf16)
+            blocks[f % slots, s, 2 * piece :, :] = down_grad[rows, columns].astype(bf16)
+        grad_copy(f).start()
+    for f in range(lines - slots, lines):
+        grad_copy(f).wait()
+    loop(chips - 2, chips, lambda j: down_copy(j).wait())
+    gather.finish()
+    loop(chips - 2, chips, lambda j: to_pair(j).wait_send())
+
+    def end(j):
+        q = chip_at(j)
         back(q, chip).wait_send()
         back(q, q).wait_recv()
         sum_ref[...] += landed[q].astype(f32)
@@ -1401,40 +1727,360 @@
     loop(1, chips, end)
 
 
-def feed_forward(collective, rows, cot, weights):
-    seqs, lines = lax.axis_size("seq"), lax.axis_size("fsdp")
-    chips = seqs // 2
-    hidden = weights.shape[2]
+def feed_forward(sizes, rows, cot, weights):
+    seqs, lines, chips = sizes.seqs, sizes.lines, sizes.chips
+    hidden = sizes.slab * lines
     dma = pltpu.SemaphoreType.DMA
     any_spec, vmem_spec = pl.BlockSpec(memory_space=pl.ANY), pl.BlockSpec(memory_space=pltpu.VMEM)
     half = pltpu.VMEM((chips, SEG, D), bf16)
+    slots = lines if lines <= 4 else 2
     return pl.pallas_call(
-        partial(ffn_kernel, (seqs, lines)),
+        partial(ffn_kernel, sizes),
         out_shape=[
             jax.ShapeDtypeStruct((SEG, D), f32),
             jax.ShapeDtypeStruct((seqs, SEG, D), bf16),
-            jax.ShapeDtypeStruct((3, D, hidden), bf16),
+            jax.ShapeDtypeStruct(weights.shape, bf16),
         ],
-        in_specs=[vmem_spec, any_spec, vmem_spec],
-        out_specs=[vmem_spec, any_spec, vmem_spec],
+        in_specs=[vmem_spec, any_spec, any_spec],
+        out_specs=[vmem_spec, any_spec, any_spec],
         scratch_shapes=[
             pltpu.VMEM((seqs, SEG, D), bf16),
+            pltpu.VMEM((2, SEG, D), bf16),
             half,
             half,
-            half,
-            pltpu.VMEM((2, SEG, D), bf16),
-            pltpu.VMEM((2, SEG, D), bf16),
-            pltpu.VMEM((3, D, hidden), f32),
+            pltpu.VMEM((2, 2, SEG, D), bf16),
+            pltpu.VMEM((2, 2, SEG, D), bf16),
+            pltpu.VMEM((D, 2 * hidden), bf16),
+            pltpu.VMEM((D, hidden), bf16),
+            pltpu.VMEM((D, 2 * hidden), f32),
+            pltpu.VMEM((D, hidden), f32),
+            pltpu.VMEM((chips, 2 * SEG, 3 * hidden), bf16),
+            pltpu.VMEM((2 * SEG, D), f32),
+            pltpu.VMEM((slots,) + weights.shape[1:], bf16),
+            dma((slots,)),
         ]
-        + [dma((chips,))] * 8
-        + [dma((2,)), dma((2,)), dma((1,))],
+        + [dma((2,)), dma((chips,)), dma((chips,)), dma((chips,))]
+        + [dma((2,)), dma((2,))]
+        + PlaneGather.sems(seqs),
         compiler_params=pltpu.CompilerParams(
-            collective_id=collective, has_side_effects=True, vmem_limit_bytes=VMEM_GRANT
+            collective_id=2, has_side_effects=True, vmem_limit_bytes=VMEM_GRANT
         ),
         name="feed_forward",
     )(rows, cot, weights)
 
 
+def last_kernel(
+    sizes,
+    grad_ref,
+    normed_ref,
+    matrix_ref,
+    mem_ref,
+    taps_ref,
+    persist_ref,
+    bias_ref,
+    gain_two_ref,
+    ffn_ref,
+    out_ref,
+    token_ref,
+    middle_ref,
+    gain_ref,
+    qkv_ref,
+    gate_ref,
+    own_gain_ref,
+    token_grad,
+    qkv_grad,
+    gate_grad,
+    mem_grad,
+    conv_grad,
+    persist_grad,
+    out_grad,
+    gain_one_grad,
+    gain_two_grad,
+    ffn_gate_grad,
+    ffn_up_grad,
+    ffn_down_grad,
+    bias_grad,
+    normed_slot,
+    matrix_grad,
+    pack,
+    pack_rows,
+    pack_landed,
+    pack_sums,
+    pack_got,
+    out_blocks,
+    out_got,
+    persist_got,
+    ffn_got,
+    other,
+    pair,
+    landed,
+    conv_full,
+    normed_sem,
+    pair_send,
+    pair_recv,
+    back_send,
+    back_recv,
+    *sems,
+):
+    seqs, lines, chips = sizes.seqs, sizes.lines, sizes.chips
+    share, width, heads = sizes.share, sizes.width, sizes.heads
+    seq, line = lax.axis_index("seq"), lax.axis_index("fsdp")
+    me = seq * lines + line
+    group = seq // sizes.copies
+    chip, core = seq // 2, lax.rem(seq, 2)
+    sibling = (2 * chip + 1 - core, line)
+    side = math.isqrt(chips)
+
+    def chip_at(k):
+        across = lax.rem(lax.rem(chip, side) + lax.rem(k, side), side)
+        along = lax.rem(chip // side + k // side, side)
+        return along * side + across
+
+    def loop(first, last, body):
+        def step(k, carry):
+            body(k)
+            return carry
+
+        lax.fori_loop(first, last, step, 0)
+
+    def remote(source, target, send, recv, place):
+        return pltpu.make_async_remote_copy(
+            src_ref=source,
+            dst_ref=target,
+            send_sem=send,
+            recv_sem=recv,
+            device_id=place,
+            device_id_type=MESH,
+        )
+
+    def to_pair(k):
+        q, slot = chip_at(lax.rem(k, chips)), lax.rem(k, 2)
+        return remote(other.at[slot], pair.at[q], pair_send.at[slot], pair_recv.at[q], sibling)
+
+    def back(q, slot):
+        place = (2 * q + core, line)
+        return remote(pair.at[q], landed.at[slot], back_send.at[q], back_recv.at[slot], place)
+
+    def normed_copy(q, slot):
+        return pltpu.make_async_copy(
+            normed_ref.at[pl.ds(2 * q, 2)], normed_slot.at[slot], normed_sem.at[slot]
+        )
+
+    axes = (seqs, lines)
+    greet_all(axes, ("plane", "line"))
+    ffn = exchange_phases(axes, (0, 1, 0, 0, 0, 0, 0, 0), [ffn_ref], [ffn_got], sems[0:3])
+    outs = exchange_phases(
+        axes, (0, 0, 2, 0, 0, 0, 0, 0), [out_blocks, persist_ref], [out_got, persist_got], sems[3:9]
+    )
+    grads = exchange_phases(
+        axes, (0, 0, 0, 0, 0, 0, 0, 1), [pack], [pack_got], [pack_landed, pack_sums, *sems[9:14]]
+    )
+    normed_copy(0, 0).start()
+    ffn[0]()
+
+    def gather_grad(q):
+        slot = lax.rem(q, 2)
+
+        @pl.when(q + 1 < chips)
+        def _():
+            normed_copy(q + 1, lax.rem(q + 1, 2)).start()
+
+        normed_copy(q, slot).wait()
+        grad = grad_ref[pl.ds(2 * q, 2)].reshape(2 * SEG, 4 * LANES)
+        new = dot_tn(normed_slot[slot].reshape(2 * SEG, D), grad)
+
+        @pl.when(q == 0)
+        def _():
+            matrix_grad[...] = new
+
+        @pl.when(q > 0)
+        def _():
+            matrix_grad[...] += new
+
+    loop(0, chips, gather_grad)
+    mem_at, rest_at = sizes.grad_mem_at, sizes.grad_rest_at
+    pack_rows[...] = jnp.zeros_like(pack_rows)
+    for tap in range(4):
+        for part in range(3):
+            at = rest_at + 3 * tap + part
+            pack_rows[at : at + 1, :] = taps_ref[tap : tap + 1, part * LANES : (part + 1) * LANES]
+    pack_rows[rest_at + 12 : rest_at + 13, :] = bias_ref[0:1, :]
+    for i in range(sizes.devices):
+        rows = slice(i * share, (i + 1) * share)
+        for part in range(4):
+            pack_rows[part * share : (part + 1) * share, :] = matrix_grad[
+                rows, part * LANES : (part + 1) * LANES
+            ]
+        for head in range(heads):
+            first = mem_at + head * sizes.memory
+            pack_rows[first : first + sizes.memory, :] = mem_ref[
+                head, i * sizes.memory : (i + 1) * sizes.memory, :
+            ]
+        pack_rows[rest_at + 13 : rest_at + 14, :share] = gain_two_ref[0:1, rows]
+        pack[i % lines, i // lines] = pack_rows[...].astype(bf16)
+    grads[0]()
+    for f in range(lines):
+        out_blocks[f] = out_ref[f * share : (f + 1) * share, :].astype(bf16)
+    outs[0]()
+
+    def spread(k):
+        q = chip_at(lax.rem(k, chips))
+        grad = grad_ref[pl.ds(2 * q, 2)].reshape(2 * SEG, 4 * LANES)
+        if sizes.copies > 1:
+            grad = grad * jnp.where(lax.rem(seq, sizes.copies) == 0, 1.0, 0.0).astype(bf16)
+        whole = dot_nt(grad, matrix_ref[...])
+        first_core, second_core = whole[:SEG], whole[SEG:]
+
+        @pl.when(k >= 3)
+        def _():
+            to_pair(k - 2).wait_send()
+
+        other[lax.rem(k, 2)] = jnp.where(core == 0, second_core, first_core).astype(bf16)
+        to_pair(k).start()
+        own = jnp.where(core == 0, first_core, second_core)
+        to_pair(k).wait_recv()
+        own = own + pair[q].astype(f32)
+
+        @pl.when(k == chips)
+        def _():
+            token_grad[...] = own
+
+        @pl.when(k < chips)
+        def _():
+            pair[q] = own.astype(bf16)
+            back(q, chip).start()
+
+    loop(1, chips + 1, spread)
+    grads[1]()
+
+    def add_back(k):
+        q = chip_at(k)
+        back(q, q).wait_recv()
+        token_grad[...] += landed[q].astype(f32)
+
+    loop(1, chips, add_back)
+    rows = token_ref[...].astype(f32)
+    scale = norm_scale(rows)
+    token_grad[...] = middle_ref[...] + norm_pull(rows, scale, gain_ref[4:5, :], token_grad[...])
+
+    ffn[2]()
+    piece, slab = sizes.piece, sizes.slab
+    for s in range(seqs):
+        columns = slice(s * slab, (s + 1) * slab)
+        ffn_gate_grad[:, columns] = ffn_got[s, :piece, :].astype(f32)
+        ffn_up_grad[:, columns] = ffn_got[s, piece : 2 * piece, :].astype(f32)
+        ffn_down_grad[columns, :] = jnp.transpose(ffn_got[s, 2 * piece :, :].astype(f32))
+    outs[2]()
+    out_sum = out_got[0].astype(f32)
+    persist_sum = persist_got[0]
+    for f in range(1, lines):
+        out_sum = out_sum + out_got[f].astype(f32)
+        persist_sum = persist_sum + persist_got[f]
+    out_grad[...] = out_sum
+    inside = lax.rem(LANES - (me * share - group * width), LANES)
+    persist_grad[...] = pltpu.roll(persist_sum, inside, 1)[:, :share]
+
+    grads[2]()
+    gates = jnp.zeros((share, 3 * HEAD_COUNT), f32)
+    bias = jnp.zeros((8, 3 * HEAD_COUNT), f32)
+    gain_two = jnp.zeros((1, share), f32)
+    conv_full[...] = jnp.zeros_like(conv_full)
+    for s in range(seqs):
+        block = pack_got[s].astype(f32)
+        gain_two = gain_two + block[rest_at + 13 : rest_at + 14, :share]
+        if s % sizes.copies:
+            continue
+        other_group = s // sizes.copies
+        for part in range(3):
+            first = part * D + other_group * width
+            qkv_grad[:, first : first + width] = block[
+                part * share : (part + 1) * share, :width
+            ]
+            for tap in range(4):
+                at = rest_at + 3 * tap + part
+                conv_full[tap : tap + 1, first : first + width] = block[at : at + 1, :width]
+        choice = gate_choice(sizes, other_group, True)
+        gates = gates + dot_nn(block[3 * share : 4 * share].astype(bf16), choice)
+        rest = block[rest_at + 8 : rest_at + 16].astype(bf16)
+        bias = bias + dot_nn(rest, choice)
+        for head in range(heads):
+            first = mem_at + head * sizes.memory
+            mem_grad[other_group * heads + head] = block[first : first + sizes.memory]
+    gate_grad[...] = gates
+    bias_grad[...] = bias[4:5]
+    gain_two_grad[...] = gain_two
+    along = jnp.sum(qkv_grad[...] * qkv_ref[...].astype(f32), axis=1, keepdims=True)
+    along = along + jnp.sum(gates * gate_ref[...].astype(f32), axis=1, keepdims=True)
+    gain_one_grad[...] = along / own_gain_ref[...].astype(f32)
+    turned = pltpu.roll(conv_full[...], lax.rem(3 * D - me * 3 * share, 3 * D), 1)
+    conv_grad[...] = turned[:, : 3 * share]
+
+    def end(k):
+        q = chip_at(k)
+        back(q, chip).wait_send()
+
+    loop(1, chips, end)
+    loop(chips - 1, chips + 1, lambda k: to_pair(k).wait_send())
+
+
+def last_call(sizes, *operands):
+    seqs, lines, chips, share = sizes.seqs, sizes.lines, sizes.chips, sizes.share
+    dma = pltpu.SemaphoreType.DMA
+    any_spec, vmem_spec = pl.BlockSpec(memory_space=pl.ANY), pl.BlockSpec(memory_space=pltpu.VMEM)
+    shape = jax.ShapeDtypeStruct
+    half = pltpu.VMEM((chips, SEG, D), bf16)
+    in_specs = [vmem_spec] * len(operands)
+    in_specs[1] = any_spec
+    in_specs[8] = any_spec
+    pack_shape = (lines, seqs, sizes.grad_rows, LANES)
+    return pl.pallas_call(
+        partial(last_kernel, sizes),
+        out_shape=[
+            shape((SEG, D), f32),
+            shape((share, 3 * D), f32),
+            shape((share, 3 * HEAD_COUNT), f32),
+            shape((HEAD_COUNT, sizes.memory, LANES), f32),
+            shape((8, 3 * share), f32),
+            shape((2 * P_SIZE, share), f32),
+            shape((share, D), f32),
+            shape((share, 1), f32),
+            shape((1, share), f32),
+            shape((sizes.piece, sizes.hidden), f32),
+            shape((sizes.piece, sizes.hidden), f32),
+            shape((sizes.hidden, sizes.piece), f32),
+            shape((1, 3 * HEAD_COUNT), f32),
+        ],
+        in_specs=in_specs,
+        out_specs=[vmem_spec] * 13,
+        scratch_shapes=[
+            pltpu.VMEM((2, 2, SEG, D), bf16),
+            pltpu.VMEM((D, 4 * LANES), f32),
+            pltpu.VMEM(pack_shape, bf16),
+            pltpu.VMEM(pack_shape[2:], f32),
+            pltpu.VMEM(pack_shape, bf16),
+            pltpu.VMEM(pack_shape[1:], bf16),
+            pltpu.VMEM(pack_shape[1:], bf16),
+            pltpu.VMEM((lines, share, D), bf16),
+            pltpu.VMEM((lines, share, D), bf16),
+            pltpu.VMEM((lines, 2 * P_SIZE, LANES), f32),
+            pltpu.VMEM((seqs, 3 * sizes.piece, sizes.slab), bf16),
+            pltpu.VMEM((2, SEG, D), bf16),
+            half,
+            half,
+            pltpu.VMEM((8, 3 * D), f32),
+            dma((2,)),
+        ]
+        + [dma((2,)), dma((chips,)), dma((chips,)), dma((chips,))]
+        + [dma((1,)), dma((seqs,)), dma((seqs,))]
+        + [dma((1,)), dma((lines,)), dma((lines,))] * 2
+        + [dma((1,)), dma((lines,)), dma((lines,)), dma((seqs,)), dma((seqs,))],
+        compiler_params=pltpu.CompilerParams(
+            collective_id=5, has_side_effects=True, vmem_limit_bytes=VMEM_GRANT
+        ),
+        name="last",
+    )(*operands)
+
+
 def norm_scale(values):
     return lax.rsqrt(jnp.mean(values * values, axis=-1, keepdims=True) + NORM_EPS)
 
@@ -1442,10 +2088,6 @@
 def norm_pull(values, scale, gain, grad):
     inner = jnp.mean(grad * gain * values, axis=-1, keepdims=True)
     return scale * (grad * gain - values * (scale * scale) * inner)
-
-
-def swish_slope(values, sigmoid):
-    return sigmoid * (1.0 + values * (1.0 - sigmoid))
 
 
 def widen(rows, width):
@@ -1472,144 +2114,81 @@
     live_mask,
     cotangent,
 ):
-    seqs, lines = lax.axis_size("seq"), lax.axis_size("fsdp")
-    devices = seqs * lines
-    seq, line = lax.axis_index("seq"), lax.axis_index("fsdp")
-    me = seq * lines + line
-    groups = min(HEAD_COUNT, seqs)
-    copies = seqs // groups
-    heads = HEAD_COUNT // groups
-    width = heads * HEAD_SIZE
-    group = seq // copies
-    first_copy = (seq % copies == 0).astype(f32)
-    share = D // devices
-    hidden_share = MH // devices
+    sizes = Sizes(lax.axis_size("seq"), lax.axis_size("fsdp"))
+    seqs, lines, groups = sizes.seqs, sizes.lines, sizes.groups
+    heads, width, share = sizes.heads, sizes.width, sizes.share
     length = seqs * SEG
-    piece = D // seqs
-    slab = ffn_gate.shape[1] // seqs
-
-    def for_copies(array):
-        return jnp.repeat(array, copies, axis=0) if copies > 1 else array
-
-    qkv_blocks = qkv_weight.reshape(share, 3, groups, width).transpose(2, 1, 0, 3)
-    qkv_blocks = widen(qkv_blocks, LANES).reshape(groups, 3 * share, LANES)
     memory_pack = jnp.concatenate([memory_w1.transpose(0, 2, 1), memory_w2], axis=2)
-    memory_blocks = memory_pack.reshape(groups, heads * hidden_share, LANES)
-    persistent = jnp.concatenate([persistent_keys, persistent_values], axis=0)
-    gate_part = jnp.pad(gate_weight, ((0, 2 * P_SIZE - share), (0, HEAD_SIZE - 3 * HEAD_COUNT)))
-    small_pack = jnp.concatenate(
-        [
-            jnp.concatenate([gate_part, widen(persistent, HEAD_SIZE)], axis=1),
-            widen(conv_weight, LANES),
-            widen(norm1_gain[None], LANES),
-            widen(norm2_gain[None], LANES),
-            live_mask[0].astype(bf16).reshape(SEG // LANES, LANES),
-        ],
-        axis=0,
+    (
+        normed,
+        raw,
+        gates,
+        matrix,
+        memory_both,
+        memory_turned,
+        gains,
+        taps,
+        persistent,
+        live,
+        ffn_part,
+        out_rows,
+    ) = first_call(
+        sizes,
+        tokens[0],
+        qkv_weight,
+        gate_weight,
+        conv_weight,
+        persistent_keys,
+        persistent_values,
+        norm1_gain[None],
+        norm2_gain[None],
+        live_mask,
+        memory_pack,
+        ffn_gate,
+        ffn_up,
+        ffn_down,
+        out_weight,
     )
-    small_pack = jnp.broadcast_to(small_pack, (groups,) + small_pack.shape)
-    weight_pack = jnp.concatenate([qkv_blocks, memory_blocks, small_pack], axis=1)
-    weight_pack = jnp.pad(weight_pack, ((0, 0), (0, -weight_pack.shape[1] % 16), (0, 0)))
-    ffn_local = jnp.stack([ffn_gate, ffn_up, ffn_down.T])
-    ffn_blocks = ffn_local.reshape(3, piece, seqs, slab).transpose(2, 0, 1, 3)
-    ffn_blocks = ffn_blocks.reshape(seqs, 3 * piece, slab)
-    token_rows, ffn_got, out_rows, weights_got = exchange(
-        "first_exchange",
-        0,
-        gathers=[tokens[0]],
-        planes=[ffn_blocks],
-        to_line=[out_weight],
-        relays=[for_copies(weight_pack)],
-    )
-    ffn_part = ffn_got.reshape(seqs, 3, piece, slab).transpose(1, 0, 2, 3).reshape(3 * D, slab)
-    ffn_full = lax.all_gather(ffn_part, "fsdp", axis=1, tiled=True).reshape(3, D, lines * slab)
-
-    token_rows = token_rows.reshape(length, D)
-    memory_at = 3 * share
-    small_at = memory_at + heads * hidden_share
-    qkv_matrix = weights_got[:, :, :memory_at].reshape(lines, seqs, 3, share, LANES)
-    qkv_matrix = qkv_matrix.transpose(1, 0, 3, 2, 4).reshape(D, 3 * LANES)
-    memory_both = weights_got[:, :, memory_at:small_at]
-    memory_both = memory_both.reshape(lines, seqs, heads, hidden_share, LANES)
-    memory_both = memory_both.transpose(2, 1, 0, 3, 4).reshape(heads, MH, LANES)
-    memory_turned = jnp.concatenate(
-        [memory_both[..., HEAD_SIZE:], memory_both[..., :HEAD_SIZE]], axis=-1
-    )
-    small_got = weights_got[:, :, small_at:].transpose(1, 0, 2, 3)
-    small_all = small_got.reshape((devices,) + small_got.shape[2:])
-    gate_matrix = small_all[:, :share, : 3 * HEAD_COUNT].reshape(D, 3, HEAD_COUNT)
-    gate_rows = gate_matrix.transpose(1, 2, 0)
-    gate_rows = lax.dynamic_slice_in_dim(gate_rows, group * heads, heads, 1)
-    gate_rows = jnp.pad(gate_rows, ((0, 0), (0, 8 - heads), (0, 0))).reshape(24, D)
-    after = 2 * P_SIZE
-    taps = small_all[:, after : after + 4, : 3 * share].transpose(1, 0, 2)
-    taps = taps.reshape(4, 3, groups, width)
-    taps = lax.dynamic_slice_in_dim(taps, group, 1, 2)[:, :, 0]
-    taps = jnp.pad(widen(taps, LANES).reshape(4, 3 * LANES), ((0, 4), (0, 0))).astype(f32)
-    persistent = small_all[:, :after, HEAD_SIZE : HEAD_SIZE + share].transpose(1, 0, 2)
-    persistent = persistent.reshape(after, D)
-    persistent = widen(lax.dynamic_slice_in_dim(persistent, group * width, width, 1), LANES)
-    pkeys, pvalues = persistent[:P_SIZE], persistent[P_SIZE:]
-    gain_one = small_all[:, after + 4, :share].reshape(1, D).astype(f32)
-    gain_two = small_all[:, after + 5, :share].reshape(1, D).astype(f32)
-    live_all = small_got[:, :, after + 6 : after + 6 + SEG // LANES].reshape(seqs, lines, SEG)
-    live_all = lax.dynamic_index_in_dim(live_all, line, 1, False).astype(f32)
-
-    lengths = doc_lengths[0]
-    starts = jnp.cumsum(lengths) - lengths
-
-    def place_of(positions):
-        inside = starts <= positions[..., None]
-        return positions - jnp.max(jnp.where(inside, starts, -1), axis=-1)
-
-    place_rows = place_of(jnp.arange(length, dtype=jnp.int32).reshape(seqs, SEG))
-    place_column = place_of(jnp.arange(length, dtype=jnp.int32).reshape(length, 1))
-
-    wide_tokens = token_rows.astype(f32)
-    normed = (wide_tokens * norm_scale(wide_tokens) * gain_one).astype(bf16)
-    raw = jnp.dot(normed, qkv_matrix, preferred_element_type=f32).astype(bf16)
-    gate_input = dot_nt(gate_rows, normed)
-    shift = lax.dynamic_slice_in_dim(gate_bias, group * heads, heads, 1)
-    shift = shift * jnp.array([[3.0], [1.0], [1.0]], f32) + jnp.array([[-7.5], [1.5], [0.0]], f32)
-    shift = jnp.pad(shift, ((0, 0), (0, 8 - heads))).reshape(24, 1)
-    gate_input = (gate_input + shift).reshape(24, seqs, SEG).transpose(1, 0, 2)
-    extra = jnp.stack([place_rows.astype(f32), live_all], axis=1)
-    gates = jnp.concatenate([gate_input, jnp.pad(extra, ((0, 0), (0, 6), (0, 0)))], axis=1)
-    constants = (taps, memory_both, memory_turned, pkeys, pvalues)
+    ffn_full = lax.all_gather(ffn_part, "fsdp")
+
+    constants = (taps, memory_both, memory_turned, persistent, doc_lengths, gate_bias)
+    raw = raw.reshape(length, 3 * LANES)
+    gates = gates.reshape(length, LANES)
     plan = Exchange(gathers=[out_rows.reshape(lines * share, D), cotangent[0]])
     mixed, keys, values, totals, states, out_matrix, cot_rows = mix_forward(
-        6, plan, heads, raw, gates, place_column, *constants
+        6, plan, heads, raw, gates, live, *constants
     )
     out_matrix = out_matrix.reshape(D, D)
 
     (mixed_got,) = exchange("to_segments", 1, planes=[mixed.reshape(seqs, SEG, LANES)])
-    combined = mixed_got[::copies, :, :width].transpose(1, 0, 2).reshape(SEG, D)
+    combined = mixed_got[:: sizes.copies, :, :width].transpose(1, 0, 2).reshape(SEG, D)
     inputs = tokens[0].astype(f32)
+    gain_two = gains[5:6]
     middle = inputs + jnp.dot(combined, out_matrix, preferred_element_type=f32)
     scale_two = norm_scale(middle)
     normed_two_own = (middle * scale_two * gain_two).astype(bf16)
-    grad_normed_two, down_part, ffn_grads = feed_forward(
-        2, normed_two_own, cot_rows, ffn_full
-    )
-    ffn_grads = ffn_grads.reshape(3 * D, lines * slab)
-    ffn_grads = lax.psum_scatter(ffn_grads, "fsdp", scatter_dimension=1, tiled=True)
+
+    grad_normed_two, down_part, ffn_grads = feed_forward(sizes, normed_two_own, cot_rows, ffn_full)
+    ffn_grads = lax.psum_scatter(ffn_grads, "fsdp")
 
     grad_middle = cotangent[0].astype(f32) + norm_pull(middle, scale_two, gain_two, grad_normed_two)
     grad_gain_two = jnp.sum(grad_normed_two * middle * scale_two, axis=0, keepdims=True)
     grad_branch = grad_middle.astype(bf16)
     grad_combined = dot_nt(grad_branch, out_matrix).astype(bf16)
     grad_out = dot_tn(combined, grad_branch).astype(bf16)
-    plan = Exchange(scatters=[down_part, grad_out.reshape(seqs, piece, D)])
+    plan = Exchange(scatters=[down_part, grad_out.reshape(seqs, sizes.piece, D)])
     blocks = widen(grad_combined.reshape(SEG, groups, width).transpose(1, 0, 2), LANES)
-    (grad_mixed,) = exchange("to_heads", 4, planes=[for_copies(blocks)])
-
-    grad_raw, grad_gates, grad_memory, grad_taps, grad_pkeys, grad_pvalues, down_sum, grad_out = mix_backward(
+    if sizes.copies > 1:
+        blocks = jnp.repeat(blocks, sizes.copies, axis=0)
+    (grad_mixed,) = exchange("to_heads", 4, planes=[blocks])
+
+    grad_all, grad_memory, grad_taps, grad_persistent, grad_bias, down_sum, grad_out = mix_backward(
         7,
         plan,
         heads,
         raw,
         gates,
-        place_column,
+        live,
         keys,
         values,
         totals,
@@ -1618,84 +2197,56 @@
         *constants,
     )
     output = (middle + down_sum).astype(bf16)
-    grad_gates = grad_gates.transpose(1, 0, 2).reshape(24, length)
-    grad_gates_low = grad_gates.astype(bf16)
-    grad_gate_rows = dot_nn(grad_gates_low, normed)
-    grad_normed = dot_nt(grad_raw, qkv_matrix) + dot_tn(grad_gates_low, gate_rows)
-    grad_normed = (grad_normed * first_copy).astype(bf16).reshape(seqs, SEG, D)
-
-    qkv_part = dot_tn(normed, grad_raw).astype(bf16).reshape(seqs, lines, share, 3, LANES)
-    qkv_part = qkv_part.transpose(1, 0, 3, 2, 4).reshape(lines, seqs, 3 * share, LANES)
-    memory_part = grad_memory.astype(bf16).reshape(heads, seqs, lines, hidden_share, LANES)
-    memory_part = memory_part.transpose(2, 1, 0, 3, 4)
-    memory_part = memory_part.reshape(lines, seqs, heads * hidden_share, LANES)
-    owner_rows = jnp.concatenate([grad_gate_rows, grad_gain_two], axis=0).astype(bf16)
-    owner_rows = owner_rows.reshape(25, seqs, lines, share).transpose(2, 1, 0, 3)
-    bias_sums = widen(jnp.sum(grad_gates, axis=1)[None], LANES)
-    shared_rows = jnp.concatenate([grad_taps[:4].reshape(12, LANES), bias_sums], axis=0)
-    shared_rows = jnp.broadcast_to(shared_rows.astype(bf16), (lines, seqs, 13, LANES))
-    grad_pack = jnp.concatenate(
-        [qkv_part, memory_part, widen(owner_rows, LANES), shared_rows], axis=2
+    (
+        input_grad,
+        grad_qkv,
+        grad_gate,
+        grad_memory,
+        grad_conv,
+        grad_persistent,
+        grad_out,
+        grad_gain_one,
+        grad_gain_two,
+        grad_ffn_gate,
+        grad_ffn_up,
+        grad_ffn_down,
+        grad_bias,
+    ) = last_call(
+        sizes,
+        grad_all.reshape(seqs, SEG, 4 * LANES),
+        normed,
+        matrix,
+        grad_memory,
+        grad_taps,
+        grad_persistent,
+        grad_bias,
+        grad_gain_two,
+        ffn_grads,
+        grad_out,
+        tokens[0],
+        grad_middle,
+        gains,
+        qkv_weight,
+        gate_weight,
+        norm1_gain[:, None],
     )
-    grad_pack = jnp.pad(grad_pack, ((0, 0), (0, 0), (0, -grad_pack.shape[2] % 16), (0, 0)))
-    line_pack = jnp.concatenate([grad_pkeys, grad_pvalues], axis=0)
-    out_part = grad_out.astype(bf16).reshape(lines, share, D)
-    ffn_out = ffn_grads.reshape(3, seqs, piece, slab).transpose(1, 0, 2, 3)
-    ffn_got, out_got, line_got, grad_normed, grads_got = exchange(
-        "last_exchange",
-        5,
-        planes=[ffn_out.reshape(seqs, 3 * piece, slab)],
-        to_line=[out_part, line_pack],
-        scatters=[grad_normed],
-        merges=[grad_pack],
-    )
-
-    scale_one = norm_scale(inputs)
-    input_grad = grad_middle + norm_pull(inputs, scale_one, gain_one, grad_normed)
-
-    grad_sums = grads_got[::copies].astype(f32)
-    grad_qkv = grad_sums[:, : 3 * share].reshape(groups, 3, share, LANES)[..., :width]
-    grad_qkv = grad_qkv.transpose(2, 1, 0, 3).reshape(share, 3 * D)
-    owner_at = small_at
-    grad_memory = grad_sums[:, memory_at:owner_at].reshape(HEAD_COUNT, hidden_share, LANES)
-    grad_memory_w1 = grad_memory[..., :HEAD_SIZE].transpose(0, 2, 1)
-    grad_memory_w2 = grad_memory[..., HEAD_SIZE:]
-    grad_gate = grad_sums[:, owner_at : owner_at + 24, :share]
-    grad_gate = grad_gate.reshape(groups, 3, 8, share)[:, :, :heads].transpose(3, 1, 0, 2)
-    grad_gate = grad_gate.reshape(share, 3 * HEAD_COUNT)
-    grad_gain_two = jnp.sum(grads_got[:, owner_at + 24, :share].astype(f32), axis=0)
-    own_gain = norm1_gain.astype(f32)
-    along = jnp.sum(grad_qkv * qkv_weight.astype(f32), axis=1)
-    along = along + jnp.sum(grad_gate * gate_weight.astype(f32), axis=1)
-    grad_gain_one = along / own_gain
-    shared_at = owner_at + 25
-    grad_conv = grad_sums[:, shared_at : shared_at + 12].reshape(groups, 4, 3, LANES)[..., :width]
-    grad_conv = grad_conv.transpose(1, 2, 0, 3).reshape(4, 3 * D)
-    grad_conv = lax.dynamic_slice_in_dim(grad_conv, me * 3 * share, 3 * share, 1)
-    grad_bias = grad_sums[:, shared_at + 12, :24].reshape(groups, 3, 8)[:, :, :heads]
-    grad_bias = grad_bias.transpose(1, 0, 2).reshape(3, HEAD_COUNT)
-    grad_bias = grad_bias * jnp.array([[3.0], [1.0], [1.0]], f32)
-    line_sums = jnp.sum(line_got, axis=0)
-    line_sums = lax.dynamic_slice_in_dim(line_sums, me * share - group * width, share, 1)
-    ffn_sums = ffn_got.astype(f32).reshape(seqs, 3, piece, slab).transpose(1, 2, 0, 3)
-    ffn_sums = ffn_sums.reshape(3, piece, seqs * slab)
     return (
         output[None],
         input_grad[None],
-        grad_gain_one,
+        grad_gain_one[:, 0],
         grad_qkv,
         grad_gate,
-        grad_conv,
-        grad_memory_w1,
-        grad_memory_w2,
-        line_sums[:P_SIZE],
-        line_sums[P_SIZE:],
-        jnp.sum(out_got.astype(f32), axis=0),
-        grad_gain_two,
-        ffn_sums[0],
-        ffn_sums[1],
-        ffn_sums[2].T,
-        grad_bias,
+        grad_conv[:4],
+        grad_memory[..., :HEAD_SIZE].transpose(0, 2, 1),
+        grad_memory[..., HEAD_SIZE:],
+        grad_persistent[:P_SIZE],
+        grad_persistent[P_SIZE:],
+        grad_out,
+        grad_gain_two[0],
+        grad_ffn_gate,
+        grad_ffn_up,
+        grad_ffn_down,
+        grad_bias.reshape(3, HEAD_COUNT) * jnp.array([[3.0], [1.0], [1.0]], f32),
     )
 
 

time: 411 us -> 357 us (0.87)
  local copies, waits for them, and re-layouts: 48.8 us -> 19.3 us
  other arithmetic: 35.4 us -> 10.5 us
  matrix products: 29.1 us -> 5.4 us
  Pallas kernels: 278 us -> 296 us
  waiting for transfers between devices: 0.04 us -> 10.4 us
    pallas_call x1 -> x3, Pallas kernels: 58.3 us -> 167 us  [the longest x1 59.3 us: feed_forward(): pl.pallas_call(partial(ffn_kernel, sizes), out_shape=[jax.ShapeDtypeStruc...]
    pallas_call x4 -> x2, Pallas kernels: 102 us -> 17.9 us  [exchange(): pl.pallas_call(partial(exchange_kernel, plan), out_shape=plan.shapes, in_...]
    convert_element_type x10 -> x0, other arithmetic: 13.6 us -> none  [the longest x2 9.24 us: on_device(): normed = (wide_tokens * norm_scale(wide_tokens) * gain_one).astype(bf16)]
    all_gather x1, waiting for transfers between devices: 0.01 us -> 10.3 us  [on_device(): ffn_full = lax.all_gather(ffn_part, 'fsdp')]
    reduce_sum x8 -> x0, other arithmetic: 9.16 us -> none  [the longest x2 4.59 us: norm_scale(): jnp.mean(values * values, axis=-1, keepdims=True) + NORM_EPS]
    dot_general x2 -> x0, matrix products: 8.69 us -> none  [the longest x1 5.73 us: on_device(): raw = jnp.dot(normed, qkv_matrix, preferred_element_type=f32).astype(bf16)]
    dot_general x3 -> x1, matrix products: 10.3 us -> 2.05 us  [dot_tn(): lax.dot_general(left, right, (((0,), (0,)), ((), ())), preferred_element_...]
    slice x19 -> x4, local copies, waits for them, and re-layouts: 11.7 us -> 5.04 us  [the longest x1 1.63 us: on_device(): grad_memory[..., HEAD_SIZE:]]
  transfers between devices with their start and end apart: 2 -> 2, of which waited for: 0 -> 1; matrix products, arithmetic and copies ran while one was open for 18% -> 5% of each run, Pallas kernels for 33% -> 36%
where the time goes in v3:
time: 357 us; the launch traced here: 356 us
  Pallas kernels  296 us (83%)
  local copies, waits for them, and re-layouts  19.3 us (5%)
  between operations  14.3 us (4%)
  other arithmetic  10.5 us (3%)
  waiting for transfers between devices  10.4 us (3%)
  matrix products  5.4 us (2%)
    pallas_call x1, Pallas kernels, mix_backward(): pl.pallas_call(partial(backward_kernel, heads, plan), grid=(count,), in_s...  66.9 us
    pallas_call x1, Pallas kernels, feed_forward(): pl.pallas_call(partial(ffn_kernel, sizes), out_shape=[jax.ShapeDtypeStruc...  59.3 us
    pallas_call x1, Pallas kernels, first_call(): pl.pallas_call(partial(first_kernel, sizes), out_shape=[shape((seqs, SEG,...  57.4 us
    pallas_call x1, Pallas kernels, last_call(): pl.pallas_call(partial(last_kernel, sizes), out_shape=[shape((SEG, D), f3...  49.8 us
    pallas_call x1, Pallas kernels, mix_forward(): pl.pallas_call(partial(forward_kernel, heads, plan), grid=(count,), in_sp...  44.9 us
    pallas_call x2, Pallas kernels, exchange(): pl.pallas_call(partial(exchange_kernel, plan), out_shape=plan.shapes, in_...  17.9 us
    all_gather x1, waiting for transfers between devices, on_device(): ffn_full = lax.all_gather(ffn_part, 'fsdp')  10.3 us
    unnamed x38, local copies, waits for them, and re-layouts  8.9 us
  transfers between devices with their start and end apart: 2, of which 1 were waited for; matrix products, arithmetic and copies ran while one was open for 5% of the time, Pallas kernels for 36%

profile of v3, /device:TPU:0, one launch (start us, length us, event | category | flops | bytes accessed | tf_op | source)
XLA Modules:
  0.0 356.0 jit_solution(16030912334414207659)
XLA Ops:
  7.2 1.5 pad_maximum_fusion.mem_ref
  8.7 57.4 %first.1 = (bf16[8,256,1024]{2,1,0:T(8,128)(2,1)}, bf16[8,256,384]{2,1,0:T(8,128)(2,1)}, f32[8,256,128]{2,1,0:T(8,128)}, bf16[1024,512]{1,0:T(8,128)(2,1)}, bf16...) custom-call(bf16[256,1024]{1,0:T(8,128)(2,1)} %bitcast.46, ...), custom_call_target="tpu_custom_call" | custom-call | tf_op jit(solution)/shard_map/first/pallas_call | solution.py:1478
  66.2 44.9 %mix_forward.1 = (bf16[2048,128]{1,0:T(8,128)(2,1)}, bf16[2048,128]{1,0:T(8,128)(2,1)}, bf16[2048,128]{1,0:T(8,128)(2,1)}, f32[2048,8]{1,0:T(8,128)}, bf16[8,2,2...) custom-call(bf16[2048,384]{1,0:T(8,128)(2,1)} %bitcast.41, ...), custom_call_target="tpu_custom_call" | custom-call | tf_op jit(solution)/shard_map/mix_forward/pallas_call | solution.py:594
  111.1 8.8 %to_segments.1 = bf16[8,256,128]{2,1,0:T(8,128)(2,1)} custom-call(bf16[8,256,128]{2,1,0:T(8,128)(2,1)} %bitcast.60), custom_call_target="tpu_custom_call" | custom-call | tf_op jit(solution)/shard_map/to_segments/pallas_call | solution.py:1264
  120.7 2.6 multiply_reduce_fusion.2
  123.3 1.0 multiply_convert_fusion.rows_ref
  124.3 10.3 %all-gather.3.cloned.1.call-done = bf16[32,384,128]{2,1,0:T(8,128)(2,1)} async-done(((bf16[8,384,128]{2,1,0:T(8,128)(2,1)}), bf16[32,384,128]{2,1,0:T(8,128)(2,1)}) %all-gather.3.cloned.1.call-update) | async-done | bytes 3145744 | tf_op jit(solution)/shard_map/all_gather | solution.py:2152
  134.6 59.3 %feed_forward.1 = (f32[256,1024]{1,0:T(8,128)}, bf16[8,256,1024]{2,1,0:T(8,128)(2,1)}, bf16[4,8,384,128]{3,2,1,0:T(8,128)(2,1)}) custom-call(bf16[256,1024]{1,0:T(8,128)(2,1)} %multiply_convert_fusion.rows_ref, bf16[8,256,1024]{2,1,0:T(8,128)(2,1)} %get-tuple-element.73.cot_ref, bf16[4,8,384,128]{3,2,1,0:T(8,128)(2,1)} %bitcast.51), custom_call_target="tpu_custom_call" | custom-call | tf_op jit(solution)/shard_map/feed_forward/pallas_call | solution.py:1737
  193.9 1.0 copy-done.3
  194.9 1.0 copy.42
  197.6 1.7 multiply_add_fusion.middle_ref
  200.7 1.0 copy.40
  201.7 2.0 copy.41
  203.7 9.0 %to_heads.1 = bf16[8,256,128]{2,1,0:T(8,128)(2,1)} custom-call(bf16[8,256,128]{2,1,0:T(8,128)(2,1)} %bitcast.56), custom_call_target="tpu_custom_call" | custom-call | tf_op jit(solution)/shard_map/to_heads/pallas_call | solution.py:1264
  212.8 2.0 convolution_convert_fusion
  214.8 66.9 %mix_backward.1 = (bf16[2048,512]{1,0:T(8,128)(2,1)}, f32[2,256,128]{2,1,0:T(8,128)}, f32[8,384]{1,0:T(8,128)}, f32[32,128]{1,0:T(8,128)}, f32[8,128]{1,0:T(8,12...) custom-call(bf16[2048,384]{1,0:T(8,128)(2,1)} %bitcast.42, bf16[2048,384]{1,0:T(8,128)(2,1)} %bitcast.43, ...), custom_call_target="tpu_custom_call" | custom-call | tf_op jit(solution)/shard_map/mix_backward/pallas_call | solution.py:656
  281.7 2.1 fusion.1
  283.8 49.8 %last.1 = (f32[256,1024]{1,0:T(8,128)}, f32[32,3072]{1,0:T(8,128)}, f32[32,48]{1,0:T(8,128)}, f32[16,8,128]{2,1,0:T(8,128)}, f32[8,96]{1,0:T(8,128)}, /*index=5*...) custom-call(bf16[8,256,512]{2,1,0:T(8,128)(2,1)} %bitcast.52, ...), custom_call_target="tpu_custom_call" | custom-call | tf_op jit(solution)/shard_map/last/pallas_call | solution.py:2036
  333.7 1.3 slice.19
  335.1 1.6 fusion.6
  336.7 1.3 fusion.7
  338.0 1.3 reduce
  339.9 1.3 reduce.4
  341.9 2.4 copy.52
  (50 shorter events, 10.1 us)
Async XLA Ops:
  7.2 127.4 %all-gather.3.cloned.1.call-start = ((), (), s32[]{:S(2)}) async-start(), calls=%async_computation.2 | async-start | bytes 3932160 | tf_op jit(solution)/shard_map/all_gather | solution.py:2152
  66.1 217.7 %reduce-scatter.2.cloned.1.call-start = ((), (), s32[]{:S(2)}) async-start(), calls=%async_computation.1 | async-start | bytes 3932160 | tf_op jit(solution)/shard_map/reduce_scatter | solution.py:2172
  66.1 54.6 %copy-start.2 = (bf16[1,256,1024]{2,1,0:T(8,128)(2,1)S(1)}, bf16[1,256,1024]{2,1,0:T(8,128)(2,1)}, u32[]{:S(2)}) copy-start(bf16[1,256,1024]{2,1,0:T(8,128)(2,1)} %param.19) | copy-start | bytes 1572868
  193.9 1.0 copy-start.3
  193.9 2.0 copy-start.12
  193.9 2.7 copy-start.4
  197.6 2.3 copy-start.1
  199.3 13.5 %copy-start = (f32[256,1024]{1,0:T(8,128)}, f32[256,1024]{1,0:T(8,128)S(1)}, u32[]{:S(2)}) copy-start(f32[256,1024]{1,0:T(8,128)S(1)} %multiply_add_fusion.middle_ref) | copy-start | bytes 3145732
  200.6 12.1 %copy-start.5 = (bf16[256,8,128]{0,2,1:T(8,128)(2,1)S(1)}, bf16[256,8,128]{0,2,1:T(8,128)(2,1)}, u32[]{:S(2)}) copy-start(bf16[256,8,128]{0,2,1:T(8,128)(2,1)} %copy.42) | copy-start | bytes 1572868
  283.8 57.4 %copy-start.13 = (f32[3]{0:T(128)S(1)}, f32[3]{0:T(128)}, u32[]{:S(2)}) copy-start(f32[3]{0:T(128)} %constant.18) | copy-start | bytes 40
  333.7 10.6 %copy-start.9 = (f32[32,3072]{1,0:T(8,128)S(1)}, f32[32,3072]{1,0:T(8,128)}, u32[]{:S(2)}) copy-start(f32[32,3072]{1,0:T(8,128)} %get-tuple-element.129) | copy-start | bytes 1179652
  333.7 11.3 %copy-start.11 = (f32[32,48]{1,0:T(8,128)S(1)}, f32[32,48]{1,0:T(8,128)}, u32[]{:S(2)}) copy-start(f32[32,48]{1,0:T(8,128)} %get-tuple-element.130) | copy-start | bytes 18436
  333.7 11.9 %copy-start.10 = (f32[32,1024]{1,0:T(8,128)S(1)}, f32[32,1024]{1,0:T(8,128)}, u32[]{:S(2)}) copy-start(f32[32,1024]{1,0:T(8,128)} %get-tuple-element.136) | copy-start | bytes 393220
  333.7 12.5 %copy-start.14 = (f32[1,32]{1,0:T(1,128)S(1)}, f32[1,32]{1,0:T(1,128)}, u32[]{:S(2)}) copy-start(f32[1,32]{1,0:T(1,128)} %get-tuple-element.95) | copy-start | bytes 388
  333.7 13.0 %copy-start.8 = (f32[128,1024]{1,0:T(8,128)S(1)}, f32[128,1024]{1,0:T(8,128)}, u32[]{:S(2)}) copy-start(f32[128,1024]{1,0:T(8,128)} %get-tuple-element.138) | copy-start | bytes 1572868
  341.9 5.7 %copy-start.7 = (f32[128,1024]{1,0:T(8,128)S(1)}, f32[128,1024]{1,0:T(8,128)}, u32[]{:S(2)}) copy-start(f32[128,1024]{1,0:T(8,128)} %get-tuple-element.139) | copy-start | bytes 1572868
  344.2 4.1 %copy-start.6 = (f32[1024,128]{1,0:T(8,128)S(1)}, f32[1024,128]{1,0:T(8,128)}, u32[]{:S(2)}) copy-start(f32[1024,128]{1,0:T(8,128)} %get-tuple-element.140) | copy-start | bytes 1572868
Sparse Core Ops, SparseCore 0:
  66.2 68.3 all-gather.2
  194.1 58.6 reduce-scatter.1

commit v4 on v3

--- a/solution.py
+++ b/solution.py
@@ -23,7 +23,8 @@
 MEMORY_SCALE = 8.0
 THETA_SCALE = 0.0005
 MASKED = -1000000000.0
-VMEM_GRANT = 56 * 1024 * 1024
+LEAST_SHIFT = -30.0
+VMEM_GRANT = 62 * 1024 * 1024
 MESH = pl.DeviceIdType.MESH
 
 f32 = jnp.float32
@@ -44,10 +45,6 @@
 
 def lane_index(shape):
     return lax.broadcasted_iota(jnp.int32, shape, 1)
-
-
-def to_low(rows, head):
-    return rows if head == 0 else pltpu.roll(rows, HEAD_SIZE, 1)
 
 
 def swap_halves(rows):
@@ -152,19 +149,31 @@
     return jnp.where(low, keep_all, fade_all), mix_all
 
 
-def visible_masks(place, live_prev, live_now):
+def half_swish(inner):
+    turn = jnp.tanh(0.5 * inner)
+    sigmoid = 0.5 * turn + 0.5
+    active = inner * sigmoid
+    slope = sigmoid + active * (1.0 - sigmoid)
+    return turn, sigmoid, active, slope
+
+
+def fill_bias(bias_ref, place, live_prev, live_now):
     row = lax.broadcasted_iota(jnp.int32, (SEG, SEG), 0)
     gap = row - lane_index((SEG, SEG))
-    now = (gap >= 0) & (gap <= place) & (live_now > 0.5)
-    prev = (gap < 0) & (gap + SEG <= place) & (live_prev > 0.5)
-    return prev, now
-
-
-def layer_scores(query, key_prev, key_now, pkeys, masks):
-    fixed = dot_nt(query, pkeys)
-    prev = jnp.where(masks[0], SCORE_SCALE * dot_nt(query, key_prev), MASKED)
-    now = jnp.where(masks[1], SCORE_SCALE * dot_nt(query, key_now), MASKED)
-    return fixed, prev, now
+    hidden_prev = jnp.where(live_prev > 0.5, 0.0, MASKED)
+    hidden_now = jnp.where(live_now > 0.5, 0.0, MASKED)
+    bias_ref[:, :SEG] = jnp.where((gap < 0) & (gap + SEG <= place), hidden_prev, MASKED)
+    bias_ref[:, SEG : 2 * SEG] = jnp.where((gap >= 0) & (gap <= place), hidden_now, MASKED)
+
+
+def fill_persistent(bias_ref, keys_all, values_all, persist_ref):
+    lane = lane_index((SEG, LANES))
+    bias_ref[:, 2 * SEG :] = jnp.where(lane < P_SIZE, 0.0, MASKED)
+    keys_all[2 * SEG :, :] = jnp.zeros((LANES, LANES), bf16)
+    values_all[2 * SEG :, :] = jnp.zeros((LANES, LANES), bf16)
+    pkeys = persist_ref[0:P_SIZE, :].astype(f32) * (1.0 / SCORE_SCALE)
+    keys_all[2 * SEG : 2 * SEG + P_SIZE, :] = pkeys.astype(bf16)
+    values_all[2 * SEG : 2 * SEG + P_SIZE, :] = persist_ref[P_SIZE:, :]
 
 
 def forward_kernel(heads, plan, *refs):
@@ -173,7 +182,7 @@
     sent, refs = refs[:carried], refs[carried:]
     made, refs = refs[:5], refs[5:]
     got, refs = refs[:carried], refs[carried:]
-    begin, middle, finish = plan.phases(sent, got, refs[5:])
+    begin, middle, finish = plan.phases(sent, got, refs[6:])
     at, last = pl.program_id(0), pl.num_programs(0) - 1
 
     @pl.when(at == 0)
@@ -181,7 +190,7 @@
         greet_all(plan.axes, plan.kinds)
         begin()
 
-    forward_step(heads, *own, *made, *refs[:5])
+    forward_step(heads, *own, *made, *refs[:6])
 
     @pl.when(at == (5 * last) // 8)
     def _():
@@ -209,102 +218,119 @@
     total_out,
     state_out,
     ext,
-    key_prev,
-    value_prev,
+    keys_all,
+    values_all,
     live_prev,
     state,
+    hidden,
 ):
     at = pl.program_id(0)
 
     @pl.when(at == 0)
     def _():
         ext[0:8, :] = jnp.zeros((8, 3 * LANES), f32)
-        key_prev[...] = jnp.zeros_like(key_prev)
-        value_prev[...] = jnp.zeros_like(value_prev)
+        keys_all[SEG : 2 * SEG, :] = jnp.zeros((SEG, LANES), bf16)
+        values_all[SEG : 2 * SEG, :] = jnp.zeros((SEG, LANES), bf16)
         live_prev[...] = jnp.zeros_like(live_prev)
         state[...] = jnp.zeros_like(state)
+        fill_persistent(hidden, keys_all, values_all, persist_ref)
 
     low = lane_index((SEG, LANES)) < HEAD_SIZE
     ext[8 : 8 + SEG, :] = raw_ref[...].astype(f32)
     place = places(length_ref, at * SEG + lax.broadcasted_iota(jnp.int32, (SEG, 1), 0))
     place_row = places(length_ref, at * SEG + lane_index((1, SEG)))
-    pkeys, pvalues = persist_ref[0:P_SIZE, :], persist_ref[P_SIZE:, :]
     first_head = (lax.axis_index("seq") * HEAD_COUNT) // lax.axis_size("seq")
     mixed = mix_taps(ext, conv_ref, place)
     ext[0:8, :] = ext[SEG : SEG + 8, :]
     query_unit, _ = unit_pair(mixed[:, :LANES], low)
     key_unit, _ = unit_pair(mixed[:, LANES : 2 * LANES], low)
     value = mixed[:, 2 * LANES :]
-    key_now = key_unit.astype(bf16)
-    value_now = value.astype(bf16)
-    key_out[...] = key_now
-    value_out[...] = value_now
+    keys_all[0:SEG, :] = keys_all[SEG : 2 * SEG, :]
+    values_all[0:SEG, :] = values_all[SEG : 2 * SEG, :]
+    keys_all[SEG : 2 * SEG, :] = key_unit.astype(bf16)
+    values_all[SEG : 2 * SEG, :] = value.astype(bf16)
+    key_out[...] = keys_all[SEG : 2 * SEG, :]
+    value_out[...] = values_all[SEG : 2 * SEG, :]
     scan = gate_scan(heads, first_head, gate_ref[...], bias_ref, place_row, live_ref[0, 0:1, :])
     columns = write_columns(scan)
-    masks = visible_masks(place, live_prev[0:1, :], scan["live"])
+    fill_bias(hidden, place, live_prev[0:1, :], scan["live"])
+    live_prev[...] = jnp.broadcast_to(scan["live"], (8, SEG))
     older = jnp.where(place > lax.broadcasted_iota(jnp.int32, (SEG, 1), 0), 1.0, 0.0)
-    kept_prev, kept_value = key_prev[...], value_prev[...]
+    query = query_unit * SCORE_SCALE
+    key = key_unit * MEMORY_SCALE
+    queries = (query, swap_halves(query))
+    keys = (key, swap_halves(key))
+    values = (value, swap_halves(value))
+    every = range(heads)
+    owns = (low, jnp.logical_not(low))
+
+    mems, swaps = [mem_ref[head] for head in every], [swap_ref[head] for head in every]
+    states = [(state[head, 0], state[head, 1]) for head in every]
+    for head in every:
+        state_out[0, head, 0] = states[head][0].astype(bf16)
+        state_out[0, head, 1] = states[head][1].astype(bf16)
+    scores = [
+        dot_nt(jnp.where(owns[head], query, 0.0).astype(bf16), keys_all[...]) for head in every
+    ]
+    key_cuts = [jnp.where(low, keys[head], 0.0) for head in every]
+    inners = [dot_nt(key_cuts[head].astype(bf16), mems[head]) for head in every]
+    firsts = [jnp.where(low, mems[head].astype(f32), states[head][0]).astype(bf16) for head in every]
+    seconds = [
+        jnp.where(low, swaps[head].astype(f32), states[head][1]).astype(bf16) for head in every
+    ]
+    asked = [
+        jnp.where(low, queries[head], older * queries[1 - head]).astype(bf16) for head in every
+    ]
+    asked = [dot_nt(asked[head], firsts[head]) for head in every]
+    log_totals = jnp.zeros((SEG, 8), f32)
     combined = jnp.zeros((SEG, LANES), f32)
-    log_totals = jnp.zeros((SEG, 8), f32)
-    for head in range(heads):
-        own = low if head == 0 else jnp.logical_not(low)
-        query = jnp.where(own, query_unit, 0.0).astype(bf16)
-        fixed, prev, now = layer_scores(query, kept_prev, key_now, pkeys, masks)
-        highest = jnp.maximum(
-            jnp.max(fixed, axis=1, keepdims=True),
-            jnp.maximum(
-                jnp.max(prev, axis=1, keepdims=True), jnp.max(now, axis=1, keepdims=True)
-            ),
-        )
-        fixed, prev, now = (jnp.exp(member - highest) for member in (fixed, prev, now))
-        summed = lane_sum(fixed) + lane_sum(prev + now)
-        inverse = 1.0 / summed
-        attended = dot_nn((prev * inverse).astype(bf16), kept_value)
-        attended = attended + dot_nn((now * inverse).astype(bf16), value_now)
-        attended = attended + dot_nn((fixed * inverse).astype(bf16), pvalues)
+    attended = []
+    for head in every:
+        shown = scores[head] + hidden[...]
+        highest = jnp.max(shown[:, 2 * SEG :], axis=1, keepdims=True)
+        highest = jnp.maximum(highest, LEAST_SHIFT)
+        weights = jnp.exp(shown - highest)
+        summed = lane_sum(weights)
+        attended.append(dot_nn(weights.astype(bf16), values_all[...]) * (1.0 / summed))
         log_totals = jnp.where(lane_index((SEG, 8)) == head, highest + jnp.log(summed), log_totals)
-
-        key_low = to_low(key_unit, head) * MEMORY_SCALE
-        value_low = to_low(value, head)
-        query_low = to_low(query_unit, head) * MEMORY_SCALE
-        mem, swap = mem_ref[head], swap_ref[head]
-        state_one, state_two = state[head, 0], state[head, 1]
-        state_out[0, head, 0] = state_one.astype(bf16)
-        state_out[0, head, 1] = state_two.astype(bf16)
-
-        first = jnp.where(low, mem.astype(f32), state_one).astype(bf16)
-        second = jnp.where(low, swap.astype(f32), state_two).astype(bf16)
-        asked = jnp.where(low, query_low, older * swap_halves(query_low)).astype(bf16)
-        inner = dot_nt(asked, first)
-        answer = dot_nn((inner * jax.nn.sigmoid(inner)).astype(bf16), second)
-        recalled = jnp.where(low, answer, 0.0) + jnp.where(low, older * swap_halves(answer), 0.0)
-        if head:
-            recalled = swap_halves(recalled)
-        combined = combined + jnp.where(own, attended, 0.0) + recalled
-
-        key_cut = jnp.where(low, key_low, 0.0)
-        inner = dot_nt(key_cut.astype(bf16), mem)
-        sigmoid = jax.nn.sigmoid(inner)
-        active = inner * sigmoid
-        slope = sigmoid * (1.0 + inner - active)
-        active = active.astype(bf16)
-        error = jnp.where(low, dot_nn(active, swap) - value_low, 0.0)
-        descent = (dot_nt(error.astype(bf16), swap) * slope).astype(bf16)
+    total_out[...] = log_totals
+    actives, slopes = [], []
+    for head in every:
+        _, _, active, slope = half_swish(inners[head])
+        actives.append(active.astype(bf16))
+        slopes.append(slope)
+    errors = [
+        jnp.where(low, dot_nn(actives[head], swaps[head]) - values[head], 0.0) for head in every
+    ]
+    answers = []
+    for head in every:
+        _, _, active, _ = half_swish(asked[head])
+        answers.append(dot_nn(active.astype(bf16), seconds[head]))
+    descents = [
+        (dot_nt(errors[head].astype(bf16), swaps[head]) * slopes[head]).astype(bf16)
+        for head in every
+    ]
+    for head in every:
+        answer = answers[head]
+        turned = swap_halves(answer)
+        if head == 0:
+            recalled = jnp.where(low, answer + older * turned, 0.0)
+        else:
+            recalled = jnp.where(low, 0.0, turned + older * answer)
+        combined = combined + jnp.where(owns[head], attended[head], 0.0) + recalled
+    comb_ref[...] = combined.astype(bf16)
+    for head in every:
         scale = jnp.where(low, columns[:, head : head + 1], columns[:, 8 + head : 9 + head])
-        key_scaled = ((key_cut + swap_halves(key_cut)) * scale).astype(bf16)
-        error_scaled = ((error + swap_halves(error)) * scale).astype(bf16)
+        key_scaled = (jnp.where(low, keys[head], keys[1 - head]) * scale).astype(bf16)
+        error_scaled = ((errors[head] + swap_halves(errors[head])) * scale).astype(bf16)
         factor, blend = state_factors(scan["totals"], head, low)
-        for member, old, added in (
-            (0, state_one, dot_tn(descent, key_scaled)),
-            (1, state_two, dot_tn(active, error_scaled)),
+        for member, added in (
+            (0, dot_tn(descents[head], key_scaled)),
+            (1, dot_tn(actives[head], error_scaled)),
         ):
+            old = states[head][member]
             turned = jnp.where(low, 0.0, blend * swap_halves(old))
             state[head, member] = factor * old + turned + added
-    comb_ref[...] = combined.astype(bf16)
-    total_out[...] = log_totals
-    key_prev[...] = key_now
-    value_prev[...] = value_now
-    live_prev[...] = jnp.broadcast_to(scan["live"], (8, SEG))
 
 
 def chain_rows(factor, term, start, lane):
@@ -326,7 +352,7 @@
     sent, refs = refs[:carried], refs[carried:]
     made, refs = refs[:5], refs[5:]
     got, refs = refs[:carried], refs[carried:]
-    begin, middle, finish = plan.phases(sent, got, refs[5:])
+    begin, middle, finish = plan.phases(sent, got, refs[8:])
     at, last = pl.program_id(0), pl.num_programs(0) - 1
 
     @pl.when(at == 0)
@@ -334,7 +360,7 @@
         greet_all(plan.axes, plan.kinds)
         begin()
 
-    backward_step(heads, *own, *made, *refs[:5])
+    backward_step(heads, *own, *made, *refs[:8])
 
     @pl.when(at == 1)
     def _():
@@ -375,6 +401,9 @@
     key_carry,
     value_carry,
     late,
+    keys_all,
+    values_all,
+    hidden,
 ):
     at = pl.program_id(0)
 
@@ -388,6 +417,7 @@
         key_carry[...] = jnp.zeros_like(key_carry)
         value_carry[...] = jnp.zeros_like(value_carry)
         late[...] = jnp.zeros_like(late)
+        fill_persistent(hidden, keys_all, values_all, persist_ref)
 
     low = lane_index((SEG, LANES)) < HEAD_SIZE
     ext[0:8, :] = tail_ref[8:16, :].astype(f32)
@@ -395,119 +425,151 @@
     here = (pl.num_programs(0) - 1 - at) * SEG
     place = places(length_ref, here + lax.broadcasted_iota(jnp.int32, (SEG, 1), 0))
     place_row = places(length_ref, here + lane_index((1, SEG)))
-    pkeys, pvalues = persist_ref[0:P_SIZE, :], persist_ref[P_SIZE:, :]
     first_head = (lax.axis_index("seq") * HEAD_COUNT) // lax.axis_size("seq")
     mixed = mix_taps(ext, conv_ref, place)
     query_unit, query_inverse = unit_pair(mixed[:, :LANES], low)
     key_unit, key_inverse = unit_pair(mixed[:, LANES : 2 * LANES], low)
     value = mixed[:, 2 * LANES :]
-    key_now, key_prev = key_ref[...], key_prev_ref[...]
-    value_now, value_prev = value_ref[...], value_prev_ref[...]
+    keys_all[0:SEG, :] = key_prev_ref[...]
+    values_all[0:SEG, :] = value_prev_ref[...]
+    keys_all[SEG : 2 * SEG, :] = key_ref[...]
+    values_all[SEG : 2 * SEG, :] = value_ref[...]
     scan = gate_scan(heads, first_head, gate_ref[...], bias_ref, place_row, live_ref[0, 0:1, :])
     columns = write_columns(scan)
-    masks = visible_masks(place, live_prev_ref[0, 0:1, :], scan["live"])
+    fill_bias(hidden, place, live_prev_ref[0, 0:1, :], scan["live"])
     older = jnp.where(place > lax.broadcasted_iota(jnp.int32, (SEG, 1), 0), 1.0, 0.0)
     grad = grad_ref[...].astype(f32)
+    query = query_unit * SCORE_SCALE
+    key = key_unit * MEMORY_SCALE
+    queries = (query, swap_halves(query))
+    keys = (key, swap_halves(key))
+    values = (value, swap_halves(value))
+    grads = (grad, swap_halves(grad))
+    every = range(heads)
+    owns = (low, jnp.logical_not(low))
     grad_query = jnp.zeros((SEG, LANES), f32)
     grad_key = key_carry[...]
     grad_value = value_carry[...]
-    carry_key = jnp.zeros((SEG, LANES), f32)
-    carry_value = jnp.zeros((SEG, LANES), f32)
     wide = lane_index((SEG, LANES))
     write_grads = jnp.zeros((SEG, LANES), f32)
     sublane = lax.broadcasted_iota(jnp.int32, (8, 1), 0)
     keep_start = jnp.zeros((8, 1), f32)
     mix_start = jnp.zeros((8, 1), f32)
     fade_start = jnp.zeros((8, 1), f32)
-    for head in range(heads):
-        own = low if head == 0 else jnp.logical_not(low)
-        query = jnp.where(own, query_unit, 0.0).astype(bf16)
-        grad_own = jnp.where(own, grad, 0.0).astype(bf16)
-        total = total_ref[:, head : head + 1]
-        scores = layer_scores(query, key_prev, key_now, pkeys, masks)
-        probs = [jnp.exp(member - total) for member in scores]
-        grads = [
-            dot_nt(grad_own, pvalues),
-            dot_nt(grad_own, value_prev),
-            dot_nt(grad_own, value_now),
-        ]
-        spread = lane_sum(probs[0] * grads[0]) + lane_sum(probs[1] * grads[1] + probs[2] * grads[2])
-        score_grads = [(one * (other - spread)).astype(bf16) for one, other in zip(probs, grads)]
-        probs = [member.astype(bf16) for member in probs]
-        back = dot_nn(score_grads[1], key_prev) + dot_nn(score_grads[2], key_now)
-        back = SCORE_SCALE * back + dot_nn(score_grads[0], pkeys)
-        grad_query = grad_query + jnp.where(own, back, 0.0)
-        carry_key = carry_key + SCORE_SCALE * dot_tn(score_grads[1], query)
-        grad_key = grad_key + SCORE_SCALE * dot_tn(score_grads[2], query)
-        carry_value = carry_value + dot_tn(probs[1], grad_own)
-        grad_value = grad_value + dot_tn(probs[2], grad_own)
-        dpersist_ref[0:P_SIZE, :] += dot_tn(score_grads[0], query)
-        dpersist_ref[P_SIZE:, :] += dot_tn(probs[0], grad_own)
-
-        mem, swap = mem_ref[head], swap_ref[head]
-        state_one, state_two = (state_ref[0, head, member].astype(f32) for member in range(2))
-        late_one, late_two = late[head, 0], late[head, 1]
-
-        query_low = to_low(query_unit, head) * MEMORY_SCALE
-        grad_low = to_low(grad, head)
-        first = jnp.where(low, mem.astype(f32), state_one).astype(bf16)
-        second = jnp.where(low, swap.astype(f32), state_two).astype(bf16)
-        asked = jnp.where(low, query_low, older * swap_halves(query_low)).astype(bf16)
-        told = jnp.where(low, grad_low, older * swap_halves(grad_low)).astype(bf16)
-        inner = dot_nt(asked, first)
-        sigmoid = jax.nn.sigmoid(inner)
-        active = inner * sigmoid
-        slope = sigmoid * (1.0 + inner - active)
-        grad_inner = (dot_nt(told, second) * slope).astype(bf16)
-        back = dot_nn(grad_inner, first)
-        back = jnp.where(low, MEMORY_SCALE * (back + older * swap_halves(back)), 0.0)
-        grad_query = grad_query + (back if head == 0 else swap_halves(back))
-        read_one = dot_tn(grad_inner, asked)
-        read_two = dot_tn(active.astype(bf16), told)
-
-        key_low = to_low(key_unit, head) * MEMORY_SCALE
-        key_cut = jnp.where(low, key_low, 0.0)
-        key_bf = key_cut.astype(bf16)
-        inner = dot_nt(key_bf, mem)
-        sigmoid = jax.nn.sigmoid(inner)
-        active = inner * sigmoid
-        slope = sigmoid * (1.0 + inner - active)
-        curve = sigmoid * (1.0 - sigmoid) * (2.0 + inner - 2.0 * active)
-        active = active.astype(bf16)
-        error = jnp.where(low, dot_nn(active, swap) - to_low(value, head), 0.0)
-        error_bf = error.astype(bf16)
-        pulled = dot_nt(error_bf, swap)
-        descent = (pulled * slope).astype(bf16)
-        scale = jnp.where(low, columns[:, head : head + 1], columns[:, 8 + head : 9 + head])
-        key_twice = key_cut + swap_halves(key_cut)
-        error_twice = error + swap_halves(error)
-        key_scaled = (key_twice * scale).astype(bf16)
-        error_scaled = (error_twice * scale).astype(bf16)
-        late_one_bf, late_two_bf = late_one.astype(bf16), late_two.astype(bf16)
-        grad_descent = dot_nt(key_scaled, late_one_bf)
-        back_key = dot_nn(descent, late_one_bf)
-        back_error = dot_nn(active, late_two_bf)
-        weight_grad = key_twice * back_key + error_twice * back_error
+
+    query_own = [jnp.where(owns[head], query, 0.0).astype(bf16) for head in every]
+    grad_own = [jnp.where(owns[head], grad, 0.0).astype(bf16) for head in every]
+    scores = [dot_nt(query_own[head], keys_all[...]) for head in every]
+    prob_grads = [dot_nt(grad_own[head], values_all[...]) for head in every]
+    probs, score_grads = [], []
+    for head in every:
+        prob = jnp.exp(scores[head] + hidden[...] - total_ref[:, head : head + 1])
+        spread = lane_sum(prob * prob_grads[head])
+        score_grads.append((prob * (prob_grads[head] - spread)).astype(bf16))
+        probs.append(prob.astype(bf16))
+    back_keys = dot_tn(score_grads[0], query_own[0])
+    back_values = dot_tn(probs[0], grad_own[0])
+    for head in every[1:]:
+        back_keys = back_keys + dot_tn(score_grads[head], query_own[head])
+        back_values = back_values + dot_tn(probs[head], grad_own[head])
+    for head in every:
+        back = dot_nn(score_grads[head], keys_all[...])
+        grad_query = grad_query + jnp.where(owns[head], SCORE_SCALE * back, 0.0)
+    key_carry[...] = back_keys[0:SEG]
+    value_carry[...] = back_values[0:SEG]
+    grad_key = grad_key + back_keys[SEG : 2 * SEG]
+    grad_value = grad_value + back_values[SEG : 2 * SEG]
+    back_pkeys = back_keys[2 * SEG : 2 * SEG + P_SIZE] * (1.0 / SCORE_SCALE)
+    dpersist_ref[0:P_SIZE, :] += back_pkeys
+    dpersist_ref[P_SIZE:, :] += back_values[2 * SEG : 2 * SEG + P_SIZE]
+
+    mems, swaps = [mem_ref[head] for head in every], [swap_ref[head] for head in every]
+    states = [[state_ref[0, head, member].astype(f32) for member in range(2)] for head in every]
+    lates = [[late[head, member] for member in range(2)] for head in every]
+    firsts = [jnp.where(low, mems[head].astype(f32), states[head][0]).astype(bf16) for head in every]
+    seconds = [
+        jnp.where(low, swaps[head].astype(f32), states[head][1]).astype(bf16) for head in every
+    ]
+    asked = [
+        jnp.where(low, queries[head], older * queries[1 - head]).astype(bf16) for head in every
+    ]
+    told = [jnp.where(low, grads[head], older * grads[1 - head]).astype(bf16) for head in every]
+    key_bfs = [jnp.where(low, keys[head], 0.0).astype(bf16) for head in every]
+    read_inners = [dot_nt(asked[head], firsts[head]) for head in every]
+    read_grads = [dot_nt(told[head], seconds[head]) for head in every]
+    inners = [dot_nt(key_bfs[head], mems[head]) for head in every]
+    key_twices = [jnp.where(low, keys[head], keys[1 - head]) for head in every]
+    scales = [
+        jnp.where(low, columns[:, head : head + 1], columns[:, 8 + head : 9 + head])
+        for head in every
+    ]
+    late_bfs = [[member.astype(bf16) for member in lates[head]] for head in every]
+    key_scaled = [(key_twices[head] * scales[head]).astype(bf16) for head in every]
+    grad_descents = [dot_nt(key_scaled[head], late_bfs[head][0]) for head in every]
+    read_backs, reads = [], []
+    for head in every:
+        _, _, active, slope = half_swish(read_inners[head])
+        grad_inner = (read_grads[head] * slope).astype(bf16)
+        read_backs.append(dot_nn(grad_inner, firsts[head]))
+        reads.append((dot_tn(grad_inner, asked[head]), dot_tn(active.astype(bf16), told[head])))
+    actives, slopes, curves = [], [], []
+    for head in every:
+        turn, _, active, slope = half_swish(inners[head])
+        actives.append(active.astype(bf16))
+        slopes.append(slope)
+        curves.append(0.5 - turn * (slope - 0.5))
+    errors = [
+        jnp.where(low, dot_nn(actives[head], swaps[head]) - values[head], 0.0) for head in every
+    ]
+    error_bfs = [error.astype(bf16) for error in errors]
+    pulled = [dot_nt(error_bfs[head], swaps[head]) for head in every]
+    active_backs = [dot_nn(actives[head], late_bfs[head][1]) for head in every]
+    for head in every:
+        back = read_backs[head]
+        turned = swap_halves(back)
+        if head == 0:
+            back = jnp.where(low, MEMORY_SCALE * (back + older * turned), 0.0)
+        else:
+            back = jnp.where(low, 0.0, MEMORY_SCALE * (turned + older * back))
+        grad_query = grad_query + back
+    descents = [(pulled[head] * slopes[head]).astype(bf16) for head in every]
+    grad_pulled = [(grad_descents[head] * slopes[head]).astype(bf16) for head in every]
+    curved = [grad_descents[head] * pulled[head] * curves[head] for head in every]
+    back_keys = [dot_nn(descents[head], late_bfs[head][0]) for head in every]
+    pulled_backs = [dot_nn(grad_pulled[head], swaps[head]) for head in every]
+    error_twices = [errors[head] + swap_halves(errors[head]) for head in every]
+    error_scaled = [(error_twices[head] * scales[head]).astype(bf16) for head in every]
+    error_backs = []
+    for head in every:
+        weight_grad = key_twices[head] * back_keys[head] + error_twices[head] * active_backs[head]
         grad_state_weight = lane_sum(jnp.where(low, weight_grad, 0.0))
         grad_write_weight = lane_sum(jnp.where(low, 0.0, weight_grad))
         write_grads = jnp.where(wide == head, grad_state_weight, write_grads)
         write_grads = jnp.where(wide == 8 + head, grad_write_weight, write_grads)
-        grad_pulled = (grad_descent * slope).astype(bf16)
-        back_error = back_error * scale
-        back_error = back_error + swap_halves(back_error) + dot_nn(grad_pulled, swap)
-        back_error = jnp.where(low, back_error, 0.0)
-        back_error_bf = back_error.astype(bf16)
-        grad_active = dot_nt(error_scaled, late_two_bf) + dot_nt(back_error_bf, swap)
-        grad_inner = (grad_descent * pulled * curve + grad_active * slope).astype(bf16)
-        back_key = back_key * scale
-        back_key = back_key + swap_halves(back_key) + dot_nn(grad_inner, mem)
-        back_key = jnp.where(low, MEMORY_SCALE * back_key, 0.0)
-        grad_key = grad_key + (back_key if head == 0 else swap_halves(back_key))
-        grad_value = grad_value - (back_error if head == 0 else swap_halves(back_error))
-        write_one = dot_tn(grad_inner, key_bf)
-        write_two = dot_tn(grad_pulled, error_bf) + dot_tn(active, back_error_bf)
+        back = active_backs[head] * scales[head]
+        back = jnp.where(low, back + swap_halves(back) + pulled_backs[head], 0.0)
+        error_backs.append(back)
+        grad_value = grad_value - (back if head == 0 else swap_halves(back))
+    back_bfs = [back.astype(bf16) for back in error_backs]
+    grad_actives = [
+        dot_nt(error_scaled[head], late_bfs[head][1]) + dot_nt(back_bfs[head], swaps[head])
+        for head in every
+    ]
+    grad_inners = [
+        (curved[head] + grad_actives[head] * slopes[head]).astype(bf16) for head in every
+    ]
+    for head in every:
+        back = back_keys[head] * scales[head]
+        back = back + swap_halves(back) + dot_nn(grad_inners[head], mems[head])
+        back = jnp.where(low, MEMORY_SCALE * back, 0.0)
+        grad_key = grad_key + (back if head == 0 else swap_halves(back))
+        write_one = dot_tn(grad_inners[head], key_bfs[head])
+        write_two = dot_tn(grad_pulled[head], error_bfs[head])
+        write_two = write_two + dot_tn(actives[head], back_bfs[head])
+        read_one, read_two = reads[head]
         dmem_ref[head] += jnp.where(low, read_one + write_one, swap_halves(read_two + write_two))
 
+        (late_one, late_two), (state_one, state_two) = lates[head], states[head]
         factor, blend = state_factors(scan["totals"], head, low)
         same = late_one * state_one + late_two * state_two
         cross = late_one * swap_halves(state_one) + late_two * swap_halves(state_two)
@@ -550,8 +612,6 @@
     dbias_ref[0:1, :] += jnp.sum(gate_back, axis=0, keepdims=True)
     draw_ref[:, 3 * LANES :] = gate_back.astype(bf16)
 
-    key_carry[...] = carry_key
-    value_carry[...] = carry_value
     grad_mixed = jnp.concatenate(
         [
             unit_pair_pull(query_unit, query_inverse, grad_query, low),
@@ -574,10 +634,6 @@
             kept * ext[8 - offset : 8 - offset + SEG, :], axis=0, keepdims=True
         )
     draw_ref[:, : 3 * LANES] = back.astype(bf16)
-
-
-def block_of(shape, index):
-    return pl.BlockSpec(shape, index)
 
 
 def whole_of(array):
@@ -620,10 +676,11 @@
         + plan.shapes,
         scratch_shapes=[
             pltpu.VMEM((SEG + 8, 3 * LANES), f32),
-            pltpu.VMEM((SEG, LANES), bf16),
-            pltpu.VMEM((SEG, LANES), bf16),
+            pltpu.VMEM((2 * SEG + LANES, LANES), bf16),
+            pltpu.VMEM((2 * SEG + LANES, LANES), bf16),
             pltpu.VMEM((8, SEG), f32),
             pltpu.VMEM((heads, 2, MH, LANES), f32),
+            pltpu.VMEM((SEG, 2 * SEG + LANES), f32),
         ]
         + plan.scratch,
         compiler_params=pltpu.CompilerParams(
@@ -695,6 +752,9 @@
             pltpu.VMEM((SEG, LANES), f32),
             pltpu.VMEM((SEG, LANES), f32),
             pltpu.VMEM((heads, 2, MH, LANES), f32),
+            pltpu.VMEM((2 * SEG + LANES, LANES), bf16),
+            pltpu.VMEM((2 * SEG + LANES, LANES), bf16),
+            pltpu.VMEM((SEG, 2 * SEG + LANES), f32),
         ]
         + plan.scratch,
         compiler_params=pltpu.CompilerParams(
@@ -841,6 +901,155 @@
         else:
             self.loop(1, lambda k: self.far(self.chip_at(k), self.chip_at(k)).wait_send())
 
+class LineGather:
+    def __init__(self, lines, source, target, sems, keep=True):
+        self.lines, self.source, self.target = lines, source, target
+        self.local, self.send, self.recv = sems
+        self.keep = keep
+        self.seq, self.line = lax.axis_index("seq"), lax.axis_index("fsdp")
+
+    @staticmethod
+    def sems(lines):
+        dma = pltpu.SemaphoreType.DMA
+        return [dma((1,)), dma((lines,)), dma((lines,))]
+
+    def at(self, k):
+        return lax.rem(self.line + k, self.lines)
+
+    def copy(self, source, target, send, recv, to):
+        return pltpu.make_async_remote_copy(
+            src_ref=source,
+            dst_ref=target,
+            send_sem=send,
+            recv_sem=recv,
+            device_id=(self.seq, to),
+            device_id_type=MESH,
+        )
+
+    def own(self):
+        return pltpu.make_async_copy(self.source, self.target.at[self.line], self.local.at[0])
+
+    def far(self, i, slot):
+        source = self.source if self.keep else self.target.at[self.line]
+        return self.copy(source, self.target.at[slot], self.send.at[i], self.recv.at[slot], i)
+
+    def loop(self, body):
+        def step(k, carry):
+            body(k)
+            return carry
+
+        lax.fori_loop(1, self.lines, step, 0)
+
+    def start_one(self, k):
+        self.far(self.at(k), self.line).start()
+
+    def start(self):
+        self.loop(self.start_one)
+        if self.keep:
+            self.own().start()
+
+    def arrive(self):
+        if self.keep:
+            self.own().wait()
+        self.loop(lambda k: self.far(self.at(k), self.at(k)).wait_recv())
+
+    def finish(self):
+        self.loop(lambda k: self.far(self.at(k), self.at(k)).wait_send())
+
+
+class LineSum:
+    def __init__(self, lines, source, landed, target, sems):
+        self.lines, self.source, self.landed, self.target = lines, source, landed, target
+        self.send, self.recv, self.relay_send, self.relay_recv = sems
+        self.seq, self.line = lax.axis_index("seq"), lax.axis_index("fsdp")
+        self.relayed = lines == 4
+        self.half = source.shape[1] // 2
+
+    @staticmethod
+    def sems(lines):
+        dma = pltpu.SemaphoreType.DMA
+        return [dma((lines,)), dma((lines,)), dma((2,)), dma((2,))]
+
+    def at(self, k):
+        return lax.rem(self.line + k, self.lines)
+
+    def copy(self, source, target, send, recv, to):
+        return pltpu.make_async_remote_copy(
+            src_ref=source,
+            dst_ref=target,
+            send_sem=send,
+            recv_sem=recv,
+            device_id=(self.seq, to),
+            device_id_type=MESH,
+        )
+
+    def far(self, i, slot):
+        return self.copy(
+            self.source.at[i], self.landed.at[slot], self.send.at[i], self.recv.at[slot], i
+        )
+
+    def relay(self, part, to):
+        rows = pl.ds(part * self.half, self.half)
+        return self.copy(
+            self.source.at[self.at(2), rows],
+            self.landed.at[to, rows],
+            self.relay_send.at[part],
+            self.relay_recv.at[part],
+            to,
+        )
+
+    def loop(self, body):
+        def step(k, carry):
+            body(k)
+            return carry
+
+        lax.fori_loop(1, self.lines, step, 0)
+
+    def start(self):
+        if self.relayed:
+            self.relay(0, self.at(1)).start()
+            self.relay(1, self.at(3)).start()
+        else:
+            self.loop(lambda k: self.far(self.at(k), self.line).start())
+
+    def middle(self):
+        if not self.relayed:
+            return
+        for part, to in ((0, self.at(1)), (1, self.at(3))):
+            rows = pl.ds(part * self.half, self.half)
+            block = self.landed.at[self.line, rows]
+            send, recv = self.relay_send.at[part], self.relay_recv.at[part]
+            self.copy(block, block, send, recv, to).wait_recv()
+
+            def add(i, carry, to=to, part=part):
+                at = part * self.half + i
+                both = self.source[to, at].astype(f32) + self.landed[self.line, at].astype(f32)
+                self.source[to, at] = both.astype(bf16)
+                return carry
+
+            lax.fori_loop(0, self.half, add, 0)
+            self.far(to, self.line).start()
+
+    def others(self):
+        return (self.at(1), self.at(3)) if self.relayed else [self.at(k) for k in range(1, self.lines)]
+
+    def arrive(self):
+        for i in self.others():
+            self.far(i, i).wait_recv()
+
+    def total(self, i):
+        whole = self.source[self.line, i].astype(f32)
+        for other in self.others():
+            whole = whole + self.landed[other, i].astype(f32)
+        return whole
+
+    def finish(self):
+        for i in self.others():
+            self.far(i, i).wait_send()
+        if self.relayed:
+            self.relay(0, self.at(1)).wait_send()
+            self.relay(1, self.at(3)).wait_send()
+
 
 def exchange_phases(axes, counts, inputs, outputs, scratch):
     seqs, lines = axes
@@ -963,57 +1172,11 @@
             starts.append(start)
             direct.append((own, copy, mine, number))
 
-    relays = []
-    for source, target in zip(*groups[6]):
-        local, plane_send, plane_recv, line_send, line_recv = take(5)
-
-        def copy(i, slot, source=source, target=target, send=plane_send, recv=plane_recv):
-            return pltpu.make_async_remote_copy(
-                src_ref=source.at[i],
-                dst_ref=target.at[line, slot],
-                send_sem=send.at[i],
-                recv_sem=recv.at[slot],
-                device_id=(i, line),
-                device_id_type=MESH,
-            )
-
-        def own(source=source, target=target, local=local):
-            return pltpu.make_async_copy(source.at[seq], target.at[line, seq], local.at[0])
-
-        def onward(i, slot, target=target, send=line_send, recv=line_recv):
-            return pltpu.make_async_remote_copy(
-                src_ref=target.at[slot],
-                dst_ref=target.at[slot],
-                send_sem=send.at[i],
-                recv_sem=recv.at[slot],
-                device_id=(seq, i),
-                device_id_type=MESH,
-            )
-
-        def start(copy=copy, own=own):
-            loop(1, seqs, lambda k: copy(lax.rem(seq + k, seqs), seq).start())
-            own().start()
-
-        starts.insert(0, start)
-        relays.append((own, copy, onward))
-
     merges = []
     rows = 32
     for source, target in zip(*groups[7]):
-        landed, summed, local, line_send, line_recv, plane_send, plane_recv = take(7)
-
-        def copy(i, slot, source=source, landed=landed, send=line_send, recv=line_recv):
-            return pltpu.make_async_remote_copy(
-                src_ref=source.at[i],
-                dst_ref=landed.at[slot],
-                send_sem=send.at[i],
-                recv_sem=recv.at[slot],
-                device_id=(seq, i),
-                device_id_type=MESH,
-            )
-
-        def own(source=source, landed=landed, local=local):
-            return pltpu.make_async_copy(source.at[line], landed.at[line], local.at[0])
+        landed, summed, local, plane_send, plane_recv = take(5)
+        line_sum = LineSum(lines, source, landed, target, take(4))
 
         def onward(i, slot, summed=summed, target=target, send=plane_send, recv=plane_recv):
             return pltpu.make_async_remote_copy(
@@ -1028,12 +1191,14 @@
         def keep(summed=summed, target=target, local=local):
             return pltpu.make_async_copy(summed.at[seq], target.at[seq], local.at[0])
 
-        def start(copy=copy, own=own):
-            loop(1, lines, lambda k: copy(lax.rem(line + k, lines), line).start())
-            own().start()
-
-        starts.insert(0, start)
-        merges.append((landed, summed, own, copy, onward, keep))
+        starts.insert(0, line_sum.start)
+        merges.append((summed, line_sum, onward, keep))
+
+    line_gathers = []
+    for source, target in zip(*groups[8]):
+        gather = LineGather(lines, source, target, take(3))
+        starts.append(gather.start)
+        line_gathers.append(gather)
 
     def begin():
         for start in starts:
@@ -1058,23 +1223,16 @@
                     far_copy(q, chip).start()
 
             loop(1, chips + 1, combine)
-        for own, copy, onward in relays:
-            loop(1, seqs, lambda k, f=copy: f(lax.rem(seq + k, seqs), lax.rem(seq + k, seqs)).wait_recv())
-            own().wait()
-            loop(1, lines, lambda k, f=onward: f(lax.rem(line + k, lines), line).start())
         for gather in spread:
             gather.step(0)
             gather.step(1)
-        for landed, summed, own, copy, onward, keep in merges:
-            loop(1, lines, lambda k, f=copy: f(lax.rem(line + k, lines), lax.rem(line + k, lines)).wait_recv())
-            own().wait()
-
-            def add_up(k, landed=landed, summed=summed, onward=onward):
+        for summed, line_sum, onward, keep in merges:
+            line_sum.middle()
+            line_sum.arrive()
+
+            def add_up(k, summed=summed, line_sum=line_sum, onward=onward):
                 i = lax.rem(seq + k, seqs)
-                whole = landed[0, i].astype(f32)
-                for member in range(1, lines):
-                    whole = whole + landed[member, i].astype(f32)
-                summed[i] = whole.astype(bf16)
+                summed[i] = line_sum.total(i).astype(bf16)
 
                 @pl.when(k < seqs)
                 def _():
@@ -1084,6 +1242,8 @@
             keep().start()
 
     def finish():
+        for gather in spread:
+            gather.loop(2, gather.step)
         for own, copy, mine, number in direct:
 
             def end(k, copy=copy, mine=mine, number=number):
@@ -1093,17 +1253,10 @@
 
             loop(1, number, end)
             own().wait()
-        for own, copy, onward in relays:
-            loop(1, seqs, lambda k, f=copy: f(lax.rem(seq + k, seqs), seq).wait_send())
-
-            def end_relay(k, onward=onward):
-                i = lax.rem(line + k, lines)
-                onward(i, i).wait_recv()
-                onward(i, line).wait_send()
-
-            loop(1, lines, end_relay)
         for gather in spread:
-            gather.loop(2, gather.step)
+            gather.finish()
+        for gather in line_gathers:
+            gather.arrive()
             gather.finish()
         for source, target, pair, landed, pair_copy, far_copy in sums:
 
@@ -1123,8 +1276,8 @@
             loop(0, target.shape[0] // rows, add_all)
             loop(1, chips, lambda k, f=far_copy: f(lax.rem(chip + k, chips), chip).wait_send())
             loop(0, chips, lambda q, f=pair_copy: f(q).wait_send())
-        for landed, summed, own, copy, onward, keep in merges:
-            loop(1, lines, lambda k, f=copy: f(lax.rem(line + k, lines), line).wait_send())
+        for summed, line_sum, onward, keep in merges:
+            line_sum.finish()
 
             def end_merge(k, onward=onward):
                 i = lax.rem(seq + k, seqs)
@@ -1173,7 +1326,17 @@
     pl.semaphore_wait(barrier, met)
 
 
-KINDS = ("gathers", "planes", "to_line", "everys", "alls", "scatters", "relays", "merges")
+KINDS = (
+    "gathers",
+    "planes",
+    "to_line",
+    "everys",
+    "alls",
+    "scatters",
+    "relays",
+    "merges",
+    "line_gathers",
+)
 
 
 class Exchange:
@@ -1208,24 +1371,19 @@
                     half = pltpu.VMEM((chips,) + shape[1:], bf16)
                     scratch[kind] += [half, half] + [dma((chips,))] * 4
                     shape, dtype = shape[1:], f32
-                elif kind == "relays":
-                    scratch[kind] += [dma((1,))] + [dma((seqs,))] * 2 + [dma((lines,))] * 2
+                elif kind == "line_gathers":
+                    scratch[kind] += LineGather.sems(lines)
                     shape = (lines,) + shape
                 else:
-                    scratch[kind] += [pltpu.VMEM(shape, bf16), pltpu.VMEM(shape[1:], bf16), dma((1,))]
-                    scratch[kind] += [dma((lines,))] * 2 + [dma((seqs,))] * 2
-                    shape = shape[1:]
+                    raise ValueError(kind)
                 shapes.append(jax.ShapeDtypeStruct(shape, dtype))
                 self.in_vmem.append(kind == "scatters")
                 if kind in ("everys", "alls"):
                     kinds.add("all")
-                if kind not in ("to_line",):
-                    kinds.add("plane")
-                if kind in ("to_line", "relays", "merges"):
-                    kinds.add("line")
+                kinds.add("line" if kind in ("to_line", "line_gathers") else "plane")
         self.kinds = kinds
         self.shapes = shapes
-        order = ("scatters", "gathers", "planes", "to_line", "everys", "alls", "relays", "merges")
+        order = ("scatters", "gathers", "planes", "to_line", "everys", "alls", "line_gathers")
         self.scratch = [member for kind in order for member in scratch[kind]]
 
     def specs(self, gridded):
@@ -1251,27 +1409,10 @@
         return exchange_phases(self.axes, self.counts, inputs, outputs, scratch)
 
 
-def exchange_kernel(plan, *refs):
-    number = len(plan.arrays)
-    greet_all(plan.axes, plan.kinds)
-    for phase in plan.phases(refs[:number], refs[number : 2 * number], refs[2 * number :]):
-        phase()
-
-
-def exchange(name, collective, **arrays):
-    plan = Exchange(**arrays)
-    in_specs, out_specs = plan.specs(False)
-    return pl.pallas_call(
-        partial(exchange_kernel, plan),
-        out_shape=plan.shapes,
-        in_specs=in_specs,
-        out_specs=out_specs,
-        scratch_shapes=plan.scratch,
-        compiler_params=pltpu.CompilerParams(
-            collective_id=collective, has_side_effects=True, vmem_limit_bytes=VMEM_GRANT
-        ),
-        name=name,
-    )(*plan.arrays)
+PLANE = (0, 1, 0, 0, 0, 0, 0, 0, 0)
+TO_LINE = (0, 0, 1, 0, 0, 0, 0, 0, 0)
+
+MERGE = (0, 0, 0, 0, 0, 0, 0, 1, 0)
 
 
 def round_up(number, step):
@@ -1337,11 +1478,14 @@
     persist_out,
     live_out,
     ffn_out,
+    ffn_relayed,
     out_rows,
+    out_all,
     rows_all,
     pack,
     pack_rows,
     ffn_pack,
+    ffn_relay,
     got,
     conv_full,
     persist_full,
@@ -1355,10 +1499,17 @@
     axes = (seqs, lines)
     greet_all(axes, ("plane", "line"))
     gather = PlaneGather(seqs, token_ref, rows_all, sems[:7])
-    gather.start()
-    weights = exchange_phases(axes, (0, 0, 0, 0, 0, 0, 1, 0), [pack], [got], sems[7:12])
-    ffn = exchange_phases(axes, (0, 1, 0, 0, 0, 0, 0, 0), [ffn_pack], [ffn_out], sems[12:15])
-    outs = exchange_phases(axes, (0, 0, 1, 0, 0, 0, 0, 0), [out_ref], [out_rows], sems[15:18])
+    weights = exchange_phases(axes, PLANE, [pack], [got.at[line]], sems[7:10])
+    weights_line = LineGather(lines, None, got, sems[10:13], keep=False)
+    ffn = exchange_phases(axes, PLANE, [ffn_pack], [ffn_out], sems[13:16])
+    outs = exchange_phases(axes, TO_LINE, [out_ref], [out_rows], sems[16:19])
+    relay = exchange_phases(axes, PLANE, [ffn_relay], [ffn_relayed.at[line]], sems[19:22])
+    relay_line = LineGather(lines, None, ffn_relayed, sems[22:25], keep=False)
+    out_gather = PlaneGather(seqs, out_rows, out_all, sems[25:32])
+    for to in range(seqs):
+        ffn_relay[to] = ffn_gate_ref[:, to * sizes.slab : (to + 1) * sizes.slab]
+    relay[0]()
+    outs[0]()
 
     gate_at, mem_at, rest_at = sizes.gate_at, sizes.mem_at, sizes.rest_at
     pack_rows[...] = jnp.zeros_like(pack_rows)
@@ -1388,19 +1539,32 @@
             )
         pack[to] = pack_rows[...].astype(bf16)
     weights[0]()
+    gather.start()
+    piece = sizes.piece
     for to in range(seqs):
         columns = slice(to * sizes.slab, (to + 1) * sizes.slab)
-        piece = sizes.piece
-        ffn_pack[to, :piece, :] = ffn_gate_ref[:, columns]
-        ffn_pack[to, piece : 2 * piece, :] = ffn_up_ref[:, columns]
+        ffn_pack[to, :piece, :] = ffn_up_ref[:, columns]
         turned = jnp.transpose(ffn_down_ref[columns, :].astype(f32))
-        ffn_pack[to, 2 * piece :, :] = turned.astype(bf16)
+        ffn_pack[to, piece:, :] = turned.astype(bf16)
     ffn[0]()
-    outs[0]()
-    weights[1]()
+    relay[2]()
+    relay_line.start_one(1)
+    weights[2]()
+    weights_line.start_one(1)
+    weights_line.start_one(2)
     gather.step(0)
     gather.step(1)
-    weights[2]()
+    weights_line.start_one(3)
+    outs[2]()
+    out_gather.start()
+    for k in range(2, lines):
+        relay_line.start_one(k)
+    gather.loop(2, gather.step)
+    for k in range(4, lines):
+        weights_line.start_one(k)
+    out_gather.step(0)
+    out_gather.loop(1, out_gather.step)
+    weights_line.arrive()
 
     aligned = share % 16 == 0
     matrix = matrix_out if aligned else matrix_full
@@ -1449,11 +1613,6 @@
 
     def work(k, carry):
         q = gather.chip_at(k)
-
-        @pl.when(k > 1)
-        def _():
-            gather.step(k)
-
         both = pl.ds(2 * q, 2)
         rows = rows_all[both].reshape(2 * SEG, D).astype(f32)
         normed = (rows * norm_scale(rows) * gain).astype(bf16)
@@ -1465,8 +1624,11 @@
 
     lax.fori_loop(0, sizes.chips, work, 0)
     gather.finish()
+    out_gather.finish()
     ffn[2]()
-    outs[2]()
+    weights_line.finish()
+    relay_line.arrive()
+    relay_line.finish()
 
 
 def first_call(sizes, tokens, *operands):
@@ -1488,16 +1650,19 @@
             shape((8, 3 * LANES), f32),
             shape((2 * P_SIZE, LANES), bf16),
             shape((seqs, 8, SEG), f32),
-            shape((seqs, 3 * sizes.piece, sizes.slab), bf16),
+            shape((seqs, 2 * sizes.piece, sizes.slab), bf16),
+            shape((lines, seqs, sizes.piece, sizes.slab), bf16),
             shape((lines, sizes.share, D), bf16),
+            shape((seqs, lines, sizes.share, D), bf16),
         ],
         in_specs=[any_spec] + [vmem_spec] * 12 + [any_spec],
-        out_specs=[vmem_spec] * 10 + [any_spec] * 2,
+        out_specs=[vmem_spec] * 10 + [any_spec] * 4,
         scratch_shapes=[
             pltpu.VMEM((seqs, SEG, D), bf16),
             pltpu.VMEM((seqs, sizes.weight_rows, LANES), bf16),
             pltpu.VMEM((sizes.weight_rows, LANES), f32),
-            pltpu.VMEM((seqs, 3 * sizes.piece, sizes.slab), bf16),
+            pltpu.VMEM((seqs, 2 * sizes.piece, sizes.slab), bf16),
+            pltpu.VMEM((seqs, sizes.piece, sizes.slab), bf16),
             pltpu.VMEM((lines, seqs, sizes.weight_rows, LANES), bf16),
             pltpu.VMEM((8, 3 * D), f32),
             pltpu.VMEM((2 * P_SIZE, LANES), f32),
@@ -1505,9 +1670,13 @@
             pltpu.VMEM((8, LANES) if sizes.share % 16 == 0 else matrix_shape, f32),
         ]
         + PlaneGather.sems(seqs)
-        + [dma((1,)), dma((seqs,)), dma((seqs,)), dma((lines,)), dma((lines,))]
         + [dma((1,)), dma((seqs,)), dma((seqs,))]
-        + [dma((1,)), dma((lines,)), dma((lines,))],
+        + LineGather.sems(lines)
+        + [dma((1,)), dma((seqs,)), dma((seqs,))]
+        + [dma((1,)), dma((lines,)), dma((lines,))]
+        + [dma((1,)), dma((seqs,)), dma((seqs,))]
+        + LineGather.sems(lines)
+        + PlaneGather.sems(seqs),
         compiler_params=pltpu.CompilerParams(
             collective_id=0, has_side_effects=True, vmem_limit_bytes=VMEM_GRANT
         ),
@@ -1515,14 +1684,27 @@
     )(tokens, *operands)
 
 
-def ffn_kernel(
+def middle_kernel(
     sizes,
-    rows_ref,
+    mixed_ref,
+    token_ref,
+    cot_own_ref,
+    out_ref,
+    gain_ref,
     cot_ref,
+    gate_weight_ref,
     weight_ref,
-    sum_ref,
+    middle_ref,
+    grad_middle_ref,
+    gain_grad_ref,
+    out_grad_ref,
+    grad_mixed_ref,
     down_ref,
     grad_ref,
+    mixed_got,
+    combined,
+    rows_ref,
+    sum_ref,
     rows_all,
     other,
     pair,
@@ -1534,16 +1716,16 @@
     both_grad,
     down_grad,
     acts,
-    part,
     blocks,
     block_sem,
+    gate_sem,
     pair_send,
     pair_recv,
     back_send,
     back_recv,
     cot_sem,
     down_sem,
-    *gather_sems,
+    *sems,
 ):
     seqs, lines, chips = sizes.seqs, sizes.lines, sizes.chips
     hidden_size, slab, piece = sizes.slab * sizes.lines, sizes.slab, sizes.piece
@@ -1568,13 +1750,9 @@
             device_id_type=MESH,
         )
 
-    gather = PlaneGather(seqs, rows_ref, rows_all, gather_sems)
-
-    def order(j):
-        return jnp.where(j >= 2, 5 - j, j) if chips == 4 else j
-
-    def chip_at(j):
-        return gather.chip_at(order(j))
+    gather = PlaneGather(seqs, rows_ref, rows_all, sems[:7])
+
+    chip_at = gather.chip_at
 
     def to_pair(j):
         q, slot = chip_at(j), lax.rem(j, 2)
@@ -1584,31 +1762,50 @@
         place = (2 * q + core, line)
         return remote(pair.at[q], landed.at[slot], back_send.at[q], back_recv.at[slot], place)
 
+    resident = chips <= 4
+
     def cot_copy(j, slot):
+        if resident:
+            both = pl.ds(2 * chip_at(j), 2)
+            return pltpu.make_async_copy(cot_ref.at[both], cot_slot.at[both], cot_sem.at[j])
         return pltpu.make_async_copy(
             cot_ref.at[pl.ds(2 * chip_at(j), 2)], cot_slot.at[slot], cot_sem.at[slot]
         )
 
     def down_copy(j):
-        slot = lax.rem(j, 2)
+        slot = j % 2 if isinstance(j, int) else lax.rem(j, 2)
         return pltpu.make_async_copy(
             down_slot.at[slot], down_ref.at[pl.ds(2 * chip_at(j), 2)], down_sem.at[slot]
         )
 
-    greet_all((seqs, lines), ("plane",))
-    gather.start()
-    cot_copy(0, 0).start()
+    axes = (seqs, lines)
+    to_segments = exchange_phases(axes, PLANE, [mixed_ref], [mixed_got], sems[7:10])
+    to_heads = exchange_phases(axes, PLANE, [mixed_got], [grad_mixed_ref], sems[10:13])
+    greet_all(axes, ("plane",))
+    to_segments[0]()
+    if resident:
+        for j in range(chips):
+            cot_copy(j, 0).start()
+    else:
+        cot_copy(0, 0).start()
     slots = blocks.shape[0]
 
+    def gate_copy(f):
+        target = blocks.at[f % slots, :, pl.ds(0, piece)]
+        return pltpu.make_async_copy(gate_weight_ref.at[f], target, gate_sem.at[f % slots])
+
     def weight_copy(f):
-        return pltpu.make_async_copy(weight_ref.at[f], blocks.at[f % slots], block_sem.at[f % slots])
+        target = blocks.at[f % slots, :, pl.ds(piece, 2 * piece)]
+        return pltpu.make_async_copy(weight_ref.at[f], target, block_sem.at[f % slots])
 
     def grad_copy(f):
         return pltpu.make_async_copy(blocks.at[f % slots], grad_ref.at[f], block_sem.at[f % slots])
 
     for f in range(slots):
+        gate_copy(f).start()
         weight_copy(f).start()
     for f in range(lines):
+        gate_copy(f).wait()
         weight_copy(f).wait()
         columns = slice(f * slab, (f + 1) * slab)
         up_columns = slice(hidden_size + f * slab, hidden_size + (f + 1) * slab)
@@ -1618,39 +1815,54 @@
             both_matrix[rows, up_columns] = blocks[f % slots, s, piece : 2 * piece, :]
             down_matrix[rows, columns] = blocks[f % slots, s, 2 * piece :, :]
         if f + slots < lines:
+            gate_copy(f + slots).start()
             weight_copy(f + slots).start()
 
+    width, copies = sizes.width, sizes.copies
+    to_segments[2]()
+    for group in range(sizes.groups):
+        combined[:, group * width : (group + 1) * width] = mixed_got[group * copies, :, :width]
+    middle = token_ref[...].astype(f32) + dot_nn(combined[...], out_ref[...])
+    middle_ref[...] = middle
+    rows_ref[...] = (middle * norm_scale(middle) * gain_ref[5:6, :]).astype(bf16)
+    gather.start()
+
     def forth(j):
-        k, q = order(j), chip_at(j)
-        gather.step(k)
+        q = chip_at(j)
+        gather.step(j)
         cot_copy(j, lax.rem(j, 2)).wait()
 
-        @pl.when(jnp.logical_and(j > 0, j + 1 < chips))
-        def _():
-            cot_copy(j + 1, lax.rem(j + 1, 2)).start()
+        if not resident:
+
+            @pl.when(jnp.logical_and(j > 0, j + 1 < chips))
+            def _():
+                cot_copy(j + 1, lax.rem(j + 1, 2)).start()
 
         rows = rows_all[pl.ds(2 * q, 2)].reshape(2 * SEG, D)
-        cot = cot_slot[lax.rem(j, 2)].reshape(2 * SEG, D)
+        cot = cot_slot[pl.ds(2 * q, 2)] if resident else cot_slot[lax.rem(j, 2)]
+        cot = cot.reshape(2 * SEG, D)
         grad_hidden = dot_nn(cot, down_matrix[...])
         ups = dot_nn(rows, both_matrix[...])
         gate_act, up_act = ups[:, :hidden_size], ups[:, hidden_size:]
         sigmoid = jax.nn.sigmoid(gate_act)
         swish = gate_act * sigmoid
         slope = sigmoid * (1.0 + gate_act - swish)
-        acts[j, :, :hidden_size] = (grad_hidden * up_act * slope).astype(bf16)
-        acts[j, :, hidden_size : 2 * hidden_size] = (grad_hidden * swish).astype(bf16)
-        acts[j, :, 2 * hidden_size :] = (swish * up_act).astype(bf16)
-        part[...] = dot_nt(acts[j, :, : 2 * hidden_size], both_matrix[...])
+        acts[q, :, :hidden_size] = (grad_hidden * up_act * slope).astype(bf16)
+        acts[q, :, hidden_size : 2 * hidden_size] = (grad_hidden * swish).astype(bf16)
+        acts[q, :, 2 * hidden_size :] = (swish * up_act).astype(bf16)
+        theirs = acts[q, pl.ds(pl.multiple_of((1 - core) * SEG, SEG), SEG), : 2 * hidden_size]
+        theirs = dot_nt(theirs, both_matrix[...])
 
         @pl.when(j >= 2)
         def _():
             to_pair(j - 2).wait_send()
 
-        theirs = part[pl.ds(pl.multiple_of((1 - core) * SEG, SEG), SEG), :].astype(bf16)
-        other[lax.rem(j, 2)] = theirs
+        other[lax.rem(j, 2)] = theirs.astype(bf16)
         to_pair(j).start()
+        own = acts[q, pl.ds(pl.multiple_of(core * SEG, SEG), SEG), : 2 * hidden_size]
+        own = dot_nt(own, both_matrix[...])
         to_pair(j).wait_recv()
-        own = part[pl.ds(pl.multiple_of(core * SEG, SEG), SEG), :] + pair[q].astype(f32)
+        own = own + pair[q].astype(f32)
 
         @pl.when(j == 0)
         def _():
@@ -1677,12 +1889,12 @@
         def _():
             down_copy(j - 2).wait()
 
-        hidden = acts[j, :, 2 * hidden_size :]
+        hidden = acts[q, :, 2 * hidden_size :]
         down_slot[slot] = dot_nt(hidden, down_matrix[...]).astype(bf16).reshape(2, SEG, D)
         down_copy(j).start()
         rows = rows_all[pl.ds(2 * q, 2)].reshape(2 * SEG, D)
         cot = cot_slot[slot].reshape(2 * SEG, D)
-        both_new = dot_tn(rows, acts[j, :, : 2 * hidden_size])
+        both_new = dot_tn(rows, acts[q, :, : 2 * hidden_size])
         down_new = dot_tn(cot, hidden)
 
         @pl.when(j == 0)
@@ -1695,12 +1907,30 @@
             both_grad[...] += both_new
             down_grad[...] += down_new
 
-    forth(jnp.int32(0))
-    weigh(jnp.int32(0))
-    cot_copy(1, 1).start()
-    loop(1, chips, forth)
-    cot_copy(1, 1).start()
-    loop(1, chips, weigh)
+    def weigh_all():
+        rows = rows_all[...].reshape(seqs * SEG, D)
+        cot = cot_slot[...].reshape(seqs * SEG, D)
+        kept = acts[...].reshape(seqs * SEG, 3 * hidden_size)
+        both, hidden = kept[:, : 2 * hidden_size], kept[:, 2 * hidden_size :]
+        both_grad[...] = dot_tn(rows, both)
+        down_grad[...] = dot_tn(cot, hidden)
+        for j in range(chips):
+            if j >= 2:
+                down_copy(j - 2).wait()
+            back_rows = dot_nt(acts[chip_at(j), :, 2 * hidden_size :], down_matrix[...])
+            down_slot[j % 2] = back_rows.astype(bf16).reshape(2, SEG, D)
+            down_copy(j).start()
+
+    if resident:
+        loop(0, chips, forth)
+        weigh_all()
+    else:
+        forth(jnp.int32(0))
+        weigh(jnp.int32(0))
+        cot_copy(1, 1).start()
+        loop(1, chips, forth)
+        cot_copy(1, 1).start()
+        loop(1, chips, weigh)
     for f in range(lines):
         if f >= slots:
             grad_copy(f - slots).wait()
@@ -1726,47 +1956,77 @@
 
     loop(1, chips, end)
 
-
-def feed_forward(sizes, rows, cot, weights):
+    middle = middle_ref[...]
+    scale = norm_scale(middle)
+    grad = sum_ref[...]
+    gain_grad_ref[...] = jnp.sum(grad * middle * scale, axis=0, keepdims=True)
+    grad = cot_own_ref[...].astype(f32) + norm_pull(middle, scale, gain_ref[5:6, :], grad)
+    grad_middle_ref[...] = grad
+    branch = grad.astype(bf16)
+    grad_combined = dot_nt(branch, out_ref[...]).astype(bf16)
+    if width < LANES:
+        mixed_got[...] = jnp.zeros_like(mixed_got)
+    for to in range(seqs):
+        first = to // copies * width
+        mixed_got[to, :, :width] = grad_combined[:, first : first + width]
+    to_heads[0]()
+    out_grad = dot_tn(combined[...], branch).astype(bf16)
+    out_grad_ref[...] = out_grad.reshape(seqs, piece, D)
+    to_heads[2]()
+
+
+def middle_call(sizes, *operands):
     seqs, lines, chips = sizes.seqs, sizes.lines, sizes.chips
     hidden = sizes.slab * lines
     dma = pltpu.SemaphoreType.DMA
     any_spec, vmem_spec = pl.BlockSpec(memory_space=pl.ANY), pl.BlockSpec(memory_space=pltpu.VMEM)
     half = pltpu.VMEM((chips, SEG, D), bf16)
     slots = lines if lines <= 4 else 2
+    block_shape = (lines, seqs, 3 * sizes.piece, sizes.slab)
+    cot_shape = (seqs, SEG, D) if chips <= 4 else (2, 2, SEG, D)
+    shape = jax.ShapeDtypeStruct
     return pl.pallas_call(
-        partial(ffn_kernel, sizes),
+        partial(middle_kernel, sizes),
         out_shape=[
-            jax.ShapeDtypeStruct((SEG, D), f32),
-            jax.ShapeDtypeStruct((seqs, SEG, D), bf16),
-            jax.ShapeDtypeStruct(weights.shape, bf16),
+            shape((SEG, D), f32),
+            shape((SEG, D), f32),
+            shape((1, D), f32),
+            shape((seqs, sizes.piece, D), bf16),
+            shape((seqs, SEG, LANES), bf16),
+            shape((seqs, SEG, D), bf16),
+            shape(block_shape, bf16),
         ],
-        in_specs=[vmem_spec, any_spec, any_spec],
-        out_specs=[vmem_spec, any_spec, any_spec],
+        in_specs=[any_spec] + [vmem_spec] * 4 + [any_spec] * 3,
+        out_specs=[vmem_spec] * 4 + [any_spec] * 3,
         scratch_shapes=[
+            pltpu.VMEM((seqs, SEG, LANES), bf16),
+            pltpu.VMEM((SEG, D), bf16),
+            pltpu.VMEM((SEG, D), bf16),
+            pltpu.VMEM((SEG, D), f32),
             pltpu.VMEM((seqs, SEG, D), bf16),
             pltpu.VMEM((2, SEG, D), bf16),
             half,
             half,
-            pltpu.VMEM((2, 2, SEG, D), bf16),
+            pltpu.VMEM(cot_shape, bf16),
             pltpu.VMEM((2, 2, SEG, D), bf16),
             pltpu.VMEM((D, 2 * hidden), bf16),
             pltpu.VMEM((D, hidden), bf16),
             pltpu.VMEM((D, 2 * hidden), f32),
             pltpu.VMEM((D, hidden), f32),
             pltpu.VMEM((chips, 2 * SEG, 3 * hidden), bf16),
-            pltpu.VMEM((2 * SEG, D), f32),
-            pltpu.VMEM((slots,) + weights.shape[1:], bf16),
+            pltpu.VMEM((slots,) + block_shape[1:], bf16),
+            dma((slots,)),
             dma((slots,)),
         ]
         + [dma((2,)), dma((chips,)), dma((chips,)), dma((chips,))]
-        + [dma((2,)), dma((2,))]
-        + PlaneGather.sems(seqs),
+        + [dma((max(chips, 2),)), dma((2,))]
+        + PlaneGather.sems(seqs)
+        + [dma((1,)), dma((seqs,)), dma((seqs,))] * 2,
         compiler_params=pltpu.CompilerParams(
             collective_id=2, has_side_effects=True, vmem_limit_bytes=VMEM_GRANT
         ),
-        name="feed_forward",
-    )(rows, cot, weights)
+        name="middle",
+    )(*operands)
 
 
 def last_kernel(
@@ -1781,40 +2041,21 @@
     gain_two_ref,
     ffn_ref,
     out_ref,
-    token_ref,
-    middle_ref,
-    gain_ref,
-    qkv_ref,
-    gate_ref,
-    own_gain_ref,
     token_grad,
-    qkv_grad,
-    gate_grad,
-    mem_grad,
-    conv_grad,
-    persist_grad,
-    out_grad,
-    gain_one_grad,
-    gain_two_grad,
-    ffn_gate_grad,
-    ffn_up_grad,
-    ffn_down_grad,
-    bias_grad,
+    pack_got,
+    out_got,
+    persist_got,
+    ffn_got,
     normed_slot,
     matrix_grad,
     pack,
     pack_rows,
     pack_landed,
     pack_sums,
-    pack_got,
     out_blocks,
-    out_got,
-    persist_got,
-    ffn_got,
     other,
     pair,
     landed,
-    conv_full,
     normed_sem,
     pair_send,
     pair_recv,
@@ -1823,10 +2064,8 @@
     *sems,
 ):
     seqs, lines, chips = sizes.seqs, sizes.lines, sizes.chips
-    share, width, heads = sizes.share, sizes.width, sizes.heads
+    share, heads = sizes.share, sizes.heads
     seq, line = lax.axis_index("seq"), lax.axis_index("fsdp")
-    me = seq * lines + line
-    group = seq // sizes.copies
     chip, core = seq // 2, lax.rem(seq, 2)
     sibling = (2 * chip + 1 - core, line)
     side = math.isqrt(chips)
@@ -1868,12 +2107,12 @@
 
     axes = (seqs, lines)
     greet_all(axes, ("plane", "line"))
-    ffn = exchange_phases(axes, (0, 1, 0, 0, 0, 0, 0, 0), [ffn_ref], [ffn_got], sems[0:3])
+    ffn = exchange_phases(axes, PLANE, [ffn_ref], [ffn_got], sems[0:3])
     outs = exchange_phases(
-        axes, (0, 0, 2, 0, 0, 0, 0, 0), [out_blocks, persist_ref], [out_got, persist_got], sems[3:9]
+        axes, (0, 0, 2, 0, 0, 0, 0, 0, 0), [out_blocks, persist_ref], [out_got, persist_got], sems[3:9]
     )
     grads = exchange_phases(
-        axes, (0, 0, 0, 0, 0, 0, 0, 1), [pack], [pack_got], [pack_landed, pack_sums, *sems[9:14]]
+        axes, MERGE, [pack], [pack_got], [pack_landed, pack_sums, *sems[9:16]]
     )
     normed_copy(0, 0).start()
     ffn[0]()
@@ -1959,18 +2198,63 @@
         token_grad[...] += landed[q].astype(f32)
 
     loop(1, chips, add_back)
+    ffn[2]()
+    outs[2]()
+    grads[2]()
+
+    def end(k):
+        q = chip_at(k)
+        back(q, chip).wait_send()
+
+    loop(1, chips, end)
+    loop(chips - 1, chips + 1, lambda k: to_pair(k).wait_send())
+
+def unpack_kernel(
+    sizes,
+    sum_ref,
+    pack_got,
+    out_got,
+    persist_got,
+    ffn_got,
+    token_ref,
+    middle_ref,
+    gain_ref,
+    qkv_ref,
+    gate_ref,
+    own_gain_ref,
+    token_grad,
+    qkv_grad,
+    gate_grad,
+    first_grad,
+    second_grad,
+    conv_grad,
+    pkey_grad,
+    pvalue_grad,
+    out_grad,
+    gain_one_grad,
+    gain_two_grad,
+    ffn_gate_grad,
+    ffn_up_grad,
+    ffn_down_grad,
+    bias_grad,
+    conv_full,
+):
+    seqs, lines = sizes.seqs, sizes.lines
+    share, width, heads = sizes.share, sizes.width, sizes.heads
+    seq, line = lax.axis_index("seq"), lax.axis_index("fsdp")
+    me = seq * lines + line
+    group = seq // sizes.copies
+    mem_at, rest_at = sizes.grad_mem_at, sizes.grad_rest_at
     rows = token_ref[...].astype(f32)
     scale = norm_scale(rows)
-    token_grad[...] = middle_ref[...] + norm_pull(rows, scale, gain_ref[4:5, :], token_grad[...])
-
-    ffn[2]()
+    token_grad[...] = middle_ref[...] + norm_pull(rows, scale, gain_ref[4:5, :], sum_ref[...])
+
     piece, slab = sizes.piece, sizes.slab
     for s in range(seqs):
         columns = slice(s * slab, (s + 1) * slab)
         ffn_gate_grad[:, columns] = ffn_got[s, :piece, :].astype(f32)
         ffn_up_grad[:, columns] = ffn_got[s, piece : 2 * piece, :].astype(f32)
         ffn_down_grad[columns, :] = jnp.transpose(ffn_got[s, 2 * piece :, :].astype(f32))
-    outs[2]()
     out_sum = out_got[0].astype(f32)
     persist_sum = persist_got[0]
     for f in range(1, lines):
@@ -1978,9 +2262,10 @@
         persist_sum = persist_sum + persist_got[f]
     out_grad[...] = out_sum
     inside = lax.rem(LANES - (me * share - group * width), LANES)
-    persist_grad[...] = pltpu.roll(persist_sum, inside, 1)[:, :share]
-
-    grads[2]()
+    persist_sum = pltpu.roll(persist_sum, inside, 1)[:, :share]
+    pkey_grad[...] = persist_sum[:P_SIZE]
+    pvalue_grad[...] = persist_sum[P_SIZE:]
+
     gates = jnp.zeros((share, 3 * HEAD_COUNT), f32)
     bias = jnp.zeros((8, 3 * HEAD_COUNT), f32)
     gain_two = jnp.zeros((1, share), f32)
@@ -2005,22 +2290,20 @@
         bias = bias + dot_nn(rest, choice)
         for head in range(heads):
             first = mem_at + head * sizes.memory
-            mem_grad[other_group * heads + head] = block[first : first + sizes.memory]
+            member = other_group * heads + head
+            rows = block[first : first + 8]
+            second_grad[member] = rows[: sizes.memory, HEAD_SIZE:]
+            first_grad[member] = jnp.transpose(rows)[:HEAD_SIZE, : sizes.memory]
     gate_grad[...] = gates
-    bias_grad[...] = bias[4:5]
+    bias_grad[0:1, :] = 3.0 * bias[4:5, :HEAD_COUNT]
+    bias_grad[1:2, :] = bias[4:5, HEAD_COUNT : 2 * HEAD_COUNT]
+    bias_grad[2:3, :] = bias[4:5, 2 * HEAD_COUNT :]
     gain_two_grad[...] = gain_two
     along = jnp.sum(qkv_grad[...] * qkv_ref[...].astype(f32), axis=1, keepdims=True)
     along = along + jnp.sum(gates * gate_ref[...].astype(f32), axis=1, keepdims=True)
-    gain_one_grad[...] = along / own_gain_ref[...].astype(f32)
+    gain_one_grad[...] = jnp.transpose(along)[0:1] / own_gain_ref[...].astype(f32)
     turned = pltpu.roll(conv_full[...], lax.rem(3 * D - me * 3 * share, 3 * D), 1)
-    conv_grad[...] = turned[:, : 3 * share]
-
-    def end(k):
-        q = chip_at(k)
-        back(q, chip).wait_send()
-
-    loop(1, chips, end)
-    loop(chips - 1, chips + 1, lambda k: to_pair(k).wait_send())
+    conv_grad[...] = turned[:4, : 3 * share]
 
 
 def last_call(sizes, *operands):
@@ -2037,21 +2320,13 @@
         partial(last_kernel, sizes),
         out_shape=[
             shape((SEG, D), f32),
-            shape((share, 3 * D), f32),
-            shape((share, 3 * HEAD_COUNT), f32),
-            shape((HEAD_COUNT, sizes.memory, LANES), f32),
-            shape((8, 3 * share), f32),
-            shape((2 * P_SIZE, share), f32),
-            shape((share, D), f32),
-            shape((share, 1), f32),
-            shape((1, share), f32),
-            shape((sizes.piece, sizes.hidden), f32),
-            shape((sizes.piece, sizes.hidden), f32),
-            shape((sizes.hidden, sizes.piece), f32),
-            shape((1, 3 * HEAD_COUNT), f32),
+            shape(pack_shape[1:], bf16),
+            shape((lines, share, D), bf16),
+            shape((lines, 2 * P_SIZE, LANES), f32),
+            shape((seqs, 3 * sizes.piece, sizes.slab), bf16),
         ],
         in_specs=in_specs,
-        out_specs=[vmem_spec] * 13,
+        out_specs=[vmem_spec] + [any_spec] * 4,
         scratch_shapes=[
             pltpu.VMEM((2, 2, SEG, D), bf16),
             pltpu.VMEM((D, 4 * LANES), f32),
@@ -2059,21 +2334,17 @@
             pltpu.VMEM(pack_shape[2:], f32),
             pltpu.VMEM(pack_shape, bf16),
             pltpu.VMEM(pack_shape[1:], bf16),
-            pltpu.VMEM(pack_shape[1:], bf16),
             pltpu.VMEM((lines, share, D), bf16),
-            pltpu.VMEM((lines, share, D), bf16),
-            pltpu.VMEM((lines, 2 * P_SIZE, LANES), f32),
-            pltpu.VMEM((seqs, 3 * sizes.piece, sizes.slab), bf16),
             pltpu.VMEM((2, SEG, D), bf16),
             half,
             half,
-            pltpu.VMEM((8, 3 * D), f32),
             dma((2,)),
         ]
         + [dma((2,)), dma((chips,)), dma((chips,)), dma((chips,))]
         + [dma((1,)), dma((seqs,)), dma((seqs,))]
         + [dma((1,)), dma((lines,)), dma((lines,))] * 2
-        + [dma((1,)), dma((lines,)), dma((lines,)), dma((seqs,)), dma((seqs,))],
+        + [dma((1,)), dma((seqs,)), dma((seqs,))]
+        + LineSum.sems(lines),
         compiler_params=pltpu.CompilerParams(
             collective_id=5, has_side_effects=True, vmem_limit_bytes=VMEM_GRANT
         ),
@@ -2081,6 +2352,37 @@
     )(*operands)
 
 
+def unpack_call(sizes, *operands):
+    share, memory = sizes.share, sizes.memory
+    vmem_spec = pl.BlockSpec(memory_space=pltpu.VMEM)
+    shape = jax.ShapeDtypeStruct
+    return pl.pallas_call(
+        partial(unpack_kernel, sizes),
+        out_shape=[
+            shape((SEG, D), f32),
+            shape((share, 3 * D), f32),
+            shape((share, 3 * HEAD_COUNT), f32),
+            shape((HEAD_COUNT, HEAD_SIZE, memory), f32),
+            shape((HEAD_COUNT, memory, HEAD_SIZE), f32),
+            shape((4, 3 * share), f32),
+            shape((P_SIZE, share), f32),
+            shape((P_SIZE, share), f32),
+            shape((share, D), f32),
+            shape((1, share), f32),
+            shape((1, share), f32),
+            shape((sizes.piece, sizes.hidden), f32),
+            shape((sizes.piece, sizes.hidden), f32),
+            shape((sizes.hidden, sizes.piece), f32),
+            shape((3, HEAD_COUNT), f32),
+        ],
+        in_specs=[vmem_spec] * len(operands),
+        out_specs=[vmem_spec] * 15,
+        scratch_shapes=[pltpu.VMEM((8, 3 * D), f32)],
+        compiler_params=pltpu.CompilerParams(vmem_limit_bytes=VMEM_GRANT),
+        name="unpack",
+    )(*operands)
+
+
 def norm_scale(values):
     return lax.rsqrt(jnp.mean(values * values, axis=-1, keepdims=True) + NORM_EPS)
 
@@ -2088,10 +2390,6 @@
 def norm_pull(values, scale, gain, grad):
     inner = jnp.mean(grad * gain * values, axis=-1, keepdims=True)
     return scale * (grad * gain - values * (scale * scale) * inner)
-
-
-def widen(rows, width):
-    return jnp.pad(rows, [(0, 0)] * (rows.ndim - 1) + [(0, width - rows.shape[-1])])
 
 
 def on_device(
@@ -2115,8 +2413,7 @@
     cotangent,
 ):
     sizes = Sizes(lax.axis_size("seq"), lax.axis_size("fsdp"))
-    seqs, lines, groups = sizes.seqs, sizes.lines, sizes.groups
-    heads, width, share = sizes.heads, sizes.width, sizes.share
+    seqs, heads = sizes.seqs, sizes.heads
     length = seqs * SEG
     memory_pack = jnp.concatenate([memory_w1.transpose(0, 2, 1), memory_w2], axis=2)
     (
@@ -2131,7 +2428,9 @@
         persistent,
         live,
         ffn_part,
-        out_rows,
+        ffn_gates,
+        _,
+        out_matrix,
     ) = first_call(
         sizes,
         tokens[0],
@@ -2149,39 +2448,27 @@
         ffn_down,
         out_weight,
     )
-    ffn_full = lax.all_gather(ffn_part, "fsdp")
 
     constants = (taps, memory_both, memory_turned, persistent, doc_lengths, gate_bias)
     raw = raw.reshape(length, 3 * LANES)
     gates = gates.reshape(length, LANES)
-    plan = Exchange(gathers=[out_rows.reshape(lines * share, D), cotangent[0]])
-    mixed, keys, values, totals, states, out_matrix, cot_rows = mix_forward(
+    plan = Exchange(gathers=[cotangent[0]], line_gathers=[ffn_part])
+    mixed, keys, values, totals, states, cot_rows, ffn_full = mix_forward(
         6, plan, heads, raw, gates, live, *constants
     )
-    out_matrix = out_matrix.reshape(D, D)
-
-    (mixed_got,) = exchange("to_segments", 1, planes=[mixed.reshape(seqs, SEG, LANES)])
-    combined = mixed_got[:: sizes.copies, :, :width].transpose(1, 0, 2).reshape(SEG, D)
-    inputs = tokens[0].astype(f32)
-    gain_two = gains[5:6]
-    middle = inputs + jnp.dot(combined, out_matrix, preferred_element_type=f32)
-    scale_two = norm_scale(middle)
-    normed_two_own = (middle * scale_two * gain_two).astype(bf16)
-
-    grad_normed_two, down_part, ffn_grads = feed_forward(sizes, normed_two_own, cot_rows, ffn_full)
+    middle, grad_middle, grad_gain_two, grad_out, grad_mixed, down_part, ffn_grads = middle_call(
+        sizes,
+        mixed.reshape(seqs, SEG, LANES),
+        tokens[0],
+        cotangent[0],
+        out_matrix.reshape(D, D),
+        gains,
+        cot_rows,
+        ffn_gates,
+        ffn_full,
+    )
     ffn_grads = lax.psum_scatter(ffn_grads, "fsdp")
-
-    grad_middle = cotangent[0].astype(f32) + norm_pull(middle, scale_two, gain_two, grad_normed_two)
-    grad_gain_two = jnp.sum(grad_normed_two * middle * scale_two, axis=0, keepdims=True)
-    grad_branch = grad_middle.astype(bf16)
-    grad_combined = dot_nt(grad_branch, out_matrix).astype(bf16)
-    grad_out = dot_tn(combined, grad_branch).astype(bf16)
-    plan = Exchange(scatters=[down_part, grad_out.reshape(seqs, sizes.piece, D)])
-    blocks = widen(grad_combined.reshape(SEG, groups, width).transpose(1, 0, 2), LANES)
-    if sizes.copies > 1:
-        blocks = jnp.repeat(blocks, sizes.copies, axis=0)
-    (grad_mixed,) = exchange("to_heads", 4, planes=[blocks])
-
+    plan = Exchange(scatters=[down_part, grad_out])
     grad_all, grad_memory, grad_taps, grad_persistent, grad_bias, down_sum, grad_out = mix_backward(
         7,
         plan,
@@ -2197,21 +2484,7 @@
         *constants,
     )
     output = (middle + down_sum).astype(bf16)
-    (
-        input_grad,
-        grad_qkv,
-        grad_gate,
-        grad_memory,
-        grad_conv,
-        grad_persistent,
-        grad_out,
-        grad_gain_one,
-        grad_gain_two,
-        grad_ffn_gate,
-        grad_ffn_up,
-        grad_ffn_down,
-        grad_bias,
-    ) = last_call(
+    token_sum, pack_got, out_got, persist_got, ffn_got = last_call(
         sizes,
         grad_all.reshape(seqs, SEG, 4 * LANES),
         normed,
@@ -2223,30 +2496,55 @@
         grad_gain_two,
         ffn_grads,
         grad_out,
+    )
+    grads = unpack_call(
+        sizes,
+        token_sum,
+        pack_got,
+        out_got,
+        persist_got,
+        ffn_got,
         tokens[0],
         grad_middle,
         gains,
         qkv_weight,
         gate_weight,
-        norm1_gain[:, None],
+        norm1_gain[None],
     )
+    (
+        input_grad,
+        grad_qkv,
+        grad_gate,
+        grad_first,
+        grad_second,
+        grad_conv,
+        grad_pkeys,
+        grad_pvalues,
+        grad_out,
+        grad_gain_one,
+        grad_gain_two,
+        grad_ffn_gate,
+        grad_ffn_up,
+        grad_ffn_down,
+        grad_bias,
+    ) = grads
     return (
         output[None],
         input_grad[None],
-        grad_gain_one[:, 0],
+        grad_gain_one[0],
         grad_qkv,
         grad_gate,
-        grad_conv[:4],
-        grad_memory[..., :HEAD_SIZE].transpose(0, 2, 1),
-        grad_memory[..., HEAD_SIZE:],
-        grad_persistent[:P_SIZE],
-        grad_persistent[P_SIZE:],
+        grad_conv,
+        grad_first,
+        grad_second,
+        grad_pkeys,
+        grad_pvalues,
         grad_out,
         grad_gain_two[0],
         grad_ffn_gate,
         grad_ffn_up,
         grad_ffn_down,
-        grad_bias.reshape(3, HEAD_COUNT) * jnp.array([[3.0], [1.0], [1.0]], f32),
+        grad_bias,
     )
 
 

time: 357 us -> 325 us (0.910)
  local copies, waits for them, and re-layouts: 19.3 us -> 1.86 us
  other arithmetic: 10.5 us -> 3.63 us
  matrix products: 5.4 us -> 0 us
  waiting for transfers between devices: 10.4 us -> 5.79 us
    all_gather x1 -> x0, waiting for transfers between devices: 10.3 us -> none  [on_device(): ffn_full = lax.all_gather(ffn_part, 'fsdp')]
    unnamed x38 -> x3, local copies, waits for them, and re-layouts: 8.9 us -> 1.86 us
    pallas_call x1, Pallas kernels: 57.4 us -> 64.2 us  [first_call(): pl.pallas_call(partial(first_kernel, sizes), out_shape=[shape((seqs, SEG,...]
    reduce_scatter x1, waiting for transfers between devices: 0.01 us -> 5.77 us  [on_device(): ffn_grads = lax.psum_scatter(ffn_grads, 'fsdp')]
    dot_general x3 -> x0, matrix products: 5.4 us -> none  [the longest x1 2.57 us: on_device(): middle = inputs + jnp.dot(combined, out_matrix, preferred_element_type=f32)]
    slice x4 -> x0, local copies, waits for them, and re-layouts: 5.04 us -> none  [the longest x1 1.63 us: on_device(): grad_memory[..., HEAD_SIZE:]]
    pallas_call x1, Pallas kernels: 66.9 us -> 62.7 us  [mix_backward(): pl.pallas_call(partial(backward_kernel, heads, plan), grid=(count,), in_s...]
    pallas_call x3 -> x2, Pallas kernels: 77.2 us -> 77.2 us  [the longest x1 72.5 us: middle_call(): pl.pallas_call(partial(middle_kernel, sizes), out_shape=[shape((SEG, D),...]
  transfers between devices with their start and end apart: 2 -> 1, of which waited for: 1 -> 1; matrix products, arithmetic and copies ran while one was open for 5% -> 1% of each run, Pallas kernels for 36% -> 19%
where the time goes in v4:
time: 325 us; the launch traced here: 324 us
  Pallas kernels  299 us (92%)
  between operations  14.1 us (4%)
  waiting for transfers between devices  5.79 us (2%)
  other arithmetic  3.63 us (1%)
    pallas_call x1, Pallas kernels, middle_call(): pl.pallas_call(partial(middle_kernel, sizes), out_shape=[shape((SEG, D),...  72.5 us
    pallas_call x1, Pallas kernels, first_call(): pl.pallas_call(partial(first_kernel, sizes), out_shape=[shape((seqs, SEG,...  64.2 us
    pallas_call x1, Pallas kernels, mix_backward(): pl.pallas_call(partial(backward_kernel, heads, plan), grid=(count,), in_s...  62.7 us
    pallas_call x1, Pallas kernels, last_call(): pl.pallas_call(partial(last_kernel, sizes), out_shape=[shape((SEG, D), f3...  48.9 us
    pallas_call x1, Pallas kernels, mix_forward(): pl.pallas_call(partial(forward_kernel, heads, plan), grid=(count,), in_sp...  45.9 us
  transfers between devices with their start and end apart: 1, of which 1 were waited for; matrix products, arithmetic and copies ran while one was open for 1% of the time, Pallas kernels for 19%

profile of v4, /device:TPU:0, one launch (start us, length us, event | category | flops | bytes accessed | tf_op | source)
XLA Modules:
  0.0 324.4 jit_solution(9504014270337272085)
XLA Ops:
  7.2 0.0 reduce-scatter.2.cloned.1.call-start
  7.2 1.5 pad_maximum_fusion.mem_ref
  8.7 64.2 %first.1 = (bf16[8,256,1024]{2,1,0:T(8,128)(2,1)}, bf16[8,256,384]{2,1,0:T(8,128)(2,1)}, f32[8,256,128]{2,1,0:T(8,128)}, bf16[1024,512]{1,0:T(8,128)(2,1)}, bf16...) custom-call(bf16[256,1024]{1,0:T(8,128)(2,1)} %bitcast.20, ...), custom_call_target="tpu_custom_call" | custom-call | tf_op jit(solution)/shard_map/first/pallas_call | solution.py:1640
  72.9 45.9 %mix_forward.1 = (bf16[2048,128]{1,0:T(8,128)(2,1)}, bf16[2048,128]{1,0:T(8,128)(2,1)}, bf16[2048,128]{1,0:T(8,128)(2,1)}, f32[2048,8]{1,0:T(8,128)}, bf16[8,2,2...) custom-call(bf16[2048,384]{1,0:T(8,128)(2,1)} %bitcast.17, ...), custom_call_target="tpu_custom_call" | custom-call | tf_op jit(solution)/shard_map/mix_forward/pallas_call | solution.py:650
  118.9 72.5 %middle.1 = (f32[256,1024]{1,0:T(8,128)}, f32[256,1024]{1,0:T(8,128)}, f32[1,1024]{1,0:T(1,128)}, bf16[8,128,1024]{2,1,0:T(8,128)(2,1)}, bf16[8,256,128]{2,1,0:T...) custom-call(bf16[8,256,128]{2,1,0:T(8,128)(2,1)} %bitcast.31, bf16[256,1024]{1,0:T(8,128)(2,1)} %bitcast.21, ...), custom_call_target="tpu_custom_call" | custom-call | tf_op jit(solution)/shard_map/middle/pallas_call | solution.py:1988
  191.4 0.0 reduce-scatter.2.cloned.1.call-update
  191.4 0.0 copy-start
  191.4 62.7 %mix_backward.1 = (bf16[2048,512]{1,0:T(8,128)(2,1)}, f32[2,256,128]{2,1,0:T(8,128)}, f32[8,384]{1,0:T(8,128)}, f32[32,128]{1,0:T(8,128)}, f32[8,128]{1,0:T(8,12...) custom-call(bf16[2048,384]{1,0:T(8,128)(2,1)} %bitcast.18, bf16[2048,384]{1,0:T(8,128)(2,1)} %bitcast.19, ...), custom_call_target="tpu_custom_call" | custom-call | tf_op jit(solution)/shard_map/mix_backward/pallas_call | solution.py:713
  254.1 0.0 copy-done
  254.1 2.2 fusion
  256.3 5.8 %reduce-scatter.2.cloned.1.call-done = bf16[1,8,384,128]{3,2,1,0:T(8,128)(2,1)} async-done(((bf16[4,8,384,128]{3,2,1,0:T(8,128)(2,1)}), bf16[1,8,384,128]{3,2,1,0:T(8,128)(2,1)}) %reduce-scatter.2.cloned.1.call-update) | async-done | bytes 786448 | tf_op jit(solution)/shard_map/reduce_scatter | solution.py:2470
  262.1 48.9 %last.1 = (f32[256,1024]{1,0:T(8,128)}, bf16[8,160,128]{2,1,0:T(8,128)(2,1)}, bf16[4,32,1024]{2,1,0:T(8,128)(2,1)}, f32[4,32,128]{2,1,0:T(8,128)}, bf16[8,384,128]{2,1,0:T(8,128)(2,1)}) custom-call(bf16[8,256,512]{2,1,0:T(8,128)(2,1)} %bitcast.25, bf16[8,256,1024]{2,1,0:T(8,128)(2,1)} %get-tuple-element.94.normed_ref, ...), custom_call_target="tpu_custom_call" | custom-call | tf_op jit(solution)/shard_map/last/pallas_call | solution.py:2319
  311.0 4.7 %unpack.1 = (f32[256,1024]{1,0:T(8,128)}, f32[32,3072]{1,0:T(8,128)}, f32[32,48]{1,0:T(8,128)}, f32[16,64,8]{2,1,0:T(8,128)}, f32[16,8,64]{2,1,0:T(8,128)}, /*in...) custom-call(f32[256,1024]{1,0:T(8,128)} %get-tuple-element.103.sum_r, ...), custom_call_target="tpu_custom_call" | custom-call | tf_op jit(solution)/shard_map/unpack/pallas_call | solution.py:2359
  315.7 1.9 copy.34
Async XLA Ops:
  7.2 254.9 %reduce-scatter.2.cloned.1.call-start = ((), (), s32[]{:S(2)}) async-start(), calls=%async_computation.1 | async-start | bytes 3932160 | tf_op jit(solution)/shard_map/reduce_scatter | solution.py:2470
  191.4 62.8 %copy-start = (f32[256,1024]{1,0:T(8,128)S(1)}, f32[256,1024]{1,0:T(8,128)}, u32[]{:S(2)}) copy-start(f32[256,1024]{1,0:T(8,128)} %get-tuple-element.84) | copy-start | bytes 3145732
Sparse Core Ops, SparseCore 0:
  191.5 70.5 reduce-scatter.1

commit v5 on v4

--- a/solution.py
+++ b/solution.py
@@ -176,32 +176,8 @@
     values_all[2 * SEG : 2 * SEG + P_SIZE, :] = persist_ref[P_SIZE:, :]
 
 
-def forward_kernel(heads, plan, *refs):
-    carried = len(plan.arrays)
-    own, refs = refs[:9], refs[9:]
-    sent, refs = refs[:carried], refs[carried:]
-    made, refs = refs[:5], refs[5:]
-    got, refs = refs[:carried], refs[carried:]
-    begin, middle, finish = plan.phases(sent, got, refs[6:])
-    at, last = pl.program_id(0), pl.num_programs(0) - 1
-
-    @pl.when(at == 0)
-    def _():
-        greet_all(plan.axes, plan.kinds)
-        begin()
-
-    forward_step(heads, *own, *made, *refs[:6])
-
-    @pl.when(at == (5 * last) // 8)
-    def _():
-        middle()
-
-    @pl.when(at == last)
-    def _():
-        finish()
-
-
 def forward_step(
+    at,
     heads,
     raw_ref,
     gate_ref,
@@ -224,8 +200,6 @@
     state,
     hidden,
 ):
-    at = pl.program_id(0)
-
     @pl.when(at == 0)
     def _():
         ext[0:8, :] = jnp.zeros((8, 3 * LANES), f32)
@@ -641,58 +615,6 @@
     return pl.BlockSpec(array.shape, lambda n: zeros)
 
 
-def mix_forward(collective, plan, heads, raw, gates, live, *constants):
-    length = raw.shape[0]
-    count = length // SEG
-    row_block = pl.BlockSpec((SEG, LANES), lambda n: (n, 0))
-    smem = pl.BlockSpec(memory_space=pltpu.SMEM)
-    carried_in, carried_out = plan.specs(True)
-    return pl.pallas_call(
-        partial(forward_kernel, heads, plan),
-        grid=(count,),
-        in_specs=[
-            pl.BlockSpec((SEG, 3 * LANES), lambda n: (n, 0)),
-            row_block,
-            pl.BlockSpec((1, 8, SEG), lambda n: (n, 0, 0)),
-        ]
-        + [whole_of(member) for member in constants[:4]]
-        + [smem, smem]
-        + carried_in,
-        out_specs=[
-            row_block,
-            row_block,
-            row_block,
-            pl.BlockSpec((SEG, 8), lambda n: (n, 0)),
-            pl.BlockSpec((1, heads, 2, MH, LANES), lambda n: (n, 0, 0, 0, 0)),
-        ]
-        + carried_out,
-        out_shape=[
-            jax.ShapeDtypeStruct((length, LANES), bf16),
-            jax.ShapeDtypeStruct((length, LANES), bf16),
-            jax.ShapeDtypeStruct((length, LANES), bf16),
-            jax.ShapeDtypeStruct((length, 8), f32),
-            jax.ShapeDtypeStruct((count, heads, 2, MH, LANES), bf16),
-        ]
-        + plan.shapes,
-        scratch_shapes=[
-            pltpu.VMEM((SEG + 8, 3 * LANES), f32),
-            pltpu.VMEM((2 * SEG + LANES, LANES), bf16),
-            pltpu.VMEM((2 * SEG + LANES, LANES), bf16),
-            pltpu.VMEM((8, SEG), f32),
-            pltpu.VMEM((heads, 2, MH, LANES), f32),
-            pltpu.VMEM((SEG, 2 * SEG + LANES), f32),
-        ]
-        + plan.scratch,
-        compiler_params=pltpu.CompilerParams(
-            dimension_semantics=("arbitrary",),
-            collective_id=collective,
-            has_side_effects=True,
-            vmem_limit_bytes=VMEM_GRANT,
-        ),
-        name="mix_forward",
-    )(raw, gates, live, *constants, *plan.arrays)
-
-
 def mix_backward(
     collective, plan, heads, raw, gates, live, keys, values, totals, states, grad, *constants
 ):
@@ -903,58 +825,77 @@
 
 class LineGather:
     def __init__(self, lines, source, target, sems, keep=True):
-        self.lines, self.source, self.target = lines, source, target
-        self.local, self.send, self.recv = sems
-        self.keep = keep
+        self.lines, self.source, self.target, self.keep = lines, source, target, keep
+        self.local, self.right_send, self.left_send, self.recv = sems
         self.seq, self.line = lax.axis_index("seq"), lax.axis_index("fsdp")
 
     @staticmethod
     def sems(lines):
         dma = pltpu.SemaphoreType.DMA
-        return [dma((1,)), dma((lines,)), dma((lines,))]
-
-    def at(self, k):
-        return lax.rem(self.line + k, self.lines)
-
-    def copy(self, source, target, send, recv, to):
+        return [dma((1,)), dma((lines,)), dma((lines,)), dma((lines,))]
+
+    def own(self):
+        return pltpu.make_async_copy(self.source, self.target.at[self.line], self.local.at[0])
+
+    def hop(self, block, step, own=False):
+        send = self.right_send if step > 0 else self.left_send
         return pltpu.make_async_remote_copy(
-            src_ref=source,
-            dst_ref=target,
-            send_sem=send,
-            recv_sem=recv,
-            device_id=(self.seq, to),
+            src_ref=self.source if own and self.keep else self.target.at[block],
+            dst_ref=self.target.at[block],
+            send_sem=send.at[block],
+            recv_sem=self.recv.at[block],
+            device_id=(self.seq, lax.rem(self.line + step + self.lines, self.lines)),
             device_id_type=MESH,
         )
 
-    def own(self):
-        return pltpu.make_async_copy(self.source, self.target.at[self.line], self.local.at[0])
-
-    def far(self, i, slot):
-        source = self.source if self.keep else self.target.at[self.line]
-        return self.copy(source, self.target.at[slot], self.send.at[i], self.recv.at[slot], i)
-
-    def loop(self, body):
-        def step(k, carry):
-            body(k)
-            return carry
-
-        lax.fori_loop(1, self.lines, step, 0)
-
-    def start_one(self, k):
-        self.far(self.at(k), self.line).start()
-
     def start(self):
-        self.loop(self.start_one)
+        @pl.when(self.line < self.lines - 1)
+        def _():
+            self.hop(self.line, 1, True).start()
+
+        @pl.when(self.line > 0)
+        def _():
+            self.hop(self.line, -1, True).start()
+
         if self.keep:
             self.own().start()
 
-    def arrive(self):
+    def round(self, distance):
+        before, after = self.line - distance, self.line + distance
+
+        @pl.when(before >= 0)
+        def _():
+            self.hop(before, 1).wait_recv()
+
+            @pl.when(self.line < self.lines - 1)
+            def _():
+                self.hop(before, 1).start()
+
+        @pl.when(after < self.lines)
+        def _():
+            self.hop(after, -1).wait_recv()
+
+            @pl.when(self.line > 0)
+            def _():
+                self.hop(after, -1).start()
+
+    def rounds(self, first=1):
+        for distance in range(first, self.lines):
+            self.round(distance)
+
+    def finish(self):
         if self.keep:
             self.own().wait()
-        self.loop(lambda k: self.far(self.at(k), self.at(k)).wait_recv())
-
-    def finish(self):
-        self.loop(lambda k: self.far(self.at(k), self.at(k)).wait_send())
+        for distance in range(self.lines):
+            before, after = self.line - distance, self.line + distance
+
+            @pl.when(jnp.logical_and(before >= 0, self.line < self.lines - 1))
+            def _(before=before):
+                self.hop(before, 1).wait_send()
+
+            @pl.when(jnp.logical_and(after < self.lines, self.line > 0))
+            def _(after=after):
+                self.hop(after, -1).wait_send()
 
 
 class LineSum:
@@ -1194,12 +1135,6 @@
         starts.insert(0, line_sum.start)
         merges.append((summed, line_sum, onward, keep))
 
-    line_gathers = []
-    for source, target in zip(*groups[8]):
-        gather = LineGather(lines, source, target, take(3))
-        starts.append(gather.start)
-        line_gathers.append(gather)
-
     def begin():
         for start in starts:
             start()
@@ -1254,9 +1189,6 @@
             loop(1, number, end)
             own().wait()
         for gather in spread:
-            gather.finish()
-        for gather in line_gathers:
-            gather.arrive()
             gather.finish()
         for source, target, pair, landed, pair_copy, far_copy in sums:
 
@@ -1335,7 +1267,6 @@
     "scatters",
     "relays",
     "merges",
-    "line_gathers",
 )
 
 
@@ -1371,19 +1302,16 @@
                     half = pltpu.VMEM((chips,) + shape[1:], bf16)
                     scratch[kind] += [half, half] + [dma((chips,))] * 4
                     shape, dtype = shape[1:], f32
-                elif kind == "line_gathers":
-                    scratch[kind] += LineGather.sems(lines)
-                    shape = (lines,) + shape
                 else:
                     raise ValueError(kind)
                 shapes.append(jax.ShapeDtypeStruct(shape, dtype))
                 self.in_vmem.append(kind == "scatters")
                 if kind in ("everys", "alls"):
                     kinds.add("all")
-                kinds.add("line" if kind in ("to_line", "line_gathers") else "plane")
+                kinds.add("line" if kind == "to_line" else "plane")
         self.kinds = kinds
         self.shapes = shapes
-        order = ("scatters", "gathers", "planes", "to_line", "everys", "alls", "line_gathers")
+        order = ("scatters", "gathers", "planes", "to_line", "everys", "alls")
         self.scratch = [member for kind in order for member in scratch[kind]]
 
     def specs(self, gridded):
@@ -1409,10 +1337,10 @@
         return exchange_phases(self.axes, self.counts, inputs, outputs, scratch)
 
 
-PLANE = (0, 1, 0, 0, 0, 0, 0, 0, 0)
-TO_LINE = (0, 0, 1, 0, 0, 0, 0, 0, 0)
-
-MERGE = (0, 0, 0, 0, 0, 0, 0, 1, 0)
+PLANE = (0, 1, 0, 0, 0, 0, 0, 0)
+TO_LINE = (0, 0, 1, 0, 0, 0, 0, 0)
+
+MERGE = (0, 0, 0, 0, 0, 0, 0, 1)
 
 
 def round_up(number, step):
@@ -1467,7 +1395,9 @@
     ffn_up_ref,
     ffn_down_ref,
     out_ref,
-    normed_out,
+    cot_ref,
+    length_ref,
+    bias_ref,
     raw_out,
     gate_out,
     matrix_out,
@@ -1477,10 +1407,18 @@
     taps_out,
     persist_out,
     live_out,
+    mixed_out,
+    key_out,
+    value_out,
+    total_out,
+    state_out,
+    normed_out,
     ffn_out,
+    ffn_rest,
     ffn_relayed,
     out_rows,
     out_all,
+    cot_all,
     rows_all,
     pack,
     pack_rows,
@@ -1491,6 +1429,13 @@
     persist_full,
     mem_full,
     matrix_full,
+    ext,
+    keys_all,
+    values_all,
+    live_prev,
+    state,
+    hidden,
+    normed_sem,
     *sems,
 ):
     seqs, lines, share, width = sizes.seqs, sizes.lines, sizes.share, sizes.width
@@ -1500,12 +1445,15 @@
     greet_all(axes, ("plane", "line"))
     gather = PlaneGather(seqs, token_ref, rows_all, sems[:7])
     weights = exchange_phases(axes, PLANE, [pack], [got.at[line]], sems[7:10])
-    weights_line = LineGather(lines, None, got, sems[10:13], keep=False)
-    ffn = exchange_phases(axes, PLANE, [ffn_pack], [ffn_out], sems[13:16])
-    outs = exchange_phases(axes, TO_LINE, [out_ref], [out_rows], sems[16:19])
-    relay = exchange_phases(axes, PLANE, [ffn_relay], [ffn_relayed.at[line]], sems[19:22])
-    relay_line = LineGather(lines, None, ffn_relayed, sems[22:25], keep=False)
-    out_gather = PlaneGather(seqs, out_rows, out_all, sems[25:32])
+    weights_line = LineGather(lines, None, got, sems[10:14], keep=False)
+    ffn = exchange_phases(axes, PLANE, [ffn_pack], [ffn_out], sems[14:17])
+    outs = exchange_phases(axes, TO_LINE, [out_ref], [out_rows], sems[17:20])
+    relay = exchange_phases(axes, PLANE, [ffn_relay], [ffn_relayed.at[line]], sems[20:23])
+    relay_line = LineGather(lines, None, ffn_relayed, sems[23:27], keep=False)
+    out_gather = PlaneGather(seqs, out_rows, out_all, sems[27:34])
+    cot_gather = PlaneGather(seqs, cot_ref, cot_all, sems[34:41])
+    piece = sizes.piece
+    rest_line = LineGather(lines, ffn_out, ffn_rest, sems[41:45])
     for to in range(seqs):
         ffn_relay[to] = ffn_gate_ref[:, to * sizes.slab : (to + 1) * sizes.slab]
     relay[0]()
@@ -1540,31 +1488,26 @@
         pack[to] = pack_rows[...].astype(bf16)
     weights[0]()
     gather.start()
-    piece = sizes.piece
     for to in range(seqs):
         columns = slice(to * sizes.slab, (to + 1) * sizes.slab)
         ffn_pack[to, :piece, :] = ffn_up_ref[:, columns]
         turned = jnp.transpose(ffn_down_ref[columns, :].astype(f32))
         ffn_pack[to, piece:, :] = turned.astype(bf16)
     ffn[0]()
-    relay[2]()
-    relay_line.start_one(1)
     weights[2]()
-    weights_line.start_one(1)
-    weights_line.start_one(2)
+    weights_line.start()
     gather.step(0)
     gather.step(1)
-    weights_line.start_one(3)
+    weights_line.round(1)
     outs[2]()
     out_gather.start()
-    for k in range(2, lines):
-        relay_line.start_one(k)
     gather.loop(2, gather.step)
-    for k in range(4, lines):
-        weights_line.start_one(k)
-    out_gather.step(0)
-    out_gather.loop(1, out_gather.step)
-    weights_line.arrive()
+    weights_line.rounds(2)
+    relay[2]()
+    relay_line.start()
+    cot_gather.start()
+    ffn[2]()
+    rest_line.start()
 
     aligned = share % 16 == 0
     matrix = matrix_out if aligned else matrix_full
@@ -1610,53 +1553,121 @@
         live_out[s, 0:1, LANES:] = block[rest_at + 7 : rest_at + 8]
 
     gain = gain_out[4:5, :]
-
-    def work(k, carry):
-        q = gather.chip_at(k)
+    gather.finish()
+
+    def normed_copy(q):
+        both = pl.ds(2 * q, 2)
+        return pltpu.make_async_copy(rows_all.at[both], normed_out.at[both], normed_sem.at[q])
+
+    def work(q, carry):
         both = pl.ds(2 * q, 2)
         rows = rows_all[both].reshape(2 * SEG, D).astype(f32)
         normed = (rows * norm_scale(rows) * gain).astype(bf16)
         projected = dot_nn(normed, matrix_out[...])
-        normed_out[both] = normed.reshape(2, SEG, D)
+        rows_all[both] = normed.reshape(2, SEG, D)
+        normed_copy(q).start()
         raw_out[both] = projected[:, : 3 * LANES].astype(bf16).reshape(2, SEG, 3 * LANES)
         gate_out[both] = projected[:, 3 * LANES :].reshape(2, SEG, LANES)
         return carry
 
     lax.fori_loop(0, sizes.chips, work, 0)
-    gather.finish()
+
+    def segment(n, carry):
+        @pl.when(n == 1)
+        def _():
+            relay_line.round(1)
+
+        @pl.when(n == 2)
+        def _():
+            out_gather.step(0)
+            out_gather.step(1)
+            cot_gather.step(0)
+            cot_gather.step(1)
+
+        @pl.when(n == 3)
+        def _():
+            relay_line.round(2)
+
+        @pl.when(n == 4)
+        def _():
+            rest_line.round(1)
+
+        @pl.when(n == 6)
+        def _():
+            out_gather.loop(2, out_gather.step)
+            cot_gather.loop(2, cot_gather.step)
+
+        forward_step(
+            n,
+            sizes.heads,
+            raw_out.at[n],
+            gate_out.at[n],
+            live_out.at[pl.ds(n, 1)],
+            taps_out,
+            mem_out,
+            swap_out,
+            persist_out,
+            length_ref,
+            bias_ref,
+            mixed_out.at[n],
+            key_out.at[n],
+            value_out.at[n],
+            total_out.at[n],
+            state_out.at[pl.ds(n, 1)],
+            ext,
+            keys_all,
+            values_all,
+            live_prev,
+            state,
+            hidden,
+        )
+        return carry
+
+    lax.fori_loop(0, seqs, segment, 0)
+    lax.fori_loop(0, sizes.chips, lambda q, carry: (normed_copy(q).wait(), carry)[1], 0)
     out_gather.finish()
-    ffn[2]()
+    cot_gather.finish()
     weights_line.finish()
-    relay_line.arrive()
+    relay_line.rounds(3)
+    rest_line.rounds(2)
     relay_line.finish()
-
-
-def first_call(sizes, tokens, *operands):
-    seqs, lines = sizes.seqs, sizes.lines
+    rest_line.finish()
+
+
+def first_call(sizes, *operands):
+    seqs, lines, heads = sizes.seqs, sizes.lines, sizes.heads
     dma = pltpu.SemaphoreType.DMA
     any_spec, vmem_spec = pl.BlockSpec(memory_space=pl.ANY), pl.BlockSpec(memory_space=pltpu.VMEM)
+    smem_spec = pl.BlockSpec(memory_space=pltpu.SMEM)
     shape = jax.ShapeDtypeStruct
     matrix_shape = (D, 4 * LANES)
     return pl.pallas_call(
         partial(first_kernel, sizes),
         out_shape=[
-            shape((seqs, SEG, D), bf16),
             shape((seqs, SEG, 3 * LANES), bf16),
             shape((seqs, SEG, LANES), f32),
             shape(matrix_shape, bf16),
-            shape((sizes.heads, MH, LANES), bf16),
-            shape((sizes.heads, MH, LANES), bf16),
+            shape((heads, MH, LANES), bf16),
+            shape((heads, MH, LANES), bf16),
             shape((8, D), f32),
             shape((8, 3 * LANES), f32),
             shape((2 * P_SIZE, LANES), bf16),
             shape((seqs, 8, SEG), f32),
+            shape((seqs, SEG, LANES), bf16),
+            shape((seqs, SEG, LANES), bf16),
+            shape((seqs, SEG, LANES), bf16),
+            shape((seqs, SEG, 8), f32),
+            shape((seqs, heads, 2, MH, LANES), bf16),
+            shape((seqs, SEG, D), bf16),
             shape((seqs, 2 * sizes.piece, sizes.slab), bf16),
+            shape((lines, seqs, 2 * sizes.piece, sizes.slab), bf16),
             shape((lines, seqs, sizes.piece, sizes.slab), bf16),
             shape((lines, sizes.share, D), bf16),
             shape((seqs, lines, sizes.share, D), bf16),
+            shape((seqs, SEG, D), bf16),
         ],
-        in_specs=[any_spec] + [vmem_spec] * 12 + [any_spec],
-        out_specs=[vmem_spec] * 10 + [any_spec] * 4,
+        in_specs=[any_spec] + [vmem_spec] * 12 + [any_spec] * 2 + [smem_spec] * 2,
+        out_specs=[vmem_spec] * 14 + [any_spec] * 7,
         scratch_shapes=[
             pltpu.VMEM((seqs, SEG, D), bf16),
             pltpu.VMEM((seqs, sizes.weight_rows, LANES), bf16),
@@ -1666,8 +1677,15 @@
             pltpu.VMEM((lines, seqs, sizes.weight_rows, LANES), bf16),
             pltpu.VMEM((8, 3 * D), f32),
             pltpu.VMEM((2 * P_SIZE, LANES), f32),
-            pltpu.VMEM((sizes.heads, MH, LANES), f32),
+            pltpu.VMEM((heads, MH, LANES), f32),
             pltpu.VMEM((8, LANES) if sizes.share % 16 == 0 else matrix_shape, f32),
+            pltpu.VMEM((SEG + 8, 3 * LANES), f32),
+            pltpu.VMEM((2 * SEG + LANES, LANES), bf16),
+            pltpu.VMEM((2 * SEG + LANES, LANES), bf16),
+            pltpu.VMEM((8, SEG), f32),
+            pltpu.VMEM((heads, 2, MH, LANES), f32),
+            pltpu.VMEM((SEG, 2 * SEG + LANES), f32),
+            dma((sizes.chips,)),
         ]
         + PlaneGather.sems(seqs)
         + [dma((1,)), dma((seqs,)), dma((seqs,))]
@@ -1676,12 +1694,13 @@
         + [dma((1,)), dma((lines,)), dma((lines,))]
         + [dma((1,)), dma((seqs,)), dma((seqs,))]
         + LineGather.sems(lines)
-        + PlaneGather.sems(seqs),
+        + PlaneGather.sems(seqs) * 2
+        + LineGather.sems(lines),
         compiler_params=pltpu.CompilerParams(
             collective_id=0, has_side_effects=True, vmem_limit_bytes=VMEM_GRANT
         ),
         name="first",
-    )(tokens, *operands)
+    )(*operands)
 
 
 def middle_kernel(
@@ -2109,7 +2128,7 @@
     greet_all(axes, ("plane", "line"))
     ffn = exchange_phases(axes, PLANE, [ffn_ref], [ffn_got], sems[0:3])
     outs = exchange_phases(
-        axes, (0, 0, 2, 0, 0, 0, 0, 0, 0), [out_blocks, persist_ref], [out_got, persist_got], sems[3:9]
+        axes, (0, 0, 2, 0, 0, 0, 0, 0), [out_blocks, persist_ref], [out_got, persist_got], sems[3:9]
     )
     grads = exchange_phases(
         axes, MERGE, [pack], [pack_got], [pack_landed, pack_sums, *sems[9:16]]
@@ -2222,6 +2241,9 @@
     qkv_ref,
     gate_ref,
     own_gain_ref,
+    rows_ref,
+    down_ref,
+    output_ref,
     token_grad,
     qkv_grad,
     gate_grad,
@@ -2245,6 +2267,7 @@
     me = seq * lines + line
     group = seq // sizes.copies
     mem_at, rest_at = sizes.grad_mem_at, sizes.grad_rest_at
+    output_ref[...] = (rows_ref[...] + down_ref[...]).astype(bf16)
     rows = token_ref[...].astype(f32)
     scale = norm_scale(rows)
     token_grad[...] = middle_ref[...] + norm_pull(rows, scale, gain_ref[4:5, :], sum_ref[...])
@@ -2359,6 +2382,7 @@
     return pl.pallas_call(
         partial(unpack_kernel, sizes),
         out_shape=[
+            shape((SEG, D), bf16),
             shape((SEG, D), f32),
             shape((share, 3 * D), f32),
             shape((share, 3 * HEAD_COUNT), f32),
@@ -2376,7 +2400,7 @@
             shape((3, HEAD_COUNT), f32),
         ],
         in_specs=[vmem_spec] * len(operands),
-        out_specs=[vmem_spec] * 15,
+        out_specs=[vmem_spec] * 16,
         scratch_shapes=[pltpu.VMEM((8, 3 * D), f32)],
         compiler_params=pltpu.CompilerParams(vmem_limit_bytes=VMEM_GRANT),
         name="unpack",
@@ -2417,7 +2441,6 @@
     length = seqs * SEG
     memory_pack = jnp.concatenate([memory_w1.transpose(0, 2, 1), memory_w2], axis=2)
     (
-        normed,
         raw,
         gates,
         matrix,
@@ -2427,10 +2450,18 @@
         taps,
         persistent,
         live,
-        ffn_part,
+        mixed,
+        keys,
+        values,
+        totals,
+        states,
+        normed,
+        _,
+        ffn_rest,
         ffn_gates,
         _,
         out_matrix,
+        cot_rows,
     ) = first_call(
         sizes,
         tokens[0],
@@ -2447,25 +2478,21 @@
         ffn_up,
         ffn_down,
         out_weight,
+        cotangent[0],
+        doc_lengths,
+        gate_bias,
     )
-
     constants = (taps, memory_both, memory_turned, persistent, doc_lengths, gate_bias)
-    raw = raw.reshape(length, 3 * LANES)
-    gates = gates.reshape(length, LANES)
-    plan = Exchange(gathers=[cotangent[0]], line_gathers=[ffn_part])
-    mixed, keys, values, totals, states, cot_rows, ffn_full = mix_forward(
-        6, plan, heads, raw, gates, live, *constants
-    )
     middle, grad_middle, grad_gain_two, grad_out, grad_mixed, down_part, ffn_grads = middle_call(
         sizes,
-        mixed.reshape(seqs, SEG, LANES),
+        mixed,
         tokens[0],
         cotangent[0],
         out_matrix.reshape(D, D),
         gains,
         cot_rows,
         ffn_gates,
-        ffn_full,
+        ffn_rest,
     )
     ffn_grads = lax.psum_scatter(ffn_grads, "fsdp")
     plan = Exchange(scatters=[down_part, grad_out])
@@ -2473,17 +2500,16 @@
         7,
         plan,
         heads,
-        raw,
-        gates,
+        raw.reshape(length, 3 * LANES),
+        gates.reshape(length, LANES),
         live,
-        keys,
-        values,
-        totals,
+        keys.reshape(length, LANES),
+        values.reshape(length, LANES),
+        totals.reshape(length, 8),
         states,
         grad_mixed.reshape(length, LANES),
         *constants,
     )
-    output = (middle + down_sum).astype(bf16)
     token_sum, pack_got, out_got, persist_got, ffn_got = last_call(
         sizes,
         grad_all.reshape(seqs, SEG, 4 * LANES),
@@ -2510,8 +2536,11 @@
         qkv_weight,
         gate_weight,
         norm1_gain[None],
+        middle,
+        down_sum,
     )
     (
+        output,
         input_grad,
         grad_qkv,
         grad_gate,

time: 325 us -> 305 us (0.938)
  Pallas kernels: 299 us -> 287 us
  waiting for transfers between devices: 5.79 us -> 0.04 us
    pallas_call x1 -> x0, Pallas kernels: 45.9 us -> none  [mix_forward(): pl.pallas_call(partial(forward_kernel, heads, plan), grid=(count,), in_sp...]
    pallas_call x1, Pallas kernels: 64.2 us -> 102 us  [first_call(): pl.pallas_call(partial(first_kernel, sizes), out_shape=[shape((seqs, SEG,...]
    reduce_scatter x1, waiting for transfers between devices: 5.77 us -> 0.02 us  [on_device(): ffn_grads = lax.psum_scatter(ffn_grads, 'fsdp')]
    pallas_call x1, Pallas kernels: 48.9 us -> 44.6 us  [last_call(): pl.pallas_call(partial(last_kernel, sizes), out_shape=[shape((SEG, D), f3...]
  transfers between devices with their start and end apart: 1 -> 1, of which waited for: 1 -> 0; matrix products, arithmetic and copies ran while one was open for 1% -> 0% of each run, Pallas kernels for 19% -> 20%
where the time goes in v5:
time: 305 us
  Pallas kernels  287 us (94%)
  between operations  14.1 us (5%)
    pallas_call x1, Pallas kernels, first_call(): pl.pallas_call(partial(first_kernel, sizes), out_shape=[shape((seqs, SEG,...  102 us
    pallas_call x1, Pallas kernels, middle_call(): pl.pallas_call(partial(middle_kernel, sizes), out_shape=[shape((SEG, D),...  73.1 us
    pallas_call x1, Pallas kernels, mix_backward(): pl.pallas_call(partial(backward_kernel, heads, plan), grid=(count,), in_s...  61.9 us
    pallas_call x1, Pallas kernels, last_call(): pl.pallas_call(partial(last_kernel, sizes), out_shape=[shape((SEG, D), f3...  44.6 us
  transfers between devices with their start and end apart: 1, of which 0 were waited for; matrix products, arithmetic and copies ran while one was open for 0% of the time, Pallas kernels for 20%

profile of v5, /device:TPU:0, one launch (start us, length us, event | category | flops | bytes accessed | tf_op | source)
XLA Modules:
  0.0 304.6 jit_solution(10391326418245276226)
XLA Ops:
  7.2 0.0 reduce-scatter.2.cloned.1.call-start
  7.2 1.5 pad_maximum_fusion.mem_ref
  8.7 101.9 %first.1 = (bf16[8,256,384]{2,1,0:T(8,128)(2,1)}, f32[8,256,128]{2,1,0:T(8,128)}, bf16[1024,512]{1,0:T(8,128)(2,1)}, bf16[2,256,128]{2,1,0:T(8,128)(2,1)}, bf16[...) custom-call(bf16[256,1024]{1,0:T(8,128)(2,1)} %bitcast.20, ...), custom_call_target="tpu_custom_call" | custom-call | tf_op jit(solution)/shard_map/first/pallas_call | solution.py:1644
  110.6 73.1 %middle.1 = (f32[256,1024]{1,0:T(8,128)}, f32[256,1024]{1,0:T(8,128)}, f32[1,1024]{1,0:T(1,128)}, bf16[8,128,1024]{2,1,0:T(8,128)(2,1)}, bf16[8,256,128]{2,1,0:T...) custom-call(bf16[8,256,128]{2,1,0:T(8,128)(2,1)} %get-tuple-element.77.mixed_ref, ...), custom_call_target="tpu_custom_call" | custom-call | tf_op jit(solution)/shard_map/middle/pallas_call | solution.py:2007
  183.7 0.0 reduce-scatter.2.cloned.1.call-update
  183.8 61.9 %mix_backward.1 = (bf16[2048,512]{1,0:T(8,128)(2,1)}, f32[2,256,128]{2,1,0:T(8,128)}, f32[8,384]{1,0:T(8,128)}, f32[32,128]{1,0:T(8,128)}, f32[8,128]{1,0:T(8,12...) custom-call(bf16[2048,384]{1,0:T(8,128)(2,1)} %bitcast.18, bf16[2048,384]{1,0:T(8,128)(2,1)} %bitcast.19, ...), custom_call_target="tpu_custom_call" | custom-call | tf_op jit(solution)/shard_map/mix_backward/pallas_call | solution.py:635
  245.7 0.0 reduce-scatter.2.cloned.1.call-done
  245.7 44.6 %last.1 = (f32[256,1024]{1,0:T(8,128)}, bf16[8,160,128]{2,1,0:T(8,128)(2,1)}, bf16[4,32,1024]{2,1,0:T(8,128)(2,1)}, f32[4,32,128]{2,1,0:T(8,128)}, bf16[8,384,128]{2,1,0:T(8,128)(2,1)}) custom-call(bf16[8,256,512]{2,1,0:T(8,128)(2,1)} %bitcast.27, bf16[8,256,1024]{2,1,0:T(8,128)(2,1)} %get-tuple-element.91.normed_ref, ...), custom_call_target="tpu_custom_call" | custom-call | tf_op jit(solution)/shard_map/last/pallas_call | solution.py:2342
  290.3 5.6 %unpack.1 = (bf16[256,1024]{1,0:T(8,128)(2,1)}, f32[256,1024]{1,0:T(8,128)}, f32[32,3072]{1,0:T(8,128)}, f32[32,48]{1,0:T(8,128)}, f32[16,64,8]{2,1,0:T(8,128)},...) custom-call(f32[256,1024]{1,0:T(8,128)} %get-tuple-element.100.sum_r, ...), custom_call_target="tpu_custom_call" | custom-call | tf_op jit(solution)/shard_map/unpack/pallas_call | solution.py:2382
  295.9 1.9 copy.34
Async XLA Ops:
  7.2 238.5 %reduce-scatter.2.cloned.1.call-start = ((), (), s32[]{:S(2)}) async-start(), calls=%async_computation.1 | async-start | bytes 3932160 | tf_op jit(solution)/shard_map/reduce_scatter | solution.py:2497
Sparse Core Ops, SparseCore 0:
  183.9 59.8 reduce-scatter.1

commit v6 on v5

--- a/solution.py
+++ b/solution.py
@@ -1390,7 +1390,8 @@
     gain_one_ref,
     gain_two_ref,
     live_ref,
-    mem_ref,
+    first_ref,
+    second_ref,
     ffn_gate_ref,
     ffn_up_ref,
     ffn_down_ref,
@@ -1407,11 +1408,11 @@
     taps_out,
     persist_out,
     live_out,
-    mixed_out,
     key_out,
     value_out,
     total_out,
     state_out,
+    mixed_got,
     normed_out,
     ffn_out,
     ffn_rest,
@@ -1436,6 +1437,10 @@
     state,
     hidden,
     normed_sem,
+    mixed_out,
+    mixed_local,
+    mixed_send,
+    mixed_recv,
     *sems,
 ):
     seqs, lines, share, width = sizes.seqs, sizes.lines, sizes.share, sizes.width
@@ -1458,6 +1463,8 @@
         ffn_relay[to] = ffn_gate_ref[:, to * sizes.slab : (to + 1) * sizes.slab]
     relay[0]()
     outs[0]()
+    relay[2]()
+    relay_line.start()
 
     gate_at, mem_at, rest_at = sizes.gate_at, sizes.mem_at, sizes.rest_at
     pack_rows[...] = jnp.zeros_like(pack_rows)
@@ -1481,10 +1488,10 @@
         chosen = dot_nn(gate, gate_choice(sizes, other, False))
         pack_rows[gate_at : gate_at + share, :HEAD_SIZE] = chosen[:, :HEAD_SIZE]
         for head in range(sizes.heads):
-            first = mem_at + head * sizes.memory
-            pack_rows[first : first + sizes.memory, :] = mem_ref[other * sizes.heads + head].astype(
-                f32
-            )
+            rows = slice(mem_at + head * sizes.memory, mem_at + (head + 1) * sizes.memory)
+            member = other * sizes.heads + head
+            pack_rows[rows, :HEAD_SIZE] = first_ref[member].astype(f32)
+            pack_rows[rows, HEAD_SIZE:] = second_ref[member].astype(f32)
         pack[to] = pack_rows[...].astype(bf16)
     weights[0]()
     gather.start()
@@ -1503,8 +1510,7 @@
     out_gather.start()
     gather.loop(2, gather.step)
     weights_line.rounds(2)
-    relay[2]()
-    relay_line.start()
+    relay_line.round(1)
     cot_gather.start()
     ffn[2]()
     rest_line.start()
@@ -1572,10 +1578,23 @@
 
     lax.fori_loop(0, sizes.chips, work, 0)
 
+    def mixed_own():
+        return pltpu.make_async_copy(mixed_out.at[seq], mixed_got.at[seq], mixed_local.at[0])
+
+    def mixed_copy(to, slot):
+        return pltpu.make_async_remote_copy(
+            src_ref=mixed_out.at[to],
+            dst_ref=mixed_got.at[slot],
+            send_sem=mixed_send.at[to],
+            recv_sem=mixed_recv.at[slot],
+            device_id=(to, line),
+            device_id_type=MESH,
+        )
+
     def segment(n, carry):
         @pl.when(n == 1)
         def _():
-            relay_line.round(1)
+            relay_line.round(2)
 
         @pl.when(n == 2)
         def _():
@@ -1585,10 +1604,6 @@
             cot_gather.step(1)
 
         @pl.when(n == 3)
-        def _():
-            relay_line.round(2)
-
-        @pl.when(n == 4)
         def _():
             rest_line.round(1)
 
@@ -1621,12 +1636,30 @@
             state,
             hidden,
         )
+
+        @pl.when(n == seq)
+        def _():
+            mixed_own().start()
+
+        @pl.when(n != seq)
+        def _():
+            mixed_copy(n, seq).start()
+
         return carry
 
     lax.fori_loop(0, seqs, segment, 0)
     lax.fori_loop(0, sizes.chips, lambda q, carry: (normed_copy(q).wait(), carry)[1], 0)
     out_gather.finish()
     cot_gather.finish()
+
+    def mixed_end(k, carry):
+        i = lax.rem(seq + k, seqs)
+        mixed_copy(i, i).wait_recv()
+        mixed_copy(i, i).wait_send()
+        return carry
+
+    mixed_own().wait()
+    lax.fori_loop(1, seqs, mixed_end, 0)
     weights_line.finish()
     relay_line.rounds(3)
     rest_line.rounds(2)
@@ -1655,9 +1688,9 @@
             shape((seqs, 8, SEG), f32),
             shape((seqs, SEG, LANES), bf16),
             shape((seqs, SEG, LANES), bf16),
-            shape((seqs, SEG, LANES), bf16),
             shape((seqs, SEG, 8), f32),
             shape((seqs, heads, 2, MH, LANES), bf16),
+            shape((seqs, SEG, LANES), bf16),
             shape((seqs, SEG, D), bf16),
             shape((seqs, 2 * sizes.piece, sizes.slab), bf16),
             shape((lines, seqs, 2 * sizes.piece, sizes.slab), bf16),
@@ -1666,8 +1699,8 @@
             shape((seqs, lines, sizes.share, D), bf16),
             shape((seqs, SEG, D), bf16),
         ],
-        in_specs=[any_spec] + [vmem_spec] * 12 + [any_spec] * 2 + [smem_spec] * 2,
-        out_specs=[vmem_spec] * 14 + [any_spec] * 7,
+        in_specs=[any_spec] + [vmem_spec] * 13 + [any_spec] * 2 + [smem_spec] * 2,
+        out_specs=[vmem_spec] * 13 + [any_spec] * 8,
         scratch_shapes=[
             pltpu.VMEM((seqs, SEG, D), bf16),
             pltpu.VMEM((seqs, sizes.weight_rows, LANES), bf16),
@@ -1686,6 +1719,10 @@
             pltpu.VMEM((heads, 2, MH, LANES), f32),
             pltpu.VMEM((SEG, 2 * SEG + LANES), f32),
             dma((sizes.chips,)),
+            pltpu.VMEM((seqs, SEG, LANES), bf16),
+            dma((1,)),
+            dma((seqs,)),
+            dma((seqs,)),
         ]
         + PlaneGather.sems(seqs)
         + [dma((1,)), dma((seqs,)), dma((seqs,))]
@@ -1798,10 +1835,10 @@
         )
 
     axes = (seqs, lines)
-    to_segments = exchange_phases(axes, PLANE, [mixed_ref], [mixed_got], sems[7:10])
+    to_segment = pltpu.make_async_copy(mixed_ref, mixed_got, sems[7].at[0])
     to_heads = exchange_phases(axes, PLANE, [mixed_got], [grad_mixed_ref], sems[10:13])
     greet_all(axes, ("plane",))
-    to_segments[0]()
+    to_segment.start()
     if resident:
         for j in range(chips):
             cot_copy(j, 0).start()
@@ -1838,7 +1875,7 @@
             weight_copy(f + slots).start()
 
     width, copies = sizes.width, sizes.copies
-    to_segments[2]()
+    to_segment.wait()
     for group in range(sizes.groups):
         combined[:, group * width : (group + 1) * width] = mixed_got[group * copies, :, :width]
     middle = token_ref[...].astype(f32) + dot_nn(combined[...], out_ref[...])
@@ -2316,7 +2353,7 @@
             member = other_group * heads + head
             rows = block[first : first + 8]
             second_grad[member] = rows[: sizes.memory, HEAD_SIZE:]
-            first_grad[member] = jnp.transpose(rows)[:HEAD_SIZE, : sizes.memory]
+            first_grad[member] = rows[: sizes.memory, :HEAD_SIZE]
     gate_grad[...] = gates
     bias_grad[0:1, :] = 3.0 * bias[4:5, :HEAD_COUNT]
     bias_grad[1:2, :] = bias[4:5, HEAD_COUNT : 2 * HEAD_COUNT]
@@ -2386,7 +2423,7 @@
             shape((SEG, D), f32),
             shape((share, 3 * D), f32),
             shape((share, 3 * HEAD_COUNT), f32),
-            shape((HEAD_COUNT, HEAD_SIZE, memory), f32),
+            shape((HEAD_COUNT, memory, HEAD_SIZE), f32),
             shape((HEAD_COUNT, memory, HEAD_SIZE), f32),
             shape((4, 3 * share), f32),
             shape((P_SIZE, share), f32),
@@ -2439,7 +2476,6 @@
     sizes = Sizes(lax.axis_size("seq"), lax.axis_size("fsdp"))
     seqs, heads = sizes.seqs, sizes.heads
     length = seqs * SEG
-    memory_pack = jnp.concatenate([memory_w1.transpose(0, 2, 1), memory_w2], axis=2)
     (
         raw,
         gates,
@@ -2450,11 +2486,11 @@
         taps,
         persistent,
         live,
-        mixed,
         keys,
         values,
         totals,
         states,
+        mixed,
         normed,
         _,
         ffn_rest,
@@ -2473,7 +2509,8 @@
         norm1_gain[None],
         norm2_gain[None],
         live_mask,
-        memory_pack,
+        memory_w1.transpose(0, 2, 1),
+        memory_w2,
         ffn_gate,
         ffn_up,
         ffn_down,
@@ -2564,7 +2601,7 @@
         grad_qkv,
         grad_gate,
         grad_conv,
-        grad_first,
+        grad_first.transpose(0, 2, 1),
         grad_second,
         grad_pkeys,
         grad_pvalues,

time: 305 us -> 296 us (0.970)
  Pallas kernels: 287 us -> 282 us
    pallas_call x1, Pallas kernels: 73.1 us -> 69.4 us  [middle_call(): pl.pallas_call(partial(middle_kernel, sizes), out_shape=[shape((SEG, D),...]
  transfers between devices with their start and end apart: 1 -> 1, of which waited for: 0 -> 0; matrix products, arithmetic and copies ran while one was open for 0% -> 0% of each run, Pallas kernels for 20% -> 21%
where the time goes in v6:
time: 296 us
  Pallas kernels  282 us (95%)
  between operations  14.1 us (5%)
    pallas_call x1, Pallas kernels, first_call(): pl.pallas_call(partial(first_kernel, sizes), out_shape=[shape((seqs, SEG,...  101 us
    pallas_call x1, Pallas kernels, middle_call(): pl.pallas_call(partial(middle_kernel, sizes), out_shape=[shape((SEG, D),...  69.4 us
    pallas_call x1, Pallas kernels, mix_backward(): pl.pallas_call(partial(backward_kernel, heads, plan), grid=(count,), in_s...  61.5 us
    pallas_call x1, Pallas kernels, last_call(): pl.pallas_call(partial(last_kernel, sizes), out_shape=[shape((SEG, D), f3...  44.1 us
  transfers between devices with their start and end apart: 1, of which 0 were waited for; matrix products, arithmetic and copies ran while one was open for 0% of the time, Pallas kernels for 21%

profile of v6, /device:TPU:0, one launch (start us, length us, event | category | flops | bytes accessed | tf_op | source)
XLA Modules:
  0.0 295.9 jit_solution(10563999200636953187)
XLA Ops:
  7.2 0.0 reduce-scatter.2.cloned.1.call-start
  7.2 101.2 %first.1 = (bf16[8,256,384]{2,1,0:T(8,128)(2,1)}, f32[8,256,128]{2,1,0:T(8,128)}, bf16[1024,512]{1,0:T(8,128)(2,1)}, bf16[2,256,128]{2,1,0:T(8,128)(2,1)}, bf16[...) custom-call(bf16[256,1024]{1,0:T(8,128)(2,1)} %bitcast.21, ...), custom_call_target="tpu_custom_call" | custom-call | tf_op jit(solution)/shard_map/first/pallas_call | solution.py:1677
  108.4 69.4 %middle.1 = (f32[256,1024]{1,0:T(8,128)}, f32[256,1024]{1,0:T(8,128)}, f32[1,1024]{1,0:T(1,128)}, bf16[8,128,1024]{2,1,0:T(8,128)(2,1)}, bf16[8,256,128]{2,1,0:T...) custom-call(bf16[8,256,128]{2,1,0:T(8,128)(2,1)} %get-tuple-element.77.mixed_ref, ...), custom_call_target="tpu_custom_call" | custom-call | tf_op jit(solution)/shard_map/middle/pallas_call | solution.py:2044
  177.9 0.0 reduce-scatter.2.cloned.1.call-update
  177.9 61.5 %mix_backward.1 = (bf16[2048,512]{1,0:T(8,128)(2,1)}, f32[2,256,128]{2,1,0:T(8,128)}, f32[8,384]{1,0:T(8,128)}, f32[32,128]{1,0:T(8,128)}, f32[8,128]{1,0:T(8,12...) custom-call(bf16[2048,384]{1,0:T(8,128)(2,1)} %bitcast.19, bf16[2048,384]{1,0:T(8,128)(2,1)} %bitcast.20, ...), custom_call_target="tpu_custom_call" | custom-call | tf_op jit(solution)/shard_map/mix_backward/pallas_call | solution.py:635
  239.4 0.0 reduce-scatter.2.cloned.1.call-done
  239.5 44.1 %last.1 = (f32[256,1024]{1,0:T(8,128)}, bf16[8,160,128]{2,1,0:T(8,128)(2,1)}, bf16[4,32,1024]{2,1,0:T(8,128)(2,1)}, f32[4,32,128]{2,1,0:T(8,128)}, bf16[8,384,128]{2,1,0:T(8,128)(2,1)}) custom-call(bf16[8,256,512]{2,1,0:T(8,128)(2,1)} %bitcast.28, bf16[8,256,1024]{2,1,0:T(8,128)(2,1)} %get-tuple-element.91.normed_ref, ...), custom_call_target="tpu_custom_call" | custom-call | tf_op jit(solution)/shard_map/last/pallas_call | solution.py:2379
  283.6 5.5 %unpack.1 = (bf16[256,1024]{1,0:T(8,128)(2,1)}, f32[256,1024]{1,0:T(8,128)}, f32[32,3072]{1,0:T(8,128)}, f32[32,48]{1,0:T(8,128)}, f32[16,8,64]{2,1,0:T(8,128)},...) custom-call(f32[256,1024]{1,0:T(8,128)} %get-tuple-element.100.sum_r, ...), custom_call_target="tpu_custom_call" | custom-call | tf_op jit(solution)/shard_map/unpack/pallas_call | solution.py:2419
Async XLA Ops:
  7.2 232.3 %reduce-scatter.2.cloned.1.call-start = ((), (), s32[]{:S(2)}) async-start(), calls=%async_computation.1 | async-start | bytes 3932160 | tf_op jit(solution)/shard_map/reduce_scatter | solution.py:2534
Sparse Core Ops, SparseCore 0:
  178.0 59.4 reduce-scatter.1

commit v7 on v6

--- a/solution.py
+++ b/solution.py
@@ -1987,19 +1987,6 @@
         loop(1, chips, forth)
         cot_copy(1, 1).start()
         loop(1, chips, weigh)
-    for f in range(lines):
-        if f >= slots:
-            grad_copy(f - slots).wait()
-        columns = slice(f * slab, (f + 1) * slab)
-        up_columns = slice(hidden_size + f * slab, hidden_size + (f + 1) * slab)
-        for s in range(seqs):
-            rows = slice(s * piece, (s + 1) * piece)
-            blocks[f % slots, s, :piece, :] = both_grad[rows, columns].astype(bf16)
-            blocks[f % slots, s, piece : 2 * piece, :] = both_grad[rows, up_columns].astype(bf16)
-            blocks[f % slots, s, 2 * piece :, :] = down_grad[rows, columns].astype(bf16)
-        grad_copy(f).start()
-    for f in range(lines - slots, lines):
-        grad_copy(f).wait()
     loop(chips - 2, chips, lambda j: down_copy(j).wait())
     gather.finish()
     loop(chips - 2, chips, lambda j: to_pair(j).wait_send())
@@ -2026,6 +2013,19 @@
         first = to // copies * width
         mixed_got[to, :, :width] = grad_combined[:, first : first + width]
     to_heads[0]()
+    for f in range(lines):
+        if f >= slots:
+            grad_copy(f - slots).wait()
+        columns = slice(f * slab, (f + 1) * slab)
+        up_columns = slice(hidden_size + f * slab, hidden_size + (f + 1) * slab)
+        for s in range(seqs):
+            rows = slice(s * piece, (s + 1) * piece)
+            blocks[f % slots, s, :piece, :] = both_grad[rows, columns].astype(bf16)
+            blocks[f % slots, s, piece : 2 * piece, :] = both_grad[rows, up_columns].astype(bf16)
+            blocks[f % slots, s, 2 * piece :, :] = down_grad[rows, columns].astype(bf16)
+        grad_copy(f).start()
+    for f in range(lines - slots, lines):
+        grad_copy(f).wait()
     out_grad = dot_tn(combined[...], branch).astype(bf16)
     out_grad_ref[...] = out_grad.reshape(seqs, piece, D)
     to_heads[2]()
@@ -2162,6 +2162,10 @@
         )
 
     axes = (seqs, lines)
+    resident = chips <= 4
+    all_normed = pltpu.make_async_copy(normed_ref, normed_slot, normed_sem.at[0])
+    if resident:
+        all_normed.start()
     greet_all(axes, ("plane", "line"))
     ffn = exchange_phases(axes, PLANE, [ffn_ref], [ffn_got], sems[0:3])
     outs = exchange_phases(
@@ -2170,7 +2174,6 @@
     grads = exchange_phases(
         axes, MERGE, [pack], [pack_got], [pack_landed, pack_sums, *sems[9:16]]
     )
-    normed_copy(0, 0).start()
     ffn[0]()
 
     def gather_grad(q):
@@ -2192,7 +2195,13 @@
         def _():
             matrix_grad[...] += new
 
-    loop(0, chips, gather_grad)
+    if resident:
+        all_normed.wait()
+        rows = normed_slot[...].reshape(seqs * SEG, D)
+        matrix_grad[...] = dot_tn(rows, grad_ref[...].reshape(seqs * SEG, 4 * LANES))
+    else:
+        normed_copy(0, 0).start()
+        loop(0, chips, gather_grad)
     mem_at, rest_at = sizes.grad_mem_at, sizes.grad_rest_at
     pack_rows[...] = jnp.zeros_like(pack_rows)
     for tap in range(4):
@@ -2388,7 +2397,7 @@
         in_specs=in_specs,
         out_specs=[vmem_spec] + [any_spec] * 4,
         scratch_shapes=[
-            pltpu.VMEM((2, 2, SEG, D), bf16),
+            pltpu.VMEM((seqs, SEG, D) if chips <= 4 else (2, 2, SEG, D), bf16),
             pltpu.VMEM((D, 4 * LANES), f32),
             pltpu.VMEM(pack_shape, bf16),
             pltpu.VMEM(pack_shape[2:], f32),

time: 296 us -> 294 us (level)
  no operation moved by 1% of the time
where the time goes in v7:
time: 294 us
  Pallas kernels  280 us (95%)
  between operations  14.1 us (5%)
    pallas_call x1, Pallas kernels, first_call(): pl.pallas_call(partial(first_kernel, sizes), out_shape=[shape((seqs, SEG,...  101 us
    pallas_call x1, Pallas kernels, middle_call(): pl.pallas_call(partial(middle_kernel, sizes), out_shape=[shape((SEG, D),...  69.3 us
    pallas_call x1, Pallas kernels, mix_backward(): pl.pallas_call(partial(backward_kernel, heads, plan), grid=(count,), in_s...  61.5 us
    pallas_call x1, Pallas kernels, last_call(): pl.pallas_call(partial(last_kernel, sizes), out_shape=[shape((SEG, D), f3...  42.3 us
  transfers between devices with their start and end apart: 1, of which 0 were waited for; matrix products, arithmetic and copies ran while one was open for 0% of the time, Pallas kernels for 21%

profile of v7, /device:TPU:0, one launch (start us, length us, event | category | flops | bytes accessed | tf_op | source)
XLA Modules:
  0.0 293.9 jit_solution(17857998577690551137)
XLA Ops:
  7.2 0.0 reduce-scatter.2.cloned.1.call-start
  7.2 101.2 %first.1 = (bf16[8,256,384]{2,1,0:T(8,128)(2,1)}, f32[8,256,128]{2,1,0:T(8,128)}, bf16[1024,512]{1,0:T(8,128)(2,1)}, bf16[2,256,128]{2,1,0:T(8,128)(2,1)}, bf16[...) custom-call(bf16[256,1024]{1,0:T(8,128)(2,1)} %bitcast.21, ...), custom_call_target="tpu_custom_call" | custom-call | tf_op jit(solution)/shard_map/first/pallas_call | solution.py:1677
  108.4 69.3 %middle.1 = (f32[256,1024]{1,0:T(8,128)}, f32[256,1024]{1,0:T(8,128)}, f32[1,1024]{1,0:T(1,128)}, bf16[8,128,1024]{2,1,0:T(8,128)(2,1)}, bf16[8,256,128]{2,1,0:T...) custom-call(bf16[8,256,128]{2,1,0:T(8,128)(2,1)} %get-tuple-element.77.mixed_ref, ...), custom_call_target="tpu_custom_call" | custom-call | tf_op jit(solution)/shard_map/middle/pallas_call | solution.py:2044
  177.7 0.0 reduce-scatter.2.cloned.1.call-update
  177.8 61.5 %mix_backward.1 = (bf16[2048,512]{1,0:T(8,128)(2,1)}, f32[2,256,128]{2,1,0:T(8,128)}, f32[8,384]{1,0:T(8,128)}, f32[32,128]{1,0:T(8,128)}, f32[8,128]{1,0:T(8,12...) custom-call(bf16[2048,384]{1,0:T(8,128)(2,1)} %bitcast.19, bf16[2048,384]{1,0:T(8,128)(2,1)} %bitcast.20, ...), custom_call_target="tpu_custom_call" | custom-call | tf_op jit(solution)/shard_map/mix_backward/pallas_call | solution.py:635
  239.3 0.0 reduce-scatter.2.cloned.1.call-done
  239.3 42.3 %last.1 = (f32[256,1024]{1,0:T(8,128)}, bf16[8,160,128]{2,1,0:T(8,128)(2,1)}, bf16[4,32,1024]{2,1,0:T(8,128)(2,1)}, f32[4,32,128]{2,1,0:T(8,128)}, bf16[8,384,128]{2,1,0:T(8,128)(2,1)}) custom-call(bf16[8,256,512]{2,1,0:T(8,128)(2,1)} %bitcast.28, bf16[8,256,1024]{2,1,0:T(8,128)(2,1)} %get-tuple-element.91.normed_ref, ...), custom_call_target="tpu_custom_call" | custom-call | tf_op jit(solution)/shard_map/last/pallas_call | solution.py:2388
  281.6 5.5 %unpack.1 = (bf16[256,1024]{1,0:T(8,128)(2,1)}, f32[256,1024]{1,0:T(8,128)}, f32[32,3072]{1,0:T(8,128)}, f32[32,48]{1,0:T(8,128)}, f32[16,8,64]{2,1,0:T(8,128)},...) custom-call(f32[256,1024]{1,0:T(8,128)} %get-tuple-element.100.sum_r, ...), custom_call_target="tpu_custom_call" | custom-call | tf_op jit(solution)/shard_map/unpack/pallas_call | solution.py:2428
Async XLA Ops:
  7.2 232.1 %reduce-scatter.2.cloned.1.call-start = ((), (), s32[]{:S(2)}) async-start(), calls=%async_computation.1 | async-start | bytes 3932160 | tf_op jit(solution)/shard_map/reduce_scatter | solution.py:2543
Sparse Core Ops, SparseCore 0:
  177.9 59.4 reduce-scatter.1
